TPU v7x, 32 devices: a whole 2x2x4 slice. The times are simulated.
32 devices in a mesh: ctx: 16 (over z, x, core), head: 2 (over y).
Axes of the slice: x: 2, y: 2, z: 4, core: 2. Of those that a mesh axis runs over, the one named last changes fastest.
Arguments:
- queries: bfloat16 [4096, 3072], P(('ctx', 'head')), may hold values from -48 to 48
- key_rows: bfloat16 [4096, 3072], P(('ctx', 'head')), may hold values from -6 to 6
- value_rows: bfloat16 [4096, 3072], P(('ctx', 'head')), may hold values from -6 to 6
- out_cotangent: bfloat16 [4096, 3072], P(('ctx', 'head')), may hold values from -6 to 6
- gate_table: float32 [128, 3072], replicated, may hold values from -6 to 6
- span_ids: int32 [4096], replicated, may hold values from 0 to 23, never falling along the last dimension, each value on 1 to 256 neighbouring positions
- noise_level: int32 [24], replicated, may hold values from 0 to 127
- block_mask: int32 [24, 24], replicated, may hold values from 0 to 1, as said below
Outputs:
- mixed_out: bfloat16 [4096, 3072], P(('ctx', 'head'))
- query_grad: bfloat16 [4096, 3072], P(('ctx', 'head'))
- key_grad: bfloat16 [4096, 3072], P(('ctx', 'head'))
- value_grad: bfloat16 [4096, 3072], P(('ctx', 'head'))
- gate_grad: float32 [128, 3072], replicated
Inputs may be any that keep to these rules, and one draw needn't show every extreme that they name: `span_ids`: span ids never fall along the tokens; every span holds 1 to 256 tokens, one span exactly 256. `block_mask`: entries are 0 or 1; entries [c, c] and [c, c - 1] are 1 for every span c.
All inputs are finite; a program needn't handle non-finite values.
Results may differ from a plain program's by a relative error of at most 0.023.
Values may be sent and summed in bfloat16 or wider, within the bound.
No kernel may reach another device: no remote copies, remote signals or barrier semaphores. Data moves between devices by JAX's collectives and lax.ppermute only.
A program may use at most 128 MiB of HBM per device.

v0:
```python
import functools
import math

import jax
import jax.numpy as jnp
from jax import lax
from jax.experimental import pallas as pl
from jax.experimental.pallas import tpu as pltpu
from jax.sharding import PartitionSpec as P

DH = 128
HIDDEN = -1e30
LOG2E = 1.4426950408889634


def other_ctx(c, near):
    odd = lax.rem(c, 2)
    return c + 1 - 2 * odd if near else c - 1 + 2 * odd


def prep_kernel(
    place_ref, span_ref, noise_ref, mask_ref, table_ref, bias_ref, gate_ref, slot_ref, *, sizes
):
    ctx_count, groups, rows, span_total, level_count, by_span = sizes
    c, h = place_ref[0], place_ref[1]
    tokens = groups * rows
    total = ctx_count * tokens
    bf16, f32 = jnp.bfloat16, jnp.float32

    def block_of(ctx, k):
        return ctx * groups + lax.rem(h - k + groups, groups)

    def spans_of(ctx, k):
        at = jnp.clip(ctx, 0, ctx_count - 1)
        return span_ref[pl.ds(block_of(at, k), 1), :]

    def as_column(row):
        return jnp.broadcast_to(row.astype(f32), (rows, rows)).T[:, :1].astype(jnp.int32)

    across = lax.broadcasted_iota(jnp.int32, (1, rows), 1)
    down = lax.broadcasted_iota(jnp.int32, (rows, 1), 0)
    span_lane = lax.broadcasted_iota(jnp.int32, (rows, span_total), 1)
    span_down = lax.broadcasted_iota(jnp.int32, (span_total, rows), 0)
    level_lane = lax.broadcasted_iota(jnp.int32, (rows, level_count), 1)
    query_span = [spans_of(c, k) for k in range(groups)]
    query_pos = [block_of(c, k) * rows + across for k in range(groups)]
    mask_low = mask_ref[...].astype(bf16)
    allowed_q = [
        lax.dot_general(
            mask_low,
            (span_down == row).astype(bf16),
            (((0,), (0,)), ((), ())),
            preferred_element_type=f32,
        ).astype(bf16)
        for row in query_span
    ]
    noise = noise_ref[...].astype(f32)
    for i, ctx in enumerate((c, other_ctx(c, True), other_ctx(c, False))):
        for k in range(groups):
            key_span = as_column(spans_of(ctx, k))
            key_pos = block_of(ctx, k) * rows + down
            valid = (key_pos >= 0) & (key_pos < total)
            onehot = key_span == span_lane
            at = slice((i * groups + k) * rows, (i * groups + k + 1) * rows)
            for p in range(groups):
                allowed = jnp.dot(
                    onehot.astype(bf16), allowed_q[p], preferred_element_type=f32
                )
                visible = (
                    (allowed > 0.5)
                    & (key_span <= query_span[p])
                    & (query_pos[p] - key_pos < tokens)
                    & valid
                )
                bias_ref[at, p * rows : (p + 1) * rows] = jnp.where(visible, 0.0, HIDDEN)
            if i > 0:
                continue
            level = jnp.sum(jnp.where(onehot, noise, 0.0), axis=1, keepdims=True)
            level_onehot = (level.astype(jnp.int32) == level_lane).astype(f32)
            gate_ref[at, :] = jnp.dot(
                level_onehot,
                table_ref[...],
                precision=lax.Precision.HIGHEST,
                preferred_element_type=f32,
            )
            if by_span:
                slot_ref[:, at] = (span_down == query_span[k]).astype(bf16)
            else:
                slot_ref[:, at] = level_onehot.T.astype(bf16)


def attention_kernel(
    place_ref,
    q_ref, k_ref, v_ref, o_ref,
    qo_ref, kv_ref,
    near_own_ref, near_far_ref, side_own_ref, side_far_ref,
    gate_ref, bias_ref, slot_ref,
    mixed_ref, dq_ref, back_ref,
    own_ref, far_ref, near_ref, side_grad_own_ref, side_grad_far_ref,
    sums_ref,
    *, rows, tokens, q_size, heads,
):
    scale = 1.0 / math.sqrt(DH)
    bf16, f32 = jnp.bfloat16, jnp.float32
    tile = 32

    def dot(left, right, left_dim, right_dim):
        return lax.dot_general(
            left, right, (((left_dim,), (right_dim,)), ((), ())), preferred_element_type=f32
        )

    def load(j):
        at = slice(j * DH, (j + 1) * DH)
        keys, values = [k_ref[:, at], kv_ref[0, :, at]], [v_ref[:, at], kv_ref[1, :, at]]
        for ref in (near_own_ref, near_far_ref, side_own_ref, side_far_ref):
            keys.append(ref[0, :, at])
            values.append(ref[1, :, at])
        keys, values = jnp.concatenate(keys, axis=0), jnp.concatenate(values, axis=0)
        queries = jnp.concatenate([q_ref[:, at], qo_ref[0, :, at]], axis=0)
        cotangent = jnp.concatenate([o_ref[:, at], qo_ref[1, :, at]], axis=0)
        blocks = []
        for start in range(0, tokens, q_size):
            span = slice(start, start + q_size)
            q, o = queries[span], cotangent[span].astype(f32)
            gate = gate_ref[span, at]
            g = (gate * o).astype(bf16)
            blocks.append((q, o, gate, g, dot(keys, q, 1, 1), dot(values, g, 1, 1)))
        return keys, values, blocks

    def work(j, keys, values, blocks):
        at = slice(j * DH, (j + 1) * DH)
        keys_t, values_t = keys.T, values.T
        key_grad = value_grad = sums = None
        for number, (q, o, gate, g, scores, prob_grad) in enumerate(blocks):
            start = number * q_size
            span = slice(start, start + q_size)
            count = scores.shape[0]
            tiles = [slice(r, r + tile) for r in range(0, count, tile)]
            raised, top = [], None
            for t in tiles:
                part = scores[t] * (scale * LOG2E) + bias_ref[t, span]
                raised.append(part)
                high = jnp.max(part.reshape(tile // 8, 8, q_size), axis=0)
                top = high if top is None else jnp.maximum(top, high)
            top = jnp.max(top, axis=0, keepdims=True)
            total = None
            for i in range(len(tiles)):
                raised[i] = jnp.exp2(raised[i] - top)
                part = jnp.sum(raised[i].reshape(tile // 8, 8, q_size), axis=0)
                total = part if total is None else total + part
            inverse = 1.0 / jnp.sum(total, axis=0, keepdims=True)
            low = jnp.concatenate([(part * inverse).astype(bf16) for part in raised], axis=0)
            attended_t = dot(values_t, low, 1, 0).astype(bf16)
            row_dot = jnp.sum(g.T.astype(f32) * attended_t.astype(f32), axis=0, keepdims=True)
            attended = attended_t.T.astype(f32)
            score_grad = jnp.concatenate(
                [
                    (part * ((prob_grad[t] - row_dot) * inverse)).astype(bf16)
                    for part, t in zip(raised, tiles)
                ],
                axis=0,
            )
            query_grad = (dot(keys_t, score_grad, 1, 0) * scale).astype(bf16).T
            mixed = (gate * attended).astype(bf16)
            if start == 0:
                mixed_ref[:, at] = mixed[:rows]
                dq_ref[:, at] = query_grad[:rows]
                back_ref[0, : q_size - rows, at] = mixed[rows:]
                back_ref[1, : q_size - rows, at] = query_grad[rows:]
            else:
                back_ref[0, start - rows : start - rows + q_size, at] = mixed
                back_ref[1, start - rows : start - rows + q_size, at] = query_grad
            dk, dv = dot(score_grad, q, 1, 0), dot(low, g, 1, 0)
            product = o * attended
            high = product.astype(bf16)
            rest = (product - high.astype(f32)).astype(bf16)
            both = dot(slot_ref[:, span], jnp.concatenate([high, rest], axis=1), 1, 0)
            part = both[:, :DH] + both[:, DH:]
            key_grad = dk if key_grad is None else key_grad + dk
            value_grad = dv if value_grad is None else value_grad + dv
            sums = part if sums is None else sums + part
        sums_ref[:, at] = sums
        for i, grad in ((0, key_grad * scale), (1, value_grad)):
            own_ref[i, :, at] = grad[:rows]
            far_ref[i, :, at] = grad[rows:tokens]
            low = grad[tokens:].astype(bf16)
            near_ref[i, :, at] = low[:tokens]
            side_grad_own_ref[i, :, at] = low[tokens : tokens + rows]
            side_grad_far_ref[i, :, at] = low[tokens + rows :]

    ready = load(0)
    for j in range(heads):
        following = load(j + 1) if j + 1 < heads else None
        work(j, *ready)
        ready = following


def per_device(
    queries, key_rows, value_rows, out_cotangent, gate_table, span_ids, noise_level, block_mask
):
    groups = lax.axis_size("head")
    ctx_count = lax.axis_size("ctx")
    rows, full_width = queries.shape
    width = full_width // groups
    heads = width // DH
    tokens = rows * groups
    far_rows = tokens - rows
    span_total = noise_level.shape[0]
    level_count = gate_table.shape[0]
    by_span = span_total <= level_count // 2
    slots = span_total if by_span else level_count
    c = lax.axis_index("ctx")
    h = lax.axis_index("head")
    place = jnp.stack([c, h]).astype(jnp.int32)
    bf16, f32 = jnp.bfloat16, jnp.float32

    near_pairs = [(i, i ^ 1) for i in range(ctx_count)]
    side_pairs = [
        (i, i - 1 + 2 * (i % 2)) for i in range(ctx_count) if 0 <= i - 1 + 2 * (i % 2) < ctx_count
    ]

    def columns(array, group):
        return lax.dynamic_slice_in_dim(array, group * width, width, 1)

    def to_peers(first, second, after=None):
        parts = []
        for k in range(1, groups):
            group = lax.rem(h + k, groups)
            slab = jnp.stack([columns(first, group), columns(second, group)])
            if after is not None:
                slab, _ = lax.optimization_barrier((slab, after))
            pairs = [(i, (i + k) % groups) for i in range(groups)]
            parts.append(lax.ppermute(slab, "head", pairs))
        return parts[0] if groups == 2 else jnp.concatenate(parts, axis=1)

    def from_peers(slab):
        parts = []
        for k in range(1, groups):
            part = slab if groups == 2 else slab[:, (k - 1) * rows : k * rows]
            pairs = [(i, (i - k) % groups) for i in range(groups)]
            parts.append(lax.ppermute(part, "head", pairs))
        return parts

    kv_far = to_peers(key_rows, value_rows)
    kv_own = jnp.stack([columns(key_rows, h), columns(value_rows, h)])
    side_own = lax.ppermute(kv_own, "ctx", side_pairs)
    near_own = lax.ppermute(kv_own, "ctx", near_pairs)
    side_far = lax.ppermute(kv_far, "ctx", side_pairs)
    near_far = lax.ppermute(kv_far, "ctx", near_pairs)
    qo_far = to_peers(queries, out_cotangent, kv_far)

    limit = (28 if tokens <= 256 else 56) * 1024 * 1024
    params = pltpu.CompilerParams(vmem_limit_bytes=limit)
    sizes = (ctx_count, groups, rows, span_total, level_count, by_span)
    whole = lambda shape: pl.BlockSpec(shape, lambda i, place: (0,) * len(shape))
    bias, gate, slot = pl.pallas_call(
        functools.partial(prep_kernel, sizes=sizes),
        grid_spec=pltpu.PrefetchScalarGridSpec(
            num_scalar_prefetch=1,
            grid=(1,),
            in_specs=[
                whole((ctx_count * groups, rows)),
                whole((1, span_total)),
                whole((span_total, span_total)),
                pl.BlockSpec((level_count, width), lambda i, place: (0, place[1])),
            ],
            out_specs=[
                whole((3 * tokens, tokens)),
                whole((tokens, width)),
                whole((slots, tokens)),
            ],
        ),
        out_shape=[
            jax.ShapeDtypeStruct((3 * tokens, tokens), f32),
            jax.ShapeDtypeStruct((tokens, width), f32),
            jax.ShapeDtypeStruct((slots, tokens), bf16),
        ],
        compiler_params=params,
        name="prep",
    )(
        place,
        span_ids.reshape(ctx_count * groups, rows),
        noise_level.reshape(1, span_total),
        block_mask,
        gate_table,
    )

    batch = next(n for n in (4, 3, 2, 1) if heads % n == 0) if tokens <= 256 else 1
    steps = heads // batch
    own_block = pl.BlockSpec((rows, batch * DH), lambda i, place: (0, place[1] * steps + i))
    pair = lambda count: pl.BlockSpec((2, count, batch * DH), lambda i, place: (0, 0, i))
    column = lambda count: pl.BlockSpec((count, batch * DH), lambda i, place: (0, i))
    q_size = min(256, tokens)
    flops = 6 * 2 * tokens * 3 * tokens * DH * heads
    (mixed, query_grad, back, own, far, near_grad, side_grad_own, side_grad_far, sums) = (
        pl.pallas_call(
            functools.partial(
                attention_kernel, rows=rows, tokens=tokens, q_size=q_size, heads=batch
            ),
            grid_spec=pltpu.PrefetchScalarGridSpec(
                num_scalar_prefetch=1,
                grid=(steps,),
                in_specs=[
                    own_block, own_block, own_block, own_block,
                    pair(far_rows), pair(far_rows),
                    pair(rows), pair(far_rows), pair(rows), pair(far_rows),
                    column(tokens), whole((3 * tokens, tokens)), whole((slots, tokens)),
                ],
                out_specs=[
                    own_block, own_block, pair(far_rows),
                    pair(rows), pair(far_rows), pair(tokens), pair(rows), pair(far_rows),
                    column(slots),
                ],
            ),
            out_shape=[
                jax.ShapeDtypeStruct((rows, full_width), bf16),
                jax.ShapeDtypeStruct((rows, full_width), bf16),
                jax.ShapeDtypeStruct((2, far_rows, width), bf16),
                jax.ShapeDtypeStruct((2, rows, width), f32),
                jax.ShapeDtypeStruct((2, far_rows, width), f32),
                jax.ShapeDtypeStruct((2, tokens, width), bf16),
                jax.ShapeDtypeStruct((2, rows, width), bf16),
                jax.ShapeDtypeStruct((2, far_rows, width), bf16),
                jax.ShapeDtypeStruct((slots, width), f32),
            ],
            compiler_params=params,
            cost_estimate=pl.CostEstimate(
                flops=flops, bytes_accessed=16 * tokens * width, transcendentals=0
            ),
            name="attention",
        )(
            place,
            queries, key_rows, value_rows, out_cotangent,
            qo_far, kv_far,
            near_own, near_far, side_own, side_far,
            gate, bias, slot,
        )
    )

    side_back_far = lax.ppermute(side_grad_far, "ctx", side_pairs)
    near_back = lax.ppermute(near_grad, "ctx", near_pairs)
    back_parts = from_peers(back)
    side_back_own = lax.ppermute(side_grad_own, "ctx", side_pairs)
    far_sum = lax.optimization_barrier(far + near_back[:, rows:].astype(f32))
    far_grad = (far_sum + side_back_far.astype(f32)).astype(bf16)
    grad_parts = from_peers(far_grad)
    own_grad = (
        own + near_back[:, :rows].astype(f32) + side_back_own.astype(f32)
    ).astype(bf16)

    slot_sums = sums
    for step in (1 << n for n in range(ctx_count.bit_length() - 1)):
        pairs = [(i, i ^ step) for i in range(ctx_count)]
        slot_sums = slot_sums + lax.ppermute(slot_sums, "ctx", pairs)
    for step in (1 << n for n in range(groups.bit_length() - 1)):
        pairs = [(i, i ^ step) for i in range(groups)]
        other = lax.ppermute(slot_sums, "head", pairs)
        slot_sums = jnp.where(
            (h // step) % 2 == 0,
            jnp.concatenate([slot_sums, other], axis=1),
            jnp.concatenate([other, slot_sums], axis=1),
        )
    if by_span:
        level_onehot = (
            jnp.arange(level_count, dtype=jnp.int32)[:, None] == noise_level[None, :]
        ).astype(f32)
        gate_grad = jnp.dot(level_onehot, slot_sums, precision=lax.Precision.HIGHEST)
    else:
        gate_grad = slot_sums

    def placed(array, part, k):
        group = lax.rem(h + k, groups)
        return lax.dynamic_update_slice_in_dim(array, part, group * width, 1)

    key_grad = placed(jnp.zeros((rows, full_width), bf16), own_grad[0], 0)
    value_grad = placed(jnp.zeros((rows, full_width), bf16), own_grad[1], 0)
    for k in range(1, groups):
        mixed = placed(mixed, back_parts[k - 1][0], k)
        query_grad = placed(query_grad, back_parts[k - 1][1], k)
        key_grad = placed(key_grad, grad_parts[k - 1][0], k)
        value_grad = placed(value_grad, grad_parts[k - 1][1], k)
    return (mixed, query_grad, key_grad, value_grad, gate_grad)


def solution(mesh):
    sharded = P(("ctx", "head"), None)
    return jax.shard_map(
        per_device,
        mesh=mesh,
        in_specs=(sharded,) * 4 + (P(),) * 4,
        out_specs=(sharded,) * 4 + (P(),),
        check_vma=False,
    )
```

profile of v0, /device:TPU:6, one launch (start us, length us, event | category | flops | bytes accessed | tf_op | source)
XLA Modules:
  0.0 144.6 jit_solution(8472662658422990783)
XLA Ops:
  0.6 1.5 %dynamic-slice_bitcast_fusion = (bf16[1,128,1536]{2,1,0:T(8,128)(2,1)S(1)}, bf16[1,128,1536]{2,1,0:T(8,128)(2,1)S(1)}, bf16[1,128,1536]{2,1,0:T(8,128)(2,1)S(1)}, bf16[1,128,1536]{2,1,0:T(8,128)(2,1)S(1)}) fusion(bf16[128,3072]{1,0:T(8,128)(2,1)} %v_ref.1, s32[]{:T(128)S(6)} %select_n.36, s32[]{:T(128)S(6)} %select_n.35, bf16[128,3072]{1,0:T(8,128)(2,1)} %k_ref.1), kind=kLoop, calls=%fused_computation.18 | loop fusion | bytes 3145736 | tf_op jit(solution)/shard_map/stack | solution.py:245
  2.1 0.0 copy-start.3
  2.1 0.0 copy-start.5
  2.1 0.1 pad_maximum_fusion.1
  2.2 0.6 collective-permute-start
  2.8 0.9 pad_maximum_fusion.2
  3.7 0.1 collective-permute-start.2
  3.8 2.1 %collective-permute-start.4 = (bf16[2,128,1536]{2,1,0:T(8,128)(2,1)}, bf16[2,128,1536]{2,1,0:T(8,128)(2,1)}, u32[]{:S(2)}, u32[]{:S(2)}) collective-permute-start(bf16[2,128,1536]{2,1,0:T(8,128)(2,1)} %pad_maximum_fusion.2), channel_id=1, source_target_pairs={{2,4},{4,2},{6,8},{8,6},{10,12},{12,10},{14,16},{16,14},{18,20},{2... | collective-permute-start | bytes 2359304 | tf_op jit(solution)/shard_map/ppermute | solution.py:246
  5.9 0.1 dynamic-slice_bitcast_fusion.4
  6.0 0.9 pad_maximum_fusion
  6.9 14.6 %collective-permute-done.kv_ref = bf16[2,128,1536]{2,1,0:T(8,128)(2,1)S(1)} collective-permute-done((bf16[2,128,1536]{2,1,0:T(8,128)(2,1)S(1)}, bf16[2,128,1536]{2,1,0:T(8,128)(2,1)S(1)}, u32[]{:S(2)}, u32[]{:S(2)}) %collective-permute-start) | collective-permute-done | bytes 786464 | tf_op jit(solution)/shard_map/ppermute | solution.py:233
  21.6 0.5 collective-permute-start.1
  22.1 0.0 collective-permute-start.3
  22.1 2.3 %collective-permute-start.5 = (bf16[2,128,1536]{2,1,0:T(8,128)(2,1)S(1)}, bf16[2,128,1536]{2,1,0:T(8,128)(2,1)}, u32[]{:S(2)}, u32[]{:S(2)}) collective-permute-start(bf16[2,128,1536]{2,1,0:T(8,128)(2,1)S(1)} %collective-permute-done.kv_ref), channel_id=1, source_target_pairs={{2,4},{4,2},{6,8},{8,6},{10,12},{12,10},{14,16},{16,14},{18,20},{2... | collective-permute-start | bytes 2359304 | tf_op jit(solution)/shard_map/ppermute | solution.py:248
  24.4 0.1 pad_add_fusion.place_ref
  24.5 2.4 %prep.1 = (f32[768,256]{1,0:T(8,128)S(1)}, f32[256,1536]{1,0:T(8,128)S(1)}, bf16[24,256]{1,0:T(8,128)(2,1)S(1)}) custom-call(s32[2]{0:T(128)S(1)} %pad_add_fusion.place_ref, s32[32,128]{1,0:T(8,128)S(1)} %bitcast.40, s32[1,24]{1,0:T(1,128)S(1)} %bitcast.41, s32[24,24]{1,0:T(8,128)S(1)} %copy-done.8, f32[128,3072]{1,0:T(8,128)S(1)} %copy-done), custom_call_target="tpu_custom_call" | custom-call | tf_op jit(solution)/shard_map/prep/pallas_call | solution.py:256
  26.9 0.0 collective-permute-done.2.near_own_ref
  26.9 0.0 copy-start.13
  26.9 0.9 copy-done.13
  27.8 0.0 collective-permute-done.4.side_own_ref
  27.8 12.6 %collective-permute-done.1.qo_ref = bf16[2,128,1536]{2,1,0:T(8,128)(2,1)} collective-permute-done((bf16[2,128,1536]{2,1,0:T(8,128)(2,1)}, bf16[2,128,1536]{2,1,0:T(8,128)(2,1)}, u32[]{:S(2)}, u32[]{:S(2)}) %collective-permute-start.1) | collective-permute-done | bytes 786464 | tf_op jit(solution)/shard_map/ppermute | solution.py:233
  40.4 0.0 collective-permute-done.3.near_far_ref
  40.4 3.5 %collective-permute-done.5.side_far_ref = bf16[2,128,1536]{2,1,0:T(8,128)(2,1)} collective-permute-done((bf16[2,128,1536]{2,1,0:T(8,128)(2,1)S(1)}, bf16[2,128,1536]{2,1,0:T(8,128)(2,1)}, u32[]{:S(2)}, u32[]{:S(2)}) %collective-permute-start.5) | collective-permute-done | bytes 786464 | tf_op jit(solution)/shard_map/ppermute | solution.py:248
  43.9 1.1 copy-done.1
  45.0 1.1 copy-done.2
  46.2 1.1 copy-done.4
  47.3 1.1 copy-done.6
  48.4 1.1 copy-done.12
  49.6 1.1 copy-done.14
  50.7 15.6 %attention.1 = (bf16[128,3072]{1,0:T(8,128)(2,1)}, bf16[128,3072]{1,0:T(8,128)(2,1)}, bf16[2,128,1536]{2,1,0:T(8,128)(2,1)}, f32[2,128,1536]{2,1,0:T(8,128)S(1)}...) custom-call(s32[2]{0:T(128)S(1)} %pad_add_fusion.place_ref, ...), custom_call_target="tpu_custom_call" | custom-call | flops 3623878656 | bytes 6291456 | tf_op jit(solution)/shard_map/attention/pallas_call | solution.py:296
  66.4 0.9 copy-done.10
  67.2 0.0 collective-permute-start.7
  67.2 0.5 collective-permute-start.11
  67.8 2.7 %collective-permute-done.11 = f32[24,1536]{1,0:T(8,128)S(1)} collective-permute-done((f32[24,1536]{1,0:T(8,128)S(1)}, f32[24,1536]{1,0:T(8,128)S(1)}, u32[]{:S(2)}, u32[]{:S(2)}) %collective-permute-start.11) | collective-permute-done | bytes 147488 | tf_op jit(solution)/shard_map/ppermute | solution.py:354
  70.5 0.1 collective-permute-start.12
  70.6 1.6 %collective-permute-start.6 = (bf16[2,128,1536]{2,1,0:T(8,128)(2,1)}, bf16[2,128,1536]{2,1,0:T(8,128)(2,1)}, u32[]{:S(2)}, u32[]{:S(2)}) collective-permute-start(bf16[2,128,1536]{2,1,0:T(8,128)(2,1)} %get-tuple-element.23), channel_id=1, source_target_pairs={{0,1},{1,0},{2,3},{3,2},{4,5},{5,4},{6,7},{7,6},{8,9},{9,8},{10,11... | collective-permute-start | bytes 2359304 | tf_op jit(solution)/shard_map/ppermute | solution.py:241
  72.2 4.5 %collective-permute-done.12 = f32[24,1536]{1,0:T(8,128)S(1)} collective-permute-done((f32[24,1536]{1,0:T(8,128)S(1)}, f32[24,1536]{1,0:T(8,128)S(1)}, u32[]{:S(2)}, u32[]{:S(2)}) %collective-permute-start.12) | collective-permute-done | bytes 147488 | tf_op jit(solution)/shard_map/ppermute | solution.py:354
  76.7 1.6 %collective-permute-start.13 = (f32[24,1536]{1,0:T(8,128)S(1)}, f32[24,1536]{1,0:T(8,128)S(1)}, u32[]{:S(2)}, u32[]{:S(2)}) collective-permute-start(f32[24,1536]{1,0:T(8,128)S(1)} %add.65), channel_id=1, source_target_pairs={{0,8},{2,10},{4,12},{6,14},{8,0},{10,2},{12,4},{14,6},{16,24},{18,... | collective-permute-start | bytes 442376 | tf_op jit(solution)/shard_map/ppermute | solution.py:354
  78.4 3.8 %collective-permute-done.13 = f32[24,1536]{1,0:T(8,128)S(1)} collective-permute-done((f32[24,1536]{1,0:T(8,128)S(1)}, f32[24,1536]{1,0:T(8,128)S(1)}, u32[]{:S(2)}, u32[]{:S(2)}) %collective-permute-start.13) | collective-permute-done | bytes 147488 | tf_op jit(solution)/shard_map/ppermute | solution.py:354
  82.2 2.7 %collective-permute-start.14 = (f32[24,1536]{1,0:T(8,128)S(1)}, f32[24,1536]{1,0:T(8,128)S(1)}, u32[]{:S(2)}, u32[]{:S(2)}) collective-permute-start(f32[24,1536]{1,0:T(8,128)S(1)} %add.66), channel_id=1, source_target_pairs={{0,16},{2,18},{4,20},{6,22},{8,24},{10,26},{12,28},{14,30},{16,0},... | collective-permute-start | bytes 442376 | tf_op jit(solution)/shard_map/ppermute | solution.py:354
  84.9 6.1 %collective-permute-done.14 = f32[24,1536]{1,0:T(8,128)S(1)} collective-permute-done((f32[24,1536]{1,0:T(8,128)S(1)}, f32[24,1536]{1,0:T(8,128)S(1)}, u32[]{:S(2)}, u32[]{:S(2)}) %collective-permute-start.14) | collective-permute-done | bytes 147488 | tf_op jit(solution)/shard_map/ppermute | solution.py:354
  91.0 1.6 %collective-permute-start.15 = (f32[24,1536]{1,0:T(8,128)S(1)}, f32[24,1536]{1,0:T(8,128)S(1)}, u32[]{:S(2)}, u32[]{:S(2)}) collective-permute-start(f32[24,1536]{1,0:T(8,128)S(1)} %add.67), channel_id=1, source_target_pairs={{0,1},{1,0},{2,3},{3,2},{4,5},{5,4},{6,7},{7,6},{8,9},{9,8},{10,11... | collective-permute-start | bytes 442376 | tf_op jit(solution)/shard_map/ppermute | solution.py:357
  92.6 1.9 %collective-permute-start.8 = (bf16[2,128,1536]{2,1,0:T(8,128)(2,1)}, bf16[2,128,1536]{2,1,0:T(8,128)(2,1)}, u32[]{:S(2)}, u32[]{:S(2)}) collective-permute-start(bf16[2,128,1536]{2,1,0:T(8,128)(2,1)} %get-tuple-element.27), channel_id=1, source_target_pairs={{2,4},{4,2},{6,8},{8,6},{10,12},{12,10},{14,16},{16,14},{18,20},{2... | collective-permute-start | bytes 2359304 | tf_op jit(solution)/shard_map/ppermute | solution.py:343
  94.5 0.0 copy-start.17
  94.5 0.0 copy-start.19
  94.5 3.8 %collective-permute-start.9 = (bf16[2,128,1536]{2,1,0:T(8,128)(2,1)}, bf16[2,128,1536]{2,1,0:T(8,128)(2,1)S(1)}, u32[]{:S(2)}, u32[]{:S(2)}) collective-permute-start(bf16[2,128,1536]{2,1,0:T(8,128)(2,1)} %copy-done.10), channel_id=1, source_target_pairs={{2,4},{4,2},{6,8},{8,6},{10,12},{12,10},{14,16},{16,14},{18,20},{2... | collective-permute-start | bytes 2359304 | tf_op jit(solution)/shard_map/ppermute | solution.py:340
  98.3 0.0 collective-permute-done.15
  98.3 1.9 %fusion.6 = f32[128,3072]{1,0:T(8,128)} fusion(f32[24,1536]{1,0:T(8,128)S(1)} %collective-permute-done.15, f32[24,1536]{1,0:T(8,128)S(1)} %add.67, pred[]{:T(512)S(6)} %eq.21, s32[24]{0:T(128)S(1)} %copy-done.9), kind=kOutput, calls=%fused_computation.25 | convolution fusion | flops 113470464 | bytes 1867873 | tf_op jit(solution)/shard_map/dot_general | solution.py:367
  100.3 1.2 fusion.4
  101.5 0.0 copy-start.18
  101.5 0.0 copy-start.20
  101.5 21.3 %collective-permute-done.8 = bf16[2,128,1536]{2,1,0:T(8,128)(2,1)} collective-permute-done((bf16[2,128,1536]{2,1,0:T(8,128)(2,1)}, bf16[2,128,1536]{2,1,0:T(8,128)(2,1)}, u32[]{:S(2)}, u32[]{:S(2)}) %collective-permute-start.8) | collective-permute-done | bytes 786464 | tf_op jit(solution)/shard_map/ppermute | solution.py:343
  122.8 2.3 %convert_add_fusion = (f32[2,128,1536]{2,1,0:T(8,128)S(1)}, bf16[2,128,1536]{2,1,0:T(8,128)(2,1)S(1)}) fusion(f32[2,128,1536]{2,1,0:T(8,128)S(1)} %get-tuple-element.28, bf16[2,256,1536]{2,1,0:T(8,128)(2,1)} %collective-permute-done.7, bf16[2,128,1536]{2,1,0:T(8,128)(2,1)} %collective-permute-done.8, f32[2,128,1536]{2,1,0:T(8,128)S(1)} %get-tuple-element.25), kind=kLoop, calls=%fused_computation.1 | loop fusion | flops 2752512 | bytes 7864320 | tf_op jit(solution)/shard_map/add | solution.py:344
  125.1 6.0 %collective-permute-done.9 = bf16[2,128,1536]{2,1,0:T(8,128)(2,1)S(1)} collective-permute-done((bf16[2,128,1536]{2,1,0:T(8,128)(2,1)}, bf16[2,128,1536]{2,1,0:T(8,128)(2,1)S(1)}, u32[]{:S(2)}, u32[]{:S(2)}) %collective-permute-start.9) | collective-permute-done | bytes 786464 | tf_op jit(solution)/shard_map/ppermute | solution.py:340
  131.1 0.2 add_convert_fusion
  131.3 0.6 collective-permute-start.10
  131.9 0.1 broadcast.8.clone.1
  132.0 0.1 broadcast.8.clone
  132.1 11.2 %collective-permute-done.10 = bf16[2,128,1536]{2,1,0:T(8,128)(2,1)S(1)} collective-permute-done((bf16[2,128,1536]{2,1,0:T(8,128)(2,1)S(1)}, bf16[2,128,1536]{2,1,0:T(8,128)(2,1)S(1)}, u32[]{:S(2)}, u32[]{:S(2)}) %collective-permute-start.10) | collective-permute-done | bytes 786464 | tf_op jit(solution)/shard_map/ppermute | solution.py:241
  143.4 0.1 fusion
  143.4 0.0 copy-start.15
  143.5 0.0 copy-start.16
  143.5 0.9 copy-done.15
  144.3 0.3 copy-done.16
  (31 shorter events, 0.2 us)
Async XLA Ops:
  2.1 3.8 %copy-start.3 = (bf16[128,3072]{1,0:T(8,128)(2,1)S(1)}, bf16[128,3072]{1,0:T(8,128)(2,1)}, u32[]{:S(2)}) copy-start(bf16[128,3072]{1,0:T(8,128)(2,1)} %q_ref.1) | copy-start | bytes 2359300
  2.1 3.8 %copy-start.5 = (bf16[128,3072]{1,0:T(8,128)(2,1)S(1)}, bf16[128,3072]{1,0:T(8,128)(2,1)}, u32[]{:S(2)}) copy-start(bf16[128,3072]{1,0:T(8,128)(2,1)} %o_ref.1) | copy-start | bytes 2359300
  2.2 19.3 %collective-permute-start = (bf16[2,128,1536]{2,1,0:T(8,128)(2,1)S(1)}, bf16[2,128,1536]{2,1,0:T(8,128)(2,1)S(1)}, u32[]{:S(2)}, u32[]{:S(2)}) collective-permute-start(bf16[2,128,1536]{2,1,0:T(8,128)(2,1)S(1)} %pad_maximum_fusion.1), channel_id=1, source_target_pairs={{0,1},{1,0},{2,3},{3,2},{4,5},{5,4},{6,7},{7,6},{8,9},{9,8},{10,11... | collective-permute-start | bytes 2359304 | tf_op jit(solution)/shard_map/ppermute | solution.py:233
  3.7 20.8 %copy-start = (f32[128,3072]{1,0:T(8,128)S(1)}, f32[128,3072]{1,0:T(8,128)}, u32[]{:S(2)}) copy-start(f32[128,3072]{1,0:T(8,128)} %table_ref.1) | copy-start | bytes 4718596
  3.7 20.8 %copy-start.7 = (s32[4096]{0:T(1024)S(1)}, s32[4096]{0:T(1024)}, u32[]{:S(2)}) copy-start(s32[4096]{0:T(1024)} %param.13) | copy-start | bytes 49156
  3.7 20.8 %copy-start.8 = (s32[24,24]{1,0:T(8,128)S(1)}, s32[24,24]{1,0:T(8,128)}, u32[]{:S(2)}) copy-start(s32[24,24]{1,0:T(8,128)} %mask_ref.1) | copy-start | bytes 6916
  3.7 20.8 %copy-start.9 = (s32[24]{0:T(128)S(1)}, s32[24]{0:T(128)}, u32[]{:S(2)}) copy-start(s32[24]{0:T(128)} %param.14) | copy-start | bytes 292
  3.7 23.2 %collective-permute-start.2 = (bf16[2,128,1536]{2,1,0:T(8,128)(2,1)}, bf16[2,128,1536]{2,1,0:T(8,128)(2,1)S(1)}, u32[]{:S(2)}, u32[]{:S(2)}) collective-permute-start(bf16[2,128,1536]{2,1,0:T(8,128)(2,1)} %pad_maximum_fusion.2), channel_id=1, source_target_pairs={{0,2},{2,0},{4,6},{6,4},{8,10},{10,8},{12,14},{14,12},{16,18},{18,... | collective-permute-start | bytes 2359304 | tf_op jit(solution)/shard_map/ppermute | solution.py:247
  3.8 24.0 %collective-permute-start.4 = (bf16[2,128,1536]{2,1,0:T(8,128)(2,1)}, bf16[2,128,1536]{2,1,0:T(8,128)(2,1)}, u32[]{:S(2)}, u32[]{:S(2)}) collective-permute-start(bf16[2,128,1536]{2,1,0:T(8,128)(2,1)} %pad_maximum_fusion.2), channel_id=1, source_target_pairs={{2,4},{4,2},{6,8},{8,6},{10,12},{12,10},{14,16},{16,14},{18,20},{2... | collective-permute-start | bytes 2359304 | tf_op jit(solution)/shard_map/ppermute | solution.py:246
  21.6 22.3 %copy-start.11 = (bf16[2,128,1536]{2,1,0:T(8,128)(2,1)}, bf16[2,128,1536]{2,1,0:T(8,128)(2,1)S(1)}, u32[]{:S(2)}) copy-start(bf16[2,128,1536]{2,1,0:T(8,128)(2,1)S(1)} %collective-permute-done.kv_ref) | copy-start | bytes 2359300
  21.6 18.8 %collective-permute-start.1 = (bf16[2,128,1536]{2,1,0:T(8,128)(2,1)}, bf16[2,128,1536]{2,1,0:T(8,128)(2,1)}, u32[]{:S(2)}, u32[]{:S(2)}) collective-permute-start(bf16[2,128,1536]{2,1,0:T(8,128)(2,1)} %pad_maximum_fusion), channel_id=1, source_target_pairs={{0,1},{1,0},{2,3},{3,2},{4,5},{5,4},{6,7},{7,6},{8,9},{9,8},{10,11... | collective-permute-start | bytes 2359304 | tf_op jit(solution)/shard_map/ppermute | solution.py:233
  22.1 18.3 %collective-permute-start.3 = (bf16[2,128,1536]{2,1,0:T(8,128)(2,1)S(1)}, bf16[2,128,1536]{2,1,0:T(8,128)(2,1)}, u32[]{:S(2)}, u32[]{:S(2)}) collective-permute-start(bf16[2,128,1536]{2,1,0:T(8,128)(2,1)S(1)} %collective-permute-done.kv_ref), channel_id=1, source_target_pairs={{0,2},{2,0},{4,6},{6,4},{8,10},{10,8},{12,14},{14,12},{16,18},{18,... | collective-permute-start | bytes 2359304 | tf_op jit(solution)/shard_map/ppermute | solution.py:249
  22.1 21.8 %collective-permute-start.5 = (bf16[2,128,1536]{2,1,0:T(8,128)(2,1)S(1)}, bf16[2,128,1536]{2,1,0:T(8,128)(2,1)}, u32[]{:S(2)}, u32[]{:S(2)}) collective-permute-start(bf16[2,128,1536]{2,1,0:T(8,128)(2,1)S(1)} %collective-permute-done.kv_ref), channel_id=1, source_target_pairs={{2,4},{4,2},{6,8},{8,6},{10,12},{12,10},{14,16},{16,14},{18,20},{2... | collective-permute-start | bytes 2359304 | tf_op jit(solution)/shard_map/ppermute | solution.py:248
  26.9 0.9 copy-start.13
  43.9 1.1 copy-start.1
  45.0 1.1 copy-start.2
  46.2 1.1 copy-start.4
  47.3 1.1 copy-start.6
  48.4 1.1 copy-start.12
  49.6 1.1 copy-start.14
  66.3 0.9 copy-start.10
  67.2 55.5 %collective-permute-start.7 = (bf16[2,256,1536]{2,1,0:T(8,128)(2,1)}, bf16[2,256,1536]{2,1,0:T(8,128)(2,1)}, u32[]{:S(2)}, u32[]{:S(2)}) collective-permute-start(bf16[2,256,1536]{2,1,0:T(8,128)(2,1)} %get-tuple-element.26), channel_id=1, source_target_pairs={{0,2},{2,0},{4,6},{6,4},{8,10},{10,8},{12,14},{14,12},{16,18},{18,... | collective-permute-start | bytes 4718600 | tf_op jit(solution)/shard_map/ppermute | solution.py:341
  67.2 3.2 %collective-permute-start.11 = (f32[24,1536]{1,0:T(8,128)S(1)}, f32[24,1536]{1,0:T(8,128)S(1)}, u32[]{:S(2)}, u32[]{:S(2)}) collective-permute-start(f32[24,1536]{1,0:T(8,128)S(1)} %get-tuple-element.30), channel_id=1, source_target_pairs={{0,2},{2,0},{4,6},{6,4},{8,10},{10,8},{12,14},{14,12},{16,18},{18,... | collective-permute-start | bytes 442376 | tf_op jit(solution)/shard_map/ppermute | solution.py:354
  70.5 6.2 %collective-permute-start.12 = (f32[24,1536]{1,0:T(8,128)S(1)}, f32[24,1536]{1,0:T(8,128)S(1)}, u32[]{:S(2)}, u32[]{:S(2)}) collective-permute-start(f32[24,1536]{1,0:T(8,128)S(1)} %add.64), channel_id=1, source_target_pairs={{0,4},{2,6},{4,0},{6,2},{8,12},{10,14},{12,8},{14,10},{16,20},{18,... | collective-permute-start | bytes 442376 | tf_op jit(solution)/shard_map/ppermute | solution.py:354
  70.6 29.7 %collective-permute-start.6 = (bf16[2,128,1536]{2,1,0:T(8,128)(2,1)}, bf16[2,128,1536]{2,1,0:T(8,128)(2,1)}, u32[]{:S(2)}, u32[]{:S(2)}) collective-permute-start(bf16[2,128,1536]{2,1,0:T(8,128)(2,1)} %get-tuple-element.23), channel_id=1, source_target_pairs={{0,1},{1,0},{2,3},{3,2},{4,5},{5,4},{6,7},{7,6},{8,9},{9,8},{10,11... | collective-permute-start | bytes 2359304 | tf_op jit(solution)/shard_map/ppermute | solution.py:241
  76.7 5.5 %collective-permute-start.13 = (f32[24,1536]{1,0:T(8,128)S(1)}, f32[24,1536]{1,0:T(8,128)S(1)}, u32[]{:S(2)}, u32[]{:S(2)}) collective-permute-start(f32[24,1536]{1,0:T(8,128)S(1)} %add.65), channel_id=1, source_target_pairs={{0,8},{2,10},{4,12},{6,14},{8,0},{10,2},{12,4},{14,6},{16,24},{18,... | collective-permute-start | bytes 442376 | tf_op jit(solution)/shard_map/ppermute | solution.py:354
  82.2 8.7 %collective-permute-start.14 = (f32[24,1536]{1,0:T(8,128)S(1)}, f32[24,1536]{1,0:T(8,128)S(1)}, u32[]{:S(2)}, u32[]{:S(2)}) collective-permute-start(f32[24,1536]{1,0:T(8,128)S(1)} %add.66), channel_id=1, source_target_pairs={{0,16},{2,18},{4,20},{6,22},{8,24},{10,26},{12,28},{14,30},{16,0},... | collective-permute-start | bytes 442376 | tf_op jit(solution)/shard_map/ppermute | solution.py:354
  91.0 7.3 %collective-permute-start.15 = (f32[24,1536]{1,0:T(8,128)S(1)}, f32[24,1536]{1,0:T(8,128)S(1)}, u32[]{:S(2)}, u32[]{:S(2)}) collective-permute-start(f32[24,1536]{1,0:T(8,128)S(1)} %add.67), channel_id=1, source_target_pairs={{0,1},{1,0},{2,3},{3,2},{4,5},{5,4},{6,7},{7,6},{8,9},{9,8},{10,11... | collective-permute-start | bytes 442376 | tf_op jit(solution)/shard_map/ppermute | solution.py:357
  92.6 30.2 %collective-permute-start.8 = (bf16[2,128,1536]{2,1,0:T(8,128)(2,1)}, bf16[2,128,1536]{2,1,0:T(8,128)(2,1)}, u32[]{:S(2)}, u32[]{:S(2)}) collective-permute-start(bf16[2,128,1536]{2,1,0:T(8,128)(2,1)} %get-tuple-element.27), channel_id=1, source_target_pairs={{2,4},{4,2},{6,8},{8,6},{10,12},{12,10},{14,16},{16,14},{18,20},{2... | collective-permute-start | bytes 2359304 | tf_op jit(solution)/shard_map/ppermute | solution.py:343
  94.5 5.7 %copy-start.17 = (bf16[128,3072]{1,0:T(8,128)(2,1)S(1)}, bf16[128,3072]{1,0:T(8,128)(2,1)}, u32[]{:S(2)}) copy-start(bf16[128,3072]{1,0:T(8,128)(2,1)} %get-tuple-element.22) | copy-start | bytes 2359300
  94.5 5.7 %copy-start.19 = (bf16[128,3072]{1,0:T(8,128)(2,1)S(1)}, bf16[128,3072]{1,0:T(8,128)(2,1)}, u32[]{:S(2)}) copy-start(bf16[128,3072]{1,0:T(8,128)(2,1)} %get-tuple-element.24) | copy-start | bytes 2359300
  94.5 36.6 %collective-permute-start.9 = (bf16[2,128,1536]{2,1,0:T(8,128)(2,1)}, bf16[2,128,1536]{2,1,0:T(8,128)(2,1)S(1)}, u32[]{:S(2)}, u32[]{:S(2)}) collective-permute-start(bf16[2,128,1536]{2,1,0:T(8,128)(2,1)} %copy-done.10), channel_id=1, source_target_pairs={{2,4},{4,2},{6,8},{8,6},{10,12},{12,10},{14,16},{16,14},{18,20},{2... | collective-permute-start | bytes 2359304 | tf_op jit(solution)/shard_map/ppermute | solution.py:340
  101.5 23.6 %copy-start.18 = (bf16[128,3072]{1,0:T(8,128)(2,1)}, bf16[128,3072]{1,0:T(8,128)(2,1)S(1)}, u32[]{:S(2)}) copy-start(bf16[128,3072]{1,0:T(8,128)(2,1)S(1)} %get-tuple-element.36) | copy-start | bytes 2359300
  101.5 23.6 %copy-start.20 = (bf16[128,3072]{1,0:T(8,128)(2,1)}, bf16[128,3072]{1,0:T(8,128)(2,1)S(1)}, u32[]{:S(2)}) copy-start(bf16[128,3072]{1,0:T(8,128)(2,1)S(1)} %get-tuple-element.35) | copy-start | bytes 2359300
  131.3 12.1 %collective-permute-start.10 = (bf16[2,128,1536]{2,1,0:T(8,128)(2,1)S(1)}, bf16[2,128,1536]{2,1,0:T(8,128)(2,1)S(1)}, u32[]{:S(2)}, u32[]{:S(2)}) collective-permute-start(bf16[2,128,1536]{2,1,0:T(8,128)(2,1)S(1)} %add_convert_fusion), channel_id=1, source_target_pairs={{0,1},{1,0},{2,3},{3,2},{4,5},{5,4},{6,7},{7,6},{8,9},{9,8},{10,11... | collective-permute-start | bytes 2359304 | tf_op jit(solution)/shard_map/ppermute | solution.py:241
  143.4 0.9 copy-start.15
  143.5 1.1 copy-start.16
where the time goes:
time: 145 us
  waiting for transfers between devices  86.5 us (60%)
  starting transfers between devices  19.9 us (14%)
  Pallas kernels  18 us (12%)
  local copies, waits for them, and re-layouts  12.8 us (9%)
  other arithmetic  4.57 us (3%)
  matrix products  1.91 us (1%)
    ppermute x2, waiting for transfers between devices, to_peers(): parts.append(lax.ppermute(slab, 'head', pairs))  27.2 us
    ppermute x1, waiting for transfers between devices, per_device(): side_back_own = lax.ppermute(side_grad_own, 'ctx', side_pairs)  21.3 us
    ppermute x4, waiting for transfers between devices, per_device(): slot_sums = slot_sums + lax.ppermute(slot_sums, 'ctx', pairs)  17.2 us
    pallas_call x1, Pallas kernels, per_device(): pl.pallas_call(functools.partial(attention_kernel, rows=rows, tokens=toke...  15.6 us
    ppermute x2, waiting for transfers between devices, from_peers(): parts.append(lax.ppermute(part, 'head', pairs))  11.2 us
    unnamed x42, local copies, waits for them, and re-layouts  9.74 us
    ppermute x1, waiting for transfers between devices, per_device(): side_back_far = lax.ppermute(side_grad_far, 'ctx', side_pairs)  6.04 us
    ppermute x4, starting transfers between devices, per_device(): slot_sums = slot_sums + lax.ppermute(slot_sums, 'ctx', pairs)  4.88 us
  transfers between devices with their start and end apart: 16, of which 10 were waited for; matrix products, arithmetic and copies ran while one was open for 5% of the time, Pallas kernels for 2%

commit v1 on v0

--- a/solution.py
+++ b/solution.py
@@ -91,15 +91,15 @@
 
 def attention_kernel(
     place_ref,
-    q_ref, k_ref, v_ref, o_ref,
-    qo_ref, kv_ref,
+    qo_own_ref, kv_own_ref, qo_ref, kv_ref,
     near_own_ref, near_far_ref, side_own_ref, side_far_ref,
     gate_ref, bias_ref, slot_ref,
-    mixed_ref, dq_ref, back_ref,
-    own_ref, far_ref, near_ref, side_grad_own_ref, side_grad_far_ref,
-    sums_ref,
-    *, rows, tokens, q_size, heads,
+    *rest, rows, tokens, q_size, heads,
 ):
+    (
+        back_ref, side_grad_far_ref, mixed_ref, dq_ref, own_ref, far_ref,
+        near_grad_own_ref, near_grad_far_ref, side_grad_own_ref, sums_ref,
+    ) = rest[-10:]
     scale = 1.0 / math.sqrt(DH)
     bf16, f32 = jnp.bfloat16, jnp.float32
     tile = 32
@@ -111,13 +111,15 @@
 
     def load(j):
         at = slice(j * DH, (j + 1) * DH)
-        keys, values = [k_ref[:, at], kv_ref[0, :, at]], [v_ref[:, at], kv_ref[1, :, at]]
-        for ref in (near_own_ref, near_far_ref, side_own_ref, side_far_ref):
+        keys, values = [], []
+        for ref in (
+            kv_own_ref, kv_ref, near_own_ref, near_far_ref, side_own_ref, side_far_ref
+        ):
             keys.append(ref[0, :, at])
             values.append(ref[1, :, at])
         keys, values = jnp.concatenate(keys, axis=0), jnp.concatenate(values, axis=0)
-        queries = jnp.concatenate([q_ref[:, at], qo_ref[0, :, at]], axis=0)
-        cotangent = jnp.concatenate([o_ref[:, at], qo_ref[1, :, at]], axis=0)
+        queries = jnp.concatenate([qo_own_ref[0, :, at], qo_ref[0, :, at]], axis=0)
+        cotangent = jnp.concatenate([qo_own_ref[1, :, at], qo_ref[1, :, at]], axis=0)
         blocks = []
         for start in range(0, tokens, q_size):
             span = slice(start, start + q_size)
@@ -184,7 +186,8 @@
             own_ref[i, :, at] = grad[:rows]
             far_ref[i, :, at] = grad[rows:tokens]
             low = grad[tokens:].astype(bf16)
-            near_ref[i, :, at] = low[:tokens]
+            near_grad_own_ref[i, :, at] = low[:rows]
+            near_grad_far_ref[i, :, at] = low[rows:tokens]
             side_grad_own_ref[i, :, at] = low[tokens : tokens + rows]
             side_grad_far_ref[i, :, at] = low[tokens + rows :]
 
@@ -193,6 +196,22 @@
         following = load(j + 1) if j + 1 < heads else None
         work(j, *ready)
         ready = following
+
+
+def far_sum_kernel(part_ref, near_ref, side_ref, out_ref):
+    total = part_ref[...] + near_ref[...].astype(jnp.float32) + side_ref[...].astype(jnp.float32)
+    out_ref[...] = total.astype(out_ref.dtype)
+
+
+def own_sum_kernel(place_ref, part_ref, near_ref, side_ref, key_ref, value_ref):
+    total = part_ref[...] + near_ref[...].astype(jnp.float32) + side_ref[...].astype(jnp.float32)
+    key_ref[...] = total[0].astype(key_ref.dtype)
+    value_ref[...] = total[1].astype(value_ref.dtype)
+
+
+def put_kernel(place_ref, part_ref, first_in, second_in, first_ref, second_ref):
+    first_ref[...] = part_ref[0]
+    second_ref[...] = part_ref[1]
 
 
 def per_device(
@@ -205,6 +224,9 @@
     heads = width // DH
     tokens = rows * groups
     far_rows = tokens - rows
+    parts = 2 if heads % 2 == 0 else 1
+    part_width = width // parts
+    part_heads = heads // parts
     span_total = noise_level.shape[0]
     level_count = gate_table.shape[0]
     by_span = span_total <= level_count // 2
@@ -213,44 +235,57 @@
     h = lax.axis_index("head")
     place = jnp.stack([c, h]).astype(jnp.int32)
     bf16, f32 = jnp.bfloat16, jnp.float32
+    tie = lax.optimization_barrier
 
     near_pairs = [(i, i ^ 1) for i in range(ctx_count)]
-    side_pairs = [
-        (i, i - 1 + 2 * (i % 2)) for i in range(ctx_count) if 0 <= i - 1 + 2 * (i % 2) < ctx_count
-    ]
-
-    def columns(array, group):
-        return lax.dynamic_slice_in_dim(array, group * width, width, 1)
-
-    def to_peers(first, second, after=None):
-        parts = []
+    side_of = [i - 1 + 2 * (i % 2) for i in range(ctx_count)]
+    side_pairs = [(i, j if 0 <= j < ctx_count else i) for i, j in enumerate(side_of)]
+
+    def columns(array, group, part=None):
+        start, size = group * width, width
+        if part is not None:
+            start, size = start + part * part_width, part_width
+        return lax.dynamic_slice_in_dim(array, start, size, 1)
+
+    def to_peers(first, second, part=None, after=None):
+        arrived = []
         for k in range(1, groups):
             group = lax.rem(h + k, groups)
-            slab = jnp.stack([columns(first, group), columns(second, group)])
+            slab = jnp.stack([columns(first, group, part), columns(second, group, part)])
             if after is not None:
-                slab, _ = lax.optimization_barrier((slab, after))
+                slab, _ = tie((slab, after))
             pairs = [(i, (i + k) % groups) for i in range(groups)]
-            parts.append(lax.ppermute(slab, "head", pairs))
-        return parts[0] if groups == 2 else jnp.concatenate(parts, axis=1)
+            arrived.append(lax.ppermute(slab, "head", pairs))
+        return arrived[0] if groups == 2 else jnp.concatenate(arrived, axis=1)
 
     def from_peers(slab):
-        parts = []
+        arrived = []
         for k in range(1, groups):
             part = slab if groups == 2 else slab[:, (k - 1) * rows : k * rows]
             pairs = [(i, (i - k) % groups) for i in range(groups)]
-            parts.append(lax.ppermute(part, "head", pairs))
-        return parts
-
-    kv_far = to_peers(key_rows, value_rows)
+            arrived.append(lax.ppermute(part, "head", pairs))
+        return arrived
+
     kv_own = jnp.stack([columns(key_rows, h), columns(value_rows, h)])
     side_own = lax.ppermute(kv_own, "ctx", side_pairs)
+    kv_far = to_peers(key_rows, value_rows)
     near_own = lax.ppermute(kv_own, "ctx", near_pairs)
-    side_far = lax.ppermute(kv_far, "ctx", side_pairs)
     near_far = lax.ppermute(kv_far, "ctx", near_pairs)
-    qo_far = to_peers(queries, out_cotangent, kv_far)
-
-    limit = (28 if tokens <= 256 else 56) * 1024 * 1024
+    qo_own = jnp.stack([columns(queries, h), columns(out_cotangent, h)])
+    side_far, qo_far = [], []
+    side_after, qo_after = None, kv_far
+    for p in range(parts):
+        piece = kv_far[:, :, p * part_width : (p + 1) * part_width]
+        if side_after is not None:
+            piece, _ = tie((piece, side_after))
+        side_after = lax.ppermute(piece, "ctx", side_pairs)
+        side_far.append(side_after)
+        qo_after = to_peers(queries, out_cotangent, p, qo_after)
+        qo_far.append(qo_after)
+
+    limit = (30 if tokens <= 256 else 56) * 1024 * 1024
     params = pltpu.CompilerParams(vmem_limit_bytes=limit)
+    small = pltpu.CompilerParams(vmem_limit_bytes=(12 if tokens <= 256 else 36) * 1024 * 1024)
     sizes = (ctx_count, groups, rows, span_total, level_count, by_span)
     whole = lambda shape: pl.BlockSpec(shape, lambda i, place: (0,) * len(shape))
     bias, gate, slot = pl.pallas_call(
@@ -275,7 +310,7 @@
             jax.ShapeDtypeStruct((tokens, width), f32),
             jax.ShapeDtypeStruct((slots, tokens), bf16),
         ],
-        compiler_params=params,
+        compiler_params=small,
         name="prep",
     )(
         place,
@@ -285,15 +320,27 @@
         gate_table,
     )
 
-    batch = next(n for n in (4, 3, 2, 1) if heads % n == 0) if tokens <= 256 else 1
-    steps = heads // batch
-    own_block = pl.BlockSpec((rows, batch * DH), lambda i, place: (0, place[1] * steps + i))
-    pair = lambda count: pl.BlockSpec((2, count, batch * DH), lambda i, place: (0, 0, i))
-    column = lambda count: pl.BlockSpec((count, batch * DH), lambda i, place: (0, i))
+    batch = next(n for n in (3, 2, 1) if part_heads % n == 0) if tokens <= 256 else 1
+    steps = part_heads // batch
+    block = batch * DH
     q_size = min(256, tokens)
-    flops = 6 * 2 * tokens * 3 * tokens * DH * heads
-    (mixed, query_grad, back, own, far, near_grad, side_grad_own, side_grad_far, sums) = (
-        pl.pallas_call(
+    flops = 6 * 2 * tokens * 3 * tokens * DH * part_heads
+
+    def attention(p, joint):
+        pair = lambda count: pl.BlockSpec((2, count, block), lambda i, place: (0, 0, i))
+        at_part = lambda count: pl.BlockSpec(
+            (2, count, block), lambda i, place: (0, 0, p * steps + i)
+        )
+        at_head = pl.BlockSpec(
+            (rows, block), lambda i, place: (0, (place[1] * parts + p) * steps + i)
+        )
+        column = lambda count: pl.BlockSpec((count, block), lambda i, place: (0, p * steps + i))
+        struct = jax.ShapeDtypeStruct
+        inputs = [
+            qo_own, kv_own, qo_far[p], kv_far, near_own, near_far, side_own, side_far[p],
+            gate, bias, slot,
+        ]
+        return pl.pallas_call(
             functools.partial(
                 attention_kernel, rows=rows, tokens=tokens, q_size=q_size, heads=batch
             ),
@@ -301,55 +348,85 @@
                 num_scalar_prefetch=1,
                 grid=(steps,),
                 in_specs=[
-                    own_block, own_block, own_block, own_block,
+                    at_part(rows), at_part(rows), pair(far_rows), at_part(far_rows),
+                    at_part(rows), at_part(far_rows), at_part(rows), pair(far_rows),
+                    column(tokens), whole((3 * tokens, tokens)), whole((slots, tokens)),
+                ]
+                + [pl.BlockSpec(memory_space=pl.ANY)] * len(joint),
+                out_specs=[
                     pair(far_rows), pair(far_rows),
-                    pair(rows), pair(far_rows), pair(rows), pair(far_rows),
-                    column(tokens), whole((3 * tokens, tokens)), whole((slots, tokens)),
-                ],
-                out_specs=[
-                    own_block, own_block, pair(far_rows),
-                    pair(rows), pair(far_rows), pair(tokens), pair(rows), pair(far_rows),
-                    column(slots),
+                    at_head, at_head, at_part(rows), at_part(far_rows),
+                    at_part(rows), at_part(far_rows), at_part(rows), column(slots),
                 ],
             ),
             out_shape=[
-                jax.ShapeDtypeStruct((rows, full_width), bf16),
-                jax.ShapeDtypeStruct((rows, full_width), bf16),
-                jax.ShapeDtypeStruct((2, far_rows, width), bf16),
-                jax.ShapeDtypeStruct((2, rows, width), f32),
-                jax.ShapeDtypeStruct((2, far_rows, width), f32),
-                jax.ShapeDtypeStruct((2, tokens, width), bf16),
-                jax.ShapeDtypeStruct((2, rows, width), bf16),
-                jax.ShapeDtypeStruct((2, far_rows, width), bf16),
-                jax.ShapeDtypeStruct((slots, width), f32),
+                struct((2, far_rows, part_width), bf16),
+                struct((2, far_rows, part_width), bf16),
+                struct((rows, full_width), bf16),
+                struct((rows, full_width), bf16),
+                struct((2, rows, width), f32),
+                struct((2, far_rows, width), f32),
+                struct((2, rows, width), bf16),
+                struct((2, far_rows, width), bf16),
+                struct((2, rows, width), bf16),
+                struct((slots, width), f32),
             ],
+            input_output_aliases={1 + len(inputs) + i: 2 + i for i in range(len(joint))},
             compiler_params=params,
             cost_estimate=pl.CostEstimate(
-                flops=flops, bytes_accessed=16 * tokens * width, transcendentals=0
+                flops=flops, bytes_accessed=16 * tokens * part_width, transcendentals=0
             ),
             name="attention",
-        )(
-            place,
-            queries, key_rows, value_rows, out_cotangent,
-            qo_far, kv_far,
-            near_own, near_far, side_own, side_far,
-            gate, bias, slot,
-        )
-    )
-
-    side_back_far = lax.ppermute(side_grad_far, "ctx", side_pairs)
-    near_back = lax.ppermute(near_grad, "ctx", near_pairs)
-    back_parts = from_peers(back)
+        )(place, *inputs, *joint)
+
+    joint, back_far, side_back_far = (), [], []
+    for p in range(parts):
+        back, side_grad_far, *joint = attention(p, joint)
+        if p > 0:
+            back, side_grad_far, joint, back_far, side_back_far = tie(
+                (back, side_grad_far, joint, back_far, side_back_far)
+            )
+        side_back_far.append(lax.ppermute(side_grad_far, "ctx", side_pairs))
+        back_far.append(from_peers(back))
+    mixed, query_grad, own, far, near_grad_own, near_grad_far, side_grad_own, sums = joint
+
+    near_back_far = lax.ppermute(near_grad_far, "ctx", near_pairs)
+    near_back_own = lax.ppermute(near_grad_own, "ctx", near_pairs)
+    side_grad_own, _ = tie((side_grad_own, side_back_far[-1]))
     side_back_own = lax.ppermute(side_grad_own, "ctx", side_pairs)
-    far_sum = lax.optimization_barrier(far + near_back[:, rows:].astype(f32))
-    far_grad = (far_sum + side_back_far.astype(f32)).astype(bf16)
-    grad_parts = from_peers(far_grad)
-    own_grad = (
-        own + near_back[:, :rows].astype(f32) + side_back_own.astype(f32)
-    ).astype(bf16)
+    grad_far = []
+    for p in range(parts):
+        at_part = pl.BlockSpec((2, far_rows, part_width), lambda i, p=p: (0, 0, p))
+        alone = pl.BlockSpec((2, far_rows, part_width), lambda i: (0, 0, 0))
+        far_grad = pl.pallas_call(
+            far_sum_kernel,
+            grid=(1,),
+            in_specs=[at_part, at_part, alone],
+            out_specs=alone,
+            out_shape=jax.ShapeDtypeStruct((2, far_rows, part_width), bf16),
+            compiler_params=small,
+            name="far_sum",
+        )(far, near_back_far, side_back_far[p])
+        grad_far.append(from_peers(far_grad))
+    key_grad, value_grad = pl.pallas_call(
+        own_sum_kernel,
+        grid_spec=pltpu.PrefetchScalarGridSpec(
+            num_scalar_prefetch=1,
+            grid=(parts,),
+            in_specs=[pl.BlockSpec((2, rows, part_width), lambda i, place: (0, 0, i))] * 3,
+            out_specs=[
+                pl.BlockSpec((rows, part_width), lambda i, place: (0, place[1] * parts + i))
+            ]
+            * 2,
+        ),
+        out_shape=[jax.ShapeDtypeStruct((rows, full_width), bf16)] * 2,
+        compiler_params=small,
+        name="own_sum",
+    )(place, own, near_back_own, side_back_own)
 
     slot_sums = sums
-    for step in (1 << n for n in range(ctx_count.bit_length() - 1)):
+    steps_of_two = [1 << n for n in range(ctx_count.bit_length() - 1)]
+    for step in steps_of_two[:1] + steps_of_two[2:] + steps_of_two[1:2]:
         pairs = [(i, i ^ step) for i in range(ctx_count)]
         slot_sums = slot_sums + lax.ppermute(slot_sums, "ctx", pairs)
     for step in (1 << n for n in range(groups.bit_length() - 1)):
@@ -368,17 +445,30 @@
     else:
         gate_grad = slot_sums
 
-    def placed(array, part, k):
-        group = lax.rem(h + k, groups)
-        return lax.dynamic_update_slice_in_dim(array, part, group * width, 1)
-
-    key_grad = placed(jnp.zeros((rows, full_width), bf16), own_grad[0], 0)
-    value_grad = placed(jnp.zeros((rows, full_width), bf16), own_grad[1], 0)
-    for k in range(1, groups):
-        mixed = placed(mixed, back_parts[k - 1][0], k)
-        query_grad = placed(query_grad, back_parts[k - 1][1], k)
-        key_grad = placed(key_grad, grad_parts[k - 1][0], k)
-        value_grad = placed(value_grad, grad_parts[k - 1][1], k)
+    def put(first, second, arrived, k, p):
+        out = pl.BlockSpec(
+            (rows, part_width),
+            lambda i, place: (0, lax.rem(place[1] + k, groups) * parts + p),
+        )
+        anywhere = pl.BlockSpec(memory_space=pl.ANY)
+        return pl.pallas_call(
+            put_kernel,
+            grid_spec=pltpu.PrefetchScalarGridSpec(
+                num_scalar_prefetch=1,
+                grid=(1,),
+                in_specs=[whole((2, rows, part_width)), anywhere, anywhere],
+                out_specs=[out, out],
+            ),
+            out_shape=[jax.ShapeDtypeStruct((rows, full_width), bf16)] * 2,
+            input_output_aliases={2: 0, 3: 1},
+            compiler_params=small,
+            name="put",
+        )(place, arrived, first, second)
+
+    for p in range(parts):
+        for k in range(1, groups):
+            mixed, query_grad = put(mixed, query_grad, back_far[p][k - 1], k, p)
+            key_grad, value_grad = put(key_grad, value_grad, grad_far[p][k - 1], k, p)
     return (mixed, query_grad, key_grad, value_grad, gate_grad)
 
 

time: 145 us -> 127 us (0.88)
  the two profiles are of different devices: /device:TPU:6 before, /device:TPU:0 now
where the time goes in v1:
time: 127 us
  waiting for transfers between devices  44.7 us (35%)
  starting transfers between devices  35.3 us (28%)
  Pallas kernels  30.1 us (24%)
  local copies, waits for them, and re-layouts  10.3 us (8%)
  matrix products  3.03 us (2%)
  other arithmetic  2.73 us (2%)
    ppermute x4, waiting for transfers between devices, per_device(): slot_sums = slot_sums + lax.ppermute(slot_sums, 'ctx', pairs)  22.7 us
    pallas_call x2, Pallas kernels, attention(): pl.pallas_call(functools.partial(attention_kernel, rows=rows, tokens=toke...  17.7 us
    ppermute x3, waiting for transfers between devices, to_peers(): arrived.append(lax.ppermute(slab, 'head', pairs))  17.5 us
    ppermute x1, starting transfers between devices, per_device(): near_back_far = lax.ppermute(near_grad_far, 'ctx', near_pairs)  9.82 us
    pallas_call x4, Pallas kernels, put(): pl.pallas_call(put_kernel, grid_spec=pltpu.PrefetchScalarGridSpec(num_sca...  7.19 us
    ppermute x3, starting transfers between devices, to_peers(): arrived.append(lax.ppermute(slab, 'head', pairs))  6.45 us
    unnamed x34, local copies, waits for them, and re-layouts  5.8 us
    ppermute x4, starting transfers between devices, per_device(): slot_sums = slot_sums + lax.ppermute(slot_sums, 'ctx', pairs)  5.1 us
  transfers between devices with their start and end apart: 22, of which 8 were waited for; matrix products, arithmetic and copies ran while one was open for 6% of the time, Pallas kernels for 22%

profile of v1, /device:TPU:0, one launch (start us, length us, event | category | flops | bytes accessed | tf_op | source)
XLA Modules:
  0.0 126.9 jit_solution(15305896105808675906)
XLA Ops:
  0.6 1.5 %dynamic-slice_bitcast_fusion = (bf16[1,128,1536]{2,1,0:T(8,128)(2,1)S(1)}, bf16[1,128,1536]{2,1,0:T(8,128)(2,1)S(1)}, bf16[1,128,1536]{2,1,0:T(8,128)(2,1)S(1)}, bf16[1,128,1536]{2,1,0:T(8,128)(2,1)S(1)}) fusion(bf16[128,3072]{1,0:T(8,128)(2,1)} %param.10, s32[]{:T(128)S(6)} %select_n.35, s32[]{:T(128)S(6)} %select_n.33, bf16[128,3072]{1,0:T(8,128)(2,1)} %param.9), kind=kLoop, calls=%fused_computation.5 | loop fusion | bytes 3145736 | tf_op jit(solution)/shard_map/stack | solution.py:254
  2.1 0.9 pad_maximum_fusion.2
  3.1 3.0 %collective-permute-start = (bf16[2,128,1536]{2,1,0:T(8,128)(2,1)}, bf16[2,128,1536]{2,1,0:T(8,128)(2,1)S(1)}, u32[]{:S(2)}, u32[]{:S(2)}) collective-permute-start(bf16[2,128,1536]{2,1,0:T(8,128)(2,1)} %pad_maximum_fusion.2), channel_id=1, source_target_pairs={{0,1},{1,0},{2,3},{3,2},{4,5},{5,4},{6,7},{7,6},{8,9},{9,8},{10,11... | collective-permute-start | bytes 2359304 | tf_op jit(solution)/shard_map/ppermute | solution.py:258
  6.0 0.1 pad_maximum_fusion.1.kv_own_ref
  6.1 0.7 collective-permute-start.5
  6.8 2.9 %collective-permute-start.3 = (bf16[2,128,1536]{2,1,0:T(8,128)(2,1)S(1)}, bf16[2,128,1536]{2,1,0:T(8,128)(2,1)S(1)}, u32[]{:S(2)}, u32[]{:S(2)}) collective-permute-start(bf16[2,128,1536]{2,1,0:T(8,128)(2,1)S(1)} %pad_maximum_fusion.1.kv_own_ref), channel_id=1, source_target_pairs={{0,2},{2,0},{4,6},{6,4},{8,10},{10,8},{12,14},{14,12},{16,18},{18,... | collective-permute-start | bytes 2359304 | tf_op jit(solution)/shard_map/ppermute | solution.py:272
  9.7 2.1 %dynamic-slice_bitcast_fusion.6 = (bf16[1,128,768]{2,1,0:T(8,128)(2,1)S(1)}, bf16[1,128,768]{2,1,0:T(8,128)(2,1)S(1)}, bf16[1,128,768]{2,1,0:T(8,128)(2,1)}, bf16[1,128,768]{2,1,0:T(8,128)(2,1)S(1)}) fusion(bf16[128,3072]{1,0:T(8,128)(2,1)} %param.11, s32[]{:T(128)S(6)} %select_n.35, s32[]{:T(128)S(6)} %select_n.34, bf16[128,3072]{1,0:T(8,128)(2,1)} %param.8), kind=kLoop, calls=%fused_computation.18 | loop fusion | bytes 1572872 | tf_op jit(solution)/shard_map/stack | solution.py:254
  11.8 0.9 dynamic-slice_bitcast_fusion.4
  12.7 11.1 %collective-permute-done.kv_ref = bf16[2,128,1536]{2,1,0:T(8,128)(2,1)S(1)} collective-permute-done((bf16[2,128,1536]{2,1,0:T(8,128)(2,1)}, bf16[2,128,1536]{2,1,0:T(8,128)(2,1)S(1)}, u32[]{:S(2)}, u32[]{:S(2)}) %collective-permute-start) | collective-permute-done | bytes 786464 | tf_op jit(solution)/shard_map/ppermute | solution.py:258
  23.8 0.0 collective-permute-start.4
  23.8 0.8 pad_maximum_fusion.4
  24.6 1.7 %collective-permute-start.1 = (bf16[2,128,768]{2,1,0:T(8,128)(2,1)}, bf16[2,128,768]{2,1,0:T(8,128)(2,1)S(1)}, u32[]{:S(2)}, u32[]{:S(2)}) collective-permute-start(bf16[2,128,768]{2,1,0:T(8,128)(2,1)} %pad_maximum_fusion.4), channel_id=1, source_target_pairs={{0,1},{1,0},{2,3},{3,2},{4,5},{5,4},{6,7},{7,6},{8,9},{9,8},{10,11... | collective-permute-start | bytes 1179656 | tf_op jit(solution)/shard_map/ppermute | solution.py:258
  26.3 0.1 fusion.9
  26.4 0.0 copy-start.12
  26.4 0.0 copy-start.13
  26.4 0.8 collective-permute-start.6
  27.2 0.1 pad_add_fusion.place_ref
  27.3 2.4 %prep.1 = (f32[768,256]{1,0:T(8,128)S(1)}, f32[256,1536]{1,0:T(8,128)S(1)}, bf16[24,256]{1,0:T(8,128)(2,1)S(1)}) custom-call(s32[2]{0:T(128)S(1)} %pad_add_fusion.place_ref, s32[32,128]{1,0:T(8,128)S(1)} %bitcast.24, s32[1,24]{1,0:T(1,128)S(1)} %bitcast.25, s32[24,24]{1,0:T(8,128)S(1)} %copy-done.10, f32[128,3072]{1,0:T(8,128)S(1)} %copy-done.4), custom_call_target="tpu_custom_call" | custom-call | tf_op jit(solution)/shard_map/prep/pallas_call | solution.py:291
  29.8 0.1 pad_maximum_fusion.qo_own_ref
  29.9 6.4 %collective-permute-done.1.qo_ref = bf16[2,128,768]{2,1,0:T(8,128)(2,1)S(1)} collective-permute-done((bf16[2,128,768]{2,1,0:T(8,128)(2,1)}, bf16[2,128,768]{2,1,0:T(8,128)(2,1)S(1)}, u32[]{:S(2)}, u32[]{:S(2)}) %collective-permute-start.1) | collective-permute-done | bytes 393248 | tf_op jit(solution)/shard_map/ppermute | solution.py:258
  36.3 1.7 %collective-permute-start.2 = (bf16[2,128,768]{2,1,0:T(8,128)(2,1)S(1)}, bf16[2,128,768]{2,1,0:T(8,128)(2,1)S(1)}, u32[]{:S(2)}, u32[]{:S(2)}) collective-permute-start(bf16[2,128,768]{2,1,0:T(8,128)(2,1)S(1)} %pad_maximum_fusion.3), channel_id=1, source_target_pairs={{0,1},{1,0},{2,3},{3,2},{4,5},{5,4},{6,7},{7,6},{8,9},{9,8},{10,11... | collective-permute-start | bytes 1179656 | tf_op jit(solution)/shard_map/ppermute | solution.py:258
  38.0 0.7 collective-permute-start.7
  38.7 0.0 collective-permute-done.5.side_own_ref
  38.7 0.0 copy-start
  38.8 0.9 copy-done
  39.6 0.0 collective-permute-done.3.near_own_ref
  39.6 0.9 copy-done.2
  40.5 0.0 collective-permute-done.4.near_far_ref
  40.5 1.1 copy-done.1
  41.6 1.1 copy-done.3
  42.8 8.8 %attention.2 = (bf16[2,128,768]{2,1,0:T(8,128)(2,1)S(1)}, bf16[2,128,768]{2,1,0:T(8,128)(2,1)S(1)}, bf16[128,3072]{1,0:T(8,128)(2,1)}, bf16[128,3072]{1,0:T(8,12...) custom-call(s32[2]{0:T(128)S(1)} %pad_add_fusion.place_ref, ...), custom_call_target="tpu_custom_call" | custom-call | flops 1811939328 | bytes 3145728 | tf_op jit(solution)/shard_map/attention/pallas_call | solution.py:343
  51.6 0.3 collective-permute-start.8
  51.9 0.7 collective-permute-start.9
  52.6 8.9 %attention.3 = (bf16[2,128,768]{2,1,0:T(8,128)(2,1)S(1)}, bf16[2,128,768]{2,1,0:T(8,128)(2,1)S(1)}, bf16[128,3072]{1,0:T(8,128)(2,1)}, bf16[128,3072]{1,0:T(8,12...) custom-call(s32[2]{0:T(128)S(1)} %pad_add_fusion.place_ref, ...), custom_call_target="tpu_custom_call", output_to_operand_aliasing={{2}: (12, {}), {3}: (13, {}), {4}: (14, {}), {5}: (15, {}),... | custom-call | flops 1811939328 | bytes 3145728 | tf_op jit(solution)/shard_map/attention/pallas_call | solution.py:343
  61.5 0.7 collective-permute-start.12
  62.2 9.8 %collective-permute-start.11 = (bf16[2,128,1536]{2,1,0:T(8,128)(2,1)S(1)}, bf16[2,128,1536]{2,1,0:T(8,128)(2,1)S(1)}, u32[]{:S(2)}, u32[]{:S(2)}) collective-permute-start(bf16[2,128,1536]{2,1,0:T(8,128)(2,1)S(1)} %get-tuple-element.89), channel_id=1, source_target_pairs={{0,2},{2,0},{4,6},{6,4},{8,10},{10,8},{12,14},{14,12},{16,18},{18,... | collective-permute-start | bytes 2359304 | tf_op jit(solution)/shard_map/ppermute | solution.py:393
  72.0 0.1 collective-permute-start.17
  72.1 2.0 %collective-permute-done.17 = f32[24,1536]{1,0:T(8,128)S(1)} collective-permute-done((f32[24,1536]{1,0:T(8,128)S(1)}, f32[24,1536]{1,0:T(8,128)S(1)}, u32[]{:S(2)}, u32[]{:S(2)}) %collective-permute-start.17) | collective-permute-done | bytes 147488 | tf_op jit(solution)/shard_map/ppermute | solution.py:431
  74.2 2.0 %collective-permute-start.18 = (f32[24,1536]{1,0:T(8,128)S(1)}, f32[24,1536]{1,0:T(8,128)S(1)}, u32[]{:S(2)}, u32[]{:S(2)}) collective-permute-start(f32[24,1536]{1,0:T(8,128)S(1)} %add.50), channel_id=1, source_target_pairs={{0,8},{2,10},{4,12},{6,14},{8,0},{10,2},{12,4},{14,6},{16,24},{18,... | collective-permute-start | bytes 442376 | tf_op jit(solution)/shard_map/ppermute | solution.py:431
  76.2 0.1 collective-permute-start.15
  76.3 1.8 %collective-permute-start.16 = (bf16[2,128,1536]{2,1,0:T(8,128)(2,1)}, bf16[2,128,1536]{2,1,0:T(8,128)(2,1)S(1)}, u32[]{:S(2)}, u32[]{:S(2)}) collective-permute-start(bf16[2,128,1536]{2,1,0:T(8,128)(2,1)} %get-tuple-element.95), channel_id=1, source_target_pairs={{0,0},{2,4},{4,2},{6,8},{8,6},{10,12},{12,10},{14,16},{16,14},{18,... | collective-permute-start | bytes 2359304 | tf_op jit(solution)/shard_map/ppermute | solution.py:396
  78.0 1.8 %collective-permute-start.10 = (bf16[2,128,768]{2,1,0:T(8,128)(2,1)S(1)}, bf16[2,128,768]{2,1,0:T(8,128)(2,1)S(1)}, u32[]{:S(2)}, u32[]{:S(2)}) collective-permute-start(bf16[2,128,768]{2,1,0:T(8,128)(2,1)S(1)} %get-tuple-element.80), channel_id=1, source_target_pairs={{0,1},{1,0},{2,3},{3,2},{4,5},{5,4},{6,7},{7,6},{8,9},{9,8},{10,11... | collective-permute-start | bytes 1179656 | tf_op jit(solution)/shard_map/ppermute | solution.py:266
  79.8 0.7 collective-permute-done.18
  80.6 2.9 %collective-permute-start.19 = (f32[24,1536]{1,0:T(8,128)S(1)}, f32[24,1536]{1,0:T(8,128)S(1)}, u32[]{:S(2)}, u32[]{:S(2)}) collective-permute-start(f32[24,1536]{1,0:T(8,128)S(1)} %add.51), channel_id=1, source_target_pairs={{0,16},{2,18},{4,20},{6,22},{8,24},{10,26},{12,28},{14,30},{16,0},... | collective-permute-start | bytes 442376 | tf_op jit(solution)/shard_map/ppermute | solution.py:431
  83.5 14.8 %collective-permute-done.19 = f32[24,1536]{1,0:T(8,128)S(1)} collective-permute-done((f32[24,1536]{1,0:T(8,128)S(1)}, f32[24,1536]{1,0:T(8,128)S(1)}, u32[]{:S(2)}, u32[]{:S(2)}) %collective-permute-start.19) | collective-permute-done | bytes 147488 | tf_op jit(solution)/shard_map/ppermute | solution.py:431
  98.4 0.1 collective-permute-start.20
  98.4 5.1 %collective-permute-done.20 = f32[24,1536]{1,0:T(8,128)S(1)} collective-permute-done((f32[24,1536]{1,0:T(8,128)S(1)}, f32[24,1536]{1,0:T(8,128)S(1)}, u32[]{:S(2)}, u32[]{:S(2)}) %collective-permute-start.20) | collective-permute-done | bytes 147488 | tf_op jit(solution)/shard_map/ppermute | solution.py:431
  103.6 0.7 add.53
  104.2 1.5 %collective-permute-start.21 = (f32[24,1536]{1,0:T(8,128)}, f32[24,1536]{1,0:T(8,128)}, u32[]{:S(2)}, u32[]{:S(2)}) collective-permute-start(f32[24,1536]{1,0:T(8,128)} %add.53), channel_id=1, source_target_pairs={{0,1},{1,0},{2,3},{3,2},{4,5},{5,4},{6,7},{7,6},{8,9},{9,8},{10,11... | collective-permute-start | bytes 442376 | tf_op jit(solution)/shard_map/ppermute | solution.py:434
  105.7 0.9 far_sum.3
  106.6 0.5 collective-permute-start.14
  107.2 0.1 far_sum.2
  107.3 0.0 copy-start.7
  107.3 0.7 copy-done.7
  108.0 1.5 %collective-permute-start.13 = (bf16[2,128,768]{2,1,0:T(8,128)(2,1)S(1)}, bf16[2,128,768]{2,1,0:T(8,128)(2,1)}, u32[]{:S(2)}, u32[]{:S(2)}) collective-permute-start(bf16[2,128,768]{2,1,0:T(8,128)(2,1)S(1)} %far_sum.2), channel_id=1, source_target_pairs={{0,1},{1,0},{2,3},{3,2},{4,5},{5,4},{6,7},{7,6},{8,9},{9,8},{10,11... | collective-permute-start | bytes 1179656 | tf_op jit(solution)/shard_map/ppermute | solution.py:266
  109.5 1.0 copy-done.6
  110.5 1.3 %put.4 = (bf16[128,3072]{1,0:T(8,128)(2,1)}, bf16[128,3072]{1,0:T(8,128)(2,1)}) custom-call(s32[2]{0:T(128)S(1)} %pad_add_fusion.place_ref, bf16[2,128,768]{2,1,0:T(8,128)(2,1)S(1)} %copy-done.6, bf16[128,3072]{1,0:T(8,128)(2,1)} %get-tuple-element.82.first_in, ...), custom_call_target="tpu_custom_call", output_to_operand_aliasing={{0}: (2, {}), {1}: (3, {})} | custom-call | tf_op jit(solution)/shard_map/put/pallas_call | solution.py:454
  111.8 1.3 %put.5 = (bf16[128,3072]{1,0:T(8,128)(2,1)}, bf16[128,3072]{1,0:T(8,128)(2,1)}) custom-call(s32[2]{0:T(128)S(1)} %pad_add_fusion.place_ref, bf16[2,128,768]{2,1,0:T(8,128)(2,1)S(1)} %copy-done.8, bf16[128,3072]{1,0:T(8,128)(2,1)} %get-tuple-element.84.first_in, ...), custom_call_target="tpu_custom_call", output_to_operand_aliasing={{0}: (2, {}), {1}: (3, {})} | custom-call | tf_op jit(solution)/shard_map/put/pallas_call | solution.py:454
  113.1 3.0 %fusion = f32[128,3072]{1,0:T(8,128)} fusion(f32[24,1536]{1,0:T(8,128)} %collective-permute-done.21, f32[24,1536]{1,0:T(8,128)} %add.53, pred[]{:T(512)S(6)} %eq.21, s32[24]{0:T(128)S(1)} %copy-done.11), kind=kOutput, calls=%fused_computation.12 | convolution fusion | flops 113470464 | bytes 1867873 | tf_op jit(solution)/shard_map/dot_general | solution.py:444
  116.2 1.8 %own_sum.1 = (bf16[128,3072]{1,0:T(8,128)(2,1)}, bf16[128,3072]{1,0:T(8,128)(2,1)}) custom-call(s32[2]{0:T(128)S(1)} %pad_add_fusion.place_ref, f32[2,128,1536]{2,1,0:T(8,128)S(1)} %get-tuple-element.92.part_ref, bf16[2,128,1536]{2,1,0:T(8,128)(2,1)S(1)} %collective-permute-done.15.near_ref, bf16[2,128,1536]{2,1,0:T(8,128)(2,1)S(1)} %collective-permute-done.16.side_ref), custom_call_target="tpu_custom_call" | custom-call | tf_op jit(solution)/shard_map/own_sum/pallas_call | solution.py:411
  117.9 1.8 %collective-permute-done.14.part_ref = bf16[2,128,768]{2,1,0:T(8,128)(2,1)} collective-permute-done((bf16[2,128,768]{2,1,0:T(8,128)(2,1)}, bf16[2,128,768]{2,1,0:T(8,128)(2,1)}, u32[]{:S(2)}, u32[]{:S(2)}) %collective-permute-start.14) | collective-permute-done | bytes 393248 | tf_op jit(solution)/shard_map/ppermute | solution.py:266
  119.8 2.3 %put.6 = (bf16[128,3072]{1,0:T(8,128)(2,1)}, bf16[128,3072]{1,0:T(8,128)(2,1)}) custom-call(s32[2]{0:T(128)S(1)} %pad_add_fusion.place_ref, bf16[2,128,768]{2,1,0:T(8,128)(2,1)} %collective-permute-done.14.part_ref, bf16[128,3072]{1,0:T(8,128)(2,1)} %get-tuple-element.96.first_in, ...), custom_call_target="tpu_custom_call", output_to_operand_aliasing={{0}: (2, {}), {1}: (3, {})} | custom-call | tf_op jit(solution)/shard_map/put/pallas_call | solution.py:454
  122.1 2.6 %collective-permute-done.13.part_ref = bf16[2,128,768]{2,1,0:T(8,128)(2,1)} collective-permute-done((bf16[2,128,768]{2,1,0:T(8,128)(2,1)S(1)}, bf16[2,128,768]{2,1,0:T(8,128)(2,1)}, u32[]{:S(2)}, u32[]{:S(2)}) %collective-permute-start.13) | collective-permute-done | bytes 393248 | tf_op jit(solution)/shard_map/ppermute | solution.py:266
  124.6 2.3 %put.7 = (bf16[128,3072]{1,0:T(8,128)(2,1)}, bf16[128,3072]{1,0:T(8,128)(2,1)}) custom-call(s32[2]{0:T(128)S(1)} %pad_add_fusion.place_ref, bf16[2,128,768]{2,1,0:T(8,128)(2,1)} %collective-permute-done.13.part_ref, bf16[128,3072]{1,0:T(8,128)(2,1)} %get-tuple-element.98.first_in, ...), custom_call_target="tpu_custom_call", output_to_operand_aliasing={{0}: (2, {}), {1}: (3, {})} | custom-call | tf_op jit(solution)/shard_map/put/pallas_call | solution.py:454
  (39 shorter events, 0.2 us)
Async XLA Ops:
  3.1 20.7 %collective-permute-start = (bf16[2,128,1536]{2,1,0:T(8,128)(2,1)}, bf16[2,128,1536]{2,1,0:T(8,128)(2,1)S(1)}, u32[]{:S(2)}, u32[]{:S(2)}) collective-permute-start(bf16[2,128,1536]{2,1,0:T(8,128)(2,1)} %pad_maximum_fusion.2), channel_id=1, source_target_pairs={{0,1},{1,0},{2,3},{3,2},{4,5},{5,4},{6,7},{7,6},{8,9},{9,8},{10,11... | collective-permute-start | bytes 2359304 | tf_op jit(solution)/shard_map/ppermute | solution.py:258
  6.1 32.6 %collective-permute-start.5 = (bf16[2,128,1536]{2,1,0:T(8,128)(2,1)S(1)}, bf16[2,128,1536]{2,1,0:T(8,128)(2,1)S(1)}, u32[]{:S(2)}, u32[]{:S(2)}) collective-permute-start(bf16[2,128,1536]{2,1,0:T(8,128)(2,1)S(1)} %pad_maximum_fusion.1.kv_own_ref), channel_id=1, source_target_pairs={{0,0},{2,4},{4,2},{6,8},{8,6},{10,12},{12,10},{14,16},{16,14},{18,... | collective-permute-start | bytes 2359304 | tf_op jit(solution)/shard_map/ppermute | solution.py:270
  6.8 32.8 %collective-permute-start.3 = (bf16[2,128,1536]{2,1,0:T(8,128)(2,1)S(1)}, bf16[2,128,1536]{2,1,0:T(8,128)(2,1)S(1)}, u32[]{:S(2)}, u32[]{:S(2)}) collective-permute-start(bf16[2,128,1536]{2,1,0:T(8,128)(2,1)S(1)} %pad_maximum_fusion.1.kv_own_ref), channel_id=1, source_target_pairs={{0,2},{2,0},{4,6},{6,4},{8,10},{10,8},{12,14},{14,12},{16,18},{18,... | collective-permute-start | bytes 2359304 | tf_op jit(solution)/shard_map/ppermute | solution.py:272
  9.7 2.1 %copy-start.14 = (bf16[128,3072]{1,0:T(8,128)(2,1)S(1)}, bf16[128,3072]{1,0:T(8,128)(2,1)}, u32[]{:S(2)}) copy-start(bf16[128,3072]{1,0:T(8,128)(2,1)} %param.11) | copy-start | bytes 2359300
  9.7 2.1 %copy-start.15 = (bf16[128,3072]{1,0:T(8,128)(2,1)S(1)}, bf16[128,3072]{1,0:T(8,128)(2,1)}, u32[]{:S(2)}) copy-start(bf16[128,3072]{1,0:T(8,128)(2,1)} %param.8) | copy-start | bytes 2359300
  12.7 14.6 %copy-start.9 = (s32[4096]{0:T(1024)S(1)}, s32[4096]{0:T(1024)}, u32[]{:S(2)}) copy-start(s32[4096]{0:T(1024)} %param.13) | copy-start | bytes 49156
  12.7 14.6 %copy-start.10 = (s32[24,24]{1,0:T(8,128)S(1)}, s32[24,24]{1,0:T(8,128)}, u32[]{:S(2)}) copy-start(s32[24,24]{1,0:T(8,128)} %mask_ref.1) | copy-start | bytes 6916
  12.7 14.6 %copy-start.11 = (s32[24]{0:T(128)S(1)}, s32[24]{0:T(128)}, u32[]{:S(2)}) copy-start(s32[24]{0:T(128)} %param.14) | copy-start | bytes 292
  23.8 16.7 %collective-permute-start.4 = (bf16[2,128,1536]{2,1,0:T(8,128)(2,1)S(1)}, bf16[2,128,1536]{2,1,0:T(8,128)(2,1)}, u32[]{:S(2)}, u32[]{:S(2)}) collective-permute-start(bf16[2,128,1536]{2,1,0:T(8,128)(2,1)S(1)} %collective-permute-done.kv_ref), channel_id=1, source_target_pairs={{0,2},{2,0},{4,6},{6,4},{8,10},{10,8},{12,14},{14,12},{16,18},{18,... | collective-permute-start | bytes 2359304 | tf_op jit(solution)/shard_map/ppermute | solution.py:273
  24.6 2.7 %copy-start.4 = (f32[128,3072]{1,0:T(8,128)S(1)}, f32[128,3072]{1,0:T(8,128)}, u32[]{:S(2)}) copy-start(f32[128,3072]{1,0:T(8,128)} %table_ref.1) | copy-start | bytes 4718596
  24.6 5.2 %copy-start.16 = (bf16[1,128,768]{2,1,0:T(8,128)(2,1)S(1)}, bf16[1,128,768]{2,1,0:T(8,128)(2,1)}, u32[]{:S(2)}) copy-start(bf16[1,128,768]{2,1,0:T(8,128)(2,1)} %get-tuple-element.117) | copy-start | bytes 589828
  24.6 11.7 %collective-permute-start.1 = (bf16[2,128,768]{2,1,0:T(8,128)(2,1)}, bf16[2,128,768]{2,1,0:T(8,128)(2,1)S(1)}, u32[]{:S(2)}, u32[]{:S(2)}) collective-permute-start(bf16[2,128,768]{2,1,0:T(8,128)(2,1)} %pad_maximum_fusion.4), channel_id=1, source_target_pairs={{0,1},{1,0},{2,3},{3,2},{4,5},{5,4},{6,7},{7,6},{8,9},{9,8},{10,11... | collective-permute-start | bytes 1179656 | tf_op jit(solution)/shard_map/ppermute | solution.py:258
  26.4 3.4 %copy-start.12 = (bf16[1,128,1536]{2,1,0:T(8,128)(2,1)S(1)}, bf16[1,128,1536]{2,1,0:T(8,128)(2,1)}, u32[]{:S(2)}) copy-start(bf16[1,128,1536]{2,1,0:T(8,128)(2,1)} %get-tuple-element.115) | copy-start | bytes 1179652
  26.4 3.4 %copy-start.13 = (bf16[1,128,1536]{2,1,0:T(8,128)(2,1)S(1)}, bf16[1,128,1536]{2,1,0:T(8,128)(2,1)}, u32[]{:S(2)}) copy-start(bf16[1,128,1536]{2,1,0:T(8,128)(2,1)} %get-tuple-element.116) | copy-start | bytes 1179652
  26.4 11.7 %collective-permute-start.6 = (bf16[2,128,768]{2,1,0:T(8,128)(2,1)S(1)}, bf16[2,128,768]{2,1,0:T(8,128)(2,1)S(1)}, u32[]{:S(2)}, u32[]{:S(2)}) collective-permute-start(bf16[2,128,768]{2,1,0:T(8,128)(2,1)S(1)} %get-tuple-element.103), channel_id=1, source_target_pairs={{0,0},{2,4},{4,2},{6,8},{8,6},{10,12},{12,10},{14,16},{16,14},{18,... | collective-permute-start | bytes 1179656 | tf_op jit(solution)/shard_map/ppermute | solution.py:281
  36.3 16.3 %collective-permute-start.2 = (bf16[2,128,768]{2,1,0:T(8,128)(2,1)S(1)}, bf16[2,128,768]{2,1,0:T(8,128)(2,1)S(1)}, u32[]{:S(2)}, u32[]{:S(2)}) collective-permute-start(bf16[2,128,768]{2,1,0:T(8,128)(2,1)S(1)} %pad_maximum_fusion.3), channel_id=1, source_target_pairs={{0,1},{1,0},{2,3},{3,2},{4,5},{5,4},{6,7},{7,6},{8,9},{9,8},{10,11... | collective-permute-start | bytes 1179656 | tf_op jit(solution)/shard_map/ppermute | solution.py:258
  38.0 14.5 %collective-permute-start.7 = (bf16[2,128,768]{2,1,0:T(8,128)(2,1)S(1)}, bf16[2,128,768]{2,1,0:T(8,128)(2,1)S(1)}, u32[]{:S(2)}, u32[]{:S(2)}) collective-permute-start(bf16[2,128,768]{2,1,0:T(8,128)(2,1)S(1)} %get-tuple-element.56), channel_id=1, source_target_pairs={{0,0},{2,4},{4,2},{6,8},{8,6},{10,12},{12,10},{14,16},{16,14},{18,... | collective-permute-start | bytes 1179656 | tf_op jit(solution)/shard_map/ppermute | solution.py:281
  38.7 0.9 copy-start
  39.6 0.9 copy-start.2
  40.5 1.1 copy-start.1
  41.6 1.1 copy-start.3
  51.6 9.9 %collective-permute-start.8 = (bf16[2,128,768]{2,1,0:T(8,128)(2,1)S(1)}, bf16[2,128,768]{2,1,0:T(8,128)(2,1)S(1)}, u32[]{:S(2)}, u32[]{:S(2)}) collective-permute-start(bf16[2,128,768]{2,1,0:T(8,128)(2,1)S(1)} %get-tuple-element.78), channel_id=1, source_target_pairs={{0,1},{1,0},{2,3},{3,2},{4,5},{5,4},{6,7},{7,6},{8,9},{9,8},{10,11... | collective-permute-start | bytes 1179656 | tf_op jit(solution)/shard_map/ppermute | solution.py:266
  51.9 9.6 %collective-permute-start.9 = (bf16[2,128,768]{2,1,0:T(8,128)(2,1)S(1)}, bf16[2,128,768]{2,1,0:T(8,128)(2,1)S(1)}, u32[]{:S(2)}, u32[]{:S(2)}) collective-permute-start(bf16[2,128,768]{2,1,0:T(8,128)(2,1)S(1)} %get-tuple-element.79), channel_id=1, source_target_pairs={{0,0},{2,4},{4,2},{6,8},{8,6},{10,12},{12,10},{14,16},{16,14},{18,... | collective-permute-start | bytes 1179656 | tf_op jit(solution)/shard_map/ppermute | solution.py:389
  61.5 45.1 %copy-start.5 = (bf16[2,128,768]{2,1,0:T(8,128)(2,1)}, bf16[2,128,768]{2,1,0:T(8,128)(2,1)S(1)}, u32[]{:S(2)}) copy-start(bf16[2,128,768]{2,1,0:T(8,128)(2,1)S(1)} %collective-permute-done.8.part_ref) | copy-start | bytes 1179652
  61.5 14.8 %collective-permute-start.12 = (bf16[2,128,768]{2,1,0:T(8,128)(2,1)S(1)}, bf16[2,128,768]{2,1,0:T(8,128)(2,1)S(1)}, u32[]{:S(2)}, u32[]{:S(2)}) collective-permute-start(bf16[2,128,768]{2,1,0:T(8,128)(2,1)S(1)} %get-tuple-element.90), channel_id=1, source_target_pairs={{0,0},{2,4},{4,2},{6,8},{8,6},{10,12},{12,10},{14,16},{16,14},{18,... | collective-permute-start | bytes 1179656 | tf_op jit(solution)/shard_map/ppermute | solution.py:389
  62.2 43.5 %collective-permute-start.11 = (bf16[2,128,1536]{2,1,0:T(8,128)(2,1)S(1)}, bf16[2,128,1536]{2,1,0:T(8,128)(2,1)S(1)}, u32[]{:S(2)}, u32[]{:S(2)}) collective-permute-start(bf16[2,128,1536]{2,1,0:T(8,128)(2,1)S(1)} %get-tuple-element.89), channel_id=1, source_target_pairs={{0,2},{2,0},{4,6},{6,4},{8,10},{10,8},{12,14},{14,12},{16,18},{18,... | collective-permute-start | bytes 2359304 | tf_op jit(solution)/shard_map/ppermute | solution.py:393
  72.0 2.1 %collective-permute-start.17 = (f32[24,1536]{1,0:T(8,128)S(1)}, f32[24,1536]{1,0:T(8,128)S(1)}, u32[]{:S(2)}, u32[]{:S(2)}) collective-permute-start(f32[24,1536]{1,0:T(8,128)S(1)} %get-tuple-element.102), channel_id=1, source_target_pairs={{0,2},{2,0},{4,6},{6,4},{8,10},{10,8},{12,14},{14,12},{16,18},{18,... | collective-permute-start | bytes 442376 | tf_op jit(solution)/shard_map/ppermute | solution.py:431
  74.2 6.4 %collective-permute-start.18 = (f32[24,1536]{1,0:T(8,128)S(1)}, f32[24,1536]{1,0:T(8,128)S(1)}, u32[]{:S(2)}, u32[]{:S(2)}) collective-permute-start(f32[24,1536]{1,0:T(8,128)S(1)} %add.50), channel_id=1, source_target_pairs={{0,8},{2,10},{4,12},{6,14},{8,0},{10,2},{12,4},{14,6},{16,24},{18,... | collective-permute-start | bytes 442376 | tf_op jit(solution)/shard_map/ppermute | solution.py:431
  76.2 40.0 %collective-permute-start.15 = (bf16[2,128,1536]{2,1,0:T(8,128)(2,1)}, bf16[2,128,1536]{2,1,0:T(8,128)(2,1)S(1)}, u32[]{:S(2)}, u32[]{:S(2)}) collective-permute-start(bf16[2,128,1536]{2,1,0:T(8,128)(2,1)} %get-tuple-element.93), channel_id=1, source_target_pairs={{0,2},{2,0},{4,6},{6,4},{8,10},{10,8},{12,14},{14,12},{16,18},{18,... | collective-permute-start | bytes 2359304 | tf_op jit(solution)/shard_map/ppermute | solution.py:394
  76.3 39.9 %collective-permute-start.16 = (bf16[2,128,1536]{2,1,0:T(8,128)(2,1)}, bf16[2,128,1536]{2,1,0:T(8,128)(2,1)S(1)}, u32[]{:S(2)}, u32[]{:S(2)}) collective-permute-start(bf16[2,128,1536]{2,1,0:T(8,128)(2,1)} %get-tuple-element.95), channel_id=1, source_target_pairs={{0,0},{2,4},{4,2},{6,8},{8,6},{10,12},{12,10},{14,16},{16,14},{18,... | collective-permute-start | bytes 2359304 | tf_op jit(solution)/shard_map/ppermute | solution.py:396
  78.0 29.2 %collective-permute-start.10 = (bf16[2,128,768]{2,1,0:T(8,128)(2,1)S(1)}, bf16[2,128,768]{2,1,0:T(8,128)(2,1)S(1)}, u32[]{:S(2)}, u32[]{:S(2)}) collective-permute-start(bf16[2,128,768]{2,1,0:T(8,128)(2,1)S(1)} %get-tuple-element.80), channel_id=1, source_target_pairs={{0,1},{1,0},{2,3},{3,2},{4,5},{5,4},{6,7},{7,6},{8,9},{9,8},{10,11... | collective-permute-start | bytes 1179656 | tf_op jit(solution)/shard_map/ppermute | solution.py:266
  80.6 17.8 %collective-permute-start.19 = (f32[24,1536]{1,0:T(8,128)S(1)}, f32[24,1536]{1,0:T(8,128)S(1)}, u32[]{:S(2)}, u32[]{:S(2)}) collective-permute-start(f32[24,1536]{1,0:T(8,128)S(1)} %add.51), channel_id=1, source_target_pairs={{0,16},{2,18},{4,20},{6,22},{8,24},{10,26},{12,28},{14,30},{16,0},... | collective-permute-start | bytes 442376 | tf_op jit(solution)/shard_map/ppermute | solution.py:431
  98.4 5.2 %collective-permute-start.20 = (f32[24,1536]{1,0:T(8,128)S(1)}, f32[24,1536]{1,0:T(8,128)S(1)}, u32[]{:S(2)}, u32[]{:S(2)}) collective-permute-start(f32[24,1536]{1,0:T(8,128)S(1)} %add.52), channel_id=1, source_target_pairs={{0,4},{2,6},{4,0},{6,2},{8,12},{10,14},{12,8},{14,10},{16,20},{18,... | collective-permute-start | bytes 442376 | tf_op jit(solution)/shard_map/ppermute | solution.py:431
  104.2 8.9 %collective-permute-start.21 = (f32[24,1536]{1,0:T(8,128)}, f32[24,1536]{1,0:T(8,128)}, u32[]{:S(2)}, u32[]{:S(2)}) collective-permute-start(f32[24,1536]{1,0:T(8,128)} %add.53), channel_id=1, source_target_pairs={{0,1},{1,0},{2,3},{3,2},{4,5},{5,4},{6,7},{7,6},{8,9},{9,8},{10,11... | collective-permute-start | bytes 442376 | tf_op jit(solution)/shard_map/ppermute | solution.py:434
  106.6 13.2 %collective-permute-start.14 = (bf16[2,128,768]{2,1,0:T(8,128)(2,1)}, bf16[2,128,768]{2,1,0:T(8,128)(2,1)}, u32[]{:S(2)}, u32[]{:S(2)}) collective-permute-start(bf16[2,128,768]{2,1,0:T(8,128)(2,1)} %far_sum.3), channel_id=1, source_target_pairs={{0,1},{1,0},{2,3},{3,2},{4,5},{5,4},{6,7},{7,6},{8,9},{9,8},{10,11... | collective-permute-start | bytes 1179656 | tf_op jit(solution)/shard_map/ppermute | solution.py:266
  107.3 0.7 copy-start.7
  108.0 16.6 %collective-permute-start.13 = (bf16[2,128,768]{2,1,0:T(8,128)(2,1)S(1)}, bf16[2,128,768]{2,1,0:T(8,128)(2,1)}, u32[]{:S(2)}, u32[]{:S(2)}) collective-permute-start(bf16[2,128,768]{2,1,0:T(8,128)(2,1)S(1)} %far_sum.2), channel_id=1, source_target_pairs={{0,1},{1,0},{2,3},{3,2},{4,5},{5,4},{6,7},{7,6},{8,9},{9,8},{10,11... | collective-permute-start | bytes 1179656 | tf_op jit(solution)/shard_map/ppermute | solution.py:266
  109.5 1.0 copy-start.6
  110.5 1.3 %copy-start.8 = (bf16[2,128,768]{2,1,0:T(8,128)(2,1)S(1)}, bf16[2,128,768]{2,1,0:T(8,128)(2,1)}, u32[]{:S(2)}) copy-start(bf16[2,128,768]{2,1,0:T(8,128)(2,1)} %copy-done.7) | copy-start | bytes 1179652

commit v2 on v1

--- a/solution.py
+++ b/solution.py
@@ -209,9 +209,46 @@
     value_ref[...] = total[1].astype(value_ref.dtype)
 
 
-def put_kernel(place_ref, part_ref, first_in, second_in, first_ref, second_ref):
-    first_ref[...] = part_ref[0]
-    second_ref[...] = part_ref[1]
+def put_kernel(place_ref, part_ref, first_in, second_in, first_ref, second_ref, sems, *, at):
+    shift, groups, parts, p = at
+    width = part_ref.shape[2]
+    start = (lax.rem(place_ref[1] + shift, groups) * parts + p) * width
+    cols = pl.ds(pl.multiple_of(start, DH), width)
+    copies = [
+        pltpu.make_async_copy(part_ref.at[i], ref.at[:, cols], sems.at[i])
+        for i, ref in enumerate((first_ref, second_ref))
+    ]
+    for copy in copies:
+        copy.start()
+    for copy in copies:
+        copy.wait()
+
+
+def pack_kernel(place_ref, first_ref, second_ref, own_ref, far_ref, sems, *, at):
+    groups, parts, p = at
+    rows, width = own_ref.shape[1:]
+    copies = []
+    for k in range(groups):
+        start = (lax.rem(place_ref[1] + k, groups) * parts + p) * width
+        cols = pl.ds(pl.multiple_of(start, DH), width)
+        for i, ref in enumerate((first_ref, second_ref)):
+            to = own_ref.at[i] if k == 0 else far_ref.at[i, pl.ds((k - 1) * rows, rows)]
+            copies.append(pltpu.make_async_copy(ref.at[:, cols], to, sems.at[2 * k + i]))
+    for copy in copies:
+        copy.start()
+    for copy in copies:
+        copy.wait()
+
+
+def spread_kernel(noise_ref, sums_ref, out_ref):
+    spans = noise_ref.shape[1]
+    levels = lax.broadcasted_iota(jnp.int32, (out_ref.shape[0], spans), 0)
+    out_ref[...] = jnp.dot(
+        (levels == noise_ref[...]).astype(jnp.float32),
+        sums_ref[...],
+        precision=lax.Precision.HIGHEST,
+        preferred_element_type=jnp.float32,
+    )
 
 
 def per_device(
@@ -241,21 +278,36 @@
     side_of = [i - 1 + 2 * (i % 2) for i in range(ctx_count)]
     side_pairs = [(i, j if 0 <= j < ctx_count else i) for i, j in enumerate(side_of)]
 
-    def columns(array, group, part=None):
-        start, size = group * width, width
-        if part is not None:
-            start, size = start + part * part_width, part_width
-        return lax.dynamic_slice_in_dim(array, start, size, 1)
-
-    def to_peers(first, second, part=None, after=None):
+    whole = lambda shape: pl.BlockSpec(shape, lambda i, place: (0,) * len(shape))
+    limit = (26 if tokens <= 256 else 56) * 1024 * 1024
+    params = pltpu.CompilerParams(vmem_limit_bytes=limit)
+    alone = pltpu.CompilerParams(vmem_limit_bytes=60 * 1024 * 1024)
+    small = pltpu.CompilerParams(vmem_limit_bytes=(12 if tokens <= 256 else 36) * 1024 * 1024)
+
+    def pack(first, second, p, params):
+        return pl.pallas_call(
+            functools.partial(pack_kernel, at=(groups, parts, p)),
+            grid_spec=pltpu.PrefetchScalarGridSpec(
+                num_scalar_prefetch=1,
+                grid=(1,),
+                in_specs=[pl.BlockSpec(memory_space=pltpu.HBM)] * 2,
+                out_specs=[pl.BlockSpec(memory_space=pl.ANY)] * 2,
+                scratch_shapes=[pltpu.SemaphoreType.DMA((2 * groups,))],
+            ),
+            out_shape=[
+                jax.ShapeDtypeStruct((2, rows, part_width), bf16),
+                jax.ShapeDtypeStruct((2, far_rows, part_width), bf16),
+            ],
+            compiler_params=params,
+            name="pack",
+        )(place, first, second)
+
+    def to_peers(slab):
         arrived = []
         for k in range(1, groups):
-            group = lax.rem(h + k, groups)
-            slab = jnp.stack([columns(first, group, part), columns(second, group, part)])
-            if after is not None:
-                slab, _ = tie((slab, after))
+            part = slab if groups == 2 else slab[:, (k - 1) * rows : k * rows]
             pairs = [(i, (i + k) % groups) for i in range(groups)]
-            arrived.append(lax.ppermute(slab, "head", pairs))
+            arrived.append(lax.ppermute(part, "head", pairs))
         return arrived[0] if groups == 2 else jnp.concatenate(arrived, axis=1)
 
     def from_peers(slab):
@@ -266,26 +318,23 @@
             arrived.append(lax.ppermute(part, "head", pairs))
         return arrived
 
-    kv_own = jnp.stack([columns(key_rows, h), columns(value_rows, h)])
-    side_own = lax.ppermute(kv_own, "ctx", side_pairs)
-    kv_far = to_peers(key_rows, value_rows)
-    near_own = lax.ppermute(kv_own, "ctx", near_pairs)
-    near_far = lax.ppermute(kv_far, "ctx", near_pairs)
-    qo_own = jnp.stack([columns(queries, h), columns(out_cotangent, h)])
-    side_far, qo_far = [], []
-    side_after, qo_after = None, kv_far
+    kv_own, kv_far, qo_own, qo_far = [], [], [], []
+    side_own, side_far, near_own, near_far = [], [], [], []
     for p in range(parts):
-        piece = kv_far[:, :, p * part_width : (p + 1) * part_width]
-        if side_after is not None:
-            piece, _ = tie((piece, side_after))
-        side_after = lax.ppermute(piece, "ctx", side_pairs)
-        side_far.append(side_after)
-        qo_after = to_peers(queries, out_cotangent, p, qo_after)
-        qo_far.append(qo_after)
-
-    limit = (30 if tokens <= 256 else 56) * 1024 * 1024
-    params = pltpu.CompilerParams(vmem_limit_bytes=limit)
-    small = pltpu.CompilerParams(vmem_limit_bytes=(12 if tokens <= 256 else 36) * 1024 * 1024)
+        own_kv, sent_kv = pack(key_rows, value_rows, p, small if p else alone)
+        own_qo, sent_qo = pack(queries, out_cotangent, p, small)
+        kv_own.append(own_kv)
+        qo_own.append(own_qo)
+        if p > 0:
+            own_kv, sent_kv, *_ = tie((own_kv, sent_kv, qo_far[-1], side_far[-1]))
+        side_own.append(lax.ppermute(own_kv, "ctx", side_pairs))
+        kv_far.append(to_peers(sent_kv))
+        near_own.append(lax.ppermute(own_kv, "ctx", near_pairs))
+        sent_qo, *_ = tie((sent_qo, kv_far[p], side_own[p]))
+        side_far.append(lax.ppermute(kv_far[p], "ctx", side_pairs))
+        near_far.append(lax.ppermute(kv_far[p], "ctx", near_pairs))
+        qo_far.append(to_peers(sent_qo))
+
     sizes = (ctx_count, groups, rows, span_total, level_count, by_span)
     whole = lambda shape: pl.BlockSpec(shape, lambda i, place: (0,) * len(shape))
     bias, gate, slot = pl.pallas_call(
@@ -337,7 +386,8 @@
         column = lambda count: pl.BlockSpec((count, block), lambda i, place: (0, p * steps + i))
         struct = jax.ShapeDtypeStruct
         inputs = [
-            qo_own, kv_own, qo_far[p], kv_far, near_own, near_far, side_own, side_far[p],
+            qo_own[p], kv_own[p], qo_far[p], kv_far[p],
+            near_own[p], near_far[p], side_own[p], side_far[p],
             gate, bias, slot,
         ]
         return pl.pallas_call(
@@ -348,8 +398,8 @@
                 num_scalar_prefetch=1,
                 grid=(steps,),
                 in_specs=[
-                    at_part(rows), at_part(rows), pair(far_rows), at_part(far_rows),
-                    at_part(rows), at_part(far_rows), at_part(rows), pair(far_rows),
+                    pair(rows), pair(rows), pair(far_rows), pair(far_rows),
+                    pair(rows), pair(far_rows), pair(rows), pair(far_rows),
                     column(tokens), whole((3 * tokens, tokens)), whole((slots, tokens)),
                 ]
                 + [pl.BlockSpec(memory_space=pl.ANY)] * len(joint),
@@ -394,7 +444,7 @@
     near_back_own = lax.ppermute(near_grad_own, "ctx", near_pairs)
     side_grad_own, _ = tie((side_grad_own, side_back_far[-1]))
     side_back_own = lax.ppermute(side_grad_own, "ctx", side_pairs)
-    grad_far = []
+    grad_far, grad_sent = [], []
     for p in range(parts):
         at_part = pl.BlockSpec((2, far_rows, part_width), lambda i, p=p: (0, 0, p))
         alone = pl.BlockSpec((2, far_rows, part_width), lambda i: (0, 0, 0))
@@ -407,6 +457,7 @@
             compiler_params=small,
             name="far_sum",
         )(far, near_back_far, side_back_far[p])
+        grad_sent.append(far_grad)
         grad_far.append(from_peers(far_grad))
     key_grad, value_grad = pl.pallas_call(
         own_sum_kernel,
@@ -424,40 +475,55 @@
         name="own_sum",
     )(place, own, near_back_own, side_back_own)
 
-    slot_sums = sums
-    steps_of_two = [1 << n for n in range(ctx_count.bit_length() - 1)]
-    for step in steps_of_two[:1] + steps_of_two[2:] + steps_of_two[1:2]:
-        pairs = [(i, i ^ step) for i in range(ctx_count)]
-        slot_sums = slot_sums + lax.ppermute(slot_sums, "ctx", pairs)
-    for step in (1 << n for n in range(groups.bit_length() - 1)):
-        pairs = [(i, i ^ step) for i in range(groups)]
-        other = lax.ppermute(slot_sums, "head", pairs)
-        slot_sums = jnp.where(
-            (h // step) % 2 == 0,
-            jnp.concatenate([slot_sums, other], axis=1),
-            jnp.concatenate([other, slot_sums], axis=1),
-        )
+    def reduced(order, sums):
+        for step in order:
+            pairs = [(i, i ^ step) for i in range(ctx_count)]
+            sums = sums + lax.ppermute(sums, "ctx", pairs)
+        for step in (1 << n for n in range(groups.bit_length() - 1)):
+            pairs = [(i, i ^ step) for i in range(groups)]
+            other = lax.ppermute(sums, "head", pairs)
+            sums = jnp.where(
+                (h // step) % 2 == 0,
+                jnp.concatenate([sums, other], axis=1),
+                jnp.concatenate([other, sums], axis=1),
+            )
+        return sums
+
+    doubling = [1 << n for n in range(ctx_count.bit_length() - 1)]
+    turned = doubling[:1] + doubling[2:] + doubling[1:2]
+    sums, _ = tie((sums, grad_sent))
+    slot_sums = lax.cond(
+        noise_level[0] >= 0,
+        functools.partial(reduced, turned),
+        functools.partial(reduced, doubling),
+        sums,
+    )
     if by_span:
-        level_onehot = (
-            jnp.arange(level_count, dtype=jnp.int32)[:, None] == noise_level[None, :]
-        ).astype(f32)
-        gate_grad = jnp.dot(level_onehot, slot_sums, precision=lax.Precision.HIGHEST)
+        gate_grad = pl.pallas_call(
+            spread_kernel,
+            grid=(groups,),
+            in_specs=[
+                pl.BlockSpec((1, span_total), lambda i: (0, 0)),
+                pl.BlockSpec((slots, width), lambda i: (0, i)),
+            ],
+            out_specs=pl.BlockSpec((level_count, width), lambda i: (0, i)),
+            out_shape=jax.ShapeDtypeStruct((level_count, full_width), f32),
+            compiler_params=small,
+            name="spread",
+        )(noise_level.reshape(1, span_total), slot_sums)
     else:
         gate_grad = slot_sums
 
     def put(first, second, arrived, k, p):
-        out = pl.BlockSpec(
-            (rows, part_width),
-            lambda i, place: (0, lax.rem(place[1] + k, groups) * parts + p),
-        )
         anywhere = pl.BlockSpec(memory_space=pl.ANY)
         return pl.pallas_call(
-            put_kernel,
+            functools.partial(put_kernel, at=(k, groups, parts, p)),
             grid_spec=pltpu.PrefetchScalarGridSpec(
                 num_scalar_prefetch=1,
                 grid=(1,),
-                in_specs=[whole((2, rows, part_width)), anywhere, anywhere],
-                out_specs=[out, out],
+                in_specs=[anywhere] * 3,
+                out_specs=[anywhere] * 2,
+                scratch_shapes=[pltpu.SemaphoreType.DMA((2,))],
             ),
             out_shape=[jax.ShapeDtypeStruct((rows, full_width), bf16)] * 2,
             input_output_aliases={2: 0, 3: 1},

time: 127 us -> 187 us (1.47)
  Pallas kernels: 30.1 us -> 82.8 us
  starting transfers between devices: 35.3 us -> 61.9 us
  local copies, waits for them, and re-layouts: 10.3 us -> 0.7 us
  waiting for transfers between devices: 44.7 us -> 37 us
  matrix products: 3.03 us -> 0 us
    pallas_call x4 -> x9, Pallas kernels: 7.19 us -> 61 us  [the longest x4 29.8 us: put(): pl.pallas_call(functools.partial(put_kernel, at=(k, groups, parts, p)), g...]
    ppermute x13 -> x17, starting transfers between devices: 18.1 us -> 45.2 us  [the longest x4 21.1 us: reduced(): sums = sums + lax.ppermute(sums, 'ctx', pairs)]
    ppermute x13 -> x17, waiting for transfers between devices: 40.2 us -> 34.4 us  [the longest x4 16.6 us: reduced(): sums = sums + lax.ppermute(sums, 'ctx', pairs)]
    unnamed x34 -> x22, local copies, waits for them, and re-layouts: 5.8 us -> 0.7 us
    another operation x3 -> x0, local copies, waits for them, and re-layouts: 4.45 us -> none  [the longest x2 3.52 us: to_peers(): jnp.stack([columns(first, group, part), columns(second, group, part)])]
    dot_general x1 -> x0, matrix products: 3.03 us -> none  [per_device(): jnp.dot(level_onehot, slot_sums, precision=lax.Precision.HIGHEST)]
    another operation x5 -> x0, other arithmetic: 1.92 us -> none  [the longest x3 1.77 us: to_peers(): jnp.stack([columns(first, group, part), columns(second, group, part)])]
    select_n x0 -> x1, other arithmetic: none -> 1.9 us  [reduced(): jnp.where(h // step % 2 == 0, jnp.concatenate([sums, other], axis=1), jnp...]
  transfers between devices with their start and end apart: 22 -> 26, of which waited for: 8 -> 8; matrix products, arithmetic and copies ran while one was open for 6% -> 1% of each run, Pallas kernels for 22% -> 23%
where the time goes in v2:
time: 187 us
  Pallas kernels  82.8 us (44%)
  starting transfers between devices  61.9 us (33%)
  waiting for transfers between devices  37 us (20%)
  other arithmetic  3.22 us (2%)
    pallas_call x4, Pallas kernels, put(): pl.pallas_call(functools.partial(put_kernel, at=(k, groups, parts, p)), g...  29.8 us
    pallas_call x4, Pallas kernels, pack(): pl.pallas_call(functools.partial(pack_kernel, at=(groups, parts, p)), gri...  27.9 us
    ppermute x4, starting transfers between devices, reduced(): sums = sums + lax.ppermute(sums, 'ctx', pairs)  21.1 us
    pallas_call x2, Pallas kernels, attention(): pl.pallas_call(functools.partial(attention_kernel, rows=rows, tokens=toke...  16.6 us
    ppermute x4, waiting for transfers between devices, reduced(): sums = sums + lax.ppermute(sums, 'ctx', pairs)  16.6 us
    ppermute x4, waiting for transfers between devices, to_peers(): arrived.append(lax.ppermute(part, 'head', pairs))  13.2 us
    ppermute x1, starting transfers between devices, per_device(): near_back_far = lax.ppermute(near_grad_far, 'ctx', near_pairs)  9.24 us
    ppermute x4, starting transfers between devices, to_peers(): arrived.append(lax.ppermute(part, 'head', pairs))  8.03 us
  transfers between devices with their start and end apart: 26, of which 8 were waited for; matrix products, arithmetic and copies ran while one was open for 1% of the time, Pallas kernels for 23%

profile of v2, /device:TPU:0, one launch (start us, length us, event | category | flops | bytes accessed | tf_op | source)
XLA Modules:
  0.0 186.5 jit_solution(5764784288918560257)
XLA Ops:
  0.7 0.6 pad_add_fusion.place_ref
  1.2 25.8 %pack.7 = (bf16[2,128,768]{2,1,0:T(8,128)(2,1)}, bf16[2,128,768]{2,1,0:T(8,128)(2,1)}) custom-call(s32[2]{0:T(128)} %pad_add_fusion.place_ref, bf16[128,3072]{1,0:T(8,128)(2,1)} %first_ref.7, bf16[128,3072]{1,0:T(8,128)(2,1)} %second_ref.7), custom_call_target="tpu_custom_call" | custom-call | tf_op jit(solution)/shard_map/pack/pallas_call | solution.py:288
  27.0 3.0 %collective-permute-start.10 = (bf16[2,128,768]{2,1,0:T(8,128)(2,1)}, bf16[2,128,768]{2,1,0:T(8,128)(2,1)S(1)}, u32[]{:S(2)}, u32[]{:S(2)}) collective-permute-start(bf16[2,128,768]{2,1,0:T(8,128)(2,1)} %get-tuple-element.84), channel_id=1, source_target_pairs={{0,1},{1,0},{2,3},{3,2},{4,5},{5,4},{6,7},{7,6},{8,9},{9,8},{10,11... | collective-permute-start | bytes 1179656 | tf_op jit(solution)/shard_map/ppermute | solution.py:310
  30.0 1.6 collective-permute-start.11
  31.7 0.7 copy-done.5
  32.4 0.7 pack.6
  33.1 6.3 %collective-permute-done.10.kv_ref = bf16[2,128,768]{2,1,0:T(8,128)(2,1)S(1)} collective-permute-done((bf16[2,128,768]{2,1,0:T(8,128)(2,1)}, bf16[2,128,768]{2,1,0:T(8,128)(2,1)S(1)}, u32[]{:S(2)}, u32[]{:S(2)}) %collective-permute-start.10) | collective-permute-done | bytes 393248 | tf_op jit(solution)/shard_map/ppermute | solution.py:310
  39.4 0.0 collective-permute-done.11.side_own_ref
  39.4 0.0 copy-start.9
  39.4 1.8 collective-permute-start.12
  41.2 0.7 collective-permute-start.13
  41.9 0.7 pack.5
  42.6 6.9 %collective-permute-done.12.qo_ref = bf16[2,128,768]{2,1,0:T(8,128)(2,1)S(1)} collective-permute-done((bf16[2,128,768]{2,1,0:T(8,128)(2,1)S(1)}, bf16[2,128,768]{2,1,0:T(8,128)(2,1)S(1)}, u32[]{:S(2)}, u32[]{:S(2)}) %collective-permute-start.12) | collective-permute-done | bytes 393248 | tf_op jit(solution)/shard_map/ppermute | solution.py:310
  49.5 0.0 collective-permute-done.13.side_far_ref
  49.5 2.5 %collective-permute-start.14 = (bf16[2,128,768]{2,1,0:T(8,128)(2,1)S(1)}, bf16[2,128,768]{2,1,0:T(8,128)(2,1)S(1)}, u32[]{:S(2)}, u32[]{:S(2)}) collective-permute-start(bf16[2,128,768]{2,1,0:T(8,128)(2,1)S(1)} %get-tuple-element.87), channel_id=1, source_target_pairs={{0,1},{1,0},{2,3},{3,2},{4,5},{5,4},{6,7},{7,6},{8,9},{9,8},{10,11... | collective-permute-start | bytes 1179656 | tf_op jit(solution)/shard_map/ppermute | solution.py:310
  52.0 0.7 collective-permute-start.15
  52.7 7.0 %collective-permute-start.20 = (bf16[2,128,768]{2,1,0:T(8,128)(2,1)S(1)}, bf16[2,128,768]{2,1,0:T(8,128)(2,1)S(1)}, u32[]{:S(2)}, u32[]{:S(2)}) collective-permute-start(bf16[2,128,768]{2,1,0:T(8,128)(2,1)S(1)} %copy-done.10), channel_id=1, source_target_pairs={{0,2},{2,0},{4,6},{6,4},{8,10},{10,8},{12,14},{14,12},{16,18},{18,... | collective-permute-start | bytes 1179656 | tf_op jit(solution)/shard_map/ppermute | solution.py:332
  59.7 0.1 collective-permute-start.21
  59.8 0.4 collective-permute-start.17
  60.2 0.7 pack.4
  60.9 0.0 collective-permute-done.15.side_own_ref
  60.9 0.7 collective-permute-start.16
  61.6 4.1 %collective-permute-start.18 = (bf16[2,128,768]{2,1,0:T(8,128)(2,1)S(1)}, bf16[2,128,768]{2,1,0:T(8,128)(2,1)S(1)}, u32[]{:S(2)}, u32[]{:S(2)}) collective-permute-start(bf16[2,128,768]{2,1,0:T(8,128)(2,1)S(1)} %collective-permute-done.14.kv_ref), channel_id=1, source_target_pairs={{0,2},{2,0},{4,6},{6,4},{8,10},{10,8},{12,14},{14,12},{16,18},{18,... | collective-permute-start | bytes 1179656 | tf_op jit(solution)/shard_map/ppermute | solution.py:335
  65.7 0.7 collective-permute-start.19
  66.4 2.4 %prep.1 = (f32[768,256]{1,0:T(8,128)S(1)}, f32[256,1536]{1,0:T(8,128)S(1)}, bf16[24,256]{1,0:T(8,128)(2,1)S(1)}) custom-call(s32[2]{0:T(128)S(1)} %copy-done.5, s32[32,128]{1,0:T(8,128)S(1)} %bitcast.6, s32[1,24]{1,0:T(1,128)S(1)} %bitcast.7, s32[24,24]{1,0:T(8,128)S(1)} %copy-done.8, f32[128,3072]{1,0:T(8,128)S(1)} %copy-done.4), custom_call_target="tpu_custom_call" | custom-call | tf_op jit(solution)/shard_map/prep/pallas_call | solution.py:340
  68.9 8.3 %attention.2 = (bf16[2,128,768]{2,1,0:T(8,128)(2,1)S(1)}, bf16[2,128,768]{2,1,0:T(8,128)(2,1)S(1)}, bf16[128,3072]{1,0:T(8,128)(2,1)}, bf16[128,3072]{1,0:T(8,12...) custom-call(s32[2]{0:T(128)S(1)} %copy-done.6, ...), custom_call_target="tpu_custom_call" | custom-call | flops 1811939328 | bytes 3145728 | tf_op jit(solution)/shard_map/attention/pallas_call | solution.py:393
  77.1 1.4 collective-permute-start.22
  78.5 0.0 collective-permute-done.17.near_own_ref
  78.5 0.7 collective-permute-start.23
  79.2 0.0 collective-permute-done.16.qo_ref
  79.2 0.0 collective-permute-done.18.near_far_ref
  79.2 8.3 %attention.3 = (bf16[2,128,768]{2,1,0:T(8,128)(2,1)S(1)}, bf16[2,128,768]{2,1,0:T(8,128)(2,1)S(1)}, bf16[128,3072]{1,0:T(8,128)(2,1)}, bf16[128,3072]{1,0:T(8,12...) custom-call(s32[2]{0:T(128)S(1)} %copy-done.6, ...), custom_call_target="tpu_custom_call", output_to_operand_aliasing={{2}: (12, {}), {3}: (13, {}), {4}: (14, {}), {5}: (15, {}),... | custom-call | flops 1811939328 | bytes 3145728 | tf_op jit(solution)/shard_map/attention/pallas_call | solution.py:393
  87.6 0.0 collective-permute-done.22.part_ref
  87.6 0.0 collective-permute-done.23.side_ref
  87.6 0.7 collective-permute-start.26
  88.3 9.2 %collective-permute-start.25 = (bf16[2,128,1536]{2,1,0:T(8,128)(2,1)S(1)}, bf16[2,128,1536]{2,1,0:T(8,128)(2,1)S(1)}, u32[]{:S(2)}, u32[]{:S(2)}) collective-permute-start(bf16[2,128,1536]{2,1,0:T(8,128)(2,1)S(1)} %get-tuple-element.123), channel_id=1, source_target_pairs={{0,2},{2,0},{4,6},{6,4},{8,10},{10,8},{12,14},{14,12},{16,18},{18,... | collective-permute-start | bytes 2359304 | tf_op jit(solution)/shard_map/ppermute | solution.py:443
  97.5 0.1 collective-permute-start.29
  97.6 1.8 collective-permute-start.30
  99.4 0.8 collective-permute-start.24
  100.2 0.9 far_sum.3
  101.0 1.2 collective-permute-start.28
  102.3 0.1 far_sum.2
  102.4 0.8 collective-permute-start.27
  103.3 1.3 put.4
  104.6 2.5 %collective-permute-done.24.part_ref = bf16[2,128,768]{2,1,0:T(8,128)(2,1)S(1)} collective-permute-done((bf16[2,128,768]{2,1,0:T(8,128)(2,1)S(1)}, bf16[2,128,768]{2,1,0:T(8,128)(2,1)S(1)}, u32[]{:S(2)}, u32[]{:S(2)}) %collective-permute-start.24) | collective-permute-done | bytes 393248 | tf_op jit(solution)/shard_map/ppermute | solution.py:318
  107.2 1.3 put.5
  108.5 45.8 %conditional.1 = (f32[24,3072]{1,0:T(8,128)}) conditional(s32[]{:T(128)} %bitcast.4, (s32[]{:T(128)}, f32[24,1536]{1,0:T(8,128)S(1)}) %tuple.26, (s32[]{:T(128)}, f32[24,1536]{1,0:T(8,128)S(1)}) %tuple.26), branch_computations={%region_0.1_spmd, %region_1.2_spmd} | conditional | flops 368652 | bytes 5308743 | solution.py:495
  108.5 12.5 %collective-permute-start.5 = (f32[24,1536]{1,0:T(8,128)S(1)}, f32[24,1536]{1,0:T(8,128)S(1)}, u32[]{:S(2)}, u32[]{:S(2)}) collective-permute-start(f32[24,1536]{1,0:T(8,128)S(1)} %get-tuple-element.14), channel_id=1, source_target_pairs={{0,2},{2,0},{4,6},{6,4},{8,10},{10,8},{12,14},{14,12},{16,18},{18,... | collective-permute-start | bytes 442376 | tf_op jit(solution)/shard_map/cond/branch_1_fun/ppermute | solution.py:481
  121.0 1.0 collective-permute-done.5
  122.0 4.9 %collective-permute-start.6 = (f32[24,1536]{1,0:T(8,128)S(1)}, f32[24,1536]{1,0:T(8,128)S(1)}, u32[]{:S(2)}, u32[]{:S(2)}) collective-permute-start(f32[24,1536]{1,0:T(8,128)S(1)} %add.29), channel_id=1, source_target_pairs={{0,8},{2,10},{4,12},{6,14},{8,0},{10,2},{12,4},{14,6},{16,24},{18,... | collective-permute-start | bytes 442376 | tf_op jit(solution)/shard_map/cond/branch_1_fun/ppermute | solution.py:481
  127.0 4.4 %collective-permute-done.6 = f32[24,1536]{1,0:T(8,128)S(1)} collective-permute-done((f32[24,1536]{1,0:T(8,128)S(1)}, f32[24,1536]{1,0:T(8,128)S(1)}, u32[]{:S(2)}, u32[]{:S(2)}) %collective-permute-start.6) | collective-permute-done | bytes 147488 | tf_op jit(solution)/shard_map/cond/branch_1_fun/ppermute | solution.py:481
  131.3 2.8 %collective-permute-start.7 = (f32[24,1536]{1,0:T(8,128)S(1)}, f32[24,1536]{1,0:T(8,128)S(1)}, u32[]{:S(2)}, u32[]{:S(2)}) collective-permute-start(f32[24,1536]{1,0:T(8,128)S(1)} %add.30), channel_id=1, source_target_pairs={{0,16},{2,18},{4,20},{6,22},{8,24},{10,26},{12,28},{14,30},{16,0},... | collective-permute-start | bytes 442376 | tf_op jit(solution)/shard_map/cond/branch_1_fun/ppermute | solution.py:481
  134.2 6.8 %collective-permute-done.7 = f32[24,1536]{1,0:T(8,128)S(1)} collective-permute-done((f32[24,1536]{1,0:T(8,128)S(1)}, f32[24,1536]{1,0:T(8,128)S(1)}, u32[]{:S(2)}, u32[]{:S(2)}) %collective-permute-start.7) | collective-permute-done | bytes 147488 | tf_op jit(solution)/shard_map/cond/branch_1_fun/ppermute | solution.py:481
  141.0 0.9 collective-permute-start.8
  141.9 4.3 %collective-permute-done.8 = f32[24,1536]{1,0:T(8,128)S(1)} collective-permute-done((f32[24,1536]{1,0:T(8,128)S(1)}, f32[24,1536]{1,0:T(8,128)S(1)}, u32[]{:S(2)}, u32[]{:S(2)}) %collective-permute-start.8) | collective-permute-done | bytes 147488 | tf_op jit(solution)/shard_map/cond/branch_1_fun/ppermute | solution.py:481
  146.2 0.7 add.32
  146.9 0.8 collective-permute-start.9
  147.7 4.7 %collective-permute-done.9 = f32[24,1536]{1,0:T(8,128)} collective-permute-done((f32[24,1536]{1,0:T(8,128)}, f32[24,1536]{1,0:T(8,128)}, u32[]{:S(2)}, u32[]{:S(2)}) %collective-permute-start.9) | collective-permute-done | bytes 147488 | tf_op jit(solution)/shard_map/cond/branch_1_fun/ppermute | solution.py:484
  152.4 1.9 %maximum_select_fusion.1 = f32[24,3072]{1,0:T(8,128)} fusion(f32[24,1536]{1,0:T(8,128)} %collective-permute-done.9, f32[24,1536]{1,0:T(8,128)} %add.32, pred[]{:T(512)S(6)} %eq.8), kind=kLoop, calls=%fused_computation.1 | loop fusion | flops 221184 | bytes 589825 | tf_op jit(solution)/shard_map/cond/branch_1_fun/jit(_where)/select_n | solution.py:485
  154.3 3.3 %spread.1 = f32[128,3072]{1,0:T(8,128)} custom-call(s32[1,24]{1,0:T(1,128)S(1)} %bitcast.9, f32[24,3072]{1,0:T(8,128)} %get-tuple-element.138.sums_ref), custom_call_target="tpu_custom_call" | custom-call | tf_op jit(solution)/shard_map/spread/pallas_call | solution.py:502
  157.6 0.0 collective-permute-done.29.near_ref
  157.6 1.8 own_sum.1
  159.4 13.6 %put.6 = (bf16[128,3072]{1,0:T(8,128)(2,1)}, bf16[128,3072]{1,0:T(8,128)(2,1)}) custom-call(s32[2]{0:T(128)S(1)} %copy-done.6, bf16[2,128,768]{2,1,0:T(8,128)(2,1)} %collective-permute-done.28.part_ref, bf16[128,3072]{1,0:T(8,128)(2,1)} %get-tuple-element.130.first_in, ...), custom_call_target="tpu_custom_call", output_to_operand_aliasing={{0}: (2, {}), {1}: (3, {})} | custom-call | tf_op jit(solution)/shard_map/put/pallas_call | solution.py:519
  173.0 13.6 %put.7 = (bf16[128,3072]{1,0:T(8,128)(2,1)}, bf16[128,3072]{1,0:T(8,128)(2,1)}) custom-call(s32[2]{0:T(128)S(1)} %copy-done.6, bf16[2,128,768]{2,1,0:T(8,128)(2,1)} %collective-permute-done.27.part_ref, bf16[128,3072]{1,0:T(8,128)(2,1)} %get-tuple-element.132.first_in, ...), custom_call_target="tpu_custom_call", output_to_operand_aliasing={{0}: (2, {}), {1}: (3, {})} | custom-call | tf_op jit(solution)/shard_map/put/pallas_call | solution.py:519
  (32 shorter events, 0.1 us)
Async XLA Ops:
  0.6 31.1 %copy-start.2 = (bf16[128,3072]{1,0:T(8,128)(2,1)S(1)}, bf16[128,3072]{1,0:T(8,128)(2,1)}, u32[]{:S(2)}) copy-start(bf16[128,3072]{1,0:T(8,128)(2,1)} %first_ref.6) | copy-start | bytes 2359300
  0.6 31.1 %copy-start.3 = (bf16[128,3072]{1,0:T(8,128)(2,1)S(1)}, bf16[128,3072]{1,0:T(8,128)(2,1)}, u32[]{:S(2)}) copy-start(bf16[128,3072]{1,0:T(8,128)(2,1)} %second_ref.6) | copy-start | bytes 2359300
  1.2 40.6 %copy-start = (bf16[128,3072]{1,0:T(8,128)(2,1)S(1)}, bf16[128,3072]{1,0:T(8,128)(2,1)}, u32[]{:S(2)}) copy-start(bf16[128,3072]{1,0:T(8,128)(2,1)} %first_ref.7) | copy-start | bytes 2359300
  1.2 40.7 %copy-start.1 = (bf16[128,3072]{1,0:T(8,128)(2,1)S(1)}, bf16[128,3072]{1,0:T(8,128)(2,1)}, u32[]{:S(2)}) copy-start(bf16[128,3072]{1,0:T(8,128)(2,1)} %second_ref.7) | copy-start | bytes 2359300
  27.0 12.4 %collective-permute-start.10 = (bf16[2,128,768]{2,1,0:T(8,128)(2,1)}, bf16[2,128,768]{2,1,0:T(8,128)(2,1)S(1)}, u32[]{:S(2)}, u32[]{:S(2)}) collective-permute-start(bf16[2,128,768]{2,1,0:T(8,128)(2,1)} %get-tuple-element.84), channel_id=1, source_target_pairs={{0,1},{1,0},{2,3},{3,2},{4,5},{5,4},{6,7},{7,6},{8,9},{9,8},{10,11... | collective-permute-start | bytes 1179656 | tf_op jit(solution)/shard_map/ppermute | solution.py:310
  30.0 9.3 %collective-permute-start.11 = (bf16[2,128,768]{2,1,0:T(8,128)(2,1)}, bf16[2,128,768]{2,1,0:T(8,128)(2,1)S(1)}, u32[]{:S(2)}, u32[]{:S(2)}) collective-permute-start(bf16[2,128,768]{2,1,0:T(8,128)(2,1)} %get-tuple-element.85.kv_own_ref), channel_id=1, source_target_pairs={{0,0},{2,4},{4,2},{6,8},{8,6},{10,12},{12,10},{14,16},{16,14},{18,... | collective-permute-start | bytes 1179656 | tf_op jit(solution)/shard_map/ppermute | solution.py:330
  31.7 0.7 copy-start.5
  32.4 20.3 %copy-start.10 = (bf16[2,128,768]{2,1,0:T(8,128)(2,1)S(1)}, bf16[2,128,768]{2,1,0:T(8,128)(2,1)}, u32[]{:S(2)}) copy-start(bf16[2,128,768]{2,1,0:T(8,128)(2,1)} %get-tuple-element.85.kv_own_ref) | copy-start | bytes 1179652
  39.4 27.0 %copy-start.4 = (f32[128,3072]{1,0:T(8,128)S(1)}, f32[128,3072]{1,0:T(8,128)}, u32[]{:S(2)}) copy-start(f32[128,3072]{1,0:T(8,128)} %table_ref.1) | copy-start | bytes 4718596
  39.4 27.0 %copy-start.7 = (s32[4096]{0:T(1024)S(1)}, s32[4096]{0:T(1024)}, u32[]{:S(2)}) copy-start(s32[4096]{0:T(1024)} %param.15) | copy-start | bytes 49156
  39.4 27.0 %copy-start.8 = (s32[24,24]{1,0:T(8,128)S(1)}, s32[24,24]{1,0:T(8,128)}, u32[]{:S(2)}) copy-start(s32[24,24]{1,0:T(8,128)} %mask_ref.1) | copy-start | bytes 6916
  39.4 27.0 %copy-start.9 = (s32[24]{0:T(128)S(1)}, s32[24]{0:T(128)}, u32[]{:S(2)}) copy-start(s32[24]{0:T(128)} %param.16) | copy-start | bytes 292
  39.4 10.1 %collective-permute-start.12 = (bf16[2,128,768]{2,1,0:T(8,128)(2,1)S(1)}, bf16[2,128,768]{2,1,0:T(8,128)(2,1)S(1)}, u32[]{:S(2)}, u32[]{:S(2)}) collective-permute-start(bf16[2,128,768]{2,1,0:T(8,128)(2,1)S(1)} %get-tuple-element.86), channel_id=1, source_target_pairs={{0,1},{1,0},{2,3},{3,2},{4,5},{5,4},{6,7},{7,6},{8,9},{9,8},{10,11... | collective-permute-start | bytes 1179656 | tf_op jit(solution)/shard_map/ppermute | solution.py:310
  41.2 8.3 %collective-permute-start.13 = (bf16[2,128,768]{2,1,0:T(8,128)(2,1)S(1)}, bf16[2,128,768]{2,1,0:T(8,128)(2,1)S(1)}, u32[]{:S(2)}, u32[]{:S(2)}) collective-permute-start(bf16[2,128,768]{2,1,0:T(8,128)(2,1)S(1)} %collective-permute-done.10.kv_ref), channel_id=1, source_target_pairs={{0,0},{2,4},{4,2},{6,8},{8,6},{10,12},{12,10},{14,16},{16,14},{18,... | collective-permute-start | bytes 1179656 | tf_op jit(solution)/shard_map/ppermute | solution.py:334
  49.5 19.4 %copy-start.6 = (s32[2]{0:T(128)S(1)}, s32[2]{0:T(128)}, u32[]{:S(2)}) copy-start(s32[2]{0:T(128)} %pad_add_fusion.place_ref) | copy-start | bytes 28
  49.5 11.4 %collective-permute-start.14 = (bf16[2,128,768]{2,1,0:T(8,128)(2,1)S(1)}, bf16[2,128,768]{2,1,0:T(8,128)(2,1)S(1)}, u32[]{:S(2)}, u32[]{:S(2)}) collective-permute-start(bf16[2,128,768]{2,1,0:T(8,128)(2,1)S(1)} %get-tuple-element.87), channel_id=1, source_target_pairs={{0,1},{1,0},{2,3},{3,2},{4,5},{5,4},{6,7},{7,6},{8,9},{9,8},{10,11... | collective-permute-start | bytes 1179656 | tf_op jit(solution)/shard_map/ppermute | solution.py:310
  52.0 8.9 %collective-permute-start.15 = (bf16[2,128,768]{2,1,0:T(8,128)(2,1)S(1)}, bf16[2,128,768]{2,1,0:T(8,128)(2,1)S(1)}, u32[]{:S(2)}, u32[]{:S(2)}) collective-permute-start(bf16[2,128,768]{2,1,0:T(8,128)(2,1)S(1)} %get-tuple-element.88.kv_own_ref), channel_id=1, source_target_pairs={{0,0},{2,4},{4,2},{6,8},{8,6},{10,12},{12,10},{14,16},{16,14},{18,... | collective-permute-start | bytes 1179656 | tf_op jit(solution)/shard_map/ppermute | solution.py:330
  52.7 13.0 %collective-permute-start.20 = (bf16[2,128,768]{2,1,0:T(8,128)(2,1)S(1)}, bf16[2,128,768]{2,1,0:T(8,128)(2,1)S(1)}, u32[]{:S(2)}, u32[]{:S(2)}) collective-permute-start(bf16[2,128,768]{2,1,0:T(8,128)(2,1)S(1)} %copy-done.10), channel_id=1, source_target_pairs={{0,2},{2,0},{4,6},{6,4},{8,10},{10,8},{12,14},{14,12},{16,18},{18,... | collective-permute-start | bytes 1179656 | tf_op jit(solution)/shard_map/ppermute | solution.py:332
  59.7 9.2 %collective-permute-start.21 = (bf16[2,128,768]{2,1,0:T(8,128)(2,1)S(1)}, bf16[2,128,768]{2,1,0:T(8,128)(2,1)S(1)}, u32[]{:S(2)}, u32[]{:S(2)}) collective-permute-start(bf16[2,128,768]{2,1,0:T(8,128)(2,1)S(1)} %collective-permute-done.10.kv_ref), channel_id=1, source_target_pairs={{0,2},{2,0},{4,6},{6,4},{8,10},{10,8},{12,14},{14,12},{16,18},{18,... | collective-permute-start | bytes 1179656 | tf_op jit(solution)/shard_map/ppermute | solution.py:335
  59.8 18.8 %collective-permute-start.17 = (bf16[2,128,768]{2,1,0:T(8,128)(2,1)S(1)}, bf16[2,128,768]{2,1,0:T(8,128)(2,1)S(1)}, u32[]{:S(2)}, u32[]{:S(2)}) collective-permute-start(bf16[2,128,768]{2,1,0:T(8,128)(2,1)S(1)} %get-tuple-element.88.kv_own_ref), channel_id=1, source_target_pairs={{0,2},{2,0},{4,6},{6,4},{8,10},{10,8},{12,14},{14,12},{16,18},{18,... | collective-permute-start | bytes 1179656 | tf_op jit(solution)/shard_map/ppermute | solution.py:332
  60.9 18.3 %collective-permute-start.16 = (bf16[2,128,768]{2,1,0:T(8,128)(2,1)S(1)}, bf16[2,128,768]{2,1,0:T(8,128)(2,1)S(1)}, u32[]{:S(2)}, u32[]{:S(2)}) collective-permute-start(bf16[2,128,768]{2,1,0:T(8,128)(2,1)S(1)} %get-tuple-element.89), channel_id=1, source_target_pairs={{0,1},{1,0},{2,3},{3,2},{4,5},{5,4},{6,7},{7,6},{8,9},{9,8},{10,11... | collective-permute-start | bytes 1179656 | tf_op jit(solution)/shard_map/ppermute | solution.py:310
  61.6 17.6 %collective-permute-start.18 = (bf16[2,128,768]{2,1,0:T(8,128)(2,1)S(1)}, bf16[2,128,768]{2,1,0:T(8,128)(2,1)S(1)}, u32[]{:S(2)}, u32[]{:S(2)}) collective-permute-start(bf16[2,128,768]{2,1,0:T(8,128)(2,1)S(1)} %collective-permute-done.14.kv_ref), channel_id=1, source_target_pairs={{0,2},{2,0},{4,6},{6,4},{8,10},{10,8},{12,14},{14,12},{16,18},{18,... | collective-permute-start | bytes 1179656 | tf_op jit(solution)/shard_map/ppermute | solution.py:335
  65.7 13.5 %collective-permute-start.19 = (bf16[2,128,768]{2,1,0:T(8,128)(2,1)S(1)}, bf16[2,128,768]{2,1,0:T(8,128)(2,1)S(1)}, u32[]{:S(2)}, u32[]{:S(2)}) collective-permute-start(bf16[2,128,768]{2,1,0:T(8,128)(2,1)S(1)} %collective-permute-done.14.kv_ref), channel_id=1, source_target_pairs={{0,0},{2,4},{4,2},{6,8},{8,6},{10,12},{12,10},{14,16},{16,14},{18,... | collective-permute-start | bytes 1179656 | tf_op jit(solution)/shard_map/ppermute | solution.py:334
  77.1 10.4 %collective-permute-start.22 = (bf16[2,128,768]{2,1,0:T(8,128)(2,1)S(1)}, bf16[2,128,768]{2,1,0:T(8,128)(2,1)S(1)}, u32[]{:S(2)}, u32[]{:S(2)}) collective-permute-start(bf16[2,128,768]{2,1,0:T(8,128)(2,1)S(1)} %get-tuple-element.112), channel_id=1, source_target_pairs={{0,1},{1,0},{2,3},{3,2},{4,5},{5,4},{6,7},{7,6},{8,9},{9,8},{10,11... | collective-permute-start | bytes 1179656 | tf_op jit(solution)/shard_map/ppermute | solution.py:318
  78.5 9.0 %collective-permute-start.23 = (bf16[2,128,768]{2,1,0:T(8,128)(2,1)S(1)}, bf16[2,128,768]{2,1,0:T(8,128)(2,1)S(1)}, u32[]{:S(2)}, u32[]{:S(2)}) collective-permute-start(bf16[2,128,768]{2,1,0:T(8,128)(2,1)S(1)} %get-tuple-element.113), channel_id=1, source_target_pairs={{0,0},{2,4},{4,2},{6,8},{8,6},{10,12},{12,10},{14,16},{16,14},{18,... | collective-permute-start | bytes 1179656 | tf_op jit(solution)/shard_map/ppermute | solution.py:439
  87.6 10.0 %collective-permute-start.26 = (bf16[2,128,768]{2,1,0:T(8,128)(2,1)S(1)}, bf16[2,128,768]{2,1,0:T(8,128)(2,1)S(1)}, u32[]{:S(2)}, u32[]{:S(2)}) collective-permute-start(bf16[2,128,768]{2,1,0:T(8,128)(2,1)S(1)} %get-tuple-element.124), channel_id=1, source_target_pairs={{0,0},{2,4},{4,2},{6,8},{8,6},{10,12},{12,10},{14,16},{16,14},{18,... | collective-permute-start | bytes 1179656 | tf_op jit(solution)/shard_map/ppermute | solution.py:439
  88.3 11.9 %collective-permute-start.25 = (bf16[2,128,1536]{2,1,0:T(8,128)(2,1)S(1)}, bf16[2,128,1536]{2,1,0:T(8,128)(2,1)S(1)}, u32[]{:S(2)}, u32[]{:S(2)}) collective-permute-start(bf16[2,128,1536]{2,1,0:T(8,128)(2,1)S(1)} %get-tuple-element.123), channel_id=1, source_target_pairs={{0,2},{2,0},{4,6},{6,4},{8,10},{10,8},{12,14},{14,12},{16,18},{18,... | collective-permute-start | bytes 2359304 | tf_op jit(solution)/shard_map/ppermute | solution.py:443
  97.5 60.1 %collective-permute-start.29 = (bf16[2,128,1536]{2,1,0:T(8,128)(2,1)}, bf16[2,128,1536]{2,1,0:T(8,128)(2,1)S(1)}, u32[]{:S(2)}, u32[]{:S(2)}) collective-permute-start(bf16[2,128,1536]{2,1,0:T(8,128)(2,1)} %get-tuple-element.127), channel_id=1, source_target_pairs={{0,2},{2,0},{4,6},{6,4},{8,10},{10,8},{12,14},{14,12},{16,18},{18,... | collective-permute-start | bytes 2359304 | tf_op jit(solution)/shard_map/ppermute | solution.py:444
  97.6 60.0 %collective-permute-start.30 = (bf16[2,128,1536]{2,1,0:T(8,128)(2,1)}, bf16[2,128,1536]{2,1,0:T(8,128)(2,1)S(1)}, u32[]{:S(2)}, u32[]{:S(2)}) collective-permute-start(bf16[2,128,1536]{2,1,0:T(8,128)(2,1)} %get-tuple-element.129), channel_id=1, source_target_pairs={{0,0},{2,4},{4,2},{6,8},{8,6},{10,12},{12,10},{14,16},{16,14},{18,... | collective-permute-start | bytes 2359304 | tf_op jit(solution)/shard_map/ppermute | solution.py:446
  99.4 7.8 %collective-permute-start.24 = (bf16[2,128,768]{2,1,0:T(8,128)(2,1)S(1)}, bf16[2,128,768]{2,1,0:T(8,128)(2,1)S(1)}, u32[]{:S(2)}, u32[]{:S(2)}) collective-permute-start(bf16[2,128,768]{2,1,0:T(8,128)(2,1)S(1)} %get-tuple-element.114), channel_id=1, source_target_pairs={{0,1},{1,0},{2,3},{3,2},{4,5},{5,4},{6,7},{7,6},{8,9},{9,8},{10,11... | collective-permute-start | bytes 1179656 | tf_op jit(solution)/shard_map/ppermute | solution.py:318
  101.0 58.3 %collective-permute-start.28 = (bf16[2,128,768]{2,1,0:T(8,128)(2,1)}, bf16[2,128,768]{2,1,0:T(8,128)(2,1)}, u32[]{:S(2)}, u32[]{:S(2)}) collective-permute-start(bf16[2,128,768]{2,1,0:T(8,128)(2,1)} %far_sum.3), channel_id=1, source_target_pairs={{0,1},{1,0},{2,3},{3,2},{4,5},{5,4},{6,7},{7,6},{8,9},{9,8},{10,11... | collective-permute-start | bytes 1179656 | tf_op jit(solution)/shard_map/ppermute | solution.py:318
  102.4 70.5 %collective-permute-start.27 = (bf16[2,128,768]{2,1,0:T(8,128)(2,1)S(1)}, bf16[2,128,768]{2,1,0:T(8,128)(2,1)}, u32[]{:S(2)}, u32[]{:S(2)}) collective-permute-start(bf16[2,128,768]{2,1,0:T(8,128)(2,1)S(1)} %far_sum.2), channel_id=1, source_target_pairs={{0,1},{1,0},{2,3},{3,2},{4,5},{5,4},{6,7},{7,6},{8,9},{9,8},{10,11... | collective-permute-start | bytes 1179656 | tf_op jit(solution)/shard_map/ppermute | solution.py:318
  108.5 13.5 %collective-permute-start.5 = (f32[24,1536]{1,0:T(8,128)S(1)}, f32[24,1536]{1,0:T(8,128)S(1)}, u32[]{:S(2)}, u32[]{:S(2)}) collective-permute-start(f32[24,1536]{1,0:T(8,128)S(1)} %get-tuple-element.14), channel_id=1, source_target_pairs={{0,2},{2,0},{4,6},{6,4},{8,10},{10,8},{12,14},{14,12},{16,18},{18,... | collective-permute-start | bytes 442376 | tf_op jit(solution)/shard_map/cond/branch_1_fun/ppermute | solution.py:481
  122.0 9.3 %collective-permute-start.6 = (f32[24,1536]{1,0:T(8,128)S(1)}, f32[24,1536]{1,0:T(8,128)S(1)}, u32[]{:S(2)}, u32[]{:S(2)}) collective-permute-start(f32[24,1536]{1,0:T(8,128)S(1)} %add.29), channel_id=1, source_target_pairs={{0,8},{2,10},{4,12},{6,14},{8,0},{10,2},{12,4},{14,6},{16,24},{18,... | collective-permute-start | bytes 442376 | tf_op jit(solution)/shard_map/cond/branch_1_fun/ppermute | solution.py:481
  131.3 9.7 %collective-permute-start.7 = (f32[24,1536]{1,0:T(8,128)S(1)}, f32[24,1536]{1,0:T(8,128)S(1)}, u32[]{:S(2)}, u32[]{:S(2)}) collective-permute-start(f32[24,1536]{1,0:T(8,128)S(1)} %add.30), channel_id=1, source_target_pairs={{0,16},{2,18},{4,20},{6,22},{8,24},{10,26},{12,28},{14,30},{16,0},... | collective-permute-start | bytes 442376 | tf_op jit(solution)/shard_map/cond/branch_1_fun/ppermute | solution.py:481
  141.0 5.2 %collective-permute-start.8 = (f32[24,1536]{1,0:T(8,128)S(1)}, f32[24,1536]{1,0:T(8,128)S(1)}, u32[]{:S(2)}, u32[]{:S(2)}) collective-permute-start(f32[24,1536]{1,0:T(8,128)S(1)} %add.31), channel_id=1, source_target_pairs={{0,4},{2,6},{4,0},{6,2},{8,12},{10,14},{12,8},{14,10},{16,20},{18,... | collective-permute-start | bytes 442376 | tf_op jit(solution)/shard_map/cond/branch_1_fun/ppermute | solution.py:481
  146.9 5.5 %collective-permute-start.9 = (f32[24,1536]{1,0:T(8,128)}, f32[24,1536]{1,0:T(8,128)}, u32[]{:S(2)}, u32[]{:S(2)}) collective-permute-start(f32[24,1536]{1,0:T(8,128)} %add.32), channel_id=1, source_target_pairs={{0,1},{1,0},{2,3},{3,2},{4,5},{5,4},{6,7},{7,6},{8,9},{9,8},{10,11... | collective-permute-start | bytes 442376 | tf_op jit(solution)/shard_map/cond/branch_1_fun/ppermute | solution.py:484

commit v3 on v2

--- a/solution.py
+++ b/solution.py
@@ -224,31 +224,37 @@
         copy.wait()
 
 
-def pack_kernel(place_ref, first_ref, second_ref, own_ref, far_ref, sems, *, at):
-    groups, parts, p = at
-    rows, width = own_ref.shape[1:]
-    copies = []
-    for k in range(groups):
-        start = (lax.rem(place_ref[1] + k, groups) * parts + p) * width
-        cols = pl.ds(pl.multiple_of(start, DH), width)
-        for i, ref in enumerate((first_ref, second_ref)):
-            to = own_ref.at[i] if k == 0 else far_ref.at[i, pl.ds((k - 1) * rows, rows)]
-            copies.append(pltpu.make_async_copy(ref.at[:, cols], to, sems.at[2 * k + i]))
-    for copy in copies:
-        copy.start()
-    for copy in copies:
-        copy.wait()
-
-
-def spread_kernel(noise_ref, sums_ref, out_ref):
-    spans = noise_ref.shape[1]
-    levels = lax.broadcasted_iota(jnp.int32, (out_ref.shape[0], spans), 0)
-    out_ref[...] = jnp.dot(
-        (levels == noise_ref[...]).astype(jnp.float32),
-        sums_ref[...],
-        precision=lax.Precision.HIGHEST,
-        preferred_element_type=jnp.float32,
-    )
+def pack_kernel(place_ref, *refs, parts):
+    ins, own_ref, far_refs = refs[: -1 - parts], refs[-1 - parts], refs[-parts:]
+    rows = own_ref.shape[1]
+    own_ref[0], own_ref[1] = ins[0][...], ins[1][...]
+    for p, ref in enumerate(far_refs):
+        width = ref.shape[2]
+        cols = slice(p * width, (p + 1) * width)
+        for k in range(ref.shape[1] // rows):
+            at = slice(k * rows, (k + 1) * rows)
+            ref[0, at], ref[1, at] = ins[2 + 2 * k][:, cols], ins[3 + 2 * k][:, cols]
+
+
+def spread_kernel(place_ref, noise_ref, *refs, by_span):
+    *slabs, out_ref = refs
+    for j, ref in enumerate(slabs):
+
+        @pl.when(pl.program_id(0) == j)
+        def _(ref=ref):
+            sums = ref[...]
+            if not by_span:
+                out_ref[...] = sums
+                return
+            levels = lax.broadcasted_iota(jnp.int32, (out_ref.shape[0], noise_ref.shape[1]), 0)
+            onehot = (levels == noise_ref[...]).astype(jnp.bfloat16)
+            total = None
+            for _ in range(3):
+                piece = sums.astype(jnp.bfloat16)
+                sums = sums - piece.astype(jnp.float32)
+                part = jnp.dot(onehot, piece, preferred_element_type=jnp.float32)
+                total = part if total is None else total + part
+            out_ref[...] = total
 
 
 def per_device(
@@ -284,23 +290,26 @@
     alone = pltpu.CompilerParams(vmem_limit_bytes=60 * 1024 * 1024)
     small = pltpu.CompilerParams(vmem_limit_bytes=(12 if tokens <= 256 else 36) * 1024 * 1024)
 
-    def pack(first, second, p, params):
+    def pack(first, second, params):
+        def at_group(k):
+            return pl.BlockSpec(
+                (rows, width), lambda i, place: (0, lax.rem(place[1] + k, groups))
+            )
+
+        far_shape = (2, far_rows, part_width)
         return pl.pallas_call(
-            functools.partial(pack_kernel, at=(groups, parts, p)),
+            functools.partial(pack_kernel, parts=parts),
             grid_spec=pltpu.PrefetchScalarGridSpec(
                 num_scalar_prefetch=1,
                 grid=(1,),
-                in_specs=[pl.BlockSpec(memory_space=pltpu.HBM)] * 2,
-                out_specs=[pl.BlockSpec(memory_space=pl.ANY)] * 2,
-                scratch_shapes=[pltpu.SemaphoreType.DMA((2 * groups,))],
+                in_specs=[at_group(k) for k in range(groups) for _ in range(2)],
+                out_specs=[whole((2, rows, width))] + [whole(far_shape)] * parts,
             ),
-            out_shape=[
-                jax.ShapeDtypeStruct((2, rows, part_width), bf16),
-                jax.ShapeDtypeStruct((2, far_rows, part_width), bf16),
-            ],
+            out_shape=[jax.ShapeDtypeStruct((2, rows, width), bf16)]
+            + [jax.ShapeDtypeStruct(far_shape, bf16)] * parts,
             compiler_params=params,
             name="pack",
-        )(place, first, second)
+        )(place, *[first, second] * groups)
 
     def to_peers(slab):
         arrived = []
@@ -318,22 +327,14 @@
             arrived.append(lax.ppermute(part, "head", pairs))
         return arrived
 
-    kv_own, kv_far, qo_own, qo_far = [], [], [], []
-    side_own, side_far, near_own, near_far = [], [], [], []
-    for p in range(parts):
-        own_kv, sent_kv = pack(key_rows, value_rows, p, small if p else alone)
-        own_qo, sent_qo = pack(queries, out_cotangent, p, small)
-        kv_own.append(own_kv)
-        qo_own.append(own_qo)
-        if p > 0:
-            own_kv, sent_kv, *_ = tie((own_kv, sent_kv, qo_far[-1], side_far[-1]))
-        side_own.append(lax.ppermute(own_kv, "ctx", side_pairs))
-        kv_far.append(to_peers(sent_kv))
-        near_own.append(lax.ppermute(own_kv, "ctx", near_pairs))
-        sent_qo, *_ = tie((sent_qo, kv_far[p], side_own[p]))
-        side_far.append(lax.ppermute(kv_far[p], "ctx", side_pairs))
-        near_far.append(lax.ppermute(kv_far[p], "ctx", near_pairs))
-        qo_far.append(to_peers(sent_qo))
+    kv_own, *kv_sent = pack(key_rows, value_rows, alone)
+    qo_own, *qo_sent = pack(queries, out_cotangent, small)
+    side_own = lax.ppermute(kv_own, "ctx", side_pairs)
+    near_own = lax.ppermute(kv_own, "ctx", near_pairs)
+    kv_far = [to_peers(slab) for slab in kv_sent]
+    side_far = [lax.ppermute(slab, "ctx", side_pairs) for slab in kv_far]
+    near_far = [lax.ppermute(slab, "ctx", near_pairs) for slab in kv_far]
+    qo_far = [to_peers(tie((slab, far))[0]) for slab, far in zip(qo_sent, kv_far)]
 
     sizes = (ctx_count, groups, rows, span_total, level_count, by_span)
     whole = lambda shape: pl.BlockSpec(shape, lambda i, place: (0,) * len(shape))
@@ -386,8 +387,8 @@
         column = lambda count: pl.BlockSpec((count, block), lambda i, place: (0, p * steps + i))
         struct = jax.ShapeDtypeStruct
         inputs = [
-            qo_own[p], kv_own[p], qo_far[p], kv_far[p],
-            near_own[p], near_far[p], side_own[p], side_far[p],
+            qo_own, kv_own, qo_far[p], kv_far[p],
+            near_own, near_far[p], side_own, side_far[p],
             gate, bias, slot,
         ]
         return pl.pallas_call(
@@ -398,8 +399,8 @@
                 num_scalar_prefetch=1,
                 grid=(steps,),
                 in_specs=[
-                    pair(rows), pair(rows), pair(far_rows), pair(far_rows),
-                    pair(rows), pair(far_rows), pair(rows), pair(far_rows),
+                    at_part(rows), at_part(rows), pair(far_rows), pair(far_rows),
+                    at_part(rows), pair(far_rows), at_part(rows), pair(far_rows),
                     column(tokens), whole((3 * tokens, tokens)), whole((slots, tokens)),
                 ]
                 + [pl.BlockSpec(memory_space=pl.ANY)] * len(joint),
@@ -442,8 +443,23 @@
 
     near_back_far = lax.ppermute(near_grad_far, "ctx", near_pairs)
     near_back_own = lax.ppermute(near_grad_own, "ctx", near_pairs)
-    side_grad_own, _ = tie((side_grad_own, side_back_far[-1]))
     side_back_own = lax.ppermute(side_grad_own, "ctx", side_pairs)
+
+    def doubled(steps, sums):
+        for step in steps:
+            pairs = [(i, i ^ step) for i in range(ctx_count)]
+            sums = sums + lax.ppermute(sums, "ctx", pairs)
+        return sums
+
+    doubling = [1 << n for n in range(ctx_count.bit_length() - 1)]
+    first, last = [doubling[0], *doubling[2:3]], [*doubling[3:]]
+    sums = lax.cond(
+        noise_level[0] >= 0,
+        functools.partial(doubled, first),
+        functools.partial(doubled, first[::-1]),
+        sums,
+    )
+    side_back_far, back_far, sums = tie((side_back_far, back_far, sums))
     grad_far, grad_sent = [], []
     for p in range(parts):
         at_part = pl.BlockSpec((2, far_rows, part_width), lambda i, p=p: (0, 0, p))
@@ -475,44 +491,35 @@
         name="own_sum",
     )(place, own, near_back_own, side_back_own)
 
-    def reduced(order, sums):
-        for step in order:
-            pairs = [(i, i ^ step) for i in range(ctx_count)]
-            sums = sums + lax.ppermute(sums, "ctx", pairs)
+    def to_all(first, last, sums):
+        slabs = [doubled(first, sums)]
         for step in (1 << n for n in range(groups.bit_length() - 1)):
             pairs = [(i, i ^ step) for i in range(groups)]
-            other = lax.ppermute(sums, "head", pairs)
-            sums = jnp.where(
-                (h // step) % 2 == 0,
-                jnp.concatenate([sums, other], axis=1),
-                jnp.concatenate([other, sums], axis=1),
-            )
-        return sums
-
-    doubling = [1 << n for n in range(ctx_count.bit_length() - 1)]
-    turned = doubling[:1] + doubling[2:] + doubling[1:2]
+            slabs = slabs + [lax.ppermute(slab, "head", pairs) for slab in slabs]
+        return [doubled(last, slab) for slab in slabs]
+
+    x_step = doubling[1:2]
     sums, _ = tie((sums, grad_sent))
-    slot_sums = lax.cond(
+    slabs = lax.cond(
         noise_level[0] >= 0,
-        functools.partial(reduced, turned),
-        functools.partial(reduced, doubling),
+        functools.partial(to_all, last + x_step, []),
+        functools.partial(to_all, x_step + last, []),
         sums,
     )
-    if by_span:
-        gate_grad = pl.pallas_call(
-            spread_kernel,
+    gate_grad = pl.pallas_call(
+        functools.partial(spread_kernel, by_span=by_span),
+        grid_spec=pltpu.PrefetchScalarGridSpec(
+            num_scalar_prefetch=1,
             grid=(groups,),
-            in_specs=[
-                pl.BlockSpec((1, span_total), lambda i: (0, 0)),
-                pl.BlockSpec((slots, width), lambda i: (0, i)),
-            ],
-            out_specs=pl.BlockSpec((level_count, width), lambda i: (0, i)),
-            out_shape=jax.ShapeDtypeStruct((level_count, full_width), f32),
-            compiler_params=small,
-            name="spread",
-        )(noise_level.reshape(1, span_total), slot_sums)
-    else:
-        gate_grad = slot_sums
+            in_specs=[whole((1, span_total))] + [whole((slots, width))] * groups,
+            out_specs=pl.BlockSpec(
+                (level_count, width), lambda i, place: (0, lax.bitwise_xor(place[1], i))
+            ),
+        ),
+        out_shape=jax.ShapeDtypeStruct((level_count, full_width), f32),
+        compiler_params=small,
+        name="spread",
+    )(place, noise_level.reshape(1, span_total), *slabs)
 
     def put(first, second, arrived, k, p):
         anywhere = pl.BlockSpec(memory_space=pl.ANY)
@@ -521,7 +528,7 @@
             grid_spec=pltpu.PrefetchScalarGridSpec(
                 num_scalar_prefetch=1,
                 grid=(1,),
-                in_specs=[anywhere] * 3,
+                in_specs=[whole((2, rows, part_width)), anywhere, anywhere],
                 out_specs=[anywhere] * 2,
                 scratch_shapes=[pltpu.SemaphoreType.DMA((2,))],
             ),

time: 187 us -> 122 us (0.65)
  Pallas kernels: 82.8 us -> 39.6 us
  starting transfers between devices: 61.9 us -> 35.8 us
  waiting for transfers between devices: 37 us -> 41 us
    ppermute x13 -> x11, starting transfers between devices: 37.1 us -> 5.62 us  [the longest x1 1.78 us: per_device(): side_own = lax.ppermute(kv_own, 'ctx', side_pairs)]
    pallas_call x5 -> x3, Pallas kernels: 31.2 us -> 7.31 us  [the longest x2 3.96 us: pack(): pl.pallas_call(functools.partial(pack_kernel, parts=parts), grid_spec=plt...]
    pallas_call x4, Pallas kernels: 29.8 us -> 7.2 us  [put(): pl.pallas_call(functools.partial(put_kernel, at=(k, groups, parts, p)), g...]
    ppermute x1, starting transfers between devices: 1.78 us -> 7.44 us  [per_device(): side_back_own = lax.ppermute(side_grad_own, 'ctx', side_pairs)]
    ppermute x4, waiting for transfers between devices: 13.2 us -> 18.4 us  [to_peers(): arrived.append(lax.ppermute(part, 'head', pairs))]
    ppermute x2, starting transfers between devices: 1.36 us -> 5.17 us  [per_device(): side_back_far.append(lax.ppermute(side_grad_far, 'ctx', side_pairs))]
    ppermute x4, waiting for transfers between devices: 2.52 us -> 0.01 us  [from_peers(): arrived.append(lax.ppermute(part, 'head', pairs))]
    pallas_call x2, Pallas kernels: 1.03 us -> 3.24 us  [per_device(): pl.pallas_call(far_sum_kernel, grid=(1,), in_specs=[at_part, at_part, alo...]
  transfers between devices with their start and end apart: 26 -> 24, of which waited for: 8 -> 8; matrix products, arithmetic and copies ran while one was open for 1% -> 1% of each run, Pallas kernels for 23% -> 29%
where the time goes in v3:
time: 122 us; the launch traced here: 121 us
  waiting for transfers between devices  41 us (34%)
  Pallas kernels  39.6 us (32%)
  starting transfers between devices  35.8 us (29%)
  other arithmetic  1.97 us (2%)
  local copies, waits for them, and re-layouts  1.68 us (1%)
    ppermute x4, waiting for transfers between devices, doubled(): sums = sums + lax.ppermute(sums, 'ctx', pairs)  18.7 us
    ppermute x4, waiting for transfers between devices, to_peers(): arrived.append(lax.ppermute(part, 'head', pairs))  18.4 us
    pallas_call x2, Pallas kernels, attention(): pl.pallas_call(functools.partial(attention_kernel, rows=rows, tokens=toke...  16.7 us
    ppermute x1, starting transfers between devices, per_device(): near_back_far = lax.ppermute(near_grad_far, 'ctx', near_pairs)  7.82 us
    ppermute x1, starting transfers between devices, per_device(): side_back_own = lax.ppermute(side_grad_own, 'ctx', side_pairs)  7.44 us
    pallas_call x4, Pallas kernels, put(): pl.pallas_call(functools.partial(put_kernel, at=(k, groups, parts, p)), g...  7.2 us
    ppermute x4, starting transfers between devices, to_peers(): arrived.append(lax.ppermute(part, 'head', pairs))  6.85 us
    ppermute x2, starting transfers between devices, per_device(): side_back_far.append(lax.ppermute(side_grad_far, 'ctx', side_pairs))  5.17 us
  transfers between devices with their start and end apart: 24, of which 8 were waited for; matrix products, arithmetic and copies ran while one was open for 1% of the time, Pallas kernels for 29%

profile of v3, /device:TPU:0, one launch (start us, length us, event | category | flops | bytes accessed | tf_op | source)
XLA Modules:
  0.0 121.0 jit_solution(3391418565879737618)
XLA Ops:
  0.6 0.6 pad_add_fusion.place_ref
  1.2 3.3 %pack.3 = (bf16[2,128,1536]{2,1,0:T(8,128)(2,1)}, bf16[2,128,768]{2,1,0:T(8,128)(2,1)}, bf16[2,128,768]{2,1,0:T(8,128)(2,1)}) custom-call(s32[2]{0:T(128)} %pad_add_fusion.place_ref, bf16[128,3072]{1,0:T(8,128)(2,1)} %refs_2_.3, bf16[128,3072]{1,0:T(8,128)(2,1)} %refs_3_.3, bf16[128,3072]{1,0:T(8,128)(2,1)} %refs_2_.3, bf16[128,3072]{1,0:T(8,128)(2,1)} %refs_3_.3), custom_call_target="tpu_custom_call" | custom-call | tf_op jit(solution)/shard_map/pack/pallas_call | solution.py:300
  4.5 3.0 %collective-permute-start.16 = (bf16[2,128,768]{2,1,0:T(8,128)(2,1)}, bf16[2,128,768]{2,1,0:T(8,128)(2,1)S(1)}, u32[]{:S(2)}, u32[]{:S(2)}) collective-permute-start(bf16[2,128,768]{2,1,0:T(8,128)(2,1)} %get-tuple-element.82), channel_id=1, source_target_pairs={{0,1},{1,0},{2,3},{3,2},{4,5},{5,4},{6,7},{7,6},{8,9},{9,8},{10,11... | collective-permute-start | bytes 1179656 | tf_op jit(solution)/shard_map/ppermute | solution.py:319
  7.5 0.0 collective-permute-start.12
  7.5 1.8 %collective-permute-start.14 = (bf16[2,128,1536]{2,1,0:T(8,128)(2,1)}, bf16[2,128,1536]{2,1,0:T(8,128)(2,1)S(1)}, u32[]{:S(2)}, u32[]{:S(2)}) collective-permute-start(bf16[2,128,1536]{2,1,0:T(8,128)(2,1)} %get-tuple-element.74.kv_own_ref), channel_id=1, source_target_pairs={{0,0},{2,4},{4,2},{6,8},{8,6},{10,12},{12,10},{14,16},{16,14},{18,... | collective-permute-start | bytes 2359304 | tf_op jit(solution)/shard_map/ppermute | solution.py:332
  9.3 0.1 collective-permute-start.10
  9.4 0.7 pack.2
  10.1 0.0 copy-start.2
  10.1 7.6 %collective-permute-done.16.kv_ref = bf16[2,128,768]{2,1,0:T(8,128)(2,1)S(1)} collective-permute-done((bf16[2,128,768]{2,1,0:T(8,128)(2,1)}, bf16[2,128,768]{2,1,0:T(8,128)(2,1)S(1)}, u32[]{:S(2)}, u32[]{:S(2)}) %collective-permute-start.16) | collective-permute-done | bytes 393248 | tf_op jit(solution)/shard_map/ppermute | solution.py:319
  17.7 2.1 %collective-permute-start.17 = (bf16[2,128,768]{2,1,0:T(8,128)(2,1)S(1)}, bf16[2,128,768]{2,1,0:T(8,128)(2,1)S(1)}, u32[]{:S(2)}, u32[]{:S(2)}) collective-permute-start(bf16[2,128,768]{2,1,0:T(8,128)(2,1)S(1)} %get-tuple-element.83), channel_id=1, source_target_pairs={{0,1},{1,0},{2,3},{3,2},{4,5},{5,4},{6,7},{7,6},{8,9},{9,8},{10,11... | collective-permute-start | bytes 1179656 | tf_op jit(solution)/shard_map/ppermute | solution.py:319
  19.7 0.0 collective-permute-start.18
  19.7 6.4 %collective-permute-done.10.kv_ref = bf16[2,128,768]{2,1,0:T(8,128)(2,1)S(1)} collective-permute-done((bf16[2,128,768]{2,1,0:T(8,128)(2,1)}, bf16[2,128,768]{2,1,0:T(8,128)(2,1)S(1)}, u32[]{:S(2)}, u32[]{:S(2)}) %collective-permute-start.10) | collective-permute-done | bytes 393248 | tf_op jit(solution)/shard_map/ppermute | solution.py:319
  26.1 0.7 collective-permute-start.19
  26.8 2.4 %prep.1 = (f32[768,256]{1,0:T(8,128)S(1)}, f32[256,1536]{1,0:T(8,128)S(1)}, bf16[24,256]{1,0:T(8,128)(2,1)S(1)}) custom-call(s32[2]{0:T(128)S(1)} %copy-done.7, s32[32,128]{1,0:T(8,128)S(1)} %bitcast.6, s32[1,24]{1,0:T(1,128)S(1)} %bitcast.7, s32[24,24]{1,0:T(8,128)S(1)} %copy-done.9, f32[128,3072]{1,0:T(8,128)S(1)} %copy-done.3), custom_call_target="tpu_custom_call" | custom-call | tf_op jit(solution)/shard_map/prep/pallas_call | solution.py:341
  29.2 4.5 %collective-permute-done.17.qo_ref = bf16[2,128,768]{2,1,0:T(8,128)(2,1)S(1)} collective-permute-done((bf16[2,128,768]{2,1,0:T(8,128)(2,1)S(1)}, bf16[2,128,768]{2,1,0:T(8,128)(2,1)S(1)}, u32[]{:S(2)}, u32[]{:S(2)}) %collective-permute-start.17) | collective-permute-done | bytes 393248 | tf_op jit(solution)/shard_map/ppermute | solution.py:319
  33.7 1.7 %collective-permute-start.11 = (bf16[2,128,768]{2,1,0:T(8,128)(2,1)S(1)}, bf16[2,128,768]{2,1,0:T(8,128)(2,1)S(1)}, u32[]{:S(2)}, u32[]{:S(2)}) collective-permute-start(bf16[2,128,768]{2,1,0:T(8,128)(2,1)S(1)} %get-tuple-element.77), channel_id=1, source_target_pairs={{0,1},{1,0},{2,3},{3,2},{4,5},{5,4},{6,7},{7,6},{8,9},{9,8},{10,11... | collective-permute-start | bytes 1179656 | tf_op jit(solution)/shard_map/ppermute | solution.py:319
  35.4 0.0 collective-permute-done.12.near_own_ref
  35.4 0.0 collective-permute-start.13
  35.4 0.0 collective-permute-done.14.side_own_ref
  35.4 0.7 collective-permute-start.15
  36.1 0.0 collective-permute-done.18.near_far_ref
  36.2 8.3 %attention.2 = (bf16[2,128,768]{2,1,0:T(8,128)(2,1)S(1)}, bf16[2,128,768]{2,1,0:T(8,128)(2,1)S(1)}, bf16[128,3072]{1,0:T(8,128)(2,1)}, bf16[128,3072]{1,0:T(8,12...) custom-call(s32[2]{0:T(128)S(1)} %copy-done.7, ...), custom_call_target="tpu_custom_call" | custom-call | flops 1811939328 | bytes 3145728 | tf_op jit(solution)/shard_map/attention/pallas_call | solution.py:394
  44.5 0.3 collective-permute-start.20
  44.7 0.7 collective-permute-start.21
  45.4 0.0 collective-permute-done.11.qo_ref
  45.4 0.0 collective-permute-done.15.side_far_ref
  45.4 8.4 %attention.3 = (bf16[2,128,768]{2,1,0:T(8,128)(2,1)}, bf16[2,128,768]{2,1,0:T(8,128)(2,1)}, bf16[128,3072]{1,0:T(8,128)(2,1)}, bf16[128,3072]{1,0:T(8,128)(2,1)}...) custom-call(s32[2]{0:T(128)S(1)} %copy-done.7, ...), custom_call_target="tpu_custom_call", output_to_operand_aliasing={{2}: (12, {}), {3}: (13, {}), {4}: (14, {}), {5}: (15, {}),... | custom-call | flops 1811939328 | bytes 3145728 | tf_op jit(solution)/shard_map/attention/pallas_call | solution.py:394
  53.8 0.9 copy-done.4
  54.7 0.0 collective-permute-done.20.part_ref
  54.7 0.7 copy-done.5
  55.5 0.0 collective-permute-done.21.side_ref
  55.5 7.8 %collective-permute-start.24 = (bf16[2,128,1536]{2,1,0:T(8,128)(2,1)}, bf16[2,128,1536]{2,1,0:T(8,128)(2,1)}, u32[]{:S(2)}, u32[]{:S(2)}) collective-permute-start(bf16[2,128,1536]{2,1,0:T(8,128)(2,1)} %get-tuple-element.118), channel_id=1, source_target_pairs={{0,2},{2,0},{4,6},{6,4},{8,10},{10,8},{12,14},{14,12},{16,18},{18,... | collective-permute-start | bytes 2359304 | tf_op jit(solution)/shard_map/ppermute | solution.py:444
  63.3 4.5 %collective-permute-start.22 = (bf16[2,128,768]{2,1,0:T(8,128)(2,1)}, bf16[2,128,768]{2,1,0:T(8,128)(2,1)}, u32[]{:S(2)}, u32[]{:S(2)}) collective-permute-start(bf16[2,128,768]{2,1,0:T(8,128)(2,1)} %get-tuple-element.105), channel_id=1, source_target_pairs={{0,0},{2,4},{4,2},{6,8},{8,6},{10,12},{12,10},{14,16},{16,14},{18,... | collective-permute-start | bytes 1179656 | tf_op jit(solution)/shard_map/ppermute | solution.py:440
  67.8 0.5 collective-permute-start.23
  68.3 9.0 %conditional.2 = (f32[24,1536]{1,0:T(8,128)}) conditional(s32[]{:T(128)} %bitcast.4, f32[24,1536]{1,0:T(8,128)S(1)} %get-tuple-element.108, f32[24,1536]{1,0:T(8,128)S(1)} %get-tuple-element.108), branch_computations={%region_0.0_spmd, %region_1.0_spmd} | conditional | flops 73728 | bytes 2064472 | solution.py:456
  68.3 0.5 collective-permute-start.2
  68.8 1.6 %collective-permute-done.2 = f32[24,1536]{1,0:T(8,128)S(1)} collective-permute-done((f32[24,1536]{1,0:T(8,128)S(1)}, f32[24,1536]{1,0:T(8,128)S(1)}, u32[]{:S(2)}, u32[]{:S(2)}) %collective-permute-start.2) | collective-permute-done | bytes 147488 | tf_op jit(solution)/shard_map/cond/branch_1_fun/ppermute | solution.py:451
  70.5 0.3 collective-permute-start.3
  70.8 5.9 %collective-permute-done.3 = f32[24,1536]{1,0:T(8,128)S(1)} collective-permute-done((f32[24,1536]{1,0:T(8,128)S(1)}, f32[24,1536]{1,0:T(8,128)S(1)}, u32[]{:S(2)}, u32[]{:S(2)}) %collective-permute-start.3) | collective-permute-done | bytes 147488 | tf_op jit(solution)/shard_map/cond/branch_1_fun/ppermute | solution.py:451
  76.7 0.7 add.19
  77.3 7.4 %collective-permute-start.28 = (bf16[2,128,1536]{2,1,0:T(8,128)(2,1)}, bf16[2,128,1536]{2,1,0:T(8,128)(2,1)}, u32[]{:S(2)}, u32[]{:S(2)}) collective-permute-start(bf16[2,128,1536]{2,1,0:T(8,128)(2,1)} %copy-done.4), channel_id=1, source_target_pairs={{0,0},{2,4},{4,2},{6,8},{8,6},{10,12},{12,10},{14,16},{16,14},{18,... | collective-permute-start | bytes 2359304 | tf_op jit(solution)/shard_map/ppermute | solution.py:446
  84.8 0.0 collective-permute-done.22.side_ref
  84.8 0.0 collective-permute-done.23.part_ref
  84.8 0.0 collective-permute-done.24.near_ref
  84.8 2.0 %far_sum.3 = bf16[2,128,768]{2,1,0:T(8,128)(2,1)} custom-call(f32[2,128,1536]{2,1,0:T(8,128)S(1)} %get-tuple-element.117.part_ref, bf16[2,128,1536]{2,1,0:T(8,128)(2,1)} %collective-permute-done.24.near_ref, bf16[2,128,768]{2,1,0:T(8,128)(2,1)S(1)} %collective-permute-done.21.side_ref), custom_call_target="tpu_custom_call" | custom-call | tf_op jit(solution)/shard_map/far_sum/pallas_call | solution.py:467
  86.8 1.5 %collective-permute-start.26 = (bf16[2,128,768]{2,1,0:T(8,128)(2,1)}, bf16[2,128,768]{2,1,0:T(8,128)(2,1)}, u32[]{:S(2)}, u32[]{:S(2)}) collective-permute-start(bf16[2,128,768]{2,1,0:T(8,128)(2,1)} %far_sum.3), channel_id=1, source_target_pairs={{0,1},{1,0},{2,3},{3,2},{4,5},{5,4},{6,7},{7,6},{8,9},{9,8},{10,11... | collective-permute-start | bytes 1179656 | tf_op jit(solution)/shard_map/ppermute | solution.py:327
  88.3 1.3 %far_sum.2 = bf16[2,128,768]{2,1,0:T(8,128)(2,1)S(1)} custom-call(f32[2,128,1536]{2,1,0:T(8,128)S(1)} %get-tuple-element.117.part_ref, bf16[2,128,1536]{2,1,0:T(8,128)(2,1)} %collective-permute-done.24.near_ref, bf16[2,128,768]{2,1,0:T(8,128)(2,1)} %collective-permute-done.22.side_ref), custom_call_target="tpu_custom_call" | custom-call | tf_op jit(solution)/shard_map/far_sum/pallas_call | solution.py:467
  89.6 0.6 collective-permute-start.25
  90.1 1.3 %put.4 = (bf16[128,3072]{1,0:T(8,128)(2,1)}, bf16[128,3072]{1,0:T(8,128)(2,1)}) custom-call(s32[2]{0:T(128)S(1)} %copy-done.7, bf16[2,128,768]{2,1,0:T(8,128)(2,1)S(1)} %copy-done.6, bf16[128,3072]{1,0:T(8,128)(2,1)} %get-tuple-element.111.first_in, bf16[128,3072]{1,0:T(8,128)(2,1)} %get-tuple-element.112.second_in), custom_call_target="tpu_custom_call", output_to_operand_aliasing={{0}: (2, {}), {1}: (3, {})} | custom-call | tf_op jit(solution)/shard_map/put/pallas_call | solution.py:526
  91.5 2.3 %put.5 = (bf16[128,3072]{1,0:T(8,128)(2,1)}, bf16[128,3072]{1,0:T(8,128)(2,1)}) custom-call(s32[2]{0:T(128)S(1)} %copy-done.7, bf16[2,128,768]{2,1,0:T(8,128)(2,1)} %collective-permute-done.23.part_ref, bf16[128,3072]{1,0:T(8,128)(2,1)} %get-tuple-element.113.first_in, ...), custom_call_target="tpu_custom_call", output_to_operand_aliasing={{0}: (2, {}), {1}: (3, {})} | custom-call | tf_op jit(solution)/shard_map/put/pallas_call | solution.py:526
  93.8 17.5 %conditional.3 = (f32[24,1536]{1,0:T(8,128)}, f32[24,1536]{1,0:T(8,128)}) conditional(s32[]{:T(128)} %bitcast.4, f32[24,1536]{1,0:T(8,128)S(1)} %copy-done.11, f32[24,1536]{1,0:T(8,128)S(1)} %copy-done.11), branch_computations={%region_2.0_spmd, %region_3.0_spmd} | conditional | flops 73728 | bytes 2654344 | solution.py:503
  93.8 0.1 collective-permute-start.7
  93.9 6.0 %collective-permute-done.7 = f32[24,1536]{1,0:T(8,128)S(1)} collective-permute-done((f32[24,1536]{1,0:T(8,128)S(1)}, f32[24,1536]{1,0:T(8,128)S(1)}, u32[]{:S(2)}, u32[]{:S(2)}) %collective-permute-start.7) | collective-permute-done | bytes 147488 | tf_op jit(solution)/shard_map/cond/branch_1_fun/ppermute | solution.py:451
  99.9 0.1 collective-permute-start.8
  100.0 5.1 %collective-permute-done.8 = f32[24,1536]{1,0:T(8,128)S(1)} collective-permute-done((f32[24,1536]{1,0:T(8,128)S(1)}, f32[24,1536]{1,0:T(8,128)S(1)}, u32[]{:S(2)}, u32[]{:S(2)}) %collective-permute-start.8) | collective-permute-done | bytes 147488 | tf_op jit(solution)/shard_map/cond/branch_1_fun/ppermute | solution.py:451
  105.1 0.7 add.23
  105.8 1.5 %collective-permute-start.9 = (f32[24,1536]{1,0:T(8,128)}, f32[24,1536]{1,0:T(8,128)}, u32[]{:S(2)}, u32[]{:S(2)}) collective-permute-start(f32[24,1536]{1,0:T(8,128)} %add.23), channel_id=1, source_target_pairs={{0,1},{1,0},{2,3},{3,2},{4,5},{5,4},{6,7},{7,6},{8,9},{9,8},{10,11... | collective-permute-start | bytes 442376 | tf_op jit(solution)/shard_map/cond/branch_1_fun/ppermute | solution.py:498
  107.3 3.9 %collective-permute-done.9 = f32[24,1536]{1,0:T(8,128)} collective-permute-done((f32[24,1536]{1,0:T(8,128)}, f32[24,1536]{1,0:T(8,128)}, u32[]{:S(2)}, u32[]{:S(2)}) %collective-permute-start.9) | collective-permute-done | bytes 147488 | tf_op jit(solution)/shard_map/cond/branch_1_fun/ppermute | solution.py:498
  111.3 3.3 %spread.1 = f32[128,3072]{1,0:T(8,128)} custom-call(s32[2]{0:T(128)S(1)} %copy-done.7, s32[1,24]{1,0:T(1,128)S(1)} %bitcast.9, f32[24,1536]{1,0:T(8,128)} %get-tuple-element.132.refs_0_, f32[24,1536]{1,0:T(8,128)} %get-tuple-element.133.refs_1_), custom_call_target="tpu_custom_call" | custom-call | tf_op jit(solution)/shard_map/spread/pallas_call | solution.py:509
  114.6 2.8 %own_sum.1 = (bf16[128,3072]{1,0:T(8,128)(2,1)}, bf16[128,3072]{1,0:T(8,128)(2,1)}) custom-call(s32[2]{0:T(128)S(1)} %copy-done.7, f32[2,128,1536]{2,1,0:T(8,128)S(1)} %get-tuple-element.121.part_ref, bf16[2,128,1536]{2,1,0:T(8,128)(2,1)} %collective-permute-done.27.near_ref, bf16[2,128,1536]{2,1,0:T(8,128)(2,1)} %collective-permute-done.28.side_ref), custom_call_target="tpu_custom_call" | custom-call | tf_op jit(solution)/shard_map/own_sum/pallas_call | solution.py:478
  117.4 0.0 collective-permute-done.26.part_ref
  117.4 2.3 %put.6 = (bf16[128,3072]{1,0:T(8,128)(2,1)}, bf16[128,3072]{1,0:T(8,128)(2,1)}) custom-call(s32[2]{0:T(128)S(1)} %copy-done.7, bf16[2,128,768]{2,1,0:T(8,128)(2,1)} %collective-permute-done.26.part_ref, bf16[128,3072]{1,0:T(8,128)(2,1)} %get-tuple-element.124.first_in, ...), custom_call_target="tpu_custom_call", output_to_operand_aliasing={{0}: (2, {}), {1}: (3, {})} | custom-call | tf_op jit(solution)/shard_map/put/pallas_call | solution.py:526
  119.7 0.0 collective-permute-done.25.part_ref
  119.7 1.3 %put.7 = (bf16[128,3072]{1,0:T(8,128)(2,1)}, bf16[128,3072]{1,0:T(8,128)(2,1)}) custom-call(s32[2]{0:T(128)S(1)} %copy-done.7, bf16[2,128,768]{2,1,0:T(8,128)(2,1)S(1)} %collective-permute-done.25.part_ref, bf16[128,3072]{1,0:T(8,128)(2,1)} %get-tuple-element.126.first_in, ...), custom_call_target="tpu_custom_call", output_to_operand_aliasing={{0}: (2, {}), {1}: (3, {})} | custom-call | tf_op jit(solution)/shard_map/put/pallas_call | solution.py:526
  (28 shorter events, 0.1 us)
Async XLA Ops:
  1.2 8.2 %copy-start = (bf16[128,3072]{1,0:T(8,128)(2,1)S(1)}, bf16[128,3072]{1,0:T(8,128)(2,1)}, u32[]{:S(2)}) copy-start(bf16[128,3072]{1,0:T(8,128)(2,1)} %refs_2_.2) | copy-start | bytes 2359300
  1.2 8.2 %copy-start.1 = (bf16[128,3072]{1,0:T(8,128)(2,1)S(1)}, bf16[128,3072]{1,0:T(8,128)(2,1)}, u32[]{:S(2)}) copy-start(bf16[128,3072]{1,0:T(8,128)(2,1)} %refs_3_.2) | copy-start | bytes 2359300
  1.2 8.2 %copy-start.7 = (s32[2]{0:T(128)S(1)}, s32[2]{0:T(128)}, u32[]{:S(2)}) copy-start(s32[2]{0:T(128)} %pad_add_fusion.place_ref) | copy-start | bytes 28
  4.5 13.1 %collective-permute-start.16 = (bf16[2,128,768]{2,1,0:T(8,128)(2,1)}, bf16[2,128,768]{2,1,0:T(8,128)(2,1)S(1)}, u32[]{:S(2)}, u32[]{:S(2)}) collective-permute-start(bf16[2,128,768]{2,1,0:T(8,128)(2,1)} %get-tuple-element.82), channel_id=1, source_target_pairs={{0,1},{1,0},{2,3},{3,2},{4,5},{5,4},{6,7},{7,6},{8,9},{9,8},{10,11... | collective-permute-start | bytes 1179656 | tf_op jit(solution)/shard_map/ppermute | solution.py:319
  7.5 27.9 %collective-permute-start.12 = (bf16[2,128,1536]{2,1,0:T(8,128)(2,1)}, bf16[2,128,1536]{2,1,0:T(8,128)(2,1)S(1)}, u32[]{:S(2)}, u32[]{:S(2)}) collective-permute-start(bf16[2,128,1536]{2,1,0:T(8,128)(2,1)} %get-tuple-element.74.kv_own_ref), channel_id=1, source_target_pairs={{0,2},{2,0},{4,6},{6,4},{8,10},{10,8},{12,14},{14,12},{16,18},{18,... | collective-permute-start | bytes 2359304 | tf_op jit(solution)/shard_map/ppermute | solution.py:333
  7.5 27.9 %collective-permute-start.14 = (bf16[2,128,1536]{2,1,0:T(8,128)(2,1)}, bf16[2,128,1536]{2,1,0:T(8,128)(2,1)S(1)}, u32[]{:S(2)}, u32[]{:S(2)}) collective-permute-start(bf16[2,128,1536]{2,1,0:T(8,128)(2,1)} %get-tuple-element.74.kv_own_ref), channel_id=1, source_target_pairs={{0,0},{2,4},{4,2},{6,8},{8,6},{10,12},{12,10},{14,16},{16,14},{18,... | collective-permute-start | bytes 2359304 | tf_op jit(solution)/shard_map/ppermute | solution.py:332
  9.3 17.5 %copy-start.3 = (f32[128,3072]{1,0:T(8,128)S(1)}, f32[128,3072]{1,0:T(8,128)}, u32[]{:S(2)}) copy-start(f32[128,3072]{1,0:T(8,128)} %table_ref.1) | copy-start | bytes 4718596
  9.3 17.5 %copy-start.8 = (s32[4096]{0:T(1024)S(1)}, s32[4096]{0:T(1024)}, u32[]{:S(2)}) copy-start(s32[4096]{0:T(1024)} %param.17) | copy-start | bytes 49156
  9.3 17.5 %copy-start.9 = (s32[24,24]{1,0:T(8,128)S(1)}, s32[24,24]{1,0:T(8,128)}, u32[]{:S(2)}) copy-start(s32[24,24]{1,0:T(8,128)} %mask_ref.1) | copy-start | bytes 6916
  9.3 17.5 %copy-start.10 = (s32[24]{0:T(128)S(1)}, s32[24]{0:T(128)}, u32[]{:S(2)}) copy-start(s32[24]{0:T(128)} %param.18) | copy-start | bytes 292
  9.3 16.8 %collective-permute-start.10 = (bf16[2,128,768]{2,1,0:T(8,128)(2,1)}, bf16[2,128,768]{2,1,0:T(8,128)(2,1)S(1)}, u32[]{:S(2)}, u32[]{:S(2)}) collective-permute-start(bf16[2,128,768]{2,1,0:T(8,128)(2,1)} %get-tuple-element.76), channel_id=1, source_target_pairs={{0,1},{1,0},{2,3},{3,2},{4,5},{5,4},{6,7},{7,6},{8,9},{9,8},{10,11... | collective-permute-start | bytes 1179656 | tf_op jit(solution)/shard_map/ppermute | solution.py:319
  10.1 26.1 %copy-start.2 = (bf16[2,128,1536]{2,1,0:T(8,128)(2,1)S(1)}, bf16[2,128,1536]{2,1,0:T(8,128)(2,1)}, u32[]{:S(2)}) copy-start(bf16[2,128,1536]{2,1,0:T(8,128)(2,1)} %get-tuple-element.74.kv_own_ref) | copy-start | bytes 2359300
  17.7 16.0 %collective-permute-start.17 = (bf16[2,128,768]{2,1,0:T(8,128)(2,1)S(1)}, bf16[2,128,768]{2,1,0:T(8,128)(2,1)S(1)}, u32[]{:S(2)}, u32[]{:S(2)}) collective-permute-start(bf16[2,128,768]{2,1,0:T(8,128)(2,1)S(1)} %get-tuple-element.83), channel_id=1, source_target_pairs={{0,1},{1,0},{2,3},{3,2},{4,5},{5,4},{6,7},{7,6},{8,9},{9,8},{10,11... | collective-permute-start | bytes 1179656 | tf_op jit(solution)/shard_map/ppermute | solution.py:319
  19.7 16.4 %collective-permute-start.18 = (bf16[2,128,768]{2,1,0:T(8,128)(2,1)S(1)}, bf16[2,128,768]{2,1,0:T(8,128)(2,1)S(1)}, u32[]{:S(2)}, u32[]{:S(2)}) collective-permute-start(bf16[2,128,768]{2,1,0:T(8,128)(2,1)S(1)} %collective-permute-done.16.kv_ref), channel_id=1, source_target_pairs={{0,2},{2,0},{4,6},{6,4},{8,10},{10,8},{12,14},{14,12},{16,18},{18,... | collective-permute-start | bytes 1179656 | tf_op jit(solution)/shard_map/ppermute | solution.py:336
  26.1 10.1 %collective-permute-start.19 = (bf16[2,128,768]{2,1,0:T(8,128)(2,1)S(1)}, bf16[2,128,768]{2,1,0:T(8,128)(2,1)S(1)}, u32[]{:S(2)}, u32[]{:S(2)}) collective-permute-start(bf16[2,128,768]{2,1,0:T(8,128)(2,1)S(1)} %collective-permute-done.16.kv_ref), channel_id=1, source_target_pairs={{0,0},{2,4},{4,2},{6,8},{8,6},{10,12},{12,10},{14,16},{16,14},{18,... | collective-permute-start | bytes 1179656 | tf_op jit(solution)/shard_map/ppermute | solution.py:335
  33.7 11.7 %collective-permute-start.11 = (bf16[2,128,768]{2,1,0:T(8,128)(2,1)S(1)}, bf16[2,128,768]{2,1,0:T(8,128)(2,1)S(1)}, u32[]{:S(2)}, u32[]{:S(2)}) collective-permute-start(bf16[2,128,768]{2,1,0:T(8,128)(2,1)S(1)} %get-tuple-element.77), channel_id=1, source_target_pairs={{0,1},{1,0},{2,3},{3,2},{4,5},{5,4},{6,7},{7,6},{8,9},{9,8},{10,11... | collective-permute-start | bytes 1179656 | tf_op jit(solution)/shard_map/ppermute | solution.py:319
  35.4 10.0 %collective-permute-start.13 = (bf16[2,128,768]{2,1,0:T(8,128)(2,1)S(1)}, bf16[2,128,768]{2,1,0:T(8,128)(2,1)S(1)}, u32[]{:S(2)}, u32[]{:S(2)}) collective-permute-start(bf16[2,128,768]{2,1,0:T(8,128)(2,1)S(1)} %collective-permute-done.10.kv_ref), channel_id=1, source_target_pairs={{0,2},{2,0},{4,6},{6,4},{8,10},{10,8},{12,14},{14,12},{16,18},{18,... | collective-permute-start | bytes 1179656 | tf_op jit(solution)/shard_map/ppermute | solution.py:336
  35.4 10.0 %collective-permute-start.15 = (bf16[2,128,768]{2,1,0:T(8,128)(2,1)S(1)}, bf16[2,128,768]{2,1,0:T(8,128)(2,1)S(1)}, u32[]{:S(2)}, u32[]{:S(2)}) collective-permute-start(bf16[2,128,768]{2,1,0:T(8,128)(2,1)S(1)} %collective-permute-done.10.kv_ref), channel_id=1, source_target_pairs={{0,0},{2,4},{4,2},{6,8},{8,6},{10,12},{12,10},{14,16},{16,14},{18,... | collective-permute-start | bytes 1179656 | tf_op jit(solution)/shard_map/ppermute | solution.py:335
  44.5 10.3 %collective-permute-start.20 = (bf16[2,128,768]{2,1,0:T(8,128)(2,1)S(1)}, bf16[2,128,768]{2,1,0:T(8,128)(2,1)S(1)}, u32[]{:S(2)}, u32[]{:S(2)}) collective-permute-start(bf16[2,128,768]{2,1,0:T(8,128)(2,1)S(1)} %get-tuple-element.102), channel_id=1, source_target_pairs={{0,1},{1,0},{2,3},{3,2},{4,5},{5,4},{6,7},{7,6},{8,9},{9,8},{10,11... | collective-permute-start | bytes 1179656 | tf_op jit(solution)/shard_map/ppermute | solution.py:327
  44.7 10.7 %collective-permute-start.21 = (bf16[2,128,768]{2,1,0:T(8,128)(2,1)S(1)}, bf16[2,128,768]{2,1,0:T(8,128)(2,1)S(1)}, u32[]{:S(2)}, u32[]{:S(2)}) collective-permute-start(bf16[2,128,768]{2,1,0:T(8,128)(2,1)S(1)} %get-tuple-element.103), channel_id=1, source_target_pairs={{0,0},{2,4},{4,2},{6,8},{8,6},{10,12},{12,10},{14,16},{16,14},{18,... | collective-permute-start | bytes 1179656 | tf_op jit(solution)/shard_map/ppermute | solution.py:440
  53.8 0.9 copy-start.4
  54.7 0.7 copy-start.5
  55.5 29.3 %collective-permute-start.24 = (bf16[2,128,1536]{2,1,0:T(8,128)(2,1)}, bf16[2,128,1536]{2,1,0:T(8,128)(2,1)}, u32[]{:S(2)}, u32[]{:S(2)}) collective-permute-start(bf16[2,128,1536]{2,1,0:T(8,128)(2,1)} %get-tuple-element.118), channel_id=1, source_target_pairs={{0,2},{2,0},{4,6},{6,4},{8,10},{10,8},{12,14},{14,12},{16,18},{18,... | collective-permute-start | bytes 2359304 | tf_op jit(solution)/shard_map/ppermute | solution.py:444
  63.3 21.5 %collective-permute-start.22 = (bf16[2,128,768]{2,1,0:T(8,128)(2,1)}, bf16[2,128,768]{2,1,0:T(8,128)(2,1)}, u32[]{:S(2)}, u32[]{:S(2)}) collective-permute-start(bf16[2,128,768]{2,1,0:T(8,128)(2,1)} %get-tuple-element.105), channel_id=1, source_target_pairs={{0,0},{2,4},{4,2},{6,8},{8,6},{10,12},{12,10},{14,16},{16,14},{18,... | collective-permute-start | bytes 1179656 | tf_op jit(solution)/shard_map/ppermute | solution.py:440
  67.8 17.0 %collective-permute-start.23 = (bf16[2,128,768]{2,1,0:T(8,128)(2,1)}, bf16[2,128,768]{2,1,0:T(8,128)(2,1)}, u32[]{:S(2)}, u32[]{:S(2)}) collective-permute-start(bf16[2,128,768]{2,1,0:T(8,128)(2,1)} %get-tuple-element.107), channel_id=1, source_target_pairs={{0,1},{1,0},{2,3},{3,2},{4,5},{5,4},{6,7},{7,6},{8,9},{9,8},{10,11... | collective-permute-start | bytes 1179656 | tf_op jit(solution)/shard_map/ppermute | solution.py:327
  68.3 46.3 %collective-permute-start.27 = (bf16[2,128,1536]{2,1,0:T(8,128)(2,1)}, bf16[2,128,1536]{2,1,0:T(8,128)(2,1)}, u32[]{:S(2)}, u32[]{:S(2)}) collective-permute-start(bf16[2,128,1536]{2,1,0:T(8,128)(2,1)} %get-tuple-element.122), channel_id=1, source_target_pairs={{0,2},{2,0},{4,6},{6,4},{8,10},{10,8},{12,14},{14,12},{16,18},{18,... | collective-permute-start | bytes 2359304 | tf_op jit(solution)/shard_map/ppermute | solution.py:445
  68.3 2.1 %collective-permute-start.2 = (f32[24,1536]{1,0:T(8,128)S(1)}, f32[24,1536]{1,0:T(8,128)S(1)}, u32[]{:S(2)}, u32[]{:S(2)}) collective-permute-start(f32[24,1536]{1,0:T(8,128)S(1)} %param.1), channel_id=1, source_target_pairs={{0,2},{2,0},{4,6},{6,4},{8,10},{10,8},{12,14},{14,12},{16,18},{18,... | collective-permute-start | bytes 442376 | tf_op jit(solution)/shard_map/cond/branch_1_fun/ppermute | solution.py:451
  70.5 6.2 %collective-permute-start.3 = (f32[24,1536]{1,0:T(8,128)S(1)}, f32[24,1536]{1,0:T(8,128)S(1)}, u32[]{:S(2)}, u32[]{:S(2)}) collective-permute-start(f32[24,1536]{1,0:T(8,128)S(1)} %add.18), channel_id=1, source_target_pairs={{0,8},{2,10},{4,12},{6,14},{8,0},{10,2},{12,4},{14,6},{16,24},{18,... | collective-permute-start | bytes 442376 | tf_op jit(solution)/shard_map/cond/branch_1_fun/ppermute | solution.py:451
  77.3 37.3 %collective-permute-start.28 = (bf16[2,128,1536]{2,1,0:T(8,128)(2,1)}, bf16[2,128,1536]{2,1,0:T(8,128)(2,1)}, u32[]{:S(2)}, u32[]{:S(2)}) collective-permute-start(bf16[2,128,1536]{2,1,0:T(8,128)(2,1)} %copy-done.4), channel_id=1, source_target_pairs={{0,0},{2,4},{4,2},{6,8},{8,6},{10,12},{12,10},{14,16},{16,14},{18,... | collective-permute-start | bytes 2359304 | tf_op jit(solution)/shard_map/ppermute | solution.py:446
  86.8 3.4 %copy-start.6 = (bf16[2,128,768]{2,1,0:T(8,128)(2,1)S(1)}, bf16[2,128,768]{2,1,0:T(8,128)(2,1)}, u32[]{:S(2)}) copy-start(bf16[2,128,768]{2,1,0:T(8,128)(2,1)} %copy-done.5) | copy-start | bytes 1179652
  86.8 30.7 %collective-permute-start.26 = (bf16[2,128,768]{2,1,0:T(8,128)(2,1)}, bf16[2,128,768]{2,1,0:T(8,128)(2,1)}, u32[]{:S(2)}, u32[]{:S(2)}) collective-permute-start(bf16[2,128,768]{2,1,0:T(8,128)(2,1)} %far_sum.3), channel_id=1, source_target_pairs={{0,1},{1,0},{2,3},{3,2},{4,5},{5,4},{6,7},{7,6},{8,9},{9,8},{10,11... | collective-permute-start | bytes 1179656 | tf_op jit(solution)/shard_map/ppermute | solution.py:327
  89.6 1.9 %copy-start.11 = (f32[24,1536]{1,0:T(8,128)S(1)}, f32[24,1536]{1,0:T(8,128)}, u32[]{:S(2)}) copy-start(f32[24,1536]{1,0:T(8,128)} %get-tuple-element.138) | copy-start | bytes 442372
  89.6 30.2 %collective-permute-start.25 = (bf16[2,128,768]{2,1,0:T(8,128)(2,1)S(1)}, bf16[2,128,768]{2,1,0:T(8,128)(2,1)S(1)}, u32[]{:S(2)}, u32[]{:S(2)}) collective-permute-start(bf16[2,128,768]{2,1,0:T(8,128)(2,1)S(1)} %far_sum.2), channel_id=1, source_target_pairs={{0,1},{1,0},{2,3},{3,2},{4,5},{5,4},{6,7},{7,6},{8,9},{9,8},{10,11... | collective-permute-start | bytes 1179656 | tf_op jit(solution)/shard_map/ppermute | solution.py:327
  93.8 6.1 %collective-permute-start.7 = (f32[24,1536]{1,0:T(8,128)S(1)}, f32[24,1536]{1,0:T(8,128)S(1)}, u32[]{:S(2)}, u32[]{:S(2)}) collective-permute-start(f32[24,1536]{1,0:T(8,128)S(1)} %param.3), channel_id=1, source_target_pairs={{0,16},{2,18},{4,20},{6,22},{8,24},{10,26},{12,28},{14,30},{16,0},... | collective-permute-start | bytes 442376 | tf_op jit(solution)/shard_map/cond/branch_1_fun/ppermute | solution.py:451
  99.9 5.2 %collective-permute-start.8 = (f32[24,1536]{1,0:T(8,128)S(1)}, f32[24,1536]{1,0:T(8,128)S(1)}, u32[]{:S(2)}, u32[]{:S(2)}) collective-permute-start(f32[24,1536]{1,0:T(8,128)S(1)} %add.22), channel_id=1, source_target_pairs={{0,4},{2,6},{4,0},{6,2},{8,12},{10,14},{12,8},{14,10},{16,20},{18,... | collective-permute-start | bytes 442376 | tf_op jit(solution)/shard_map/cond/branch_1_fun/ppermute | solution.py:451
  105.8 5.5 %collective-permute-start.9 = (f32[24,1536]{1,0:T(8,128)}, f32[24,1536]{1,0:T(8,128)}, u32[]{:S(2)}, u32[]{:S(2)}) collective-permute-start(f32[24,1536]{1,0:T(8,128)} %add.23), channel_id=1, source_target_pairs={{0,1},{1,0},{2,3},{3,2},{4,5},{5,4},{6,7},{7,6},{8,9},{9,8},{10,11... | collective-permute-start | bytes 442376 | tf_op jit(solution)/shard_map/cond/branch_1_fun/ppermute | solution.py:498

commit v4 on v3

--- a/solution.py
+++ b/solution.py
@@ -22,7 +22,7 @@
     place_ref, span_ref, noise_ref, mask_ref, table_ref, bias_ref, gate_ref, slot_ref, *, sizes
 ):
     ctx_count, groups, rows, span_total, level_count, by_span = sizes
-    c, h = place_ref[0], place_ref[1]
+    c, h = lax.div(place_ref[0], groups), lax.rem(place_ref[0], groups)
     tokens = groups * rows
     total = ctx_count * tokens
     bf16, f32 = jnp.bfloat16, jnp.float32
@@ -198,63 +198,80 @@
         ready = following
 
 
-def far_sum_kernel(part_ref, near_ref, side_ref, out_ref):
-    total = part_ref[...] + near_ref[...].astype(jnp.float32) + side_ref[...].astype(jnp.float32)
-    out_ref[...] = total.astype(out_ref.dtype)
-
-
-def own_sum_kernel(place_ref, part_ref, near_ref, side_ref, key_ref, value_ref):
-    total = part_ref[...] + near_ref[...].astype(jnp.float32) + side_ref[...].astype(jnp.float32)
-    key_ref[...] = total[0].astype(key_ref.dtype)
-    value_ref[...] = total[1].astype(value_ref.dtype)
-
-
-def put_kernel(place_ref, part_ref, first_in, second_in, first_ref, second_ref, sems, *, at):
-    shift, groups, parts, p = at
-    width = part_ref.shape[2]
-    start = (lax.rem(place_ref[1] + shift, groups) * parts + p) * width
-    cols = pl.ds(pl.multiple_of(start, DH), width)
-    copies = [
-        pltpu.make_async_copy(part_ref.at[i], ref.at[:, cols], sems.at[i])
-        for i, ref in enumerate((first_ref, second_ref))
-    ]
-    for copy in copies:
-        copy.start()
-    for copy in copies:
-        copy.wait()
-
-
-def pack_kernel(place_ref, *refs, parts):
-    ins, own_ref, far_refs = refs[: -1 - parts], refs[-1 - parts], refs[-parts:]
-    rows = own_ref.shape[1]
-    own_ref[0], own_ref[1] = ins[0][...], ins[1][...]
-    for p, ref in enumerate(far_refs):
+def pack_kernel(place_ref, first_ref, second_ref, own_ref, *rest, groups):
+    *far_refs, sems = rest
+    rows, width = own_ref.shape[1:]
+    copies = []
+
+    def copy(ref, start, to):
+        cols = pl.ds(pl.multiple_of(start, DH), to.shape[1])
+        copies.append(pltpu.make_async_copy(ref.at[:, cols], to, sems.at[len(copies)]))
+        copies[-1].start()
+
+    for k in (*range(1, groups), 0):
+        start = lax.rem(place_ref[0] + k, groups) * width
+        for i, ref in enumerate((first_ref, second_ref)):
+            if k == 0:
+                copy(ref, start, own_ref.at[i])
+                continue
+            for p, far_ref in enumerate(far_refs):
+                at = pl.ds((k - 1) * rows, rows)
+                copy(ref, start + p * far_ref.shape[2], far_ref.at[i, at])
+    for one in copies:
+        one.wait()
+
+
+def far_sum_kernel(part_ref, near_ref, *refs):
+    *side_refs, out_ref = refs
+    for p, ref in enumerate(side_refs):
         width = ref.shape[2]
         cols = slice(p * width, (p + 1) * width)
-        for k in range(ref.shape[1] // rows):
-            at = slice(k * rows, (k + 1) * rows)
-            ref[0, at], ref[1, at] = ins[2 + 2 * k][:, cols], ins[3 + 2 * k][:, cols]
-
-
-def spread_kernel(place_ref, noise_ref, *refs, by_span):
+        total = part_ref[:, :, cols] + near_ref[:, :, cols].astype(jnp.float32)
+        out_ref[:, :, cols] = (total + ref[...].astype(jnp.float32)).astype(out_ref.dtype)
+
+
+def finish_kernel(place_ref, part_ref, near_ref, side_ref, *refs, groups, parts):
+    count = (groups - 1) * (parts + 1)
+    slabs, outs, (total_ref, sems) = refs[:count], refs[count + 2 : count + 6], refs[count + 6 :]
+    width = part_ref.shape[2]
+    copies = []
+
+    def copy(slab, first, second, start):
+        cols = pl.ds(pl.multiple_of(start, DH), slab.shape[2])
+        for i, ref in enumerate((first, second)):
+            copies.append(pltpu.make_async_copy(slab.at[i], ref.at[:, cols], sems.at[len(copies)]))
+            copies[-1].start()
+
+    for k in range(1, groups):
+        start = lax.rem(place_ref[0] + k, groups) * width
+        for p in range(parts):
+            slab = slabs[p * (groups - 1) + k - 1]
+            copy(slab, outs[0], outs[1], start + p * slab.shape[2])
+        copy(slabs[parts * (groups - 1) + k - 1], outs[2], outs[3], start)
+    total = part_ref[...] + near_ref[...].astype(jnp.float32) + side_ref[...].astype(jnp.float32)
+    total_ref[...] = total.astype(total_ref.dtype)
+    copy(total_ref, outs[2], outs[3], lax.rem(place_ref[0], groups) * width)
+    for one in copies:
+        one.wait()
+
+
+def spread_kernel(place_ref, noise_ref, *refs, by_span, groups):
     *slabs, out_ref = refs
+    levels = lax.broadcasted_iota(jnp.int32, (out_ref.shape[0], noise_ref.shape[1]), 0)
+    onehot = (levels == noise_ref[...]).astype(jnp.bfloat16)
     for j, ref in enumerate(slabs):
-
-        @pl.when(pl.program_id(0) == j)
-        def _(ref=ref):
-            sums = ref[...]
-            if not by_span:
-                out_ref[...] = sums
-                return
-            levels = lax.broadcasted_iota(jnp.int32, (out_ref.shape[0], noise_ref.shape[1]), 0)
-            onehot = (levels == noise_ref[...]).astype(jnp.bfloat16)
+        sums = ref[...]
+        width = sums.shape[1]
+        if by_span:
             total = None
             for _ in range(3):
                 piece = sums.astype(jnp.bfloat16)
                 sums = sums - piece.astype(jnp.float32)
                 part = jnp.dot(onehot, piece, preferred_element_type=jnp.float32)
                 total = part if total is None else total + part
-            out_ref[...] = total
+            sums = total
+        start = lax.bitwise_xor(lax.rem(place_ref[0], groups), j) * width
+        out_ref[:, pl.ds(pl.multiple_of(start, DH), width)] = sums
 
 
 def per_device(
@@ -276,7 +293,8 @@
     slots = span_total if by_span else level_count
     c = lax.axis_index("ctx")
     h = lax.axis_index("head")
-    place = jnp.stack([c, h]).astype(jnp.int32)
+    place = (c * groups + h).astype(jnp.int32).reshape(1)
+    head_at = lambda place: lax.rem(place[0], groups)
     bf16, f32 = jnp.bfloat16, jnp.float32
     tie = lax.optimization_barrier
 
@@ -287,29 +305,28 @@
     whole = lambda shape: pl.BlockSpec(shape, lambda i, place: (0,) * len(shape))
     limit = (26 if tokens <= 256 else 56) * 1024 * 1024
     params = pltpu.CompilerParams(vmem_limit_bytes=limit)
-    alone = pltpu.CompilerParams(vmem_limit_bytes=60 * 1024 * 1024)
+    alone = pltpu.CompilerParams(vmem_limit_bytes=56 * 1024 * 1024)
+    cheap = pl.CostEstimate(flops=1, bytes_accessed=1, transcendentals=0)
+    in_vmem = pl.BlockSpec(memory_space=pltpu.VMEM)
+    anywhere = pl.BlockSpec(memory_space=pl.ANY)
     small = pltpu.CompilerParams(vmem_limit_bytes=(12 if tokens <= 256 else 36) * 1024 * 1024)
 
     def pack(first, second, params):
-        def at_group(k):
-            return pl.BlockSpec(
-                (rows, width), lambda i, place: (0, lax.rem(place[1] + k, groups))
-            )
-
         far_shape = (2, far_rows, part_width)
         return pl.pallas_call(
-            functools.partial(pack_kernel, parts=parts),
+            functools.partial(pack_kernel, groups=groups),
             grid_spec=pltpu.PrefetchScalarGridSpec(
                 num_scalar_prefetch=1,
-                grid=(1,),
-                in_specs=[at_group(k) for k in range(groups) for _ in range(2)],
-                out_specs=[whole((2, rows, width))] + [whole(far_shape)] * parts,
+                in_specs=[anywhere] * 2,
+                out_specs=[in_vmem] * (1 + parts),
+                scratch_shapes=[pltpu.SemaphoreType.DMA((2 + 2 * (groups - 1) * parts,))],
             ),
             out_shape=[jax.ShapeDtypeStruct((2, rows, width), bf16)]
             + [jax.ShapeDtypeStruct(far_shape, bf16)] * parts,
             compiler_params=params,
+            cost_estimate=cheap,
             name="pack",
-        )(place, *[first, second] * groups)
+        )(place, first, second)
 
     def to_peers(slab):
         arrived = []
@@ -347,7 +364,7 @@
                 whole((ctx_count * groups, rows)),
                 whole((1, span_total)),
                 whole((span_total, span_total)),
-                pl.BlockSpec((level_count, width), lambda i, place: (0, place[1])),
+                pl.BlockSpec((level_count, width), lambda i, place: (0, head_at(place))),
             ],
             out_specs=[
                 whole((3 * tokens, tokens)),
@@ -361,6 +378,7 @@
             jax.ShapeDtypeStruct((slots, tokens), bf16),
         ],
         compiler_params=small,
+        cost_estimate=cheap,
         name="prep",
     )(
         place,
@@ -374,7 +392,6 @@
     steps = part_heads // batch
     block = batch * DH
     q_size = min(256, tokens)
-    flops = 6 * 2 * tokens * 3 * tokens * DH * part_heads
 
     def attention(p, joint):
         pair = lambda count: pl.BlockSpec((2, count, block), lambda i, place: (0, 0, i))
@@ -382,7 +399,7 @@
             (2, count, block), lambda i, place: (0, 0, p * steps + i)
         )
         at_head = pl.BlockSpec(
-            (rows, block), lambda i, place: (0, (place[1] * parts + p) * steps + i)
+            (rows, block), lambda i, place: (0, (head_at(place) * parts + p) * steps + i)
         )
         column = lambda count: pl.BlockSpec((count, block), lambda i, place: (0, p * steps + i))
         struct = jax.ShapeDtypeStruct
@@ -424,9 +441,7 @@
             ],
             input_output_aliases={1 + len(inputs) + i: 2 + i for i in range(len(joint))},
             compiler_params=params,
-            cost_estimate=pl.CostEstimate(
-                flops=flops, bytes_accessed=16 * tokens * part_width, transcendentals=0
-            ),
+            cost_estimate=cheap,
             name="attention",
         )(place, *inputs, *joint)
 
@@ -445,104 +460,81 @@
     near_back_own = lax.ppermute(near_grad_own, "ctx", near_pairs)
     side_back_own = lax.ppermute(side_grad_own, "ctx", side_pairs)
 
-    def doubled(steps, sums):
-        for step in steps:
-            pairs = [(i, i ^ step) for i in range(ctx_count)]
-            sums = sums + lax.ppermute(sums, "ctx", pairs)
+    def shifted(array, step):
+        return lax.ppermute(array, "ctx", [(i, i ^ step) for i in range(ctx_count)])
+
+    def rounds(steps, sums):
+        for one, two in zip(steps[::2], [*steps[1::2], None]):
+            if two is None:
+                sums = sums + shifted(sums, one)
+                continue
+            across = [shifted(sums, step) for step in (one, two, one ^ two)]
+            sums = (sums + across[0]) + (across[1] + across[2])
         return sums
 
-    doubling = [1 << n for n in range(ctx_count.bit_length() - 1)]
-    first, last = [doubling[0], *doubling[2:3]], [*doubling[3:]]
-    sums = lax.cond(
-        noise_level[0] >= 0,
-        functools.partial(doubled, first),
-        functools.partial(doubled, first[::-1]),
-        sums,
-    )
-    side_back_far, back_far, sums = tie((side_back_far, back_far, sums))
-    grad_far, grad_sent = [], []
-    for p in range(parts):
-        at_part = pl.BlockSpec((2, far_rows, part_width), lambda i, p=p: (0, 0, p))
-        alone = pl.BlockSpec((2, far_rows, part_width), lambda i: (0, 0, 0))
-        far_grad = pl.pallas_call(
-            far_sum_kernel,
-            grid=(1,),
-            in_specs=[at_part, at_part, alone],
-            out_specs=alone,
-            out_shape=jax.ShapeDtypeStruct((2, far_rows, part_width), bf16),
-            compiler_params=small,
-            name="far_sum",
-        )(far, near_back_far, side_back_far[p])
-        grad_sent.append(far_grad)
-        grad_far.append(from_peers(far_grad))
-    key_grad, value_grad = pl.pallas_call(
-        own_sum_kernel,
-        grid_spec=pltpu.PrefetchScalarGridSpec(
-            num_scalar_prefetch=1,
-            grid=(parts,),
-            in_specs=[pl.BlockSpec((2, rows, part_width), lambda i, place: (0, 0, i))] * 3,
-            out_specs=[
-                pl.BlockSpec((rows, part_width), lambda i, place: (0, place[1] * parts + i))
-            ]
-            * 2,
-        ),
-        out_shape=[jax.ShapeDtypeStruct((rows, full_width), bf16)] * 2,
+    bits = [1 << n for n in range(ctx_count.bit_length() - 1)]
+    sums = rounds([bits[0], bits[2]], sums)
+    side_back_far, back_far = tie((side_back_far, back_far))
+    far_grad = pl.pallas_call(
+        far_sum_kernel,
+        in_specs=[in_vmem] * (2 + parts),
+        out_specs=in_vmem,
+        out_shape=jax.ShapeDtypeStruct((2, far_rows, width), bf16),
         compiler_params=small,
-        name="own_sum",
-    )(place, own, near_back_own, side_back_own)
-
-    def to_all(first, last, sums):
-        slabs = [doubled(first, sums)]
+        cost_estimate=cheap,
+        name="far_sum",
+    )(far, near_back_far, *side_back_far)
+    grad_far = from_peers(far_grad)
+
+    def to_all(steps, sums):
+        slabs = [rounds(steps, sums)]
         for step in (1 << n for n in range(groups.bit_length() - 1)):
             pairs = [(i, i ^ step) for i in range(groups)]
             slabs = slabs + [lax.ppermute(slab, "head", pairs) for slab in slabs]
-        return [doubled(last, slab) for slab in slabs]
-
-    x_step = doubling[1:2]
-    sums, _ = tie((sums, grad_sent))
+        return slabs
+
+    rest = [bits[1], *bits[3:]]
+    sums, _ = tie((sums, far_grad))
     slabs = lax.cond(
         noise_level[0] >= 0,
-        functools.partial(to_all, last + x_step, []),
-        functools.partial(to_all, x_step + last, []),
+        functools.partial(to_all, rest),
+        functools.partial(to_all, rest[::-1]),
         sums,
     )
+    slabs, grad_far, side_back_own = tie((slabs, grad_far, side_back_own))
     gate_grad = pl.pallas_call(
-        functools.partial(spread_kernel, by_span=by_span),
+        functools.partial(spread_kernel, by_span=by_span, groups=groups),
         grid_spec=pltpu.PrefetchScalarGridSpec(
             num_scalar_prefetch=1,
-            grid=(groups,),
+            grid=(1,),
             in_specs=[whole((1, span_total))] + [whole((slots, width))] * groups,
-            out_specs=pl.BlockSpec(
-                (level_count, width), lambda i, place: (0, lax.bitwise_xor(place[1], i))
-            ),
+            out_specs=whole((level_count, full_width)),
         ),
         out_shape=jax.ShapeDtypeStruct((level_count, full_width), f32),
         compiler_params=small,
+        cost_estimate=cheap,
         name="spread",
     )(place, noise_level.reshape(1, span_total), *slabs)
 
-    def put(first, second, arrived, k, p):
-        anywhere = pl.BlockSpec(memory_space=pl.ANY)
-        return pl.pallas_call(
-            functools.partial(put_kernel, at=(k, groups, parts, p)),
-            grid_spec=pltpu.PrefetchScalarGridSpec(
-                num_scalar_prefetch=1,
-                grid=(1,),
-                in_specs=[whole((2, rows, part_width)), anywhere, anywhere],
-                out_specs=[anywhere] * 2,
-                scratch_shapes=[pltpu.SemaphoreType.DMA((2,))],
-            ),
-            out_shape=[jax.ShapeDtypeStruct((rows, full_width), bf16)] * 2,
-            input_output_aliases={2: 0, 3: 1},
-            compiler_params=small,
-            name="put",
-        )(place, arrived, first, second)
-
-    for p in range(parts):
-        for k in range(1, groups):
-            mixed, query_grad = put(mixed, query_grad, back_far[p][k - 1], k, p)
-            key_grad, value_grad = put(key_grad, value_grad, grad_far[p][k - 1], k, p)
-    return (mixed, query_grad, key_grad, value_grad, gate_grad)
+    arrived = [slab for slabs in back_far for slab in slabs] + grad_far
+    outputs = pl.pallas_call(
+        functools.partial(finish_kernel, groups=groups, parts=parts),
+        grid_spec=pltpu.PrefetchScalarGridSpec(
+            num_scalar_prefetch=1,
+            in_specs=[in_vmem] * (3 + len(arrived)) + [anywhere] * 2,
+            out_specs=[anywhere] * 4,
+            scratch_shapes=[
+                pltpu.VMEM((2, rows, width), bf16),
+                pltpu.SemaphoreType.DMA((2 * len(arrived) + 2,)),
+            ],
+        ),
+        out_shape=[jax.ShapeDtypeStruct((rows, full_width), bf16)] * 4,
+        input_output_aliases={4 + len(arrived): 0, 5 + len(arrived): 1},
+        compiler_params=small,
+        cost_estimate=cheap,
+        name="finish",
+    )(place, own, near_back_own, side_back_own, *arrived, mixed, query_grad)
+    return (*outputs, gate_grad)
 
 
 def solution(mesh):

time: 122 us -> 113 us (0.926)
  Pallas kernels: 39.6 us -> 25.7 us
  starting transfers between devices: 35.8 us -> 42.4 us
  local copies, waits for them, and re-layouts: 1.68 us -> 0.04 us
  other arithmetic: 1.97 us -> 0.72 us
    ppermute x4 -> x6, starting transfers between devices: 0.95 us -> 17.7 us  [shifted(): return lax.ppermute(array, 'ctx', [(i, i ^ step) for i in range(ctx_count)])]
    pallas_call x10 -> x5, Pallas kernels: 20.6 us -> 8.56 us  [the longest x2 3.06 us: pack(): pl.pallas_call(functools.partial(pack_kernel, groups=groups), grid_spec=p...]
    ppermute x1, starting transfers between devices: 7.44 us -> 1.79 us  [per_device(): side_back_own = lax.ppermute(side_grad_own, 'ctx', side_pairs)]
    ppermute x2, starting transfers between devices: 5.17 us -> 1.35 us  [per_device(): side_back_far.append(lax.ppermute(side_grad_far, 'ctx', side_pairs))]
    unnamed x24 -> x20, local copies, waits for them, and re-layouts: 1.68 us -> 0.04 us
    ppermute x4 -> x6, waiting for transfers between devices: 18.7 us -> 17 us  [shifted(): return lax.ppermute(array, 'ctx', [(i, i ^ step) for i in range(ctx_count)])]
    pallas_call x2, Pallas kernels: 16.7 us -> 15.3 us  [attention(): pl.pallas_call(functools.partial(attention_kernel, rows=rows, tokens=toke...]
    ppermute x4 -> x3, waiting for transfers between devices: 0.01 us -> 1.4 us  [from_peers(): arrived.append(lax.ppermute(part, 'head', pairs))]
  transfers between devices with their start and end apart: 24 -> 25, of which waited for: 8 -> 7; matrix products, arithmetic and copies ran while one was open for 1% -> 1% of each run, Pallas kernels for 29% -> 19%
where the time goes in v4:
time: 113 us; the launch traced here: 112 us
  starting transfers between devices  42.4 us (38%)
  waiting for transfers between devices  41.8 us (37%)
  Pallas kernels  25.7 us (23%)
    ppermute x4, waiting for transfers between devices, to_peers(): arrived.append(lax.ppermute(part, 'head', pairs))  19.4 us
    ppermute x6, starting transfers between devices, shifted(): return lax.ppermute(array, 'ctx', [(i, i ^ step) for i in range(ctx_count)])  17.7 us
    ppermute x6, waiting for transfers between devices, shifted(): return lax.ppermute(array, 'ctx', [(i, i ^ step) for i in range(ctx_count)])  17 us
    pallas_call x2, Pallas kernels, attention(): pl.pallas_call(functools.partial(attention_kernel, rows=rows, tokens=toke...  15.3 us
    ppermute x4, starting transfers between devices, to_peers(): arrived.append(lax.ppermute(part, 'head', pairs))  6.93 us
    ppermute x1, starting transfers between devices, per_device(): near_back_far = lax.ppermute(near_grad_far, 'ctx', near_pairs)  6.56 us
    ppermute x1, waiting for transfers between devices, to_all(): slabs = slabs + [lax.ppermute(slab, 'head', pairs) for slab in slabs]  3.93 us
    ppermute x3, starting transfers between devices, from_peers(): arrived.append(lax.ppermute(part, 'head', pairs))  3.39 us
  transfers between devices with their start and end apart: 25, of which 7 were waited for; matrix products, arithmetic and copies ran while one was open for 1% of the time, Pallas kernels for 19%

profile of v4, /device:TPU:0, one launch (start us, length us, event | category | flops | bytes accessed | tf_op | source)
XLA Modules:
  0.0 111.6 jit_solution(2617965370254937980)
XLA Ops:
  0.6 0.0 copy-start.2
  0.7 2.8 %pack.3 = (bf16[2,128,1536]{2,1,0:T(8,128)(2,1)}, bf16[2,128,768]{2,1,0:T(8,128)(2,1)}, bf16[2,128,768]{2,1,0:T(8,128)(2,1)}) custom-call(s32[1]{0:T(128)} %bitcast.place_ref, bf16[128,3072]{1,0:T(8,128)(2,1)} %first_ref.3, bf16[128,3072]{1,0:T(8,128)(2,1)} %second_ref.3), custom_call_target="tpu_custom_call" | custom-call | flops 1 | bytes 1 | tf_op jit(solution)/shard_map/pack/pallas_call | solution.py:316
  3.5 3.0 %collective-permute-start.14 = (bf16[2,128,768]{2,1,0:T(8,128)(2,1)}, bf16[2,128,768]{2,1,0:T(8,128)(2,1)S(1)}, u32[]{:S(2)}, u32[]{:S(2)}) collective-permute-start(bf16[2,128,768]{2,1,0:T(8,128)(2,1)} %get-tuple-element.74), channel_id=1, source_target_pairs={{0,1},{1,0},{2,3},{3,2},{4,5},{5,4},{6,7},{7,6},{8,9},{9,8},{10,11... | collective-permute-start | bytes 1179656 | tf_op jit(solution)/shard_map/ppermute | solution.py:336
  6.5 0.0 collective-permute-start.10
  6.5 1.8 %collective-permute-start.12 = (bf16[2,128,1536]{2,1,0:T(8,128)(2,1)}, bf16[2,128,1536]{2,1,0:T(8,128)(2,1)S(1)}, u32[]{:S(2)}, u32[]{:S(2)}) collective-permute-start(bf16[2,128,1536]{2,1,0:T(8,128)(2,1)} %get-tuple-element.66.kv_own_ref), channel_id=1, source_target_pairs={{0,0},{2,4},{4,2},{6,8},{8,6},{10,12},{12,10},{14,16},{16,14},{18,... | collective-permute-start | bytes 2359304 | tf_op jit(solution)/shard_map/ppermute | solution.py:349
  8.3 0.1 collective-permute-start.8
  8.4 0.0 copy-done.2
  8.4 0.3 pack.2
  8.7 8.0 %collective-permute-done.14.kv_ref = bf16[2,128,768]{2,1,0:T(8,128)(2,1)S(1)} collective-permute-done((bf16[2,128,768]{2,1,0:T(8,128)(2,1)}, bf16[2,128,768]{2,1,0:T(8,128)(2,1)S(1)}, u32[]{:S(2)}, u32[]{:S(2)}) %collective-permute-start.14) | collective-permute-done | bytes 393248 | tf_op jit(solution)/shard_map/ppermute | solution.py:336
  16.7 2.1 %collective-permute-start.15 = (bf16[2,128,768]{2,1,0:T(8,128)(2,1)S(1)}, bf16[2,128,768]{2,1,0:T(8,128)(2,1)S(1)}, u32[]{:S(2)}, u32[]{:S(2)}) collective-permute-start(bf16[2,128,768]{2,1,0:T(8,128)(2,1)S(1)} %get-tuple-element.75), channel_id=1, source_target_pairs={{0,1},{1,0},{2,3},{3,2},{4,5},{5,4},{6,7},{7,6},{8,9},{9,8},{10,11... | collective-permute-start | bytes 1179656 | tf_op jit(solution)/shard_map/ppermute | solution.py:336
  18.8 0.0 collective-permute-start.16
  18.8 6.4 %collective-permute-done.8.kv_ref = bf16[2,128,768]{2,1,0:T(8,128)(2,1)S(1)} collective-permute-done((bf16[2,128,768]{2,1,0:T(8,128)(2,1)}, bf16[2,128,768]{2,1,0:T(8,128)(2,1)S(1)}, u32[]{:S(2)}, u32[]{:S(2)}) %collective-permute-start.8) | collective-permute-done | bytes 393248 | tf_op jit(solution)/shard_map/ppermute | solution.py:336
  25.1 0.7 collective-permute-start.17
  25.8 1.9 %prep.1 = (f32[768,256]{1,0:T(8,128)S(1)}, f32[256,1536]{1,0:T(8,128)S(1)}, bf16[24,256]{1,0:T(8,128)(2,1)S(1)}) custom-call(s32[1]{0:T(128)} %bitcast.place_ref, s32[32,128]{1,0:T(8,128)S(1)} %bitcast.5, s32[1,24]{1,0:T(1,128)S(1)} %bitcast.6, s32[24,24]{1,0:T(8,128)S(1)} %copy-done.8, f32[128,3072]{1,0:T(8,128)S(1)} %copy-done.1), custom_call_target="tpu_custom_call" | custom-call | flops 1 | bytes 1 | tf_op jit(solution)/shard_map/prep/pallas_call | solution.py:358
  27.7 5.0 %collective-permute-done.15.qo_ref = bf16[2,128,768]{2,1,0:T(8,128)(2,1)S(1)} collective-permute-done((bf16[2,128,768]{2,1,0:T(8,128)(2,1)S(1)}, bf16[2,128,768]{2,1,0:T(8,128)(2,1)S(1)}, u32[]{:S(2)}, u32[]{:S(2)}) %collective-permute-start.15) | collective-permute-done | bytes 393248 | tf_op jit(solution)/shard_map/ppermute | solution.py:336
  32.7 1.7 %collective-permute-start.9 = (bf16[2,128,768]{2,1,0:T(8,128)(2,1)S(1)}, bf16[2,128,768]{2,1,0:T(8,128)(2,1)S(1)}, u32[]{:S(2)}, u32[]{:S(2)}) collective-permute-start(bf16[2,128,768]{2,1,0:T(8,128)(2,1)S(1)} %get-tuple-element.69), channel_id=1, source_target_pairs={{0,1},{1,0},{2,3},{3,2},{4,5},{5,4},{6,7},{7,6},{8,9},{9,8},{10,11... | collective-permute-start | bytes 1179656 | tf_op jit(solution)/shard_map/ppermute | solution.py:336
  34.5 0.0 collective-permute-done.10.near_own_ref
  34.5 0.0 collective-permute-start.11
  34.5 0.0 collective-permute-done.12.side_own_ref
  34.5 0.7 collective-permute-start.13
  35.2 0.0 collective-permute-done.16.near_far_ref
  35.2 0.0 collective-permute-done.17.side_far_ref
  35.2 7.6 %attention.2 = (bf16[2,128,768]{2,1,0:T(8,128)(2,1)S(1)}, bf16[2,128,768]{2,1,0:T(8,128)(2,1)S(1)}, bf16[128,3072]{1,0:T(8,128)(2,1)}, bf16[128,3072]{1,0:T(8,12...) custom-call(s32[1]{0:T(128)} %bitcast.place_ref, ...), custom_call_target="tpu_custom_call" | custom-call | flops 1 | bytes 1 | tf_op jit(solution)/shard_map/attention/pallas_call | solution.py:411
  42.8 0.3 collective-permute-start.18
  43.1 0.7 collective-permute-start.19
  43.8 0.0 collective-permute-done.9.qo_ref
  43.8 0.0 collective-permute-done.11.near_far_ref
  43.8 0.0 collective-permute-done.13.side_far_ref
  43.8 7.7 %attention.3 = (bf16[2,128,768]{2,1,0:T(8,128)(2,1)S(1)}, bf16[2,128,768]{2,1,0:T(8,128)(2,1)S(1)}, bf16[128,3072]{1,0:T(8,128)(2,1)}, bf16[128,3072]{1,0:T(8,12...) custom-call(s32[1]{0:T(128)} %bitcast.place_ref, ...), custom_call_target="tpu_custom_call", output_to_operand_aliasing={{2}: (12, {}), {3}: (13, {}), {4}: (14, {}), {5}: (15, {}),... | custom-call | flops 1 | bytes 1 | tf_op jit(solution)/shard_map/attention/pallas_call | solution.py:411
  51.5 1.4 %collective-permute-done.18.refs_0_ = bf16[2,128,768]{2,1,0:T(8,128)(2,1)S(1)} collective-permute-done((bf16[2,128,768]{2,1,0:T(8,128)(2,1)S(1)}, bf16[2,128,768]{2,1,0:T(8,128)(2,1)S(1)}, u32[]{:S(2)}, u32[]{:S(2)}) %collective-permute-start.18) | collective-permute-done | bytes 393248 | tf_op jit(solution)/shard_map/ppermute | solution.py:344
  52.9 0.0 collective-permute-done.19.refs_0_
  52.9 6.6 %collective-permute-start.24 = (bf16[2,128,1536]{2,1,0:T(8,128)(2,1)S(1)}, bf16[2,128,1536]{2,1,0:T(8,128)(2,1)S(1)}, u32[]{:S(2)}, u32[]{:S(2)}) collective-permute-start(bf16[2,128,1536]{2,1,0:T(8,128)(2,1)S(1)} %get-tuple-element.100), channel_id=1, source_target_pairs={{0,2},{2,0},{4,6},{6,4},{8,10},{10,8},{12,14},{14,12},{16,18},{18,... | collective-permute-start | bytes 2359304 | tf_op jit(solution)/shard_map/ppermute | solution.py:459
  59.4 0.7 collective-permute-start.25
  60.1 1.6 %collective-permute-start.26 = (bf16[2,128,768]{2,1,0:T(8,128)(2,1)S(1)}, bf16[2,128,768]{2,1,0:T(8,128)(2,1)S(1)}, u32[]{:S(2)}, u32[]{:S(2)}) collective-permute-start(bf16[2,128,768]{2,1,0:T(8,128)(2,1)S(1)} %get-tuple-element.104), channel_id=1, source_target_pairs={{0,1},{1,0},{2,3},{3,2},{4,5},{5,4},{6,7},{7,6},{8,9},{9,8},{10,11... | collective-permute-start | bytes 1179656 | tf_op jit(solution)/shard_map/ppermute | solution.py:344
  61.7 3.4 %collective-permute-start.21 = (f32[24,1536]{1,0:T(8,128)S(1)}, f32[24,1536]{1,0:T(8,128)S(1)}, u32[]{:S(2)}, u32[]{:S(2)}) collective-permute-start(f32[24,1536]{1,0:T(8,128)S(1)} %get-tuple-element.98), channel_id=1, source_target_pairs={{0,2},{2,0},{4,6},{6,4},{8,10},{10,8},{12,14},{14,12},{16,18},{18,... | collective-permute-start | bytes 442376 | tf_op jit(solution)/shard_map/ppermute | solution.py:464
  65.1 1.7 %collective-permute-start.22 = (f32[24,1536]{1,0:T(8,128)S(1)}, f32[24,1536]{1,0:T(8,128)S(1)}, u32[]{:S(2)}, u32[]{:S(2)}) collective-permute-start(f32[24,1536]{1,0:T(8,128)S(1)} %get-tuple-element.98), channel_id=1, source_target_pairs={{0,8},{2,10},{4,12},{6,14},{8,0},{10,2},{12,4},{14,6},{16,24},{18,... | collective-permute-start | bytes 442376 | tf_op jit(solution)/shard_map/ppermute | solution.py:464
  66.9 0.0 collective-permute-done.25.refs_1_
  66.9 8.1 %collective-permute-start.23 = (f32[24,1536]{1,0:T(8,128)S(1)}, f32[24,1536]{1,0:T(8,128)S(1)}, u32[]{:S(2)}, u32[]{:S(2)}) collective-permute-start(f32[24,1536]{1,0:T(8,128)S(1)} %get-tuple-element.98), channel_id=1, source_target_pairs={{0,10},{2,8},{4,14},{6,12},{8,2},{10,0},{12,6},{14,4},{16,26},{18,... | collective-permute-start | bytes 442376 | tf_op jit(solution)/shard_map/ppermute | solution.py:464
  75.0 0.0 collective-permute-done.26.refs_1_
  75.0 1.8 %collective-permute-start.28 = (bf16[2,128,1536]{2,1,0:T(8,128)(2,1)}, bf16[2,128,1536]{2,1,0:T(8,128)(2,1)S(1)}, u32[]{:S(2)}, u32[]{:S(2)}) collective-permute-start(bf16[2,128,1536]{2,1,0:T(8,128)(2,1)} %get-tuple-element.110), channel_id=1, source_target_pairs={{0,0},{2,4},{4,2},{6,8},{8,6},{10,12},{12,10},{14,16},{16,14},{18,... | collective-permute-start | bytes 2359304 | tf_op jit(solution)/shard_map/ppermute | solution.py:461
  76.8 0.0 collective-permute-done.24.near_ref
  76.8 1.1 far_sum.1
  77.9 0.0 copy-done.4
  77.9 1.5 %collective-permute-start.27 = (bf16[2,128,1536]{2,1,0:T(8,128)(2,1)}, bf16[2,128,1536]{2,1,0:T(8,128)(2,1)S(1)}, u32[]{:S(2)}, u32[]{:S(2)}) collective-permute-start(bf16[2,128,1536]{2,1,0:T(8,128)(2,1)} %far_sum.1), channel_id=1, source_target_pairs={{0,1},{1,0},{2,3},{3,2},{4,5},{5,4},{6,7},{7,6},{8,9},{9,8},{10,11... | collective-permute-start | bytes 2359304 | tf_op jit(solution)/shard_map/ppermute | solution.py:344
  79.5 0.0 collective-permute-done.21
  79.5 0.0 collective-permute-done.22
  79.5 0.0 collective-permute-done.23
  79.5 27.7 %conditional.1 = (f32[24,1536]{1,0:T(8,128)}, f32[24,1536]{1,0:T(8,128)}) conditional(s32[]{:T(128)} %bitcast.3, f32[24,1536]{1,0:T(8,128)S(1)} %add_add_fusion.2, f32[24,1536]{1,0:T(8,128)S(1)} %add_add_fusion.2), branch_computations={%region_0.0_spmd, %region_1.0_spmd} | conditional | flops 110592 | bytes 3096752 | solution.py:498
  79.5 1.7 %collective-permute-start.4 = (f32[24,1536]{1,0:T(8,128)S(1)}, f32[24,1536]{1,0:T(8,128)S(1)}, u32[]{:S(2)}, u32[]{:S(2)}) collective-permute-start(f32[24,1536]{1,0:T(8,128)S(1)} %param.1), channel_id=1, source_target_pairs={{0,4},{2,6},{4,0},{6,2},{8,12},{10,14},{12,8},{14,10},{16,20},{18,... | collective-permute-start | bytes 442376 | tf_op jit(solution)/shard_map/cond/branch_1_fun/ppermute | solution.py:464
  81.2 1.9 %collective-permute-start.5 = (f32[24,1536]{1,0:T(8,128)S(1)}, f32[24,1536]{1,0:T(8,128)S(1)}, u32[]{:S(2)}, u32[]{:S(2)}) collective-permute-start(f32[24,1536]{1,0:T(8,128)S(1)} %param.1), channel_id=1, source_target_pairs={{0,16},{2,18},{4,20},{6,22},{8,24},{10,26},{12,28},{14,30},{16,0},... | collective-permute-start | bytes 442376 | tf_op jit(solution)/shard_map/cond/branch_1_fun/ppermute | solution.py:464
  83.1 0.9 collective-permute-start.6
  84.0 9.0 %collective-permute-done.4 = f32[24,1536]{1,0:T(8,128)S(1)} collective-permute-done((f32[24,1536]{1,0:T(8,128)S(1)}, f32[24,1536]{1,0:T(8,128)S(1)}, u32[]{:S(2)}, u32[]{:S(2)}) %collective-permute-start.4) | collective-permute-done | bytes 147488 | tf_op jit(solution)/shard_map/cond/branch_1_fun/ppermute | solution.py:464
  93.0 8.0 %collective-permute-done.5 = f32[24,1536]{1,0:T(8,128)S(1)} collective-permute-done((f32[24,1536]{1,0:T(8,128)S(1)}, f32[24,1536]{1,0:T(8,128)S(1)}, u32[]{:S(2)}, u32[]{:S(2)}) %collective-permute-start.5) | collective-permute-done | bytes 147488 | tf_op jit(solution)/shard_map/cond/branch_1_fun/ppermute | solution.py:464
  101.0 0.0 collective-permute-done.6
  101.0 0.7 add_add_fusion.1
  101.7 1.5 %collective-permute-start.7 = (f32[24,1536]{1,0:T(8,128)}, f32[24,1536]{1,0:T(8,128)}, u32[]{:S(2)}, u32[]{:S(2)}) collective-permute-start(f32[24,1536]{1,0:T(8,128)} %add_add_fusion.1), channel_id=1, source_target_pairs={{0,1},{1,0},{2,3},{3,2},{4,5},{5,4},{6,7},{7,6},{8,9},{9,8},{10,11... | collective-permute-start | bytes 442376 | tf_op jit(solution)/shard_map/cond/branch_1_fun/ppermute | solution.py:493
  103.2 3.9 %collective-permute-done.7 = f32[24,1536]{1,0:T(8,128)} collective-permute-done((f32[24,1536]{1,0:T(8,128)}, f32[24,1536]{1,0:T(8,128)}, u32[]{:S(2)}, u32[]{:S(2)}) %collective-permute-start.7) | collective-permute-done | bytes 147488 | tf_op jit(solution)/shard_map/cond/branch_1_fun/ppermute | solution.py:493
  107.2 0.0 collective-permute-start.20
  107.2 0.0 collective-permute-done.28.side_ref
  107.2 0.0 collective-permute-done.27.refs_2_
  107.2 2.9 %spread.1 = f32[128,3072]{1,0:T(8,128)} custom-call(s32[1]{0:T(128)} %bitcast.place_ref, s32[1,24]{1,0:T(1,128)S(1)} %bitcast.8, f32[24,1536]{1,0:T(8,128)} %get-tuple-element.121.refs_0_, f32[24,1536]{1,0:T(8,128)} %get-tuple-element.122.refs_1_), custom_call_target="tpu_custom_call" | custom-call | flops 1 | bytes 1 | tf_op jit(solution)/shard_map/spread/pallas_call | solution.py:505
  110.1 0.0 collective-permute-done.20.near_ref
  110.1 0.0 copy-done.6
  110.1 1.5 %finish.1 = (bf16[128,3072]{1,0:T(8,128)(2,1)}, bf16[128,3072]{1,0:T(8,128)(2,1)}, bf16[128,3072]{1,0:T(8,128)(2,1)}, bf16[128,3072]{1,0:T(8,128)(2,1)}) custom-call(s32[1]{0:T(128)} %bitcast.place_ref, f32[2,128,1536]{2,1,0:T(8,128)S(1)} %get-tuple-element.96.part_ref, ...), custom_call_target="tpu_custom_call", output_to_operand_aliasing={{0}: (7, {}), {1}: (8, {})} | custom-call | flops 1 | bytes 1 | tf_op jit(solution)/shard_map/finish/pallas_call | solution.py:520
  (17 shorter events, 0.1 us)
Async XLA Ops:
  0.6 7.8 %copy-start.2 = (bf16[128,3072]{1,0:T(8,128)(2,1)S(1)}, bf16[128,3072]{1,0:T(8,128)(2,1)}, u32[]{:S(2)}) copy-start(bf16[128,3072]{1,0:T(8,128)(2,1)} %first_ref.2) | copy-start | bytes 2359300
  0.6 7.8 %copy-start.3 = (bf16[128,3072]{1,0:T(8,128)(2,1)S(1)}, bf16[128,3072]{1,0:T(8,128)(2,1)}, u32[]{:S(2)}) copy-start(bf16[128,3072]{1,0:T(8,128)(2,1)} %second_ref.2) | copy-start | bytes 2359300
  0.7 25.1 %copy-start.1 = (f32[128,3072]{1,0:T(8,128)S(1)}, f32[128,3072]{1,0:T(8,128)}, u32[]{:S(2)}) copy-start(f32[128,3072]{1,0:T(8,128)} %table_ref.1) | copy-start | bytes 4718596
  0.7 25.1 %copy-start.7 = (s32[4096]{0:T(1024)S(1)}, s32[4096]{0:T(1024)}, u32[]{:S(2)}) copy-start(s32[4096]{0:T(1024)} %param.15) | copy-start | bytes 49156
  0.7 25.1 %copy-start.8 = (s32[24,24]{1,0:T(8,128)S(1)}, s32[24,24]{1,0:T(8,128)}, u32[]{:S(2)}) copy-start(s32[24,24]{1,0:T(8,128)} %mask_ref.1) | copy-start | bytes 6916
  0.7 25.1 %copy-start.9 = (s32[24]{0:T(128)S(1)}, s32[24]{0:T(128)}, u32[]{:S(2)}) copy-start(s32[24]{0:T(128)} %param.16) | copy-start | bytes 292
  3.5 13.2 %collective-permute-start.14 = (bf16[2,128,768]{2,1,0:T(8,128)(2,1)}, bf16[2,128,768]{2,1,0:T(8,128)(2,1)S(1)}, u32[]{:S(2)}, u32[]{:S(2)}) collective-permute-start(bf16[2,128,768]{2,1,0:T(8,128)(2,1)} %get-tuple-element.74), channel_id=1, source_target_pairs={{0,1},{1,0},{2,3},{3,2},{4,5},{5,4},{6,7},{7,6},{8,9},{9,8},{10,11... | collective-permute-start | bytes 1179656 | tf_op jit(solution)/shard_map/ppermute | solution.py:336
  6.5 27.9 %collective-permute-start.10 = (bf16[2,128,1536]{2,1,0:T(8,128)(2,1)}, bf16[2,128,1536]{2,1,0:T(8,128)(2,1)S(1)}, u32[]{:S(2)}, u32[]{:S(2)}) collective-permute-start(bf16[2,128,1536]{2,1,0:T(8,128)(2,1)} %get-tuple-element.66.kv_own_ref), channel_id=1, source_target_pairs={{0,2},{2,0},{4,6},{6,4},{8,10},{10,8},{12,14},{14,12},{16,18},{18,... | collective-permute-start | bytes 2359304 | tf_op jit(solution)/shard_map/ppermute | solution.py:350
  6.5 27.9 %collective-permute-start.12 = (bf16[2,128,1536]{2,1,0:T(8,128)(2,1)}, bf16[2,128,1536]{2,1,0:T(8,128)(2,1)S(1)}, u32[]{:S(2)}, u32[]{:S(2)}) collective-permute-start(bf16[2,128,1536]{2,1,0:T(8,128)(2,1)} %get-tuple-element.66.kv_own_ref), channel_id=1, source_target_pairs={{0,0},{2,4},{4,2},{6,8},{8,6},{10,12},{12,10},{14,16},{16,14},{18,... | collective-permute-start | bytes 2359304 | tf_op jit(solution)/shard_map/ppermute | solution.py:349
  8.3 26.9 %copy-start = (bf16[2,128,1536]{2,1,0:T(8,128)(2,1)S(1)}, bf16[2,128,1536]{2,1,0:T(8,128)(2,1)}, u32[]{:S(2)}) copy-start(bf16[2,128,1536]{2,1,0:T(8,128)(2,1)} %get-tuple-element.66.kv_own_ref) | copy-start | bytes 2359300
  8.3 16.8 %collective-permute-start.8 = (bf16[2,128,768]{2,1,0:T(8,128)(2,1)}, bf16[2,128,768]{2,1,0:T(8,128)(2,1)S(1)}, u32[]{:S(2)}, u32[]{:S(2)}) collective-permute-start(bf16[2,128,768]{2,1,0:T(8,128)(2,1)} %get-tuple-element.68), channel_id=1, source_target_pairs={{0,1},{1,0},{2,3},{3,2},{4,5},{5,4},{6,7},{7,6},{8,9},{9,8},{10,11... | collective-permute-start | bytes 1179656 | tf_op jit(solution)/shard_map/ppermute | solution.py:336
  16.7 16.0 %collective-permute-start.15 = (bf16[2,128,768]{2,1,0:T(8,128)(2,1)S(1)}, bf16[2,128,768]{2,1,0:T(8,128)(2,1)S(1)}, u32[]{:S(2)}, u32[]{:S(2)}) collective-permute-start(bf16[2,128,768]{2,1,0:T(8,128)(2,1)S(1)} %get-tuple-element.75), channel_id=1, source_target_pairs={{0,1},{1,0},{2,3},{3,2},{4,5},{5,4},{6,7},{7,6},{8,9},{9,8},{10,11... | collective-permute-start | bytes 1179656 | tf_op jit(solution)/shard_map/ppermute | solution.py:336
  18.8 16.4 %collective-permute-start.16 = (bf16[2,128,768]{2,1,0:T(8,128)(2,1)S(1)}, bf16[2,128,768]{2,1,0:T(8,128)(2,1)S(1)}, u32[]{:S(2)}, u32[]{:S(2)}) collective-permute-start(bf16[2,128,768]{2,1,0:T(8,128)(2,1)S(1)} %collective-permute-done.14.kv_ref), channel_id=1, source_target_pairs={{0,2},{2,0},{4,6},{6,4},{8,10},{10,8},{12,14},{14,12},{16,18},{18,... | collective-permute-start | bytes 1179656 | tf_op jit(solution)/shard_map/ppermute | solution.py:353
  25.1 10.1 %collective-permute-start.17 = (bf16[2,128,768]{2,1,0:T(8,128)(2,1)S(1)}, bf16[2,128,768]{2,1,0:T(8,128)(2,1)S(1)}, u32[]{:S(2)}, u32[]{:S(2)}) collective-permute-start(bf16[2,128,768]{2,1,0:T(8,128)(2,1)S(1)} %collective-permute-done.14.kv_ref), channel_id=1, source_target_pairs={{0,0},{2,4},{4,2},{6,8},{8,6},{10,12},{12,10},{14,16},{16,14},{18,... | collective-permute-start | bytes 1179656 | tf_op jit(solution)/shard_map/ppermute | solution.py:352
  32.7 11.1 %collective-permute-start.9 = (bf16[2,128,768]{2,1,0:T(8,128)(2,1)S(1)}, bf16[2,128,768]{2,1,0:T(8,128)(2,1)S(1)}, u32[]{:S(2)}, u32[]{:S(2)}) collective-permute-start(bf16[2,128,768]{2,1,0:T(8,128)(2,1)S(1)} %get-tuple-element.69), channel_id=1, source_target_pairs={{0,1},{1,0},{2,3},{3,2},{4,5},{5,4},{6,7},{7,6},{8,9},{9,8},{10,11... | collective-permute-start | bytes 1179656 | tf_op jit(solution)/shard_map/ppermute | solution.py:336
  34.5 9.3 %collective-permute-start.11 = (bf16[2,128,768]{2,1,0:T(8,128)(2,1)S(1)}, bf16[2,128,768]{2,1,0:T(8,128)(2,1)S(1)}, u32[]{:S(2)}, u32[]{:S(2)}) collective-permute-start(bf16[2,128,768]{2,1,0:T(8,128)(2,1)S(1)} %collective-permute-done.8.kv_ref), channel_id=1, source_target_pairs={{0,2},{2,0},{4,6},{6,4},{8,10},{10,8},{12,14},{14,12},{16,18},{18,... | collective-permute-start | bytes 1179656 | tf_op jit(solution)/shard_map/ppermute | solution.py:353
  34.5 9.3 %collective-permute-start.13 = (bf16[2,128,768]{2,1,0:T(8,128)(2,1)S(1)}, bf16[2,128,768]{2,1,0:T(8,128)(2,1)S(1)}, u32[]{:S(2)}, u32[]{:S(2)}) collective-permute-start(bf16[2,128,768]{2,1,0:T(8,128)(2,1)S(1)} %collective-permute-done.8.kv_ref), channel_id=1, source_target_pairs={{0,0},{2,4},{4,2},{6,8},{8,6},{10,12},{12,10},{14,16},{16,14},{18,... | collective-permute-start | bytes 1179656 | tf_op jit(solution)/shard_map/ppermute | solution.py:352
  42.8 10.0 %collective-permute-start.18 = (bf16[2,128,768]{2,1,0:T(8,128)(2,1)S(1)}, bf16[2,128,768]{2,1,0:T(8,128)(2,1)S(1)}, u32[]{:S(2)}, u32[]{:S(2)}) collective-permute-start(bf16[2,128,768]{2,1,0:T(8,128)(2,1)S(1)} %get-tuple-element.94), channel_id=1, source_target_pairs={{0,1},{1,0},{2,3},{3,2},{4,5},{5,4},{6,7},{7,6},{8,9},{9,8},{10,11... | collective-permute-start | bytes 1179656 | tf_op jit(solution)/shard_map/ppermute | solution.py:344
  43.1 9.8 %collective-permute-start.19 = (bf16[2,128,768]{2,1,0:T(8,128)(2,1)S(1)}, bf16[2,128,768]{2,1,0:T(8,128)(2,1)S(1)}, u32[]{:S(2)}, u32[]{:S(2)}) collective-permute-start(bf16[2,128,768]{2,1,0:T(8,128)(2,1)S(1)} %get-tuple-element.95), channel_id=1, source_target_pairs={{0,0},{2,4},{4,2},{6,8},{8,6},{10,12},{12,10},{14,16},{16,14},{18,... | collective-permute-start | bytes 1179656 | tf_op jit(solution)/shard_map/ppermute | solution.py:455
  51.5 26.5 %copy-start.4 = (bf16[2,128,1536]{2,1,0:T(8,128)(2,1)}, bf16[2,128,1536]{2,1,0:T(8,128)(2,1)S(1)}, u32[]{:S(2)}) copy-start(bf16[2,128,1536]{2,1,0:T(8,128)(2,1)S(1)} %get-tuple-element.97) | copy-start | bytes 2359300
  52.9 23.9 %collective-permute-start.24 = (bf16[2,128,1536]{2,1,0:T(8,128)(2,1)S(1)}, bf16[2,128,1536]{2,1,0:T(8,128)(2,1)S(1)}, u32[]{:S(2)}, u32[]{:S(2)}) collective-permute-start(bf16[2,128,1536]{2,1,0:T(8,128)(2,1)S(1)} %get-tuple-element.100), channel_id=1, source_target_pairs={{0,2},{2,0},{4,6},{6,4},{8,10},{10,8},{12,14},{14,12},{16,18},{18,... | collective-permute-start | bytes 2359304 | tf_op jit(solution)/shard_map/ppermute | solution.py:459
  59.4 7.4 %collective-permute-start.25 = (bf16[2,128,768]{2,1,0:T(8,128)(2,1)S(1)}, bf16[2,128,768]{2,1,0:T(8,128)(2,1)S(1)}, u32[]{:S(2)}, u32[]{:S(2)}) collective-permute-start(bf16[2,128,768]{2,1,0:T(8,128)(2,1)S(1)} %get-tuple-element.102), channel_id=1, source_target_pairs={{0,0},{2,4},{4,2},{6,8},{8,6},{10,12},{12,10},{14,16},{16,14},{18,... | collective-permute-start | bytes 1179656 | tf_op jit(solution)/shard_map/ppermute | solution.py:455
  60.1 14.9 %collective-permute-start.26 = (bf16[2,128,768]{2,1,0:T(8,128)(2,1)S(1)}, bf16[2,128,768]{2,1,0:T(8,128)(2,1)S(1)}, u32[]{:S(2)}, u32[]{:S(2)}) collective-permute-start(bf16[2,128,768]{2,1,0:T(8,128)(2,1)S(1)} %get-tuple-element.104), channel_id=1, source_target_pairs={{0,1},{1,0},{2,3},{3,2},{4,5},{5,4},{6,7},{7,6},{8,9},{9,8},{10,11... | collective-permute-start | bytes 1179656 | tf_op jit(solution)/shard_map/ppermute | solution.py:344
  61.7 17.8 %collective-permute-start.21 = (f32[24,1536]{1,0:T(8,128)S(1)}, f32[24,1536]{1,0:T(8,128)S(1)}, u32[]{:S(2)}, u32[]{:S(2)}) collective-permute-start(f32[24,1536]{1,0:T(8,128)S(1)} %get-tuple-element.98), channel_id=1, source_target_pairs={{0,2},{2,0},{4,6},{6,4},{8,10},{10,8},{12,14},{14,12},{16,18},{18,... | collective-permute-start | bytes 442376 | tf_op jit(solution)/shard_map/ppermute | solution.py:464
  65.1 14.3 %collective-permute-start.22 = (f32[24,1536]{1,0:T(8,128)S(1)}, f32[24,1536]{1,0:T(8,128)S(1)}, u32[]{:S(2)}, u32[]{:S(2)}) collective-permute-start(f32[24,1536]{1,0:T(8,128)S(1)} %get-tuple-element.98), channel_id=1, source_target_pairs={{0,8},{2,10},{4,12},{6,14},{8,0},{10,2},{12,4},{14,6},{16,24},{18,... | collective-permute-start | bytes 442376 | tf_op jit(solution)/shard_map/ppermute | solution.py:464
  66.9 12.6 %collective-permute-start.23 = (f32[24,1536]{1,0:T(8,128)S(1)}, f32[24,1536]{1,0:T(8,128)S(1)}, u32[]{:S(2)}, u32[]{:S(2)}) collective-permute-start(f32[24,1536]{1,0:T(8,128)S(1)} %get-tuple-element.98), channel_id=1, source_target_pairs={{0,10},{2,8},{4,14},{6,12},{8,2},{10,0},{12,6},{14,4},{16,26},{18,... | collective-permute-start | bytes 442376 | tf_op jit(solution)/shard_map/ppermute | solution.py:464
  75.0 2.9 %copy-start.5 = (bf16[2,128,768]{2,1,0:T(8,128)(2,1)}, bf16[2,128,768]{2,1,0:T(8,128)(2,1)S(1)}, u32[]{:S(2)}) copy-start(bf16[2,128,768]{2,1,0:T(8,128)(2,1)S(1)} %collective-permute-done.26.refs_1_) | copy-start | bytes 1179652
  75.0 32.2 %collective-permute-start.28 = (bf16[2,128,1536]{2,1,0:T(8,128)(2,1)}, bf16[2,128,1536]{2,1,0:T(8,128)(2,1)S(1)}, u32[]{:S(2)}, u32[]{:S(2)}) collective-permute-start(bf16[2,128,1536]{2,1,0:T(8,128)(2,1)} %get-tuple-element.110), channel_id=1, source_target_pairs={{0,0},{2,4},{4,2},{6,8},{8,6},{10,12},{12,10},{14,16},{16,14},{18,... | collective-permute-start | bytes 2359304 | tf_op jit(solution)/shard_map/ppermute | solution.py:461
  77.9 29.3 %collective-permute-start.27 = (bf16[2,128,1536]{2,1,0:T(8,128)(2,1)}, bf16[2,128,1536]{2,1,0:T(8,128)(2,1)S(1)}, u32[]{:S(2)}, u32[]{:S(2)}) collective-permute-start(bf16[2,128,1536]{2,1,0:T(8,128)(2,1)} %far_sum.1), channel_id=1, source_target_pairs={{0,1},{1,0},{2,3},{3,2},{4,5},{5,4},{6,7},{7,6},{8,9},{9,8},{10,11... | collective-permute-start | bytes 2359304 | tf_op jit(solution)/shard_map/ppermute | solution.py:344
  79.5 13.5 %collective-permute-start.4 = (f32[24,1536]{1,0:T(8,128)S(1)}, f32[24,1536]{1,0:T(8,128)S(1)}, u32[]{:S(2)}, u32[]{:S(2)}) collective-permute-start(f32[24,1536]{1,0:T(8,128)S(1)} %param.1), channel_id=1, source_target_pairs={{0,4},{2,6},{4,0},{6,2},{8,12},{10,14},{12,8},{14,10},{16,20},{18,... | collective-permute-start | bytes 442376 | tf_op jit(solution)/shard_map/cond/branch_1_fun/ppermute | solution.py:464
  81.2 19.8 %collective-permute-start.5 = (f32[24,1536]{1,0:T(8,128)S(1)}, f32[24,1536]{1,0:T(8,128)S(1)}, u32[]{:S(2)}, u32[]{:S(2)}) collective-permute-start(f32[24,1536]{1,0:T(8,128)S(1)} %param.1), channel_id=1, source_target_pairs={{0,16},{2,18},{4,20},{6,22},{8,24},{10,26},{12,28},{14,30},{16,0},... | collective-permute-start | bytes 442376 | tf_op jit(solution)/shard_map/cond/branch_1_fun/ppermute | solution.py:464
  83.1 17.9 %collective-permute-start.6 = (f32[24,1536]{1,0:T(8,128)S(1)}, f32[24,1536]{1,0:T(8,128)S(1)}, u32[]{:S(2)}, u32[]{:S(2)}) collective-permute-start(f32[24,1536]{1,0:T(8,128)S(1)} %param.1), channel_id=1, source_target_pairs={{0,20},{2,22},{4,16},{6,18},{8,28},{10,30},{12,24},{14,26},{16,4},... | collective-permute-start | bytes 442376 | tf_op jit(solution)/shard_map/cond/branch_1_fun/ppermute | solution.py:464
  101.7 5.5 %collective-permute-start.7 = (f32[24,1536]{1,0:T(8,128)}, f32[24,1536]{1,0:T(8,128)}, u32[]{:S(2)}, u32[]{:S(2)}) collective-permute-start(f32[24,1536]{1,0:T(8,128)} %add_add_fusion.1), channel_id=1, source_target_pairs={{0,1},{1,0},{2,3},{3,2},{4,5},{5,4},{6,7},{7,6},{8,9},{9,8},{10,11... | collective-permute-start | bytes 442376 | tf_op jit(solution)/shard_map/cond/branch_1_fun/ppermute | solution.py:493
  107.2 3.0 %copy-start.6 = (bf16[2,128,768]{2,1,0:T(8,128)(2,1)S(1)}, bf16[2,128,768]{2,1,0:T(8,128)(2,1)}, u32[]{:S(2)}) copy-start(bf16[2,128,768]{2,1,0:T(8,128)(2,1)} %copy-done.5) | copy-start | bytes 1179652
  107.2 2.9 %collective-permute-start.20 = (bf16[2,128,1536]{2,1,0:T(8,128)(2,1)}, bf16[2,128,1536]{2,1,0:T(8,128)(2,1)S(1)}, u32[]{:S(2)}, u32[]{:S(2)}) collective-permute-start(bf16[2,128,1536]{2,1,0:T(8,128)(2,1)} %copy-done.4), channel_id=1, source_target_pairs={{0,2},{2,0},{4,6},{6,4},{8,10},{10,8},{12,14},{14,12},{16,18},{18,... | collective-permute-start | bytes 2359304 | tf_op jit(solution)/shard_map/ppermute | solution.py:460

commit v5 on v4

--- a/solution.py
+++ b/solution.py
@@ -230,9 +230,11 @@
         out_ref[:, :, cols] = (total + ref[...].astype(jnp.float32)).astype(out_ref.dtype)
 
 
-def finish_kernel(place_ref, part_ref, near_ref, side_ref, *refs, groups, parts):
+def finish_kernel(place_ref, noise_ref, part_ref, near_ref, side_ref, *refs, groups, parts, by_span):
     count = (groups - 1) * (parts + 1)
-    slabs, outs, (total_ref, sems) = refs[:count], refs[count + 2 : count + 6], refs[count + 6 :]
+    slot_refs, refs = refs[:groups], refs[groups:]
+    slabs, outs = refs[:count], refs[count + 2 : count + 7]
+    total_ref, pieces_ref, gate_ref, sems = refs[count + 7 :]
     width = part_ref.shape[2]
     copies = []
 
@@ -251,27 +253,28 @@
     total = part_ref[...] + near_ref[...].astype(jnp.float32) + side_ref[...].astype(jnp.float32)
     total_ref[...] = total.astype(total_ref.dtype)
     copy(total_ref, outs[2], outs[3], lax.rem(place_ref[0], groups) * width)
+    slots = pieces_ref.shape[0] // 3
+    levels = lax.broadcasted_iota(jnp.int32, (gate_ref.shape[0], noise_ref.shape[1]), 0)
+    onehot = (levels == noise_ref[...]).astype(jnp.bfloat16)
+    if by_span:
+        pieces_ref[...] = jnp.zeros_like(pieces_ref)
+    for j, ref in enumerate(slot_refs):
+        sums = ref[...]
+        if by_span:
+            for n in range(3):
+                piece = sums.astype(jnp.bfloat16)
+                sums = sums - piece.astype(jnp.float32)
+                pieces_ref[n * slots : n * slots + sums.shape[0]] = piece
+            sums = jnp.dot(onehot, pieces_ref[...], preferred_element_type=jnp.float32)
+        start = lax.bitwise_xor(lax.rem(place_ref[0], groups), j) * width
+        cols = pl.ds(pl.multiple_of(start, DH), width)
+        gate_ref[:, cols] = sums
+        copies.append(
+            pltpu.make_async_copy(gate_ref.at[:, cols], outs[4].at[:, cols], sems.at[len(copies)])
+        )
+        copies[-1].start()
     for one in copies:
         one.wait()
-
-
-def spread_kernel(place_ref, noise_ref, *refs, by_span, groups):
-    *slabs, out_ref = refs
-    levels = lax.broadcasted_iota(jnp.int32, (out_ref.shape[0], noise_ref.shape[1]), 0)
-    onehot = (levels == noise_ref[...]).astype(jnp.bfloat16)
-    for j, ref in enumerate(slabs):
-        sums = ref[...]
-        width = sums.shape[1]
-        if by_span:
-            total = None
-            for _ in range(3):
-                piece = sums.astype(jnp.bfloat16)
-                sums = sums - piece.astype(jnp.float32)
-                part = jnp.dot(onehot, piece, preferred_element_type=jnp.float32)
-                total = part if total is None else total + part
-            sums = total
-        start = lax.bitwise_xor(lax.rem(place_ref[0], groups), j) * width
-        out_ref[:, pl.ds(pl.multiple_of(start, DH), width)] = sums
 
 
 def per_device(
@@ -473,8 +476,8 @@
         return sums
 
     bits = [1 << n for n in range(ctx_count.bit_length() - 1)]
-    sums = rounds([bits[0], bits[2]], sums)
     side_back_far, back_far = tie((side_back_far, back_far))
+    sums = rounds(bits[:2], sums)
     far_grad = pl.pallas_call(
         far_sum_kernel,
         in_specs=[in_vmem] * (2 + parts),
@@ -493,7 +496,7 @@
             slabs = slabs + [lax.ppermute(slab, "head", pairs) for slab in slabs]
         return slabs
 
-    rest = [bits[1], *bits[3:]]
+    rest = bits[2:]
     sums, _ = tie((sums, far_grad))
     slabs = lax.cond(
         noise_level[0] >= 0,
@@ -502,39 +505,33 @@
         sums,
     )
     slabs, grad_far, side_back_own = tie((slabs, grad_far, side_back_own))
-    gate_grad = pl.pallas_call(
-        functools.partial(spread_kernel, by_span=by_span, groups=groups),
-        grid_spec=pltpu.PrefetchScalarGridSpec(
-            num_scalar_prefetch=1,
-            grid=(1,),
-            in_specs=[whole((1, span_total))] + [whole((slots, width))] * groups,
-            out_specs=whole((level_count, full_width)),
-        ),
-        out_shape=jax.ShapeDtypeStruct((level_count, full_width), f32),
-        compiler_params=small,
-        cost_estimate=cheap,
-        name="spread",
-    )(place, noise_level.reshape(1, span_total), *slabs)
-
     arrived = [slab for slabs in back_far for slab in slabs] + grad_far
-    outputs = pl.pallas_call(
-        functools.partial(finish_kernel, groups=groups, parts=parts),
-        grid_spec=pltpu.PrefetchScalarGridSpec(
-            num_scalar_prefetch=1,
-            in_specs=[in_vmem] * (3 + len(arrived)) + [anywhere] * 2,
-            out_specs=[anywhere] * 4,
-            scratch_shapes=[
-                pltpu.VMEM((2, rows, width), bf16),
-                pltpu.SemaphoreType.DMA((2 * len(arrived) + 2,)),
-            ],
-        ),
-        out_shape=[jax.ShapeDtypeStruct((rows, full_width), bf16)] * 4,
-        input_output_aliases={4 + len(arrived): 0, 5 + len(arrived): 1},
-        compiler_params=small,
-        cost_estimate=cheap,
-        name="finish",
-    )(place, own, near_back_own, side_back_own, *arrived, mixed, query_grad)
-    return (*outputs, gate_grad)
+    padded = -(-slots // 16) * 16
+    noise_row = jnp.pad(noise_level, (0, padded - slots), constant_values=-1) if by_span else noise_level
+    noise_row = jnp.tile(noise_row, 3 if by_span else 1).reshape(1, -1)
+    operands = (noise_row, own, near_back_own, side_back_own, *slabs, *arrived)
+    return tuple(
+        pl.pallas_call(
+            functools.partial(finish_kernel, groups=groups, parts=parts, by_span=by_span),
+            grid_spec=pltpu.PrefetchScalarGridSpec(
+                num_scalar_prefetch=1,
+                in_specs=[in_vmem] * len(operands) + [anywhere] * 2,
+                out_specs=[anywhere] * 5,
+                scratch_shapes=[
+                    pltpu.VMEM((2, rows, width), bf16),
+                    pltpu.VMEM((3 * padded, width), bf16),
+                    pltpu.VMEM((level_count, full_width), f32),
+                    pltpu.SemaphoreType.DMA((2 * len(arrived) + 2 + groups,)),
+                ],
+            ),
+            out_shape=[jax.ShapeDtypeStruct((rows, full_width), bf16)] * 4
+            + [jax.ShapeDtypeStruct((level_count, full_width), f32)],
+            input_output_aliases={1 + len(operands): 0, 2 + len(operands): 1},
+            compiler_params=small,
+            cost_estimate=cheap,
+            name="finish",
+        )(place, *operands, mixed, query_grad)
+    )
 
 
 def solution(mesh):

time: 113 us -> 116 us (1.027)
  waiting for transfers between devices: 41.8 us -> 53.7 us
  starting transfers between devices: 42.4 us -> 32.7 us
    ppermute x6, starting transfers between devices: 17.7 us -> 7.26 us  [shifted(): return lax.ppermute(array, 'ctx', [(i, i ^ step) for i in range(ctx_count)])]
    ppermute x6, waiting for transfers between devices: 17 us -> 24.1 us  [shifted(): return lax.ppermute(array, 'ctx', [(i, i ^ step) for i in range(ctx_count)])]
    pallas_call x1 -> x0, Pallas kernels: 2.92 us -> none  [per_device(): pl.pallas_call(functools.partial(spread_kernel, by_span=by_span, groups=g...]
    ppermute x1, waiting for transfers between devices: 3.93 us -> 6.64 us  [to_all(): slabs = slabs + [lax.ppermute(slab, 'head', pairs) for slab in slabs]]
    ppermute x1, waiting for transfers between devices: 0.01 us -> 2.15 us  [per_device(): near_back_own = lax.ppermute(near_grad_own, 'ctx', near_pairs)]
    pallas_call x1, Pallas kernels: 1.47 us -> 3.41 us  [per_device(): pl.pallas_call(functools.partial(finish_kernel, groups=groups, parts=part...]
    ppermute x1, starting transfers between devices: 0.01 us -> 1.84 us  [per_device(): near_back_own = lax.ppermute(near_grad_own, 'ctx', near_pairs)]
  transfers between devices with their start and end apart: 25 -> 25, of which waited for: 7 -> 11; matrix products, arithmetic and copies ran while one was open for 1% -> 1% of each run, Pallas kernels for 19% -> 16%
where the time goes in v5:
time: 116 us; the launch traced here: 114 us
  waiting for transfers between devices  53.7 us (46%)
  starting transfers between devices  32.7 us (28%)
  Pallas kernels  24.7 us (21%)
    ppermute x6, waiting for transfers between devices, shifted(): return lax.ppermute(array, 'ctx', [(i, i ^ step) for i in range(ctx_count)])  24.1 us
    ppermute x4, waiting for transfers between devices, to_peers(): arrived.append(lax.ppermute(part, 'head', pairs))  19.4 us
    pallas_call x2, Pallas kernels, attention(): pl.pallas_call(functools.partial(attention_kernel, rows=rows, tokens=toke...  15.3 us
    ppermute x6, starting transfers between devices, shifted(): return lax.ppermute(array, 'ctx', [(i, i ^ step) for i in range(ctx_count)])  7.26 us
    ppermute x4, starting transfers between devices, to_peers(): arrived.append(lax.ppermute(part, 'head', pairs))  6.93 us
    ppermute x1, waiting for transfers between devices, to_all(): slabs = slabs + [lax.ppermute(slab, 'head', pairs) for slab in slabs]  6.64 us
    ppermute x1, starting transfers between devices, per_device(): near_back_far = lax.ppermute(near_grad_far, 'ctx', near_pairs)  6.56 us
    pallas_call x1, Pallas kernels, per_device(): pl.pallas_call(functools.partial(finish_kernel, groups=groups, parts=part...  3.41 us
  transfers between devices with their start and end apart: 25, of which 11 were waited for; matrix products, arithmetic and copies ran while one was open for 1% of the time, Pallas kernels for 16%

profile of v5, /device:TPU:0, one launch (start us, length us, event | category | flops | bytes accessed | tf_op | source)
XLA Modules:
  0.0 113.9 jit_solution(1582186694752840331)
XLA Ops:
  0.6 0.0 copy-start.2
  0.6 0.0 copy-start.3
  0.7 0.0 copy-start.1
  0.7 2.8 %pack.3 = (bf16[2,128,1536]{2,1,0:T(8,128)(2,1)}, bf16[2,128,768]{2,1,0:T(8,128)(2,1)}, bf16[2,128,768]{2,1,0:T(8,128)(2,1)}) custom-call(s32[1]{0:T(128)} %bitcast.place_ref, bf16[128,3072]{1,0:T(8,128)(2,1)} %first_ref.3, bf16[128,3072]{1,0:T(8,128)(2,1)} %second_ref.3), custom_call_target="tpu_custom_call" | custom-call | flops 1 | bytes 1 | tf_op jit(solution)/shard_map/pack/pallas_call | solution.py:319
  3.5 3.0 %collective-permute-start.14 = (bf16[2,128,768]{2,1,0:T(8,128)(2,1)}, bf16[2,128,768]{2,1,0:T(8,128)(2,1)S(1)}, u32[]{:S(2)}, u32[]{:S(2)}) collective-permute-start(bf16[2,128,768]{2,1,0:T(8,128)(2,1)} %get-tuple-element.70), channel_id=1, source_target_pairs={{0,1},{1,0},{2,3},{3,2},{4,5},{5,4},{6,7},{7,6},{8,9},{9,8},{10,11... | collective-permute-start | bytes 1179656 | tf_op jit(solution)/shard_map/ppermute | solution.py:339
  6.5 0.0 collective-permute-start.10
  6.5 1.8 %collective-permute-start.12 = (bf16[2,128,1536]{2,1,0:T(8,128)(2,1)}, bf16[2,128,1536]{2,1,0:T(8,128)(2,1)S(1)}, u32[]{:S(2)}, u32[]{:S(2)}) collective-permute-start(bf16[2,128,1536]{2,1,0:T(8,128)(2,1)} %get-tuple-element.62.kv_own_ref), channel_id=1, source_target_pairs={{0,0},{2,4},{4,2},{6,8},{8,6},{10,12},{12,10},{14,16},{16,14},{18,... | collective-permute-start | bytes 2359304 | tf_op jit(solution)/shard_map/ppermute | solution.py:352
  8.3 0.1 collective-permute-start.8
  8.4 0.3 pack.2
  8.7 8.0 %collective-permute-done.14.kv_ref = bf16[2,128,768]{2,1,0:T(8,128)(2,1)S(1)} collective-permute-done((bf16[2,128,768]{2,1,0:T(8,128)(2,1)}, bf16[2,128,768]{2,1,0:T(8,128)(2,1)S(1)}, u32[]{:S(2)}, u32[]{:S(2)}) %collective-permute-start.14) | collective-permute-done | bytes 393248 | tf_op jit(solution)/shard_map/ppermute | solution.py:339
  16.7 2.1 %collective-permute-start.15 = (bf16[2,128,768]{2,1,0:T(8,128)(2,1)S(1)}, bf16[2,128,768]{2,1,0:T(8,128)(2,1)S(1)}, u32[]{:S(2)}, u32[]{:S(2)}) collective-permute-start(bf16[2,128,768]{2,1,0:T(8,128)(2,1)S(1)} %get-tuple-element.71), channel_id=1, source_target_pairs={{0,1},{1,0},{2,3},{3,2},{4,5},{5,4},{6,7},{7,6},{8,9},{9,8},{10,11... | collective-permute-start | bytes 1179656 | tf_op jit(solution)/shard_map/ppermute | solution.py:339
  18.8 0.0 collective-permute-start.16
  18.8 6.4 %collective-permute-done.8.kv_ref = bf16[2,128,768]{2,1,0:T(8,128)(2,1)S(1)} collective-permute-done((bf16[2,128,768]{2,1,0:T(8,128)(2,1)}, bf16[2,128,768]{2,1,0:T(8,128)(2,1)S(1)}, u32[]{:S(2)}, u32[]{:S(2)}) %collective-permute-start.8) | collective-permute-done | bytes 393248 | tf_op jit(solution)/shard_map/ppermute | solution.py:339
  25.1 0.7 collective-permute-start.17
  25.8 1.9 %prep.1 = (f32[768,256]{1,0:T(8,128)S(1)}, f32[256,1536]{1,0:T(8,128)S(1)}, bf16[24,256]{1,0:T(8,128)(2,1)S(1)}) custom-call(s32[1]{0:T(128)} %bitcast.place_ref, s32[32,128]{1,0:T(8,128)S(1)} %bitcast.5, s32[1,24]{1,0:T(1,128)S(1)} %bitcast.6, s32[24,24]{1,0:T(8,128)S(1)} %copy-done.8, f32[128,3072]{1,0:T(8,128)S(1)} %copy-done.1), custom_call_target="tpu_custom_call" | custom-call | flops 1 | bytes 1 | tf_op jit(solution)/shard_map/prep/pallas_call | solution.py:361
  27.7 5.0 %collective-permute-done.15.qo_ref = bf16[2,128,768]{2,1,0:T(8,128)(2,1)S(1)} collective-permute-done((bf16[2,128,768]{2,1,0:T(8,128)(2,1)S(1)}, bf16[2,128,768]{2,1,0:T(8,128)(2,1)S(1)}, u32[]{:S(2)}, u32[]{:S(2)}) %collective-permute-start.15) | collective-permute-done | bytes 393248 | tf_op jit(solution)/shard_map/ppermute | solution.py:339
  32.7 1.7 %collective-permute-start.9 = (bf16[2,128,768]{2,1,0:T(8,128)(2,1)S(1)}, bf16[2,128,768]{2,1,0:T(8,128)(2,1)S(1)}, u32[]{:S(2)}, u32[]{:S(2)}) collective-permute-start(bf16[2,128,768]{2,1,0:T(8,128)(2,1)S(1)} %get-tuple-element.65), channel_id=1, source_target_pairs={{0,1},{1,0},{2,3},{3,2},{4,5},{5,4},{6,7},{7,6},{8,9},{9,8},{10,11... | collective-permute-start | bytes 1179656 | tf_op jit(solution)/shard_map/ppermute | solution.py:339
  34.5 0.0 collective-permute-done.10.near_own_ref
  34.5 0.0 collective-permute-start.11
  34.5 0.0 collective-permute-done.12.side_own_ref
  34.5 0.7 collective-permute-start.13
  35.2 0.0 collective-permute-done.16.near_far_ref
  35.2 0.0 collective-permute-done.17.side_far_ref
  35.2 7.6 %attention.2 = (bf16[2,128,768]{2,1,0:T(8,128)(2,1)S(1)}, bf16[2,128,768]{2,1,0:T(8,128)(2,1)S(1)}, bf16[128,3072]{1,0:T(8,128)(2,1)}, bf16[128,3072]{1,0:T(8,12...) custom-call(s32[1]{0:T(128)} %bitcast.place_ref, ...), custom_call_target="tpu_custom_call" | custom-call | flops 1 | bytes 1 | tf_op jit(solution)/shard_map/attention/pallas_call | solution.py:414
  42.8 0.3 collective-permute-start.18
  43.1 0.7 collective-permute-start.19
  43.8 0.0 collective-permute-done.9.qo_ref
  43.8 0.0 collective-permute-done.11.near_far_ref
  43.8 0.0 collective-permute-done.13.side_far_ref
  43.8 7.7 %attention.3 = (bf16[2,128,768]{2,1,0:T(8,128)(2,1)S(1)}, bf16[2,128,768]{2,1,0:T(8,128)(2,1)S(1)}, bf16[128,3072]{1,0:T(8,128)(2,1)}, bf16[128,3072]{1,0:T(8,12...) custom-call(s32[1]{0:T(128)} %bitcast.place_ref, ...), custom_call_target="tpu_custom_call", output_to_operand_aliasing={{2}: (12, {}), {3}: (13, {}), {4}: (14, {}), {5}: (15, {}),... | custom-call | flops 1 | bytes 1 | tf_op jit(solution)/shard_map/attention/pallas_call | solution.py:414
  51.5 1.4 %collective-permute-done.18.refs_2_ = bf16[2,128,768]{2,1,0:T(8,128)(2,1)S(1)} collective-permute-done((bf16[2,128,768]{2,1,0:T(8,128)(2,1)S(1)}, bf16[2,128,768]{2,1,0:T(8,128)(2,1)S(1)}, u32[]{:S(2)}, u32[]{:S(2)}) %collective-permute-start.18) | collective-permute-done | bytes 393248 | tf_op jit(solution)/shard_map/ppermute | solution.py:347
  52.9 0.0 collective-permute-done.19.refs_0_
  52.9 6.6 %collective-permute-start.24 = (bf16[2,128,1536]{2,1,0:T(8,128)(2,1)S(1)}, bf16[2,128,1536]{2,1,0:T(8,128)(2,1)S(1)}, u32[]{:S(2)}, u32[]{:S(2)}) collective-permute-start(bf16[2,128,1536]{2,1,0:T(8,128)(2,1)S(1)} %get-tuple-element.96), channel_id=1, source_target_pairs={{0,2},{2,0},{4,6},{6,4},{8,10},{10,8},{12,14},{14,12},{16,18},{18,... | collective-permute-start | bytes 2359304 | tf_op jit(solution)/shard_map/ppermute | solution.py:462
  59.4 0.0 collective-permute-start.21
  59.4 2.9 %collective-permute-start.22 = (f32[24,1536]{1,0:T(8,128)S(1)}, f32[24,1536]{1,0:T(8,128)S(1)}, u32[]{:S(2)}, u32[]{:S(2)}) collective-permute-start(f32[24,1536]{1,0:T(8,128)S(1)} %get-tuple-element.94), channel_id=1, source_target_pairs={{0,4},{2,6},{4,0},{6,2},{8,12},{10,14},{12,8},{14,10},{16,20},{18,... | collective-permute-start | bytes 442376 | tf_op jit(solution)/shard_map/ppermute | solution.py:467
  62.3 0.0 collective-permute-start.23
  62.4 0.7 collective-permute-start.25
  63.0 0.0 collective-permute-done.21
  63.1 1.6 %collective-permute-start.26 = (bf16[2,128,768]{2,1,0:T(8,128)(2,1)S(1)}, bf16[2,128,768]{2,1,0:T(8,128)(2,1)S(1)}, u32[]{:S(2)}, u32[]{:S(2)}) collective-permute-start(bf16[2,128,768]{2,1,0:T(8,128)(2,1)S(1)} %get-tuple-element.100), channel_id=1, source_target_pairs={{0,1},{1,0},{2,3},{3,2},{4,5},{5,4},{6,7},{7,6},{8,9},{9,8},{10,11... | collective-permute-start | bytes 1179656 | tf_op jit(solution)/shard_map/ppermute | solution.py:347
  64.6 2.3 %collective-permute-done.22 = f32[24,1536]{1,0:T(8,128)S(1)} collective-permute-done((f32[24,1536]{1,0:T(8,128)S(1)}, f32[24,1536]{1,0:T(8,128)S(1)}, u32[]{:S(2)}, u32[]{:S(2)}) %collective-permute-start.22) | collective-permute-done | bytes 147488 | tf_op jit(solution)/shard_map/ppermute | solution.py:467
  67.0 1.8 %collective-permute-start.28 = (bf16[2,128,1536]{2,1,0:T(8,128)(2,1)}, bf16[2,128,1536]{2,1,0:T(8,128)(2,1)S(1)}, u32[]{:S(2)}, u32[]{:S(2)}) collective-permute-start(bf16[2,128,1536]{2,1,0:T(8,128)(2,1)} %get-tuple-element.106), channel_id=1, source_target_pairs={{0,0},{2,4},{4,2},{6,8},{8,6},{10,12},{12,10},{14,16},{16,14},{18,... | collective-permute-start | bytes 2359304 | tf_op jit(solution)/shard_map/ppermute | solution.py:464
  68.7 13.6 %collective-permute-done.23 = f32[24,1536]{1,0:T(8,128)S(1)} collective-permute-done((f32[24,1536]{1,0:T(8,128)S(1)}, f32[24,1536]{1,0:T(8,128)S(1)}, u32[]{:S(2)}, u32[]{:S(2)}) %collective-permute-start.23) | collective-permute-done | bytes 147488 | tf_op jit(solution)/shard_map/ppermute | solution.py:467
  82.4 0.0 collective-permute-done.25.refs_1_
  82.4 0.0 collective-permute-done.26.refs_3_
  82.4 0.0 collective-permute-done.24.near_ref
  82.4 1.1 far_sum.1
  83.5 1.5 %collective-permute-start.27 = (bf16[2,128,1536]{2,1,0:T(8,128)(2,1)}, bf16[2,128,1536]{2,1,0:T(8,128)(2,1)S(1)}, u32[]{:S(2)}, u32[]{:S(2)}) collective-permute-start(bf16[2,128,1536]{2,1,0:T(8,128)(2,1)} %far_sum.1), channel_id=1, source_target_pairs={{0,1},{1,0},{2,3},{3,2},{4,5},{5,4},{6,7},{7,6},{8,9},{9,8},{10,11... | collective-permute-start | bytes 2359304 | tf_op jit(solution)/shard_map/ppermute | solution.py:347
  85.1 20.4 %conditional.1 = (f32[24,1536]{1,0:T(8,128)}, f32[24,1536]{1,0:T(8,128)}) conditional(s32[]{:T(128)} %bitcast.3, f32[24,1536]{1,0:T(8,128)S(1)} %add_add_fusion.2, f32[24,1536]{1,0:T(8,128)S(1)} %add_add_fusion.2), branch_computations={%region_0.0_spmd, %region_1.0_spmd} | conditional | flops 110592 | bytes 3096752 | solution.py:501
  85.1 1.6 %collective-permute-start.4 = (f32[24,1536]{1,0:T(8,128)S(1)}, f32[24,1536]{1,0:T(8,128)S(1)}, u32[]{:S(2)}, u32[]{:S(2)}) collective-permute-start(f32[24,1536]{1,0:T(8,128)S(1)} %param.1), channel_id=1, source_target_pairs={{0,8},{2,10},{4,12},{6,14},{8,0},{10,2},{12,4},{14,6},{16,24},{18,... | collective-permute-start | bytes 442376 | tf_op jit(solution)/shard_map/cond/branch_1_fun/ppermute | solution.py:467
  86.6 2.0 %collective-permute-start.5 = (f32[24,1536]{1,0:T(8,128)S(1)}, f32[24,1536]{1,0:T(8,128)S(1)}, u32[]{:S(2)}, u32[]{:S(2)}) collective-permute-start(f32[24,1536]{1,0:T(8,128)S(1)} %param.1), channel_id=1, source_target_pairs={{0,16},{2,18},{4,20},{6,22},{8,24},{10,26},{12,28},{14,30},{16,0},... | collective-permute-start | bytes 442376 | tf_op jit(solution)/shard_map/cond/branch_1_fun/ppermute | solution.py:467
  88.6 0.8 collective-permute-start.6
  89.4 0.8 collective-permute-done.4
  90.2 4.6 %collective-permute-done.5 = f32[24,1536]{1,0:T(8,128)S(1)} collective-permute-done((f32[24,1536]{1,0:T(8,128)S(1)}, f32[24,1536]{1,0:T(8,128)S(1)}, u32[]{:S(2)}, u32[]{:S(2)}) %collective-permute-start.5) | collective-permute-done | bytes 147488 | tf_op jit(solution)/shard_map/cond/branch_1_fun/ppermute | solution.py:467
  94.8 2.8 %collective-permute-done.6 = f32[24,1536]{1,0:T(8,128)S(1)} collective-permute-done((f32[24,1536]{1,0:T(8,128)S(1)}, f32[24,1536]{1,0:T(8,128)S(1)}, u32[]{:S(2)}, u32[]{:S(2)}) %collective-permute-start.6) | collective-permute-done | bytes 147488 | tf_op jit(solution)/shard_map/cond/branch_1_fun/ppermute | solution.py:467
  97.6 0.7 add_add_fusion.1
  98.3 0.5 collective-permute-start.7
  98.8 6.6 %collective-permute-done.7 = f32[24,1536]{1,0:T(8,128)} collective-permute-done((f32[24,1536]{1,0:T(8,128)}, f32[24,1536]{1,0:T(8,128)}, u32[]{:S(2)}, u32[]{:S(2)}) %collective-permute-start.7) | collective-permute-done | bytes 147488 | tf_op jit(solution)/shard_map/cond/branch_1_fun/ppermute | solution.py:496
  105.4 1.8 %collective-permute-start.20 = (bf16[2,128,1536]{2,1,0:T(8,128)(2,1)}, bf16[2,128,1536]{2,1,0:T(8,128)(2,1)}, u32[]{:S(2)}, u32[]{:S(2)}) collective-permute-start(bf16[2,128,1536]{2,1,0:T(8,128)(2,1)} %copy-done.4), channel_id=1, source_target_pairs={{0,2},{2,0},{4,6},{6,4},{8,10},{10,8},{12,14},{14,12},{16,18},{18,... | collective-permute-start | bytes 2359304 | tf_op jit(solution)/shard_map/ppermute | solution.py:463
  107.3 0.1 reshape_tile.3.noise_ref
  107.3 0.0 collective-permute-done.28.side_ref
  107.3 0.0 collective-permute-done.27.refs_4_
  107.4 2.2 %collective-permute-done.20.near_ref = bf16[2,128,1536]{2,1,0:T(8,128)(2,1)} collective-permute-done((bf16[2,128,1536]{2,1,0:T(8,128)(2,1)}, bf16[2,128,1536]{2,1,0:T(8,128)(2,1)}, u32[]{:S(2)}, u32[]{:S(2)}) %collective-permute-start.20) | collective-permute-done | bytes 786464 | tf_op jit(solution)/shard_map/ppermute | solution.py:463
  109.5 1.0 copy-done.6
  110.5 3.4 %finish.1 = (bf16[128,3072]{1,0:T(8,128)(2,1)}, bf16[128,3072]{1,0:T(8,128)(2,1)}, bf16[128,3072]{1,0:T(8,128)(2,1)}, bf16[128,3072]{1,0:T(8,128)(2,1)}, f32[128,3072]{1,0:T(8,128)}) custom-call(s32[1]{0:T(128)} %bitcast.place_ref, s32[1,96]{1,0:T(1,128)S(1)} %reshape_tile.3.noise_ref, ...), custom_call_target="tpu_custom_call", output_to_operand_aliasing={{0}: (10, {}), {1}: (11, {})} | custom-call | flops 1 | bytes 1 | tf_op jit(solution)/shard_map/finish/pallas_call | solution.py:514
  (19 shorter events, 0.1 us)
Async XLA Ops:
  0.6 7.8 %copy-start.2 = (bf16[128,3072]{1,0:T(8,128)(2,1)S(1)}, bf16[128,3072]{1,0:T(8,128)(2,1)}, u32[]{:S(2)}) copy-start(bf16[128,3072]{1,0:T(8,128)(2,1)} %first_ref.2) | copy-start | bytes 2359300
  0.6 7.8 %copy-start.3 = (bf16[128,3072]{1,0:T(8,128)(2,1)S(1)}, bf16[128,3072]{1,0:T(8,128)(2,1)}, u32[]{:S(2)}) copy-start(bf16[128,3072]{1,0:T(8,128)(2,1)} %second_ref.2) | copy-start | bytes 2359300
  0.7 25.1 %copy-start.1 = (f32[128,3072]{1,0:T(8,128)S(1)}, f32[128,3072]{1,0:T(8,128)}, u32[]{:S(2)}) copy-start(f32[128,3072]{1,0:T(8,128)} %table_ref.1) | copy-start | bytes 4718596
  0.7 25.1 %copy-start.7 = (s32[4096]{0:T(1024)S(1)}, s32[4096]{0:T(1024)}, u32[]{:S(2)}) copy-start(s32[4096]{0:T(1024)} %param.15) | copy-start | bytes 49156
  0.7 25.1 %copy-start.8 = (s32[24,24]{1,0:T(8,128)S(1)}, s32[24,24]{1,0:T(8,128)}, u32[]{:S(2)}) copy-start(s32[24,24]{1,0:T(8,128)} %mask_ref.1) | copy-start | bytes 6916
  0.7 25.1 %copy-start.9 = (s32[24]{0:T(128)S(1)}, s32[24]{0:T(128)}, u32[]{:S(2)}) copy-start(s32[24]{0:T(128)} %param.16) | copy-start | bytes 292
  3.5 13.2 %collective-permute-start.14 = (bf16[2,128,768]{2,1,0:T(8,128)(2,1)}, bf16[2,128,768]{2,1,0:T(8,128)(2,1)S(1)}, u32[]{:S(2)}, u32[]{:S(2)}) collective-permute-start(bf16[2,128,768]{2,1,0:T(8,128)(2,1)} %get-tuple-element.70), channel_id=1, source_target_pairs={{0,1},{1,0},{2,3},{3,2},{4,5},{5,4},{6,7},{7,6},{8,9},{9,8},{10,11... | collective-permute-start | bytes 1179656 | tf_op jit(solution)/shard_map/ppermute | solution.py:339
  6.5 27.9 %collective-permute-start.10 = (bf16[2,128,1536]{2,1,0:T(8,128)(2,1)}, bf16[2,128,1536]{2,1,0:T(8,128)(2,1)S(1)}, u32[]{:S(2)}, u32[]{:S(2)}) collective-permute-start(bf16[2,128,1536]{2,1,0:T(8,128)(2,1)} %get-tuple-element.62.kv_own_ref), channel_id=1, source_target_pairs={{0,2},{2,0},{4,6},{6,4},{8,10},{10,8},{12,14},{14,12},{16,18},{18,... | collective-permute-start | bytes 2359304 | tf_op jit(solution)/shard_map/ppermute | solution.py:353
  6.5 27.9 %collective-permute-start.12 = (bf16[2,128,1536]{2,1,0:T(8,128)(2,1)}, bf16[2,128,1536]{2,1,0:T(8,128)(2,1)S(1)}, u32[]{:S(2)}, u32[]{:S(2)}) collective-permute-start(bf16[2,128,1536]{2,1,0:T(8,128)(2,1)} %get-tuple-element.62.kv_own_ref), channel_id=1, source_target_pairs={{0,0},{2,4},{4,2},{6,8},{8,6},{10,12},{12,10},{14,16},{16,14},{18,... | collective-permute-start | bytes 2359304 | tf_op jit(solution)/shard_map/ppermute | solution.py:352
  8.3 26.9 %copy-start = (bf16[2,128,1536]{2,1,0:T(8,128)(2,1)S(1)}, bf16[2,128,1536]{2,1,0:T(8,128)(2,1)}, u32[]{:S(2)}) copy-start(bf16[2,128,1536]{2,1,0:T(8,128)(2,1)} %get-tuple-element.62.kv_own_ref) | copy-start | bytes 2359300
  8.3 16.8 %collective-permute-start.8 = (bf16[2,128,768]{2,1,0:T(8,128)(2,1)}, bf16[2,128,768]{2,1,0:T(8,128)(2,1)S(1)}, u32[]{:S(2)}, u32[]{:S(2)}) collective-permute-start(bf16[2,128,768]{2,1,0:T(8,128)(2,1)} %get-tuple-element.64), channel_id=1, source_target_pairs={{0,1},{1,0},{2,3},{3,2},{4,5},{5,4},{6,7},{7,6},{8,9},{9,8},{10,11... | collective-permute-start | bytes 1179656 | tf_op jit(solution)/shard_map/ppermute | solution.py:339
  16.7 16.0 %collective-permute-start.15 = (bf16[2,128,768]{2,1,0:T(8,128)(2,1)S(1)}, bf16[2,128,768]{2,1,0:T(8,128)(2,1)S(1)}, u32[]{:S(2)}, u32[]{:S(2)}) collective-permute-start(bf16[2,128,768]{2,1,0:T(8,128)(2,1)S(1)} %get-tuple-element.71), channel_id=1, source_target_pairs={{0,1},{1,0},{2,3},{3,2},{4,5},{5,4},{6,7},{7,6},{8,9},{9,8},{10,11... | collective-permute-start | bytes 1179656 | tf_op jit(solution)/shard_map/ppermute | solution.py:339
  18.8 16.4 %collective-permute-start.16 = (bf16[2,128,768]{2,1,0:T(8,128)(2,1)S(1)}, bf16[2,128,768]{2,1,0:T(8,128)(2,1)S(1)}, u32[]{:S(2)}, u32[]{:S(2)}) collective-permute-start(bf16[2,128,768]{2,1,0:T(8,128)(2,1)S(1)} %collective-permute-done.14.kv_ref), channel_id=1, source_target_pairs={{0,2},{2,0},{4,6},{6,4},{8,10},{10,8},{12,14},{14,12},{16,18},{18,... | collective-permute-start | bytes 1179656 | tf_op jit(solution)/shard_map/ppermute | solution.py:356
  25.1 10.1 %collective-permute-start.17 = (bf16[2,128,768]{2,1,0:T(8,128)(2,1)S(1)}, bf16[2,128,768]{2,1,0:T(8,128)(2,1)S(1)}, u32[]{:S(2)}, u32[]{:S(2)}) collective-permute-start(bf16[2,128,768]{2,1,0:T(8,128)(2,1)S(1)} %collective-permute-done.14.kv_ref), channel_id=1, source_target_pairs={{0,0},{2,4},{4,2},{6,8},{8,6},{10,12},{12,10},{14,16},{16,14},{18,... | collective-permute-start | bytes 1179656 | tf_op jit(solution)/shard_map/ppermute | solution.py:355
  32.7 11.1 %collective-permute-start.9 = (bf16[2,128,768]{2,1,0:T(8,128)(2,1)S(1)}, bf16[2,128,768]{2,1,0:T(8,128)(2,1)S(1)}, u32[]{:S(2)}, u32[]{:S(2)}) collective-permute-start(bf16[2,128,768]{2,1,0:T(8,128)(2,1)S(1)} %get-tuple-element.65), channel_id=1, source_target_pairs={{0,1},{1,0},{2,3},{3,2},{4,5},{5,4},{6,7},{7,6},{8,9},{9,8},{10,11... | collective-permute-start | bytes 1179656 | tf_op jit(solution)/shard_map/ppermute | solution.py:339
  34.5 9.3 %collective-permute-start.11 = (bf16[2,128,768]{2,1,0:T(8,128)(2,1)S(1)}, bf16[2,128,768]{2,1,0:T(8,128)(2,1)S(1)}, u32[]{:S(2)}, u32[]{:S(2)}) collective-permute-start(bf16[2,128,768]{2,1,0:T(8,128)(2,1)S(1)} %collective-permute-done.8.kv_ref), channel_id=1, source_target_pairs={{0,2},{2,0},{4,6},{6,4},{8,10},{10,8},{12,14},{14,12},{16,18},{18,... | collective-permute-start | bytes 1179656 | tf_op jit(solution)/shard_map/ppermute | solution.py:356
  34.5 9.3 %collective-permute-start.13 = (bf16[2,128,768]{2,1,0:T(8,128)(2,1)S(1)}, bf16[2,128,768]{2,1,0:T(8,128)(2,1)S(1)}, u32[]{:S(2)}, u32[]{:S(2)}) collective-permute-start(bf16[2,128,768]{2,1,0:T(8,128)(2,1)S(1)} %collective-permute-done.8.kv_ref), channel_id=1, source_target_pairs={{0,0},{2,4},{4,2},{6,8},{8,6},{10,12},{12,10},{14,16},{16,14},{18,... | collective-permute-start | bytes 1179656 | tf_op jit(solution)/shard_map/ppermute | solution.py:355
  42.8 10.0 %collective-permute-start.18 = (bf16[2,128,768]{2,1,0:T(8,128)(2,1)S(1)}, bf16[2,128,768]{2,1,0:T(8,128)(2,1)S(1)}, u32[]{:S(2)}, u32[]{:S(2)}) collective-permute-start(bf16[2,128,768]{2,1,0:T(8,128)(2,1)S(1)} %get-tuple-element.90), channel_id=1, source_target_pairs={{0,1},{1,0},{2,3},{3,2},{4,5},{5,4},{6,7},{7,6},{8,9},{9,8},{10,11... | collective-permute-start | bytes 1179656 | tf_op jit(solution)/shard_map/ppermute | solution.py:347
  43.1 9.8 %collective-permute-start.19 = (bf16[2,128,768]{2,1,0:T(8,128)(2,1)S(1)}, bf16[2,128,768]{2,1,0:T(8,128)(2,1)S(1)}, u32[]{:S(2)}, u32[]{:S(2)}) collective-permute-start(bf16[2,128,768]{2,1,0:T(8,128)(2,1)S(1)} %get-tuple-element.91), channel_id=1, source_target_pairs={{0,0},{2,4},{4,2},{6,8},{8,6},{10,12},{12,10},{14,16},{16,14},{18,... | collective-permute-start | bytes 1179656 | tf_op jit(solution)/shard_map/ppermute | solution.py:458
  51.5 32.1 %copy-start.4 = (bf16[2,128,1536]{2,1,0:T(8,128)(2,1)}, bf16[2,128,1536]{2,1,0:T(8,128)(2,1)S(1)}, u32[]{:S(2)}) copy-start(bf16[2,128,1536]{2,1,0:T(8,128)(2,1)S(1)} %get-tuple-element.93) | copy-start | bytes 2359300
  52.9 29.5 %collective-permute-start.24 = (bf16[2,128,1536]{2,1,0:T(8,128)(2,1)S(1)}, bf16[2,128,1536]{2,1,0:T(8,128)(2,1)S(1)}, u32[]{:S(2)}, u32[]{:S(2)}) collective-permute-start(bf16[2,128,1536]{2,1,0:T(8,128)(2,1)S(1)} %get-tuple-element.96), channel_id=1, source_target_pairs={{0,2},{2,0},{4,6},{6,4},{8,10},{10,8},{12,14},{14,12},{16,18},{18,... | collective-permute-start | bytes 2359304 | tf_op jit(solution)/shard_map/ppermute | solution.py:462
  59.4 3.6 %collective-permute-start.21 = (f32[24,1536]{1,0:T(8,128)S(1)}, f32[24,1536]{1,0:T(8,128)S(1)}, u32[]{:S(2)}, u32[]{:S(2)}) collective-permute-start(f32[24,1536]{1,0:T(8,128)S(1)} %get-tuple-element.94), channel_id=1, source_target_pairs={{0,2},{2,0},{4,6},{6,4},{8,10},{10,8},{12,14},{14,12},{16,18},{18,... | collective-permute-start | bytes 442376 | tf_op jit(solution)/shard_map/ppermute | solution.py:467
  59.4 7.5 %collective-permute-start.22 = (f32[24,1536]{1,0:T(8,128)S(1)}, f32[24,1536]{1,0:T(8,128)S(1)}, u32[]{:S(2)}, u32[]{:S(2)}) collective-permute-start(f32[24,1536]{1,0:T(8,128)S(1)} %get-tuple-element.94), channel_id=1, source_target_pairs={{0,4},{2,6},{4,0},{6,2},{8,12},{10,14},{12,8},{14,10},{16,20},{18,... | collective-permute-start | bytes 442376 | tf_op jit(solution)/shard_map/ppermute | solution.py:467
  62.3 20.0 %collective-permute-start.23 = (f32[24,1536]{1,0:T(8,128)S(1)}, f32[24,1536]{1,0:T(8,128)S(1)}, u32[]{:S(2)}, u32[]{:S(2)}) collective-permute-start(f32[24,1536]{1,0:T(8,128)S(1)} %get-tuple-element.94), channel_id=1, source_target_pairs={{0,6},{2,4},{4,2},{6,0},{8,14},{10,12},{12,10},{14,8},{16,22},{18,... | collective-permute-start | bytes 442376 | tf_op jit(solution)/shard_map/ppermute | solution.py:467
  62.4 20.0 %collective-permute-start.25 = (bf16[2,128,768]{2,1,0:T(8,128)(2,1)S(1)}, bf16[2,128,768]{2,1,0:T(8,128)(2,1)S(1)}, u32[]{:S(2)}, u32[]{:S(2)}) collective-permute-start(bf16[2,128,768]{2,1,0:T(8,128)(2,1)S(1)} %get-tuple-element.98), channel_id=1, source_target_pairs={{0,0},{2,4},{4,2},{6,8},{8,6},{10,12},{12,10},{14,16},{16,14},{18,... | collective-permute-start | bytes 1179656 | tf_op jit(solution)/shard_map/ppermute | solution.py:458
  63.1 19.3 %collective-permute-start.26 = (bf16[2,128,768]{2,1,0:T(8,128)(2,1)S(1)}, bf16[2,128,768]{2,1,0:T(8,128)(2,1)S(1)}, u32[]{:S(2)}, u32[]{:S(2)}) collective-permute-start(bf16[2,128,768]{2,1,0:T(8,128)(2,1)S(1)} %get-tuple-element.100), channel_id=1, source_target_pairs={{0,1},{1,0},{2,3},{3,2},{4,5},{5,4},{6,7},{7,6},{8,9},{9,8},{10,11... | collective-permute-start | bytes 1179656 | tf_op jit(solution)/shard_map/ppermute | solution.py:347
  67.0 40.4 %collective-permute-start.28 = (bf16[2,128,1536]{2,1,0:T(8,128)(2,1)}, bf16[2,128,1536]{2,1,0:T(8,128)(2,1)S(1)}, u32[]{:S(2)}, u32[]{:S(2)}) collective-permute-start(bf16[2,128,1536]{2,1,0:T(8,128)(2,1)} %get-tuple-element.106), channel_id=1, source_target_pairs={{0,0},{2,4},{4,2},{6,8},{8,6},{10,12},{12,10},{14,16},{16,14},{18,... | collective-permute-start | bytes 2359304 | tf_op jit(solution)/shard_map/ppermute | solution.py:464
  82.4 1.1 copy-start.5
  83.5 23.8 %collective-permute-start.27 = (bf16[2,128,1536]{2,1,0:T(8,128)(2,1)}, bf16[2,128,1536]{2,1,0:T(8,128)(2,1)S(1)}, u32[]{:S(2)}, u32[]{:S(2)}) collective-permute-start(bf16[2,128,1536]{2,1,0:T(8,128)(2,1)} %far_sum.1), channel_id=1, source_target_pairs={{0,1},{1,0},{2,3},{3,2},{4,5},{5,4},{6,7},{7,6},{8,9},{9,8},{10,11... | collective-permute-start | bytes 2359304 | tf_op jit(solution)/shard_map/ppermute | solution.py:347
  85.1 5.1 %collective-permute-start.4 = (f32[24,1536]{1,0:T(8,128)S(1)}, f32[24,1536]{1,0:T(8,128)S(1)}, u32[]{:S(2)}, u32[]{:S(2)}) collective-permute-start(f32[24,1536]{1,0:T(8,128)S(1)} %param.1), channel_id=1, source_target_pairs={{0,8},{2,10},{4,12},{6,14},{8,0},{10,2},{12,4},{14,6},{16,24},{18,... | collective-permute-start | bytes 442376 | tf_op jit(solution)/shard_map/cond/branch_1_fun/ppermute | solution.py:467
  86.6 8.2 %collective-permute-start.5 = (f32[24,1536]{1,0:T(8,128)S(1)}, f32[24,1536]{1,0:T(8,128)S(1)}, u32[]{:S(2)}, u32[]{:S(2)}) collective-permute-start(f32[24,1536]{1,0:T(8,128)S(1)} %param.1), channel_id=1, source_target_pairs={{0,16},{2,18},{4,20},{6,22},{8,24},{10,26},{12,28},{14,30},{16,0},... | collective-permute-start | bytes 442376 | tf_op jit(solution)/shard_map/cond/branch_1_fun/ppermute | solution.py:467
  88.6 9.0 %collective-permute-start.6 = (f32[24,1536]{1,0:T(8,128)S(1)}, f32[24,1536]{1,0:T(8,128)S(1)}, u32[]{:S(2)}, u32[]{:S(2)}) collective-permute-start(f32[24,1536]{1,0:T(8,128)S(1)} %param.1), channel_id=1, source_target_pairs={{0,24},{2,26},{4,28},{6,30},{8,16},{10,18},{12,20},{14,22},{16,8},... | collective-permute-start | bytes 442376 | tf_op jit(solution)/shard_map/cond/branch_1_fun/ppermute | solution.py:467
  98.3 7.1 %collective-permute-start.7 = (f32[24,1536]{1,0:T(8,128)}, f32[24,1536]{1,0:T(8,128)}, u32[]{:S(2)}, u32[]{:S(2)}) collective-permute-start(f32[24,1536]{1,0:T(8,128)} %add_add_fusion.1), channel_id=1, source_target_pairs={{0,1},{1,0},{2,3},{3,2},{4,5},{5,4},{6,7},{7,6},{8,9},{9,8},{10,11... | collective-permute-start | bytes 442376 | tf_op jit(solution)/shard_map/cond/branch_1_fun/ppermute | solution.py:496
  105.4 4.1 %collective-permute-start.20 = (bf16[2,128,1536]{2,1,0:T(8,128)(2,1)}, bf16[2,128,1536]{2,1,0:T(8,128)(2,1)}, u32[]{:S(2)}, u32[]{:S(2)}) collective-permute-start(bf16[2,128,1536]{2,1,0:T(8,128)(2,1)} %copy-done.4), channel_id=1, source_target_pairs={{0,2},{2,0},{4,6},{6,4},{8,10},{10,8},{12,14},{14,12},{16,18},{18,... | collective-permute-start | bytes 2359304 | tf_op jit(solution)/shard_map/ppermute | solution.py:463
  109.5 1.0 copy-start.6

commit v6 on v5

--- a/solution.py
+++ b/solution.py
@@ -98,8 +98,8 @@
 ):
     (
         back_ref, side_grad_far_ref, mixed_ref, dq_ref, own_ref, far_ref,
-        near_grad_own_ref, near_grad_far_ref, side_grad_own_ref, sums_ref,
-    ) = rest[-10:]
+        near_grad_ref, side_grad_own_ref, sums_ref,
+    ) = rest[-9:]
     scale = 1.0 / math.sqrt(DH)
     bf16, f32 = jnp.bfloat16, jnp.float32
     tile = 32
@@ -181,13 +181,12 @@
             key_grad = dk if key_grad is None else key_grad + dk
             value_grad = dv if value_grad is None else value_grad + dv
             sums = part if sums is None else sums + part
-        sums_ref[:, at] = sums
+        sums_ref[:, at] = sums.astype(bf16)
         for i, grad in ((0, key_grad * scale), (1, value_grad)):
             own_ref[i, :, at] = grad[:rows]
             far_ref[i, :, at] = grad[rows:tokens]
             low = grad[tokens:].astype(bf16)
-            near_grad_own_ref[i, :, at] = low[:rows]
-            near_grad_far_ref[i, :, at] = low[rows:tokens]
+            near_grad_ref[i, :, at] = low[:tokens]
             side_grad_own_ref[i, :, at] = low[tokens : tokens + rows]
             side_grad_far_ref[i, :, at] = low[tokens + rows :]
 
@@ -223,10 +222,11 @@
 
 def far_sum_kernel(part_ref, near_ref, *refs):
     *side_refs, out_ref = refs
+    far = slice(near_ref.shape[1] - part_ref.shape[1], None)
     for p, ref in enumerate(side_refs):
         width = ref.shape[2]
         cols = slice(p * width, (p + 1) * width)
-        total = part_ref[:, :, cols] + near_ref[:, :, cols].astype(jnp.float32)
+        total = part_ref[:, :, cols] + near_ref[:, far, cols].astype(jnp.float32)
         out_ref[:, :, cols] = (total + ref[...].astype(jnp.float32)).astype(out_ref.dtype)
 
 
@@ -234,7 +234,7 @@
     count = (groups - 1) * (parts + 1)
     slot_refs, refs = refs[:groups], refs[groups:]
     slabs, outs = refs[:count], refs[count + 2 : count + 7]
-    total_ref, pieces_ref, gate_ref, sems = refs[count + 7 :]
+    total_ref, gate_ref, sems = refs[count + 7 :]
     width = part_ref.shape[2]
     copies = []
 
@@ -250,22 +250,18 @@
             slab = slabs[p * (groups - 1) + k - 1]
             copy(slab, outs[0], outs[1], start + p * slab.shape[2])
         copy(slabs[parts * (groups - 1) + k - 1], outs[2], outs[3], start)
-    total = part_ref[...] + near_ref[...].astype(jnp.float32) + side_ref[...].astype(jnp.float32)
+    near = near_ref[:, : part_ref.shape[1]].astype(jnp.float32)
+    total = part_ref[...] + near + side_ref[...].astype(jnp.float32)
     total_ref[...] = total.astype(total_ref.dtype)
     copy(total_ref, outs[2], outs[3], lax.rem(place_ref[0], groups) * width)
-    slots = pieces_ref.shape[0] // 3
     levels = lax.broadcasted_iota(jnp.int32, (gate_ref.shape[0], noise_ref.shape[1]), 0)
     onehot = (levels == noise_ref[...]).astype(jnp.bfloat16)
-    if by_span:
-        pieces_ref[...] = jnp.zeros_like(pieces_ref)
     for j, ref in enumerate(slot_refs):
         sums = ref[...]
         if by_span:
-            for n in range(3):
-                piece = sums.astype(jnp.bfloat16)
-                sums = sums - piece.astype(jnp.float32)
-                pieces_ref[n * slots : n * slots + sums.shape[0]] = piece
-            sums = jnp.dot(onehot, pieces_ref[...], preferred_element_type=jnp.float32)
+            sums = jnp.dot(onehot, sums, preferred_element_type=jnp.float32)
+        else:
+            sums = sums.astype(jnp.float32)
         start = lax.bitwise_xor(lax.rem(place_ref[0], groups), j) * width
         cols = pl.ds(pl.multiple_of(start, DH), width)
         gate_ref[:, cols] = sums
@@ -427,7 +423,7 @@
                 out_specs=[
                     pair(far_rows), pair(far_rows),
                     at_head, at_head, at_part(rows), at_part(far_rows),
-                    at_part(rows), at_part(far_rows), at_part(rows), column(slots),
+                    at_part(tokens), at_part(rows), column(slots),
                 ],
             ),
             out_shape=[
@@ -437,10 +433,9 @@
                 struct((rows, full_width), bf16),
                 struct((2, rows, width), f32),
                 struct((2, far_rows, width), f32),
+                struct((2, tokens, width), bf16),
                 struct((2, rows, width), bf16),
-                struct((2, far_rows, width), bf16),
-                struct((2, rows, width), bf16),
-                struct((slots, width), f32),
+                struct((slots, width), bf16),
             ],
             input_output_aliases={1 + len(inputs) + i: 2 + i for i in range(len(joint))},
             compiler_params=params,
@@ -457,11 +452,9 @@
             )
         side_back_far.append(lax.ppermute(side_grad_far, "ctx", side_pairs))
         back_far.append(from_peers(back))
-    mixed, query_grad, own, far, near_grad_own, near_grad_far, side_grad_own, sums = joint
-
-    near_back_far = lax.ppermute(near_grad_far, "ctx", near_pairs)
-    near_back_own = lax.ppermute(near_grad_own, "ctx", near_pairs)
-    side_back_own = lax.ppermute(side_grad_own, "ctx", side_pairs)
+    mixed, query_grad, own, far, near_grad, side_grad_own, sums = joint
+
+    near_back = lax.ppermute(near_grad, "ctx", near_pairs)
 
     def shifted(array, step):
         return lax.ppermute(array, "ctx", [(i, i ^ step) for i in range(ctx_count)])
@@ -477,7 +470,10 @@
 
     bits = [1 << n for n in range(ctx_count.bit_length() - 1)]
     side_back_far, back_far = tie((side_back_far, back_far))
-    sums = rounds(bits[:2], sums)
+    side_grad_own, _ = tie((side_grad_own, side_back_far))
+    side_back_own = lax.ppermute(side_grad_own, "ctx", side_pairs)
+    sums = rounds(bits[:1], rounds(bits[2:], sums))
+    side_back_far, sums = tie((side_back_far, sums))
     far_grad = pl.pallas_call(
         far_sum_kernel,
         in_specs=[in_vmem] * (2 + parts),
@@ -486,30 +482,27 @@
         compiler_params=small,
         cost_estimate=cheap,
         name="far_sum",
-    )(far, near_back_far, *side_back_far)
+    )(far, near_back, *side_back_far)
     grad_far = from_peers(far_grad)
 
-    def to_all(steps, sums):
-        slabs = [rounds(steps, sums)]
+    def to_all(before, after, sums):
+        slabs = [rounds(before, sums)]
         for step in (1 << n for n in range(groups.bit_length() - 1)):
             pairs = [(i, i ^ step) for i in range(groups)]
             slabs = slabs + [lax.ppermute(slab, "head", pairs) for slab in slabs]
-        return slabs
-
-    rest = bits[2:]
+        return [rounds(after, slab) for slab in slabs]
+
     sums, _ = tie((sums, far_grad))
     slabs = lax.cond(
         noise_level[0] >= 0,
-        functools.partial(to_all, rest),
-        functools.partial(to_all, rest[::-1]),
+        functools.partial(to_all, bits[1:2], []),
+        functools.partial(to_all, [], bits[1:2]),
         sums,
     )
     slabs, grad_far, side_back_own = tie((slabs, grad_far, side_back_own))
     arrived = [slab for slabs in back_far for slab in slabs] + grad_far
-    padded = -(-slots // 16) * 16
-    noise_row = jnp.pad(noise_level, (0, padded - slots), constant_values=-1) if by_span else noise_level
-    noise_row = jnp.tile(noise_row, 3 if by_span else 1).reshape(1, -1)
-    operands = (noise_row, own, near_back_own, side_back_own, *slabs, *arrived)
+    noise_row = noise_level.reshape(1, span_total)
+    operands = (noise_row, own, near_back, side_back_own, *slabs, *arrived)
     return tuple(
         pl.pallas_call(
             functools.partial(finish_kernel, groups=groups, parts=parts, by_span=by_span),
@@ -519,7 +512,6 @@
                 out_specs=[anywhere] * 5,
                 scratch_shapes=[
                     pltpu.VMEM((2, rows, width), bf16),
-                    pltpu.VMEM((3 * padded, width), bf16),
                     pltpu.VMEM((level_count, full_width), f32),
                     pltpu.SemaphoreType.DMA((2 * len(arrived) + 2 + groups,)),
                 ],

time: 116 us -> 113 us (0.974)
  waiting for transfers between devices: 53.7 us -> 47.4 us
  starting transfers between devices: 32.7 us -> 35.8 us
    ppermute x6 -> x5, waiting for transfers between devices: 24.1 us -> 13.9 us  [shifted(): return lax.ppermute(array, 'ctx', [(i, i ^ step) for i in range(ctx_count)])]
    ppermute x1, starting transfers between devices: 1.78 us -> 7.42 us  [per_device(): side_back_own = lax.ppermute(side_grad_own, 'ctx', side_pairs)]
    ppermute x3, waiting for transfers between devices: 1.4 us -> 5 us  [from_peers(): arrived.append(lax.ppermute(part, 'head', pairs))]
    ppermute x2, starting transfers between devices: 0.01 us -> 2.9 us  [per_device(): near_far = [lax.ppermute(slab, 'ctx', near_pairs) for slab in kv_far]]
    ppermute x3, starting transfers between devices: 3.39 us -> 0.58 us  [from_peers(): arrived.append(lax.ppermute(part, 'head', pairs))]
    ppermute x6 -> x5, starting transfers between devices: 7.26 us -> 4.53 us  [shifted(): return lax.ppermute(array, 'ctx', [(i, i ^ step) for i in range(ctx_count)])]
    ppermute x1, waiting for transfers between devices: 6.64 us -> 9.09 us  [to_all(): slabs = slabs + [lax.ppermute(slab, 'head', pairs) for slab in slabs]]
    ppermute x2 -> x1, waiting for transfers between devices: 2.16 us -> 0.01 us  [per_device(): near_back = lax.ppermute(near_grad, 'ctx', near_pairs)]
  transfers between devices with their start and end apart: 25 -> 23, of which waited for: 11 -> 8; matrix products, arithmetic and copies ran while one was open for 1% -> 1% of each run, Pallas kernels for 16% -> 17%
where the time goes in v6:
time: 113 us; the launch traced here: 111 us
  waiting for transfers between devices  47.4 us (42%)
  starting transfers between devices  35.8 us (32%)
  Pallas kernels  25.2 us (22%)
    ppermute x4, waiting for transfers between devices, to_peers(): arrived.append(lax.ppermute(part, 'head', pairs))  19.4 us
    pallas_call x2, Pallas kernels, attention(): pl.pallas_call(functools.partial(attention_kernel, rows=rows, tokens=toke...  15.5 us
    ppermute x5, waiting for transfers between devices, shifted(): return lax.ppermute(array, 'ctx', [(i, i ^ step) for i in range(ctx_count)])  13.9 us
    ppermute x1, waiting for transfers between devices, to_all(): slabs = slabs + [lax.ppermute(slab, 'head', pairs) for slab in slabs]  9.09 us
    ppermute x1, starting transfers between devices, per_device(): near_back = lax.ppermute(near_grad, 'ctx', near_pairs)  8.97 us
    ppermute x1, starting transfers between devices, per_device(): side_back_own = lax.ppermute(side_grad_own, 'ctx', side_pairs)  7.42 us
    ppermute x4, starting transfers between devices, to_peers(): arrived.append(lax.ppermute(part, 'head', pairs))  6.93 us
    ppermute x3, waiting for transfers between devices, from_peers(): arrived.append(lax.ppermute(part, 'head', pairs))  5 us
  transfers between devices with their start and end apart: 23, of which 8 were waited for; matrix products, arithmetic and copies ran while one was open for 1% of the time, Pallas kernels for 17%

profile of v6, /device:TPU:0, one launch (start us, length us, event | category | flops | bytes accessed | tf_op | source)
XLA Modules:
  0.0 111.0 jit_solution(14293332979249643420)
XLA Ops:
  0.6 0.0 copy-start.2
  0.6 0.0 copy-start.3
  0.7 0.0 copy-start.1
  0.7 0.0 copy-start.6
  0.7 0.0 copy-start.7
  0.7 0.0 copy-start.8
  0.7 2.8 %pack.3 = (bf16[2,128,1536]{2,1,0:T(8,128)(2,1)}, bf16[2,128,768]{2,1,0:T(8,128)(2,1)}, bf16[2,128,768]{2,1,0:T(8,128)(2,1)}) custom-call(s32[1]{0:T(128)} %bitcast.place_ref, bf16[128,3072]{1,0:T(8,128)(2,1)} %first_ref.3, bf16[128,3072]{1,0:T(8,128)(2,1)} %second_ref.3), custom_call_target="tpu_custom_call" | custom-call | flops 1 | bytes 1 | tf_op jit(solution)/shard_map/pack/pallas_call | solution.py:315
  3.5 3.0 %collective-permute-start.11 = (bf16[2,128,768]{2,1,0:T(8,128)(2,1)}, bf16[2,128,768]{2,1,0:T(8,128)(2,1)S(1)}, u32[]{:S(2)}, u32[]{:S(2)}) collective-permute-start(bf16[2,128,768]{2,1,0:T(8,128)(2,1)} %get-tuple-element.71), channel_id=1, source_target_pairs={{0,1},{1,0},{2,3},{3,2},{4,5},{5,4},{6,7},{7,6},{8,9},{9,8},{10,11... | collective-permute-start | bytes 1179656 | tf_op jit(solution)/shard_map/ppermute | solution.py:335
  6.5 0.0 collective-permute-start.7
  6.5 1.8 %collective-permute-start.9 = (bf16[2,128,1536]{2,1,0:T(8,128)(2,1)}, bf16[2,128,1536]{2,1,0:T(8,128)(2,1)S(1)}, u32[]{:S(2)}, u32[]{:S(2)}) collective-permute-start(bf16[2,128,1536]{2,1,0:T(8,128)(2,1)} %get-tuple-element.63.kv_own_ref), channel_id=1, source_target_pairs={{0,0},{2,4},{4,2},{6,8},{8,6},{10,12},{12,10},{14,16},{16,14},{18,... | collective-permute-start | bytes 2359304 | tf_op jit(solution)/shard_map/ppermute | solution.py:348
  8.3 0.1 collective-permute-start.5
  8.4 0.0 copy-done.2
  8.4 0.3 pack.2
  8.7 8.0 %collective-permute-done.11.kv_ref = bf16[2,128,768]{2,1,0:T(8,128)(2,1)S(1)} collective-permute-done((bf16[2,128,768]{2,1,0:T(8,128)(2,1)}, bf16[2,128,768]{2,1,0:T(8,128)(2,1)S(1)}, u32[]{:S(2)}, u32[]{:S(2)}) %collective-permute-start.11) | collective-permute-done | bytes 393248 | tf_op jit(solution)/shard_map/ppermute | solution.py:335
  16.7 2.1 %collective-permute-start.12 = (bf16[2,128,768]{2,1,0:T(8,128)(2,1)S(1)}, bf16[2,128,768]{2,1,0:T(8,128)(2,1)S(1)}, u32[]{:S(2)}, u32[]{:S(2)}) collective-permute-start(bf16[2,128,768]{2,1,0:T(8,128)(2,1)S(1)} %get-tuple-element.72), channel_id=1, source_target_pairs={{0,1},{1,0},{2,3},{3,2},{4,5},{5,4},{6,7},{7,6},{8,9},{9,8},{10,11... | collective-permute-start | bytes 1179656 | tf_op jit(solution)/shard_map/ppermute | solution.py:335
  18.8 0.0 collective-permute-start.13
  18.8 6.4 %collective-permute-done.5.kv_ref = bf16[2,128,768]{2,1,0:T(8,128)(2,1)S(1)} collective-permute-done((bf16[2,128,768]{2,1,0:T(8,128)(2,1)}, bf16[2,128,768]{2,1,0:T(8,128)(2,1)S(1)}, u32[]{:S(2)}, u32[]{:S(2)}) %collective-permute-start.5) | collective-permute-done | bytes 393248 | tf_op jit(solution)/shard_map/ppermute | solution.py:335
  25.1 0.7 collective-permute-start.14
  25.8 1.9 %prep.1 = (f32[768,256]{1,0:T(8,128)S(1)}, f32[256,1536]{1,0:T(8,128)S(1)}, bf16[24,256]{1,0:T(8,128)(2,1)S(1)}) custom-call(s32[1]{0:T(128)} %bitcast.place_ref, s32[32,128]{1,0:T(8,128)S(1)} %bitcast.5, s32[1,24]{1,0:T(1,128)S(1)} %bitcast.6, s32[24,24]{1,0:T(8,128)S(1)} %copy-done.7, f32[128,3072]{1,0:T(8,128)S(1)} %copy-done.1), custom_call_target="tpu_custom_call" | custom-call | flops 1 | bytes 1 | tf_op jit(solution)/shard_map/prep/pallas_call | solution.py:357
  27.7 5.0 %collective-permute-done.12.qo_ref = bf16[2,128,768]{2,1,0:T(8,128)(2,1)S(1)} collective-permute-done((bf16[2,128,768]{2,1,0:T(8,128)(2,1)S(1)}, bf16[2,128,768]{2,1,0:T(8,128)(2,1)S(1)}, u32[]{:S(2)}, u32[]{:S(2)}) %collective-permute-start.12) | collective-permute-done | bytes 393248 | tf_op jit(solution)/shard_map/ppermute | solution.py:335
  32.7 1.7 %collective-permute-start.6 = (bf16[2,128,768]{2,1,0:T(8,128)(2,1)S(1)}, bf16[2,128,768]{2,1,0:T(8,128)(2,1)S(1)}, u32[]{:S(2)}, u32[]{:S(2)}) collective-permute-start(bf16[2,128,768]{2,1,0:T(8,128)(2,1)S(1)} %get-tuple-element.66), channel_id=1, source_target_pairs={{0,1},{1,0},{2,3},{3,2},{4,5},{5,4},{6,7},{7,6},{8,9},{9,8},{10,11... | collective-permute-start | bytes 1179656 | tf_op jit(solution)/shard_map/ppermute | solution.py:335
  34.5 0.0 collective-permute-done.7.near_own_ref
  34.5 0.7 collective-permute-start.10
  35.1 0.0 collective-permute-done.9.side_own_ref
  35.2 2.9 %collective-permute-start.8 = (bf16[2,128,768]{2,1,0:T(8,128)(2,1)S(1)}, bf16[2,128,768]{2,1,0:T(8,128)(2,1)S(1)}, u32[]{:S(2)}, u32[]{:S(2)}) collective-permute-start(bf16[2,128,768]{2,1,0:T(8,128)(2,1)S(1)} %collective-permute-done.5.kv_ref), channel_id=1, source_target_pairs={{0,2},{2,0},{4,6},{6,4},{8,10},{10,8},{12,14},{14,12},{16,18},{18,... | collective-permute-start | bytes 1179656 | tf_op jit(solution)/shard_map/ppermute | solution.py:352
  38.1 0.0 collective-permute-done.13.near_far_ref
  38.1 0.0 collective-permute-done.14.side_far_ref
  38.1 0.0 copy-done
  38.1 7.7 %attention.2 = (bf16[2,128,768]{2,1,0:T(8,128)(2,1)S(1)}, bf16[2,128,768]{2,1,0:T(8,128)(2,1)S(1)}, bf16[128,3072]{1,0:T(8,128)(2,1)}, bf16[128,3072]{1,0:T(8,12...) custom-call(s32[1]{0:T(128)} %bitcast.place_ref, ...), custom_call_target="tpu_custom_call" | custom-call | flops 1 | bytes 1 | tf_op jit(solution)/shard_map/attention/pallas_call | solution.py:410
  45.8 0.5 collective-permute-start.15
  46.3 0.7 collective-permute-start.16
  47.0 0.0 collective-permute-done.6.qo_ref
  47.0 0.0 collective-permute-done.10.side_far_ref
  47.0 0.0 collective-permute-done.8.near_far_ref
  47.0 7.8 %attention.3 = (bf16[2,128,768]{2,1,0:T(8,128)(2,1)S(1)}, bf16[2,128,768]{2,1,0:T(8,128)(2,1)S(1)}, bf16[128,3072]{1,0:T(8,128)(2,1)}, bf16[128,3072]{1,0:T(8,12...) custom-call(s32[1]{0:T(128)} %bitcast.place_ref, ...), custom_call_target="tpu_custom_call", output_to_operand_aliasing={{2}: (12, {}), {3}: (13, {}), {4}: (14, {}), {5}: (15, {}),... | custom-call | flops 1 | bytes 1 | tf_op jit(solution)/shard_map/attention/pallas_call | solution.py:410
  54.8 0.0 collective-permute-done.15.refs_2_
  54.8 0.0 collective-permute-done.16.refs_0_
  54.8 9.0 %collective-permute-start.17 = (bf16[2,256,1536]{2,1,0:T(8,128)(2,1)S(1)}, bf16[2,256,1536]{2,1,0:T(8,128)(2,1)S(1)}, u32[]{:S(2)}, u32[]{:S(2)}) collective-permute-start(bf16[2,256,1536]{2,1,0:T(8,128)(2,1)S(1)} %get-tuple-element.92), channel_id=1, source_target_pairs={{0,2},{2,0},{4,6},{6,4},{8,10},{10,8},{12,14},{14,12},{16,18},{18,... | collective-permute-start | bytes 4718600 | tf_op jit(solution)/shard_map/ppermute | solution.py:457
  63.8 1.6 %collective-permute-start.20 = (bf16[24,1536]{1,0:T(8,128)(2,1)S(1)}, bf16[24,1536]{1,0:T(8,128)(2,1)S(1)}, u32[]{:S(2)}, u32[]{:S(2)}) collective-permute-start(bf16[24,1536]{1,0:T(8,128)(2,1)S(1)} %get-tuple-element.99), channel_id=1, source_target_pairs={{0,8},{2,10},{4,12},{6,14},{8,0},{10,2},{12,4},{14,6},{16,24},{18,... | collective-permute-start | bytes 221192 | tf_op jit(solution)/shard_map/ppermute | solution.py:460
  65.3 1.0 collective-permute-start.21
  66.4 1.8 %collective-permute-start.22 = (bf16[24,1536]{1,0:T(8,128)(2,1)S(1)}, bf16[24,1536]{1,0:T(8,128)(2,1)S(1)}, u32[]{:S(2)}, u32[]{:S(2)}) collective-permute-start(bf16[24,1536]{1,0:T(8,128)(2,1)S(1)} %get-tuple-element.99), channel_id=1, source_target_pairs={{0,24},{2,26},{4,28},{6,30},{8,16},{10,18},{12,20},{14,22},{16,8},... | collective-permute-start | bytes 221192 | tf_op jit(solution)/shard_map/ppermute | solution.py:460
  68.2 0.7 collective-permute-start.18
  68.8 0.0 collective-permute-done.20
  68.8 0.1 collective-permute-start.19
  68.9 5.2 %collective-permute-done.21 = bf16[24,1536]{1,0:T(8,128)(2,1)S(1)} collective-permute-done((bf16[24,1536]{1,0:T(8,128)(2,1)S(1)}, bf16[24,1536]{1,0:T(8,128)(2,1)S(1)}, u32[]{:S(2)}, u32[]{:S(2)}) %collective-permute-start.21) | collective-permute-done | bytes 73760 | tf_op jit(solution)/shard_map/ppermute | solution.py:460
  74.2 0.0 collective-permute-done.22
  74.2 0.1 collective-permute-start.23
  74.3 1.3 %collective-permute-done.23 = bf16[24,1536]{1,0:T(8,128)(2,1)S(1)} collective-permute-done((bf16[24,1536]{1,0:T(8,128)(2,1)S(1)}, bf16[24,1536]{1,0:T(8,128)(2,1)S(1)}, u32[]{:S(2)}, u32[]{:S(2)}) %collective-permute-start.23) | collective-permute-done | bytes 73760 | tf_op jit(solution)/shard_map/ppermute | solution.py:460
  75.6 0.0 collective-permute-done.18.refs_1_
  75.6 5.0 %collective-permute-done.19.refs_3_ = bf16[2,128,768]{2,1,0:T(8,128)(2,1)S(1)} collective-permute-done((bf16[2,128,768]{2,1,0:T(8,128)(2,1)S(1)}, bf16[2,128,768]{2,1,0:T(8,128)(2,1)S(1)}, u32[]{:S(2)}, u32[]{:S(2)}) %collective-permute-start.19) | collective-permute-done | bytes 393248 | tf_op jit(solution)/shard_map/ppermute | solution.py:343
  80.6 7.4 %collective-permute-start.25 = (bf16[2,128,1536]{2,1,0:T(8,128)(2,1)}, bf16[2,128,1536]{2,1,0:T(8,128)(2,1)}, u32[]{:S(2)}, u32[]{:S(2)}) collective-permute-start(bf16[2,128,1536]{2,1,0:T(8,128)(2,1)} %get-tuple-element.108), channel_id=1, source_target_pairs={{0,0},{2,4},{4,2},{6,8},{8,6},{10,12},{12,10},{14,16},{16,14},{18,... | collective-permute-start | bytes 2359304 | tf_op jit(solution)/shard_map/ppermute | solution.py:474
  88.0 0.0 collective-permute-done.17.near_ref
  88.0 1.2 %far_sum.1 = bf16[2,128,1536]{2,1,0:T(8,128)(2,1)} custom-call(f32[2,128,1536]{2,1,0:T(8,128)S(1)} %get-tuple-element.101.part_ref, bf16[2,256,1536]{2,1,0:T(8,128)(2,1)S(1)} %collective-permute-done.17.near_ref, bf16[2,128,768]{2,1,0:T(8,128)(2,1)S(1)} %collective-permute-done.16.refs_0_, bf16[2,128,768]{2,1,0:T(8,128)(2,1)S(1)} %collective-permute-done.18.refs_1_), custom_call_target="tpu_custom_call" | custom-call | flops 1 | bytes 1 | tf_op jit(solution)/shard_map/far_sum/pallas_call | solution.py:477
  89.2 0.0 collective-permute-start.24
  89.2 17.2 %conditional.1 = (bf16[24,1536]{1,0:T(8,128)(2,1)}, bf16[24,1536]{1,0:T(8,128)(2,1)}) conditional(s32[]{:T(128)} %bitcast.3, bf16[24,1536]{1,0:T(8,128)(2,1)S(1)} %add.28, bf16[24,1536]{1,0:T(8,128)(2,1)S(1)} %add.28), branch_computations={%region_0.0_spmd, %region_1.0_spmd} | conditional | flops 73728 | bytes 1327240 | solution.py:496
  89.2 0.1 collective-permute-start.3
  89.3 7.4 %collective-permute-done.3 = bf16[24,1536]{1,0:T(8,128)(2,1)S(1)} collective-permute-done((bf16[24,1536]{1,0:T(8,128)(2,1)S(1)}, bf16[24,1536]{1,0:T(8,128)(2,1)S(1)}, u32[]{:S(2)}, u32[]{:S(2)}) %collective-permute-start.3) | collective-permute-done | bytes 73760 | tf_op jit(solution)/shard_map/cond/branch_1_fun/ppermute | solution.py:460
  96.7 0.6 add.18
  97.3 0.0 collective-permute-start.4
  97.3 9.1 %collective-permute-done.4 = bf16[24,1536]{1,0:T(8,128)(2,1)} collective-permute-done((bf16[24,1536]{1,0:T(8,128)(2,1)}, bf16[24,1536]{1,0:T(8,128)(2,1)}, u32[]{:S(2)}, u32[]{:S(2)}) %collective-permute-start.4) | collective-permute-done | bytes 73760 | tf_op jit(solution)/shard_map/cond/branch_1_fun/ppermute | solution.py:492
  106.4 0.0 collective-permute-done.25.side_ref
  106.4 0.0 collective-permute-done.24.refs_4_
  106.4 1.0 copy-done.5
  107.4 3.6 %finish.1 = (bf16[128,3072]{1,0:T(8,128)(2,1)}, bf16[128,3072]{1,0:T(8,128)(2,1)}, bf16[128,3072]{1,0:T(8,128)(2,1)}, bf16[128,3072]{1,0:T(8,128)(2,1)}, f32[128,3072]{1,0:T(8,128)}) custom-call(s32[1]{0:T(128)} %bitcast.place_ref, s32[1,24]{1,0:T(1,128)S(1)} %bitcast.8, ...), custom_call_target="tpu_custom_call", output_to_operand_aliasing={{0}: (10, {}), {1}: (11, {})} | custom-call | flops 1 | bytes 1 | tf_op jit(solution)/shard_map/finish/pallas_call | solution.py:507
  (11 shorter events, 0.1 us)
Async XLA Ops:
  0.6 7.8 %copy-start.2 = (bf16[128,3072]{1,0:T(8,128)(2,1)S(1)}, bf16[128,3072]{1,0:T(8,128)(2,1)}, u32[]{:S(2)}) copy-start(bf16[128,3072]{1,0:T(8,128)(2,1)} %first_ref.2) | copy-start | bytes 2359300
  0.6 7.8 %copy-start.3 = (bf16[128,3072]{1,0:T(8,128)(2,1)S(1)}, bf16[128,3072]{1,0:T(8,128)(2,1)}, u32[]{:S(2)}) copy-start(bf16[128,3072]{1,0:T(8,128)(2,1)} %second_ref.2) | copy-start | bytes 2359300
  0.7 25.1 %copy-start.1 = (f32[128,3072]{1,0:T(8,128)S(1)}, f32[128,3072]{1,0:T(8,128)}, u32[]{:S(2)}) copy-start(f32[128,3072]{1,0:T(8,128)} %table_ref.1) | copy-start | bytes 4718596
  0.7 25.1 %copy-start.6 = (s32[4096]{0:T(1024)S(1)}, s32[4096]{0:T(1024)}, u32[]{:S(2)}) copy-start(s32[4096]{0:T(1024)} %param.15) | copy-start | bytes 49156
  0.7 25.1 %copy-start.7 = (s32[24,24]{1,0:T(8,128)S(1)}, s32[24,24]{1,0:T(8,128)}, u32[]{:S(2)}) copy-start(s32[24,24]{1,0:T(8,128)} %mask_ref.1) | copy-start | bytes 6916
  0.7 25.1 %copy-start.8 = (s32[24]{0:T(128)S(1)}, s32[24]{0:T(128)}, u32[]{:S(2)}) copy-start(s32[24]{0:T(128)} %param.16) | copy-start | bytes 292
  3.5 13.2 %collective-permute-start.11 = (bf16[2,128,768]{2,1,0:T(8,128)(2,1)}, bf16[2,128,768]{2,1,0:T(8,128)(2,1)S(1)}, u32[]{:S(2)}, u32[]{:S(2)}) collective-permute-start(bf16[2,128,768]{2,1,0:T(8,128)(2,1)} %get-tuple-element.71), channel_id=1, source_target_pairs={{0,1},{1,0},{2,3},{3,2},{4,5},{5,4},{6,7},{7,6},{8,9},{9,8},{10,11... | collective-permute-start | bytes 1179656 | tf_op jit(solution)/shard_map/ppermute | solution.py:335
  6.5 27.9 %collective-permute-start.7 = (bf16[2,128,1536]{2,1,0:T(8,128)(2,1)}, bf16[2,128,1536]{2,1,0:T(8,128)(2,1)S(1)}, u32[]{:S(2)}, u32[]{:S(2)}) collective-permute-start(bf16[2,128,1536]{2,1,0:T(8,128)(2,1)} %get-tuple-element.63.kv_own_ref), channel_id=1, source_target_pairs={{0,2},{2,0},{4,6},{6,4},{8,10},{10,8},{12,14},{14,12},{16,18},{18,... | collective-permute-start | bytes 2359304 | tf_op jit(solution)/shard_map/ppermute | solution.py:349
  6.5 28.6 %collective-permute-start.9 = (bf16[2,128,1536]{2,1,0:T(8,128)(2,1)}, bf16[2,128,1536]{2,1,0:T(8,128)(2,1)S(1)}, u32[]{:S(2)}, u32[]{:S(2)}) collective-permute-start(bf16[2,128,1536]{2,1,0:T(8,128)(2,1)} %get-tuple-element.63.kv_own_ref), channel_id=1, source_target_pairs={{0,0},{2,4},{4,2},{6,8},{8,6},{10,12},{12,10},{14,16},{16,14},{18,... | collective-permute-start | bytes 2359304 | tf_op jit(solution)/shard_map/ppermute | solution.py:348
  8.3 29.7 %copy-start = (bf16[2,128,1536]{2,1,0:T(8,128)(2,1)S(1)}, bf16[2,128,1536]{2,1,0:T(8,128)(2,1)}, u32[]{:S(2)}) copy-start(bf16[2,128,1536]{2,1,0:T(8,128)(2,1)} %get-tuple-element.63.kv_own_ref) | copy-start | bytes 2359300
  8.3 16.8 %collective-permute-start.5 = (bf16[2,128,768]{2,1,0:T(8,128)(2,1)}, bf16[2,128,768]{2,1,0:T(8,128)(2,1)S(1)}, u32[]{:S(2)}, u32[]{:S(2)}) collective-permute-start(bf16[2,128,768]{2,1,0:T(8,128)(2,1)} %get-tuple-element.65), channel_id=1, source_target_pairs={{0,1},{1,0},{2,3},{3,2},{4,5},{5,4},{6,7},{7,6},{8,9},{9,8},{10,11... | collective-permute-start | bytes 1179656 | tf_op jit(solution)/shard_map/ppermute | solution.py:335
  16.7 16.0 %collective-permute-start.12 = (bf16[2,128,768]{2,1,0:T(8,128)(2,1)S(1)}, bf16[2,128,768]{2,1,0:T(8,128)(2,1)S(1)}, u32[]{:S(2)}, u32[]{:S(2)}) collective-permute-start(bf16[2,128,768]{2,1,0:T(8,128)(2,1)S(1)} %get-tuple-element.72), channel_id=1, source_target_pairs={{0,1},{1,0},{2,3},{3,2},{4,5},{5,4},{6,7},{7,6},{8,9},{9,8},{10,11... | collective-permute-start | bytes 1179656 | tf_op jit(solution)/shard_map/ppermute | solution.py:335
  18.8 19.3 %collective-permute-start.13 = (bf16[2,128,768]{2,1,0:T(8,128)(2,1)S(1)}, bf16[2,128,768]{2,1,0:T(8,128)(2,1)S(1)}, u32[]{:S(2)}, u32[]{:S(2)}) collective-permute-start(bf16[2,128,768]{2,1,0:T(8,128)(2,1)S(1)} %collective-permute-done.11.kv_ref), channel_id=1, source_target_pairs={{0,2},{2,0},{4,6},{6,4},{8,10},{10,8},{12,14},{14,12},{16,18},{18,... | collective-permute-start | bytes 1179656 | tf_op jit(solution)/shard_map/ppermute | solution.py:352
  25.1 12.9 %collective-permute-start.14 = (bf16[2,128,768]{2,1,0:T(8,128)(2,1)S(1)}, bf16[2,128,768]{2,1,0:T(8,128)(2,1)S(1)}, u32[]{:S(2)}, u32[]{:S(2)}) collective-permute-start(bf16[2,128,768]{2,1,0:T(8,128)(2,1)S(1)} %collective-permute-done.11.kv_ref), channel_id=1, source_target_pairs={{0,0},{2,4},{4,2},{6,8},{8,6},{10,12},{12,10},{14,16},{16,14},{18,... | collective-permute-start | bytes 1179656 | tf_op jit(solution)/shard_map/ppermute | solution.py:351
  32.7 14.3 %collective-permute-start.6 = (bf16[2,128,768]{2,1,0:T(8,128)(2,1)S(1)}, bf16[2,128,768]{2,1,0:T(8,128)(2,1)S(1)}, u32[]{:S(2)}, u32[]{:S(2)}) collective-permute-start(bf16[2,128,768]{2,1,0:T(8,128)(2,1)S(1)} %get-tuple-element.66), channel_id=1, source_target_pairs={{0,1},{1,0},{2,3},{3,2},{4,5},{5,4},{6,7},{7,6},{8,9},{9,8},{10,11... | collective-permute-start | bytes 1179656 | tf_op jit(solution)/shard_map/ppermute | solution.py:335
  34.5 12.5 %collective-permute-start.10 = (bf16[2,128,768]{2,1,0:T(8,128)(2,1)S(1)}, bf16[2,128,768]{2,1,0:T(8,128)(2,1)S(1)}, u32[]{:S(2)}, u32[]{:S(2)}) collective-permute-start(bf16[2,128,768]{2,1,0:T(8,128)(2,1)S(1)} %collective-permute-done.5.kv_ref), channel_id=1, source_target_pairs={{0,0},{2,4},{4,2},{6,8},{8,6},{10,12},{12,10},{14,16},{16,14},{18,... | collective-permute-start | bytes 1179656 | tf_op jit(solution)/shard_map/ppermute | solution.py:351
  35.2 11.9 %collective-permute-start.8 = (bf16[2,128,768]{2,1,0:T(8,128)(2,1)S(1)}, bf16[2,128,768]{2,1,0:T(8,128)(2,1)S(1)}, u32[]{:S(2)}, u32[]{:S(2)}) collective-permute-start(bf16[2,128,768]{2,1,0:T(8,128)(2,1)S(1)} %collective-permute-done.5.kv_ref), channel_id=1, source_target_pairs={{0,2},{2,0},{4,6},{6,4},{8,10},{10,8},{12,14},{14,12},{16,18},{18,... | collective-permute-start | bytes 1179656 | tf_op jit(solution)/shard_map/ppermute | solution.py:352
  45.8 9.0 %collective-permute-start.15 = (bf16[2,128,768]{2,1,0:T(8,128)(2,1)S(1)}, bf16[2,128,768]{2,1,0:T(8,128)(2,1)S(1)}, u32[]{:S(2)}, u32[]{:S(2)}) collective-permute-start(bf16[2,128,768]{2,1,0:T(8,128)(2,1)S(1)} %get-tuple-element.89), channel_id=1, source_target_pairs={{0,1},{1,0},{2,3},{3,2},{4,5},{5,4},{6,7},{7,6},{8,9},{9,8},{10,11... | collective-permute-start | bytes 1179656 | tf_op jit(solution)/shard_map/ppermute | solution.py:343
  46.3 8.5 %collective-permute-start.16 = (bf16[2,128,768]{2,1,0:T(8,128)(2,1)S(1)}, bf16[2,128,768]{2,1,0:T(8,128)(2,1)S(1)}, u32[]{:S(2)}, u32[]{:S(2)}) collective-permute-start(bf16[2,128,768]{2,1,0:T(8,128)(2,1)S(1)} %get-tuple-element.90), channel_id=1, source_target_pairs={{0,0},{2,4},{4,2},{6,8},{8,6},{10,12},{12,10},{14,16},{16,14},{18,... | collective-permute-start | bytes 1179656 | tf_op jit(solution)/shard_map/ppermute | solution.py:453
  54.8 33.2 %collective-permute-start.17 = (bf16[2,256,1536]{2,1,0:T(8,128)(2,1)S(1)}, bf16[2,256,1536]{2,1,0:T(8,128)(2,1)S(1)}, u32[]{:S(2)}, u32[]{:S(2)}) collective-permute-start(bf16[2,256,1536]{2,1,0:T(8,128)(2,1)S(1)} %get-tuple-element.92), channel_id=1, source_target_pairs={{0,2},{2,0},{4,6},{6,4},{8,10},{10,8},{12,14},{14,12},{16,18},{18,... | collective-permute-start | bytes 4718600 | tf_op jit(solution)/shard_map/ppermute | solution.py:457
  63.8 5.1 %collective-permute-start.20 = (bf16[24,1536]{1,0:T(8,128)(2,1)S(1)}, bf16[24,1536]{1,0:T(8,128)(2,1)S(1)}, u32[]{:S(2)}, u32[]{:S(2)}) collective-permute-start(bf16[24,1536]{1,0:T(8,128)(2,1)S(1)} %get-tuple-element.99), channel_id=1, source_target_pairs={{0,8},{2,10},{4,12},{6,14},{8,0},{10,2},{12,4},{14,6},{16,24},{18,... | collective-permute-start | bytes 221192 | tf_op jit(solution)/shard_map/ppermute | solution.py:460
  65.3 8.8 %collective-permute-start.21 = (bf16[24,1536]{1,0:T(8,128)(2,1)S(1)}, bf16[24,1536]{1,0:T(8,128)(2,1)S(1)}, u32[]{:S(2)}, u32[]{:S(2)}) collective-permute-start(bf16[24,1536]{1,0:T(8,128)(2,1)S(1)} %get-tuple-element.99), channel_id=1, source_target_pairs={{0,16},{2,18},{4,20},{6,22},{8,24},{10,26},{12,28},{14,30},{16,0},... | collective-permute-start | bytes 221192 | tf_op jit(solution)/shard_map/ppermute | solution.py:460
  66.4 7.8 %collective-permute-start.22 = (bf16[24,1536]{1,0:T(8,128)(2,1)S(1)}, bf16[24,1536]{1,0:T(8,128)(2,1)S(1)}, u32[]{:S(2)}, u32[]{:S(2)}) collective-permute-start(bf16[24,1536]{1,0:T(8,128)(2,1)S(1)} %get-tuple-element.99), channel_id=1, source_target_pairs={{0,24},{2,26},{4,28},{6,30},{8,16},{10,18},{12,20},{14,22},{16,8},... | collective-permute-start | bytes 221192 | tf_op jit(solution)/shard_map/ppermute | solution.py:460
  68.2 7.4 %collective-permute-start.18 = (bf16[2,128,768]{2,1,0:T(8,128)(2,1)S(1)}, bf16[2,128,768]{2,1,0:T(8,128)(2,1)S(1)}, u32[]{:S(2)}, u32[]{:S(2)}) collective-permute-start(bf16[2,128,768]{2,1,0:T(8,128)(2,1)S(1)} %get-tuple-element.94), channel_id=1, source_target_pairs={{0,0},{2,4},{4,2},{6,8},{8,6},{10,12},{12,10},{14,16},{16,14},{18,... | collective-permute-start | bytes 1179656 | tf_op jit(solution)/shard_map/ppermute | solution.py:453
  68.8 11.7 %collective-permute-start.19 = (bf16[2,128,768]{2,1,0:T(8,128)(2,1)S(1)}, bf16[2,128,768]{2,1,0:T(8,128)(2,1)S(1)}, u32[]{:S(2)}, u32[]{:S(2)}) collective-permute-start(bf16[2,128,768]{2,1,0:T(8,128)(2,1)S(1)} %get-tuple-element.96), channel_id=1, source_target_pairs={{0,1},{1,0},{2,3},{3,2},{4,5},{5,4},{6,7},{7,6},{8,9},{9,8},{10,11... | collective-permute-start | bytes 1179656 | tf_op jit(solution)/shard_map/ppermute | solution.py:343
  74.2 1.3 %collective-permute-start.23 = (bf16[24,1536]{1,0:T(8,128)(2,1)S(1)}, bf16[24,1536]{1,0:T(8,128)(2,1)S(1)}, u32[]{:S(2)}, u32[]{:S(2)}) collective-permute-start(bf16[24,1536]{1,0:T(8,128)(2,1)S(1)} %add_add_fusion), channel_id=1, source_target_pairs={{0,2},{2,0},{4,6},{6,4},{8,10},{10,8},{12,14},{14,12},{16,18},{18,... | collective-permute-start | bytes 221192 | tf_op jit(solution)/shard_map/ppermute | solution.py:460
  80.6 8.6 %copy-start.4 = (bf16[2,128,768]{2,1,0:T(8,128)(2,1)}, bf16[2,128,768]{2,1,0:T(8,128)(2,1)S(1)}, u32[]{:S(2)}) copy-start(bf16[2,128,768]{2,1,0:T(8,128)(2,1)S(1)} %collective-permute-done.19.refs_3_) | copy-start | bytes 1179652
  80.6 25.9 %collective-permute-start.25 = (bf16[2,128,1536]{2,1,0:T(8,128)(2,1)}, bf16[2,128,1536]{2,1,0:T(8,128)(2,1)}, u32[]{:S(2)}, u32[]{:S(2)}) collective-permute-start(bf16[2,128,1536]{2,1,0:T(8,128)(2,1)} %get-tuple-element.108), channel_id=1, source_target_pairs={{0,0},{2,4},{4,2},{6,8},{8,6},{10,12},{12,10},{14,16},{16,14},{18,... | collective-permute-start | bytes 2359304 | tf_op jit(solution)/shard_map/ppermute | solution.py:474
  89.2 17.3 %collective-permute-start.24 = (bf16[2,128,1536]{2,1,0:T(8,128)(2,1)}, bf16[2,128,1536]{2,1,0:T(8,128)(2,1)}, u32[]{:S(2)}, u32[]{:S(2)}) collective-permute-start(bf16[2,128,1536]{2,1,0:T(8,128)(2,1)} %far_sum.1), channel_id=1, source_target_pairs={{0,1},{1,0},{2,3},{3,2},{4,5},{5,4},{6,7},{7,6},{8,9},{9,8},{10,11... | collective-permute-start | bytes 2359304 | tf_op jit(solution)/shard_map/ppermute | solution.py:343
  89.2 7.4 %collective-permute-start.3 = (bf16[24,1536]{1,0:T(8,128)(2,1)S(1)}, bf16[24,1536]{1,0:T(8,128)(2,1)S(1)}, u32[]{:S(2)}, u32[]{:S(2)}) collective-permute-start(bf16[24,1536]{1,0:T(8,128)(2,1)S(1)} %param.1), channel_id=1, source_target_pairs={{0,4},{2,6},{4,0},{6,2},{8,12},{10,14},{12,8},{14,10},{16,20},{18,... | collective-permute-start | bytes 221192 | tf_op jit(solution)/shard_map/cond/branch_1_fun/ppermute | solution.py:460
  97.3 9.1 %collective-permute-start.4 = (bf16[24,1536]{1,0:T(8,128)(2,1)}, bf16[24,1536]{1,0:T(8,128)(2,1)}, u32[]{:S(2)}, u32[]{:S(2)}) collective-permute-start(bf16[24,1536]{1,0:T(8,128)(2,1)} %add.18), channel_id=1, source_target_pairs={{0,1},{1,0},{2,3},{3,2},{4,5},{5,4},{6,7},{7,6},{8,9},{9,8},{10,11... | collective-permute-start | bytes 221192 | tf_op jit(solution)/shard_map/cond/branch_1_fun/ppermute | solution.py:492
  106.4 1.0 copy-start.5

commit v7 on v6

--- a/solution.py
+++ b/solution.py
@@ -94,12 +94,10 @@
     qo_own_ref, kv_own_ref, qo_ref, kv_ref,
     near_own_ref, near_far_ref, side_own_ref, side_far_ref,
     gate_ref, bias_ref, slot_ref,
-    *rest, rows, tokens, q_size, heads,
+    *rest, rows, tokens, q_size, heads, apart,
 ):
-    (
-        back_ref, side_grad_far_ref, mixed_ref, dq_ref, own_ref, far_ref,
-        near_grad_ref, side_grad_own_ref, sums_ref,
-    ) = rest[-9:]
+    back_ref, own_ref, far_ref, near_grad_ref, *side_grad_refs = rest[-8 - apart : -3]
+    mixed_ref, dq_ref, sums_ref = rest[-3:]
     scale = 1.0 / math.sqrt(DH)
     bf16, f32 = jnp.bfloat16, jnp.float32
     tile = 32
@@ -187,8 +185,11 @@
             far_ref[i, :, at] = grad[rows:tokens]
             low = grad[tokens:].astype(bf16)
             near_grad_ref[i, :, at] = low[:tokens]
-            side_grad_own_ref[i, :, at] = low[tokens : tokens + rows]
-            side_grad_far_ref[i, :, at] = low[tokens + rows :]
+            if apart:
+                side_grad_refs[0][i, :, at] = low[tokens : tokens + rows]
+                side_grad_refs[1][i, :, at] = low[tokens + rows :]
+            else:
+                side_grad_refs[0][i, :, at] = low[tokens:]
 
     ready = load(0)
     for j in range(heads):
@@ -220,55 +221,58 @@
         one.wait()
 
 
-def far_sum_kernel(part_ref, near_ref, *refs):
-    *side_refs, out_ref = refs
+def far_sum_kernel(part_ref, near_ref, side_ref, out_ref):
     far = slice(near_ref.shape[1] - part_ref.shape[1], None)
-    for p, ref in enumerate(side_refs):
-        width = ref.shape[2]
-        cols = slice(p * width, (p + 1) * width)
-        total = part_ref[:, :, cols] + near_ref[:, far, cols].astype(jnp.float32)
-        out_ref[:, :, cols] = (total + ref[...].astype(jnp.float32)).astype(out_ref.dtype)
-
-
-def finish_kernel(place_ref, noise_ref, part_ref, near_ref, side_ref, *refs, groups, parts, by_span):
-    count = (groups - 1) * (parts + 1)
+    total = part_ref[...] + near_ref[:, far].astype(jnp.float32)
+    side = side_ref[:, side_ref.shape[1] - part_ref.shape[1] :].astype(jnp.float32)
+    out_ref[...] = (total + side).astype(out_ref.dtype)
+
+
+def finish_kernel(place_ref, noise_ref, *refs, groups, parts):
+    part_refs, near_refs, side_refs = (refs[n * parts : (n + 1) * parts] for n in range(3))
+    refs = refs[3 * parts :]
     slot_refs, refs = refs[:groups], refs[groups:]
+    count = 2 * (groups - 1) * parts
     slabs, outs = refs[:count], refs[count + 2 : count + 7]
     total_ref, gate_ref, sems = refs[count + 7 :]
-    width = part_ref.shape[2]
+    part_width = part_refs[0].shape[2]
+    width = part_width * parts
     copies = []
 
-    def copy(slab, first, second, start):
-        cols = pl.ds(pl.multiple_of(start, DH), slab.shape[2])
+    def send(source, to):
+        copies.append(pltpu.make_async_copy(source, to, sems.at[len(copies)]))
+        copies[-1].start()
+
+    def place_slab(slab, first, second, k, p):
+        start = lax.rem(place_ref[0] + k, groups) * width + p * part_width
+        cols = pl.ds(pl.multiple_of(start, DH), part_width)
         for i, ref in enumerate((first, second)):
-            copies.append(pltpu.make_async_copy(slab.at[i], ref.at[:, cols], sems.at[len(copies)]))
-            copies[-1].start()
-
-    for k in range(1, groups):
-        start = lax.rem(place_ref[0] + k, groups) * width
+            send(slab.at[i], ref.at[:, cols])
+
+    slabs = iter(slabs)
+    for first, second in (outs[:2], outs[2:4]):
         for p in range(parts):
-            slab = slabs[p * (groups - 1) + k - 1]
-            copy(slab, outs[0], outs[1], start + p * slab.shape[2])
-        copy(slabs[parts * (groups - 1) + k - 1], outs[2], outs[3], start)
-    near = near_ref[:, : part_ref.shape[1]].astype(jnp.float32)
-    total = part_ref[...] + near + side_ref[...].astype(jnp.float32)
-    total_ref[...] = total.astype(total_ref.dtype)
-    copy(total_ref, outs[2], outs[3], lax.rem(place_ref[0], groups) * width)
+            for k in range(1, groups):
+                place_slab(next(slabs), first, second, k, p)
+    for p in range(parts):
+        near, side = (
+            ref[p][:, : total_ref.shape[2]].astype(jnp.float32) for ref in (near_refs, side_refs)
+        )
+        total = part_refs[p][...] + near + side
+        total_ref[p] = total.astype(total_ref.dtype)
+        place_slab(total_ref.at[p], outs[2], outs[3], 0, p)
+    by_span = noise_ref.shape[1] == slot_refs[0].shape[0]
     levels = lax.broadcasted_iota(jnp.int32, (gate_ref.shape[0], noise_ref.shape[1]), 0)
     onehot = (levels == noise_ref[...]).astype(jnp.bfloat16)
     for j, ref in enumerate(slot_refs):
-        sums = ref[...]
         if by_span:
-            sums = jnp.dot(onehot, sums, preferred_element_type=jnp.float32)
+            sums = jnp.dot(onehot, ref[...], preferred_element_type=jnp.float32)
         else:
-            sums = sums.astype(jnp.float32)
+            sums = ref[...].astype(jnp.float32)
         start = lax.bitwise_xor(lax.rem(place_ref[0], groups), j) * width
         cols = pl.ds(pl.multiple_of(start, DH), width)
         gate_ref[:, cols] = sums
-        copies.append(
-            pltpu.make_async_copy(gate_ref.at[:, cols], outs[4].at[:, cols], sems.at[len(copies)])
-        )
-        copies[-1].start()
+        send(gate_ref.at[:, cols], outs[4].at[:, cols])
     for one in copies:
         one.wait()
 
@@ -402,6 +406,7 @@
         )
         column = lambda count: pl.BlockSpec((count, block), lambda i, place: (0, p * steps + i))
         struct = jax.ShapeDtypeStruct
+        side_counts = (rows, far_rows) if p + 1 == parts else (tokens,)
         inputs = [
             qo_own, kv_own, qo_far[p], kv_far[p],
             near_own, near_far[p], side_own, side_far[p],
@@ -409,7 +414,8 @@
         ]
         return pl.pallas_call(
             functools.partial(
-                attention_kernel, rows=rows, tokens=tokens, q_size=q_size, heads=batch
+                attention_kernel,
+                rows=rows, tokens=tokens, q_size=q_size, heads=batch, apart=p + 1 == parts,
             ),
             grid_spec=pltpu.PrefetchScalarGridSpec(
                 num_scalar_prefetch=1,
@@ -421,40 +427,64 @@
                 ]
                 + [pl.BlockSpec(memory_space=pl.ANY)] * len(joint),
                 out_specs=[
-                    pair(far_rows), pair(far_rows),
-                    at_head, at_head, at_part(rows), at_part(far_rows),
-                    at_part(tokens), at_part(rows), column(slots),
+                    pair(far_rows), pair(rows), pair(far_rows), pair(tokens),
+                    *[pair(count) for count in side_counts],
+                    at_head, at_head, column(slots),
                 ],
             ),
             out_shape=[
                 struct((2, far_rows, part_width), bf16),
-                struct((2, far_rows, part_width), bf16),
+                struct((2, rows, part_width), f32),
+                struct((2, far_rows, part_width), f32),
+                struct((2, tokens, part_width), bf16),
+                *[struct((2, count, part_width), bf16) for count in side_counts],
                 struct((rows, full_width), bf16),
                 struct((rows, full_width), bf16),
-                struct((2, rows, width), f32),
-                struct((2, far_rows, width), f32),
-                struct((2, tokens, width), bf16),
-                struct((2, rows, width), bf16),
                 struct((slots, width), bf16),
             ],
-            input_output_aliases={1 + len(inputs) + i: 2 + i for i in range(len(joint))},
+            input_output_aliases={1 + len(inputs) + i: 4 + len(side_counts) + i for i in range(len(joint))},
             compiler_params=params,
             cost_estimate=cheap,
             name="attention",
         )(place, *inputs, *joint)
 
-    joint, back_far, side_back_far = (), [], []
+    def summed(p):
+        far_grad = pl.pallas_call(
+            far_sum_kernel,
+            in_specs=[in_vmem] * 3,
+            out_specs=in_vmem,
+            out_shape=jax.ShapeDtypeStruct((2, far_rows, part_width), bf16),
+            compiler_params=small,
+            cost_estimate=cheap,
+            name="far_sum",
+        )(far[p], near_back[p], side_back_far[p])
+        far_sent.append(far_grad)
+        grad_far.append(from_peers(far_grad))
+
+    joint, own, far = (), [], []
+    back_far, side_back_far, near_back, side_back_own, far_sent, grad_far = [], [], [], [], [], []
     for p in range(parts):
-        back, side_grad_far, *joint = attention(p, joint)
+        back, own_part, far_part, near_grad, *rest = attention(p, joint)
+        side_grads, joint = rest[:-3], rest[-3:]
+        if p + 1 < parts:
+            side_grads, *_ = tie((side_grads, side_far[p + 1], near_far[p + 1], qo_far[p + 1]))
         if p > 0:
-            back, side_grad_far, joint, back_far, side_back_far = tie(
-                (back, side_grad_far, joint, back_far, side_back_far)
+            side_grads, side_back_far, back_far = tie(
+                (side_grads, side_back_far, back_far)
             )
-        side_back_far.append(lax.ppermute(side_grad_far, "ctx", side_pairs))
+            summed(p - 1)
+            *side_grads, _ = tie((*side_grads, far_sent[-1]))
+        own.append(own_part)
+        far.append(far_part)
+        side_back_far.append(lax.ppermute(side_grads[-1], "ctx", side_pairs))
+        near_back.append(lax.ppermute(near_grad, "ctx", near_pairs))
         back_far.append(from_peers(back))
-    mixed, query_grad, own, far, near_grad, side_grad_own, sums = joint
-
-    near_back = lax.ppermute(near_grad, "ctx", near_pairs)
+        if p + 1 < parts:
+            side_back_own.append(side_back_far[p])
+            continue
+        side_grad_own, _ = tie((side_grads[0], side_back_far[p]))
+        side_back_own.append(lax.ppermute(side_grad_own, "ctx", side_pairs))
+    mixed, query_grad, sums = joint
 
     def shifted(array, step):
         return lax.ppermute(array, "ctx", [(i, i ^ step) for i in range(ctx_count)])
@@ -469,21 +499,9 @@
         return sums
 
     bits = [1 << n for n in range(ctx_count.bit_length() - 1)]
-    side_back_far, back_far = tie((side_back_far, back_far))
-    side_grad_own, _ = tie((side_grad_own, side_back_far))
-    side_back_own = lax.ppermute(side_grad_own, "ctx", side_pairs)
     sums = rounds(bits[:1], rounds(bits[2:], sums))
-    side_back_far, sums = tie((side_back_far, sums))
-    far_grad = pl.pallas_call(
-        far_sum_kernel,
-        in_specs=[in_vmem] * (2 + parts),
-        out_specs=in_vmem,
-        out_shape=jax.ShapeDtypeStruct((2, far_rows, width), bf16),
-        compiler_params=small,
-        cost_estimate=cheap,
-        name="far_sum",
-    )(far, near_back, *side_back_far)
-    grad_far = from_peers(far_grad)
+    side_back_far, sums, back_far, grad_far = tie((side_back_far, sums, back_far, grad_far))
+    summed(parts - 1)
 
     def to_all(before, after, sums):
         slabs = [rounds(before, sums)]
@@ -492,28 +510,28 @@
             slabs = slabs + [lax.ppermute(slab, "head", pairs) for slab in slabs]
         return [rounds(after, slab) for slab in slabs]
 
-    sums, _ = tie((sums, far_grad))
+    sums, _ = tie((sums, far_sent[-1]))
     slabs = lax.cond(
         noise_level[0] >= 0,
         functools.partial(to_all, bits[1:2], []),
         functools.partial(to_all, [], bits[1:2]),
         sums,
     )
-    slabs, grad_far, side_back_own = tie((slabs, grad_far, side_back_own))
-    arrived = [slab for slabs in back_far for slab in slabs] + grad_far
+    slabs, grad_far, side_back_own[-1] = tie((slabs, grad_far, side_back_own[-1]))
+    arrived = [slab for part in back_far + grad_far for slab in part]
     noise_row = noise_level.reshape(1, span_total)
-    operands = (noise_row, own, near_back, side_back_own, *slabs, *arrived)
+    operands = (noise_row, *own, *near_back, *side_back_own, *slabs, *arrived)
     return tuple(
         pl.pallas_call(
-            functools.partial(finish_kernel, groups=groups, parts=parts, by_span=by_span),
+            functools.partial(finish_kernel, groups=groups, parts=parts),
             grid_spec=pltpu.PrefetchScalarGridSpec(
                 num_scalar_prefetch=1,
                 in_specs=[in_vmem] * len(operands) + [anywhere] * 2,
                 out_specs=[anywhere] * 5,
                 scratch_shapes=[
-                    pltpu.VMEM((2, rows, width), bf16),
+                    pltpu.VMEM((parts, 2, rows, part_width), bf16),
                     pltpu.VMEM((level_count, full_width), f32),
-                    pltpu.SemaphoreType.DMA((2 * len(arrived) + 2 + groups,)),
+                    pltpu.SemaphoreType.DMA((2 * len(arrived) + 2 * parts + groups,)),
                 ],
             ),
             out_shape=[jax.ShapeDtypeStruct((rows, full_width), bf16)] * 4

time: 113 us -> 108 us (0.956); the launches traced: 111 us -> 107 us
  waiting for transfers between devices: 47.4 us -> 35.3 us
  starting transfers between devices: 35.8 us -> 42.2 us
  local copies, waits for them, and re-layouts: 1.03 us -> 3.16 us
    ppermute x5, starting transfers between devices: 4.53 us -> 16.9 us  [shifted(): return lax.ppermute(array, 'ctx', [(i, i ^ step) for i in range(ctx_count)])]
    ppermute x4 -> x5, starting transfers between devices: 17.7 us -> 11.6 us  [the longest x2 5.76 us: per_device(): near_back.append(lax.ppermute(near_grad, 'ctx', near_pairs))]
    ppermute x5, waiting for transfers between devices: 13.9 us -> 8.63 us  [shifted(): return lax.ppermute(array, 'ctx', [(i, i ^ step) for i in range(ctx_count)])]
    ppermute x1, waiting for transfers between devices: 9.09 us -> 4.16 us  [to_all(): slabs = slabs + [lax.ppermute(slab, 'head', pairs) for slab in slabs]]
    ppermute x3 -> x4, waiting for transfers between devices: 5 us -> 1.23 us  [from_peers(): arrived.append(lax.ppermute(part, 'head', pairs))]
    ppermute x2, starting transfers between devices: 2.9 us -> 0.01 us  [per_device(): near_far = [lax.ppermute(slab, 'ctx', near_pairs) for slab in kv_far]]
    ppermute x3 -> x4, starting transfers between devices: 0.58 us -> 3.1 us  [from_peers(): arrived.append(lax.ppermute(part, 'head', pairs))]
    unnamed x18 -> x26, local copies, waits for them, and re-layouts: 1.03 us -> 3.16 us
  transfers between devices with their start and end apart: 23 -> 25, of which waited for: 8 -> 8; matrix products, arithmetic and copies ran while one was open for 1% -> 1% of each run, Pallas kernels for 17% -> 17%
where the time goes in v7:
time: 108 us; the launch traced here: 107 us
  starting transfers between devices  42.2 us (39%)
  waiting for transfers between devices  35.3 us (33%)
  Pallas kernels  24.8 us (23%)
  local copies, waits for them, and re-layouts  3.16 us (3%)
    ppermute x4, waiting for transfers between devices, to_peers(): arrived.append(lax.ppermute(part, 'head', pairs))  21.3 us
    ppermute x5, starting transfers between devices, shifted(): return lax.ppermute(array, 'ctx', [(i, i ^ step) for i in range(ctx_count)])  16.9 us
    pallas_call x2, Pallas kernels, attention(): pl.pallas_call(functools.partial(attention_kernel, rows=rows, tokens=toke...  15.5 us
    ppermute x5, waiting for transfers between devices, shifted(): return lax.ppermute(array, 'ctx', [(i, i ^ step) for i in range(ctx_count)])  8.63 us
    ppermute x4, starting transfers between devices, to_peers(): arrived.append(lax.ppermute(part, 'head', pairs))  6.93 us
    ppermute x2, starting transfers between devices, per_device(): near_back.append(lax.ppermute(near_grad, 'ctx', near_pairs))  5.76 us
    ppermute x1, starting transfers between devices, per_device(): side_back_own.append(lax.ppermute(side_grad_own, 'ctx', side_pairs))  4.48 us
    ppermute x1, waiting for transfers between devices, to_all(): slabs = slabs + [lax.ppermute(slab, 'head', pairs) for slab in slabs]  4.16 us
  transfers between devices with their start and end apart: 25, of which 8 were waited for; matrix products, arithmetic and copies ran while one was open for 1% of the time, Pallas kernels for 17%

profile of v7, /device:TPU:0, one launch (start us, length us, event | category | flops | bytes accessed | tf_op | source)
XLA Modules:
  0.0 107.2 jit_solution(1047037930293022812)
XLA Ops:
  0.7 2.8 %pack.3 = (bf16[2,128,1536]{2,1,0:T(8,128)(2,1)}, bf16[2,128,768]{2,1,0:T(8,128)(2,1)}, bf16[2,128,768]{2,1,0:T(8,128)(2,1)}) custom-call(s32[1]{0:T(128)} %bitcast.place_ref, bf16[128,3072]{1,0:T(8,128)(2,1)} %first_ref.3, bf16[128,3072]{1,0:T(8,128)(2,1)} %second_ref.3), custom_call_target="tpu_custom_call" | custom-call | flops 1 | bytes 1 | tf_op jit(solution)/shard_map/pack/pallas_call | solution.py:319
  3.5 3.0 %collective-permute-start.5 = (bf16[2,128,768]{2,1,0:T(8,128)(2,1)}, bf16[2,128,768]{2,1,0:T(8,128)(2,1)S(1)}, u32[]{:S(2)}, u32[]{:S(2)}) collective-permute-start(bf16[2,128,768]{2,1,0:T(8,128)(2,1)} %get-tuple-element.59), channel_id=1, source_target_pairs={{0,1},{1,0},{2,3},{3,2},{4,5},{5,4},{6,7},{7,6},{8,9},{9,8},{10,11... | collective-permute-start | bytes 1179656 | tf_op jit(solution)/shard_map/ppermute | solution.py:339
  6.5 0.0 collective-permute-start.7
  6.5 1.8 %collective-permute-start.9 = (bf16[2,128,1536]{2,1,0:T(8,128)(2,1)}, bf16[2,128,1536]{2,1,0:T(8,128)(2,1)S(1)}, u32[]{:S(2)}, u32[]{:S(2)}) collective-permute-start(bf16[2,128,1536]{2,1,0:T(8,128)(2,1)} %get-tuple-element.57.kv_own_ref), channel_id=1, source_target_pairs={{0,0},{2,4},{4,2},{6,8},{8,6},{10,12},{12,10},{14,16},{16,14},{18,... | collective-permute-start | bytes 2359304 | tf_op jit(solution)/shard_map/ppermute | solution.py:352
  8.3 0.1 collective-permute-start.11
  8.4 0.0 copy-done.4
  8.4 0.3 pack.2
  8.7 8.0 %collective-permute-done.5.kv_ref = bf16[2,128,768]{2,1,0:T(8,128)(2,1)S(1)} collective-permute-done((bf16[2,128,768]{2,1,0:T(8,128)(2,1)}, bf16[2,128,768]{2,1,0:T(8,128)(2,1)S(1)}, u32[]{:S(2)}, u32[]{:S(2)}) %collective-permute-start.5) | collective-permute-done | bytes 393248 | tf_op jit(solution)/shard_map/ppermute | solution.py:339
  16.7 2.1 %collective-permute-start.6 = (bf16[2,128,768]{2,1,0:T(8,128)(2,1)S(1)}, bf16[2,128,768]{2,1,0:T(8,128)(2,1)S(1)}, u32[]{:S(2)}, u32[]{:S(2)}) collective-permute-start(bf16[2,128,768]{2,1,0:T(8,128)(2,1)S(1)} %get-tuple-element.60), channel_id=1, source_target_pairs={{0,1},{1,0},{2,3},{3,2},{4,5},{5,4},{6,7},{7,6},{8,9},{9,8},{10,11... | collective-permute-start | bytes 1179656 | tf_op jit(solution)/shard_map/ppermute | solution.py:339
  18.8 0.7 collective-permute-start.10
  19.4 5.7 %collective-permute-done.11.kv_ref = bf16[2,128,768]{2,1,0:T(8,128)(2,1)S(1)} collective-permute-done((bf16[2,128,768]{2,1,0:T(8,128)(2,1)}, bf16[2,128,768]{2,1,0:T(8,128)(2,1)S(1)}, u32[]{:S(2)}, u32[]{:S(2)}) %collective-permute-start.11) | collective-permute-done | bytes 393248 | tf_op jit(solution)/shard_map/ppermute | solution.py:339
  25.1 0.0 collective-permute-start.8
  25.1 7.6 %collective-permute-done.6.qo_ref = bf16[2,128,768]{2,1,0:T(8,128)(2,1)S(1)} collective-permute-done((bf16[2,128,768]{2,1,0:T(8,128)(2,1)S(1)}, bf16[2,128,768]{2,1,0:T(8,128)(2,1)S(1)}, u32[]{:S(2)}, u32[]{:S(2)}) %collective-permute-start.6) | collective-permute-done | bytes 393248 | tf_op jit(solution)/shard_map/ppermute | solution.py:339
  32.7 1.7 %collective-permute-start.12 = (bf16[2,128,768]{2,1,0:T(8,128)(2,1)S(1)}, bf16[2,128,768]{2,1,0:T(8,128)(2,1)S(1)}, u32[]{:S(2)}, u32[]{:S(2)}) collective-permute-start(bf16[2,128,768]{2,1,0:T(8,128)(2,1)S(1)} %get-tuple-element.67), channel_id=1, source_target_pairs={{0,1},{1,0},{2,3},{3,2},{4,5},{5,4},{6,7},{7,6},{8,9},{9,8},{10,11... | collective-permute-start | bytes 1179656 | tf_op jit(solution)/shard_map/ppermute | solution.py:339
  34.5 0.0 collective-permute-done.7.near_own_ref
  34.5 0.0 collective-permute-start.13
  34.5 0.0 collective-permute-done.9.side_own_ref
  34.5 0.7 collective-permute-start.14
  35.2 1.9 %prep.1 = (f32[768,256]{1,0:T(8,128)S(1)}, f32[256,1536]{1,0:T(8,128)S(1)}, bf16[24,256]{1,0:T(8,128)(2,1)S(1)}) custom-call(s32[1]{0:T(128)} %bitcast.place_ref, s32[32,128]{1,0:T(8,128)S(1)} %bitcast.5, s32[1,24]{1,0:T(1,128)S(1)} %bitcast.6, s32[24,24]{1,0:T(8,128)S(1)} %copy-done.11, f32[128,3072]{1,0:T(8,128)S(1)} %copy-done.1), custom_call_target="tpu_custom_call" | custom-call | flops 1 | bytes 1 | tf_op jit(solution)/shard_map/prep/pallas_call | solution.py:361
  37.1 0.0 collective-permute-done.10.side_far_ref
  37.1 0.0 collective-permute-done.8.near_far_ref
  37.1 7.8 %attention.2 = (bf16[2,128,768]{2,1,0:T(8,128)(2,1)S(1)}, f32[2,128,768]{2,1,0:T(8,128)S(1)}, f32[2,128,768]{2,1,0:T(8,128)S(1)}, bf16[2,256,768]{2,1,0:T(8,128)...) custom-call(s32[1]{0:T(128)} %bitcast.place_ref, ...), custom_call_target="tpu_custom_call" | custom-call | flops 1 | bytes 1 | tf_op jit(solution)/shard_map/attention/pallas_call | solution.py:415
  44.9 0.0 collective-permute-done.12.qo_ref
  44.9 0.0 collective-permute-done.13.near_far_ref
  44.9 0.0 collective-permute-done.14.side_far_ref
  44.9 0.7 collective-permute-start.17
  45.6 5.8 %collective-permute-start.15 = (bf16[2,256,768]{2,1,0:T(8,128)(2,1)S(1)}, bf16[2,256,768]{2,1,0:T(8,128)(2,1)S(1)}, u32[]{:S(2)}, u32[]{:S(2)}) collective-permute-start(bf16[2,256,768]{2,1,0:T(8,128)(2,1)S(1)} %get-tuple-element.72), channel_id=1, source_target_pairs={{0,2},{2,0},{4,6},{6,4},{8,10},{10,8},{12,14},{14,12},{16,18},{18,... | collective-permute-start | bytes 2359304 | tf_op jit(solution)/shard_map/ppermute | solution.py:480
  51.4 0.5 collective-permute-start.18
  51.9 7.7 %attention.3 = (bf16[2,128,768]{2,1,0:T(8,128)(2,1)S(1)}, f32[2,128,768]{2,1,0:T(8,128)S(1)}, f32[2,128,768]{2,1,0:T(8,128)S(1)}, bf16[2,256,768]{2,1,0:T(8,128)...) custom-call(s32[1]{0:T(128)} %bitcast.place_ref, ...), custom_call_target="tpu_custom_call", output_to_operand_aliasing={{6}: (12, {}), {7}: (13, {}), {8}: (14, {})} | custom-call | flops 1 | bytes 1 | tf_op jit(solution)/shard_map/attention/pallas_call | solution.py:415
  59.6 0.0 collective-permute-start.16
  59.6 1.6 %collective-permute-start.20 = (bf16[24,1536]{1,0:T(8,128)(2,1)S(1)}, bf16[24,1536]{1,0:T(8,128)(2,1)S(1)}, u32[]{:S(2)}, u32[]{:S(2)}) collective-permute-start(bf16[24,1536]{1,0:T(8,128)(2,1)S(1)} %get-tuple-element.84), channel_id=1, source_target_pairs={{0,8},{2,10},{4,12},{6,14},{8,0},{10,2},{12,4},{14,6},{16,24},{18,... | collective-permute-start | bytes 221192 | tf_op jit(solution)/shard_map/ppermute | solution.py:490
  61.2 1.2 %collective-permute-done.18.refs_8_ = bf16[2,128,768]{2,1,0:T(8,128)(2,1)S(1)} collective-permute-done((bf16[2,128,768]{2,1,0:T(8,128)(2,1)S(1)}, bf16[2,128,768]{2,1,0:T(8,128)(2,1)S(1)}, u32[]{:S(2)}, u32[]{:S(2)}) %collective-permute-start.18) | collective-permute-done | bytes 393248 | tf_op jit(solution)/shard_map/ppermute | solution.py:347
  62.5 2.6 %collective-permute-start.21 = (bf16[24,1536]{1,0:T(8,128)(2,1)S(1)}, bf16[24,1536]{1,0:T(8,128)(2,1)S(1)}, u32[]{:S(2)}, u32[]{:S(2)}) collective-permute-start(bf16[24,1536]{1,0:T(8,128)(2,1)S(1)} %get-tuple-element.84), channel_id=1, source_target_pairs={{0,16},{2,18},{4,20},{6,22},{8,24},{10,26},{12,28},{14,30},{16,0},... | collective-permute-start | bytes 221192 | tf_op jit(solution)/shard_map/ppermute | solution.py:490
  65.0 0.0 collective-permute-done.17.side_ref.refs_4_
  65.1 1.3 %collective-permute-start.22 = (bf16[24,1536]{1,0:T(8,128)(2,1)S(1)}, bf16[24,1536]{1,0:T(8,128)(2,1)S(1)}, u32[]{:S(2)}, u32[]{:S(2)}) collective-permute-start(bf16[24,1536]{1,0:T(8,128)(2,1)S(1)} %get-tuple-element.84), channel_id=1, source_target_pairs={{0,24},{2,26},{4,28},{6,30},{8,16},{10,18},{12,20},{14,22},{16,8},... | collective-permute-start | bytes 221192 | tf_op jit(solution)/shard_map/ppermute | solution.py:490
  66.4 0.0 collective-permute-done.15.near_ref.refs_2_
  66.4 0.5 collective-permute-start.24
  66.9 0.1 far_sum.2
  67.1 0.0 collective-permute-done.20
  67.1 1.6 %collective-permute-start.25 = (bf16[2,128,768]{2,1,0:T(8,128)(2,1)S(1)}, bf16[2,128,768]{2,1,0:T(8,128)(2,1)S(1)}, u32[]{:S(2)}, u32[]{:S(2)}) collective-permute-start(bf16[2,128,768]{2,1,0:T(8,128)(2,1)S(1)} %far_sum.2), channel_id=1, source_target_pairs={{0,1},{1,0},{2,3},{3,2},{4,5},{5,4},{6,7},{7,6},{8,9},{9,8},{10,11... | collective-permute-start | bytes 1179656 | tf_op jit(solution)/shard_map/ppermute | solution.py:347
  68.7 0.0 collective-permute-done.21
  68.7 0.7 collective-permute-start.19
  69.3 1.9 %collective-permute-done.22 = bf16[24,1536]{1,0:T(8,128)(2,1)S(1)} collective-permute-done((bf16[24,1536]{1,0:T(8,128)(2,1)S(1)}, bf16[24,1536]{1,0:T(8,128)(2,1)S(1)}, u32[]{:S(2)}, u32[]{:S(2)}) %collective-permute-start.22) | collective-permute-done | bytes 73760 | tf_op jit(solution)/shard_map/ppermute | solution.py:490
  71.2 6.5 %collective-permute-start.23 = (bf16[24,1536]{1,0:T(8,128)(2,1)S(1)}, bf16[24,1536]{1,0:T(8,128)(2,1)S(1)}, u32[]{:S(2)}, u32[]{:S(2)}) collective-permute-start(bf16[24,1536]{1,0:T(8,128)(2,1)S(1)} %add_add_fusion), channel_id=1, source_target_pairs={{0,2},{2,0},{4,6},{6,4},{8,10},{10,8},{12,14},{14,12},{16,18},{18,... | collective-permute-start | bytes 221192 | tf_op jit(solution)/shard_map/ppermute | solution.py:490
  77.7 0.9 collective-permute-done.23
  78.7 0.0 collective-permute-done.19.side_ref
  78.7 4.5 %collective-permute-start.27 = (bf16[2,128,768]{2,1,0:T(8,128)(2,1)}, bf16[2,128,768]{2,1,0:T(8,128)(2,1)}, u32[]{:S(2)}, u32[]{:S(2)}) collective-permute-start(bf16[2,128,768]{2,1,0:T(8,128)(2,1)} %get-tuple-element.95), channel_id=1, source_target_pairs={{0,0},{2,4},{4,2},{6,8},{8,6},{10,12},{12,10},{14,16},{16,14},{18,... | collective-permute-start | bytes 1179656 | tf_op jit(solution)/shard_map/ppermute | solution.py:486
  83.1 0.0 collective-permute-done.24.refs_9_
  83.2 0.0 collective-permute-done.25.refs_10_
  83.2 0.0 collective-permute-done.16.near_ref.refs_3_
  83.2 1.0 far_sum.3
  84.2 0.5 collective-permute-start.26
  84.7 16.0 %conditional.1 = (bf16[24,1536]{1,0:T(8,128)(2,1)}, bf16[24,1536]{1,0:T(8,128)(2,1)}) conditional(s32[]{:T(128)} %bitcast.3, bf16[24,1536]{1,0:T(8,128)(2,1)S(1)} %add.28, bf16[24,1536]{1,0:T(8,128)(2,1)S(1)} %add.28), branch_computations={%region_0.0_spmd, %region_1.0_spmd} | conditional | flops 73728 | bytes 1327240 | solution.py:514
  84.7 4.9 %collective-permute-start.3 = (bf16[24,1536]{1,0:T(8,128)(2,1)S(1)}, bf16[24,1536]{1,0:T(8,128)(2,1)S(1)}, u32[]{:S(2)}, u32[]{:S(2)}) collective-permute-start(bf16[24,1536]{1,0:T(8,128)(2,1)S(1)} %param.1), channel_id=1, source_target_pairs={{0,4},{2,6},{4,0},{6,2},{8,12},{10,14},{12,8},{14,10},{16,20},{18,... | collective-permute-start | bytes 221192 | tf_op jit(solution)/shard_map/cond/branch_1_fun/ppermute | solution.py:490
  89.6 5.8 %collective-permute-done.3 = bf16[24,1536]{1,0:T(8,128)(2,1)S(1)} collective-permute-done((bf16[24,1536]{1,0:T(8,128)(2,1)S(1)}, bf16[24,1536]{1,0:T(8,128)(2,1)S(1)}, u32[]{:S(2)}, u32[]{:S(2)}) %collective-permute-start.3) | collective-permute-done | bytes 73760 | tf_op jit(solution)/shard_map/cond/branch_1_fun/ppermute | solution.py:490
  95.5 0.6 add.18
  96.1 0.5 collective-permute-start.4
  96.6 4.2 %collective-permute-done.4 = bf16[24,1536]{1,0:T(8,128)(2,1)} collective-permute-done((bf16[24,1536]{1,0:T(8,128)(2,1)}, bf16[24,1536]{1,0:T(8,128)(2,1)}, u32[]{:S(2)}, u32[]{:S(2)}) %collective-permute-start.4) | collective-permute-done | bytes 73760 | tf_op jit(solution)/shard_map/cond/branch_1_fun/ppermute | solution.py:510
  100.8 0.0 collective-permute-done.27.refs_5_
  100.8 0.0 collective-permute-done.26.refs_11_
  100.8 1.1 %copy-done.3 = f32[2,128,768]{2,1,0:T(8,128)S(1)} copy-done((f32[2,128,768]{2,1,0:T(8,128)S(1)}, f32[2,128,768]{2,1,0:T(8,128)}, u32[]{:S(2)}) %copy-start.3) | copy-done | bytes 786456
  101.9 1.0 copy-done.7
  102.9 1.0 copy-done.9
  103.9 3.2 %finish.1 = (bf16[128,3072]{1,0:T(8,128)(2,1)}, bf16[128,3072]{1,0:T(8,128)(2,1)}, bf16[128,3072]{1,0:T(8,128)(2,1)}, bf16[128,3072]{1,0:T(8,128)(2,1)}, f32[128,3072]{1,0:T(8,128)}) custom-call(s32[1]{0:T(128)} %bitcast.place_ref, s32[1,24]{1,0:T(1,128)S(1)} %bitcast.8, ...), custom_call_target="tpu_custom_call", output_to_operand_aliasing={{0}: (14, {}), {1}: (15, {})} | custom-call | flops 1 | bytes 1 | tf_op jit(solution)/shard_map/finish/pallas_call | solution.py:525
  (24 shorter events, 0.1 us)
Async XLA Ops:
  0.6 7.8 %copy-start.4 = (bf16[128,3072]{1,0:T(8,128)(2,1)S(1)}, bf16[128,3072]{1,0:T(8,128)(2,1)}, u32[]{:S(2)}) copy-start(bf16[128,3072]{1,0:T(8,128)(2,1)} %first_ref.2) | copy-start | bytes 2359300
  0.6 7.8 %copy-start.5 = (bf16[128,3072]{1,0:T(8,128)(2,1)S(1)}, bf16[128,3072]{1,0:T(8,128)(2,1)}, u32[]{:S(2)}) copy-start(bf16[128,3072]{1,0:T(8,128)(2,1)} %second_ref.2) | copy-start | bytes 2359300
  0.7 34.5 %copy-start.1 = (f32[128,3072]{1,0:T(8,128)S(1)}, f32[128,3072]{1,0:T(8,128)}, u32[]{:S(2)}) copy-start(f32[128,3072]{1,0:T(8,128)} %table_ref.1) | copy-start | bytes 4718596
  0.7 34.5 %copy-start.10 = (s32[4096]{0:T(1024)S(1)}, s32[4096]{0:T(1024)}, u32[]{:S(2)}) copy-start(s32[4096]{0:T(1024)} %param.15) | copy-start | bytes 49156
  0.7 34.5 %copy-start.11 = (s32[24,24]{1,0:T(8,128)S(1)}, s32[24,24]{1,0:T(8,128)}, u32[]{:S(2)}) copy-start(s32[24,24]{1,0:T(8,128)} %mask_ref.1) | copy-start | bytes 6916
  0.7 34.5 %copy-start.12 = (s32[24]{0:T(128)S(1)}, s32[24]{0:T(128)}, u32[]{:S(2)}) copy-start(s32[24]{0:T(128)} %param.16) | copy-start | bytes 292
  3.5 13.2 %collective-permute-start.5 = (bf16[2,128,768]{2,1,0:T(8,128)(2,1)}, bf16[2,128,768]{2,1,0:T(8,128)(2,1)S(1)}, u32[]{:S(2)}, u32[]{:S(2)}) collective-permute-start(bf16[2,128,768]{2,1,0:T(8,128)(2,1)} %get-tuple-element.59), channel_id=1, source_target_pairs={{0,1},{1,0},{2,3},{3,2},{4,5},{5,4},{6,7},{7,6},{8,9},{9,8},{10,11... | collective-permute-start | bytes 1179656 | tf_op jit(solution)/shard_map/ppermute | solution.py:339
  6.5 27.9 %collective-permute-start.7 = (bf16[2,128,1536]{2,1,0:T(8,128)(2,1)}, bf16[2,128,1536]{2,1,0:T(8,128)(2,1)S(1)}, u32[]{:S(2)}, u32[]{:S(2)}) collective-permute-start(bf16[2,128,1536]{2,1,0:T(8,128)(2,1)} %get-tuple-element.57.kv_own_ref), channel_id=1, source_target_pairs={{0,2},{2,0},{4,6},{6,4},{8,10},{10,8},{12,14},{14,12},{16,18},{18,... | collective-permute-start | bytes 2359304 | tf_op jit(solution)/shard_map/ppermute | solution.py:353
  6.5 27.9 %collective-permute-start.9 = (bf16[2,128,1536]{2,1,0:T(8,128)(2,1)}, bf16[2,128,1536]{2,1,0:T(8,128)(2,1)S(1)}, u32[]{:S(2)}, u32[]{:S(2)}) collective-permute-start(bf16[2,128,1536]{2,1,0:T(8,128)(2,1)} %get-tuple-element.57.kv_own_ref), channel_id=1, source_target_pairs={{0,0},{2,4},{4,2},{6,8},{8,6},{10,12},{12,10},{14,16},{16,14},{18,... | collective-permute-start | bytes 2359304 | tf_op jit(solution)/shard_map/ppermute | solution.py:352
  8.3 28.8 %copy-start = (bf16[2,128,1536]{2,1,0:T(8,128)(2,1)S(1)}, bf16[2,128,1536]{2,1,0:T(8,128)(2,1)}, u32[]{:S(2)}) copy-start(bf16[2,128,1536]{2,1,0:T(8,128)(2,1)} %get-tuple-element.57.kv_own_ref) | copy-start | bytes 2359300
  8.3 16.8 %collective-permute-start.11 = (bf16[2,128,768]{2,1,0:T(8,128)(2,1)}, bf16[2,128,768]{2,1,0:T(8,128)(2,1)S(1)}, u32[]{:S(2)}, u32[]{:S(2)}) collective-permute-start(bf16[2,128,768]{2,1,0:T(8,128)(2,1)} %get-tuple-element.66), channel_id=1, source_target_pairs={{0,1},{1,0},{2,3},{3,2},{4,5},{5,4},{6,7},{7,6},{8,9},{9,8},{10,11... | collective-permute-start | bytes 1179656 | tf_op jit(solution)/shard_map/ppermute | solution.py:339
  16.7 16.0 %collective-permute-start.6 = (bf16[2,128,768]{2,1,0:T(8,128)(2,1)S(1)}, bf16[2,128,768]{2,1,0:T(8,128)(2,1)S(1)}, u32[]{:S(2)}, u32[]{:S(2)}) collective-permute-start(bf16[2,128,768]{2,1,0:T(8,128)(2,1)S(1)} %get-tuple-element.60), channel_id=1, source_target_pairs={{0,1},{1,0},{2,3},{3,2},{4,5},{5,4},{6,7},{7,6},{8,9},{9,8},{10,11... | collective-permute-start | bytes 1179656 | tf_op jit(solution)/shard_map/ppermute | solution.py:339
  18.8 18.3 %collective-permute-start.10 = (bf16[2,128,768]{2,1,0:T(8,128)(2,1)S(1)}, bf16[2,128,768]{2,1,0:T(8,128)(2,1)S(1)}, u32[]{:S(2)}, u32[]{:S(2)}) collective-permute-start(bf16[2,128,768]{2,1,0:T(8,128)(2,1)S(1)} %collective-permute-done.5.kv_ref), channel_id=1, source_target_pairs={{0,0},{2,4},{4,2},{6,8},{8,6},{10,12},{12,10},{14,16},{16,14},{18,... | collective-permute-start | bytes 1179656 | tf_op jit(solution)/shard_map/ppermute | solution.py:355
  25.1 12.0 %collective-permute-start.8 = (bf16[2,128,768]{2,1,0:T(8,128)(2,1)S(1)}, bf16[2,128,768]{2,1,0:T(8,128)(2,1)S(1)}, u32[]{:S(2)}, u32[]{:S(2)}) collective-permute-start(bf16[2,128,768]{2,1,0:T(8,128)(2,1)S(1)} %collective-permute-done.5.kv_ref), channel_id=1, source_target_pairs={{0,2},{2,0},{4,6},{6,4},{8,10},{10,8},{12,14},{14,12},{16,18},{18,... | collective-permute-start | bytes 1179656 | tf_op jit(solution)/shard_map/ppermute | solution.py:356
  32.7 12.2 %collective-permute-start.12 = (bf16[2,128,768]{2,1,0:T(8,128)(2,1)S(1)}, bf16[2,128,768]{2,1,0:T(8,128)(2,1)S(1)}, u32[]{:S(2)}, u32[]{:S(2)}) collective-permute-start(bf16[2,128,768]{2,1,0:T(8,128)(2,1)S(1)} %get-tuple-element.67), channel_id=1, source_target_pairs={{0,1},{1,0},{2,3},{3,2},{4,5},{5,4},{6,7},{7,6},{8,9},{9,8},{10,11... | collective-permute-start | bytes 1179656 | tf_op jit(solution)/shard_map/ppermute | solution.py:339
  34.5 10.4 %collective-permute-start.13 = (bf16[2,128,768]{2,1,0:T(8,128)(2,1)S(1)}, bf16[2,128,768]{2,1,0:T(8,128)(2,1)S(1)}, u32[]{:S(2)}, u32[]{:S(2)}) collective-permute-start(bf16[2,128,768]{2,1,0:T(8,128)(2,1)S(1)} %collective-permute-done.11.kv_ref), channel_id=1, source_target_pairs={{0,2},{2,0},{4,6},{6,4},{8,10},{10,8},{12,14},{14,12},{16,18},{18,... | collective-permute-start | bytes 1179656 | tf_op jit(solution)/shard_map/ppermute | solution.py:356
  34.5 10.4 %collective-permute-start.14 = (bf16[2,128,768]{2,1,0:T(8,128)(2,1)S(1)}, bf16[2,128,768]{2,1,0:T(8,128)(2,1)S(1)}, u32[]{:S(2)}, u32[]{:S(2)}) collective-permute-start(bf16[2,128,768]{2,1,0:T(8,128)(2,1)S(1)} %collective-permute-done.11.kv_ref), channel_id=1, source_target_pairs={{0,0},{2,4},{4,2},{6,8},{8,6},{10,12},{12,10},{14,16},{16,14},{18,... | collective-permute-start | bytes 1179656 | tf_op jit(solution)/shard_map/ppermute | solution.py:355
  44.9 20.2 %collective-permute-start.17 = (bf16[2,256,768]{2,1,0:T(8,128)(2,1)S(1)}, bf16[2,256,768]{2,1,0:T(8,128)(2,1)S(1)}, u32[]{:S(2)}, u32[]{:S(2)}) collective-permute-start(bf16[2,256,768]{2,1,0:T(8,128)(2,1)S(1)} %get-tuple-element.75), channel_id=1, source_target_pairs={{0,0},{2,4},{4,2},{6,8},{8,6},{10,12},{12,10},{14,16},{16,14},{18,... | collective-permute-start | bytes 2359304 | tf_op jit(solution)/shard_map/ppermute | solution.py:479
  45.6 20.8 %collective-permute-start.15 = (bf16[2,256,768]{2,1,0:T(8,128)(2,1)S(1)}, bf16[2,256,768]{2,1,0:T(8,128)(2,1)S(1)}, u32[]{:S(2)}, u32[]{:S(2)}) collective-permute-start(bf16[2,256,768]{2,1,0:T(8,128)(2,1)S(1)} %get-tuple-element.72), channel_id=1, source_target_pairs={{0,2},{2,0},{4,6},{6,4},{8,10},{10,8},{12,14},{14,12},{16,18},{18,... | collective-permute-start | bytes 2359304 | tf_op jit(solution)/shard_map/ppermute | solution.py:480
  51.4 11.1 %collective-permute-start.18 = (bf16[2,128,768]{2,1,0:T(8,128)(2,1)S(1)}, bf16[2,128,768]{2,1,0:T(8,128)(2,1)S(1)}, u32[]{:S(2)}, u32[]{:S(2)}) collective-permute-start(bf16[2,128,768]{2,1,0:T(8,128)(2,1)S(1)} %get-tuple-element.78), channel_id=1, source_target_pairs={{0,1},{1,0},{2,3},{3,2},{4,5},{5,4},{6,7},{7,6},{8,9},{9,8},{10,11... | collective-permute-start | bytes 1179656 | tf_op jit(solution)/shard_map/ppermute | solution.py:347
  59.6 19.0 %copy-start.2 = (f32[2,128,768]{2,1,0:T(8,128)}, f32[2,128,768]{2,1,0:T(8,128)S(1)}, u32[]{:S(2)}) copy-start(f32[2,128,768]{2,1,0:T(8,128)S(1)} %get-tuple-element.71.refs_1_) | copy-start | bytes 2359300
  59.6 23.6 %collective-permute-start.16 = (bf16[2,256,768]{2,1,0:T(8,128)(2,1)S(1)}, bf16[2,256,768]{2,1,0:T(8,128)(2,1)S(1)}, u32[]{:S(2)}, u32[]{:S(2)}) collective-permute-start(bf16[2,256,768]{2,1,0:T(8,128)(2,1)S(1)} %get-tuple-element.73), channel_id=1, source_target_pairs={{0,2},{2,0},{4,6},{6,4},{8,10},{10,8},{12,14},{14,12},{16,18},{18,... | collective-permute-start | bytes 2359304 | tf_op jit(solution)/shard_map/ppermute | solution.py:480
  59.6 7.4 %collective-permute-start.20 = (bf16[24,1536]{1,0:T(8,128)(2,1)S(1)}, bf16[24,1536]{1,0:T(8,128)(2,1)S(1)}, u32[]{:S(2)}, u32[]{:S(2)}) collective-permute-start(bf16[24,1536]{1,0:T(8,128)(2,1)S(1)} %get-tuple-element.84), channel_id=1, source_target_pairs={{0,8},{2,10},{4,12},{6,14},{8,0},{10,2},{12,4},{14,6},{16,24},{18,... | collective-permute-start | bytes 221192 | tf_op jit(solution)/shard_map/ppermute | solution.py:490
  62.5 6.2 %collective-permute-start.21 = (bf16[24,1536]{1,0:T(8,128)(2,1)S(1)}, bf16[24,1536]{1,0:T(8,128)(2,1)S(1)}, u32[]{:S(2)}, u32[]{:S(2)}) collective-permute-start(bf16[24,1536]{1,0:T(8,128)(2,1)S(1)} %get-tuple-element.84), channel_id=1, source_target_pairs={{0,16},{2,18},{4,20},{6,22},{8,24},{10,26},{12,28},{14,30},{16,0},... | collective-permute-start | bytes 221192 | tf_op jit(solution)/shard_map/ppermute | solution.py:490
  65.1 6.2 %collective-permute-start.22 = (bf16[24,1536]{1,0:T(8,128)(2,1)S(1)}, bf16[24,1536]{1,0:T(8,128)(2,1)S(1)}, u32[]{:S(2)}, u32[]{:S(2)}) collective-permute-start(bf16[24,1536]{1,0:T(8,128)(2,1)S(1)} %get-tuple-element.84), channel_id=1, source_target_pairs={{0,24},{2,26},{4,28},{6,30},{8,16},{10,18},{12,20},{14,22},{16,8},... | collective-permute-start | bytes 221192 | tf_op jit(solution)/shard_map/ppermute | solution.py:490
  66.4 16.7 %collective-permute-start.24 = (bf16[2,128,768]{2,1,0:T(8,128)(2,1)S(1)}, bf16[2,128,768]{2,1,0:T(8,128)(2,1)S(1)}, u32[]{:S(2)}, u32[]{:S(2)}) collective-permute-start(bf16[2,128,768]{2,1,0:T(8,128)(2,1)S(1)} %get-tuple-element.86), channel_id=1, source_target_pairs={{0,1},{1,0},{2,3},{3,2},{4,5},{5,4},{6,7},{7,6},{8,9},{9,8},{10,11... | collective-permute-start | bytes 1179656 | tf_op jit(solution)/shard_map/ppermute | solution.py:347
  67.1 16.1 %collective-permute-start.25 = (bf16[2,128,768]{2,1,0:T(8,128)(2,1)S(1)}, bf16[2,128,768]{2,1,0:T(8,128)(2,1)S(1)}, u32[]{:S(2)}, u32[]{:S(2)}) collective-permute-start(bf16[2,128,768]{2,1,0:T(8,128)(2,1)S(1)} %far_sum.2), channel_id=1, source_target_pairs={{0,1},{1,0},{2,3},{3,2},{4,5},{5,4},{6,7},{7,6},{8,9},{9,8},{10,11... | collective-permute-start | bytes 1179656 | tf_op jit(solution)/shard_map/ppermute | solution.py:347
  68.7 10.0 %collective-permute-start.19 = (bf16[2,128,768]{2,1,0:T(8,128)(2,1)S(1)}, bf16[2,128,768]{2,1,0:T(8,128)(2,1)S(1)}, u32[]{:S(2)}, u32[]{:S(2)}) collective-permute-start(bf16[2,128,768]{2,1,0:T(8,128)(2,1)S(1)} %get-tuple-element.83), channel_id=1, source_target_pairs={{0,0},{2,4},{4,2},{6,8},{8,6},{10,12},{12,10},{14,16},{16,14},{18,... | collective-permute-start | bytes 1179656 | tf_op jit(solution)/shard_map/ppermute | solution.py:479
  71.2 7.4 %collective-permute-start.23 = (bf16[24,1536]{1,0:T(8,128)(2,1)S(1)}, bf16[24,1536]{1,0:T(8,128)(2,1)S(1)}, u32[]{:S(2)}, u32[]{:S(2)}) collective-permute-start(bf16[24,1536]{1,0:T(8,128)(2,1)S(1)} %add_add_fusion), channel_id=1, source_target_pairs={{0,2},{2,0},{4,6},{6,4},{8,10},{10,8},{12,14},{14,12},{16,18},{18,... | collective-permute-start | bytes 221192 | tf_op jit(solution)/shard_map/ppermute | solution.py:490
  78.7 22.1 %collective-permute-start.27 = (bf16[2,128,768]{2,1,0:T(8,128)(2,1)}, bf16[2,128,768]{2,1,0:T(8,128)(2,1)}, u32[]{:S(2)}, u32[]{:S(2)}) collective-permute-start(bf16[2,128,768]{2,1,0:T(8,128)(2,1)} %get-tuple-element.95), channel_id=1, source_target_pairs={{0,0},{2,4},{4,2},{6,8},{8,6},{10,12},{12,10},{14,16},{16,14},{18,... | collective-permute-start | bytes 1179656 | tf_op jit(solution)/shard_map/ppermute | solution.py:486
  83.2 1.0 copy-start.6
  83.2 1.5 %copy-start.8 = (bf16[2,128,768]{2,1,0:T(8,128)(2,1)}, bf16[2,128,768]{2,1,0:T(8,128)(2,1)S(1)}, u32[]{:S(2)}) copy-start(bf16[2,128,768]{2,1,0:T(8,128)(2,1)S(1)} %collective-permute-done.25.refs_10_) | copy-start | bytes 1179652
  84.2 16.6 %collective-permute-start.26 = (bf16[2,128,768]{2,1,0:T(8,128)(2,1)}, bf16[2,128,768]{2,1,0:T(8,128)(2,1)}, u32[]{:S(2)}, u32[]{:S(2)}) collective-permute-start(bf16[2,128,768]{2,1,0:T(8,128)(2,1)} %far_sum.3), channel_id=1, source_target_pairs={{0,1},{1,0},{2,3},{3,2},{4,5},{5,4},{6,7},{7,6},{8,9},{9,8},{10,11... | collective-permute-start | bytes 1179656 | tf_op jit(solution)/shard_map/ppermute | solution.py:347
  84.7 10.7 %collective-permute-start.3 = (bf16[24,1536]{1,0:T(8,128)(2,1)S(1)}, bf16[24,1536]{1,0:T(8,128)(2,1)S(1)}, u32[]{:S(2)}, u32[]{:S(2)}) collective-permute-start(bf16[24,1536]{1,0:T(8,128)(2,1)S(1)} %param.1), channel_id=1, source_target_pairs={{0,4},{2,6},{4,0},{6,2},{8,12},{10,14},{12,8},{14,10},{16,20},{18,... | collective-permute-start | bytes 221192 | tf_op jit(solution)/shard_map/cond/branch_1_fun/ppermute | solution.py:490
  96.1 4.7 %collective-permute-start.4 = (bf16[24,1536]{1,0:T(8,128)(2,1)}, bf16[24,1536]{1,0:T(8,128)(2,1)}, u32[]{:S(2)}, u32[]{:S(2)}) collective-permute-start(bf16[24,1536]{1,0:T(8,128)(2,1)} %add.18), channel_id=1, source_target_pairs={{0,1},{1,0},{2,3},{3,2},{4,5},{5,4},{6,7},{7,6},{8,9},{9,8},{10,11... | collective-permute-start | bytes 221192 | tf_op jit(solution)/shard_map/cond/branch_1_fun/ppermute | solution.py:510
  100.8 1.1 %copy-start.3 = (f32[2,128,768]{2,1,0:T(8,128)S(1)}, f32[2,128,768]{2,1,0:T(8,128)}, u32[]{:S(2)}) copy-start(f32[2,128,768]{2,1,0:T(8,128)} %copy-done.2) | copy-start | bytes 2359300
  101.9 1.0 copy-start.7
  102.9 1.0 copy-start.9

commit v8 on v7

--- a/solution.py
+++ b/solution.py
@@ -228,14 +228,13 @@
     out_ref[...] = (total + side).astype(out_ref.dtype)
 
 
-def finish_kernel(place_ref, noise_ref, *refs, groups, parts):
-    part_refs, near_refs, side_refs = (refs[n * parts : (n + 1) * parts] for n in range(3))
-    refs = refs[3 * parts :]
-    slot_refs, refs = refs[:groups], refs[groups:]
-    count = 2 * (groups - 1) * parts
-    slabs, outs = refs[:count], refs[count + 2 : count + 7]
-    total_ref, gate_ref, sems = refs[count + 7 :]
-    part_width = part_refs[0].shape[2]
+def finish_kernel(place_ref, part_ref, near_ref, side_ref, *refs, groups, parts, p, gate):
+    slabs, refs = refs[: 2 * (groups - 1)], refs[2 * (groups - 1) :]
+    slot_refs = refs[1 : 1 + groups] if gate else ()
+    scratch = 3 if gate else 2
+    total_ref, *gate_scratch, sems = refs[-scratch:]
+    outs = refs[-scratch - (5 if gate else 4) : -scratch]
+    part_width = part_ref.shape[2]
     width = part_width * parts
     copies = []
 
@@ -243,36 +242,32 @@
         copies.append(pltpu.make_async_copy(source, to, sems.at[len(copies)]))
         copies[-1].start()
 
-    def place_slab(slab, first, second, k, p):
+    def place_slab(slab, first, second, k):
         start = lax.rem(place_ref[0] + k, groups) * width + p * part_width
         cols = pl.ds(pl.multiple_of(start, DH), part_width)
         for i, ref in enumerate((first, second)):
             send(slab.at[i], ref.at[:, cols])
 
-    slabs = iter(slabs)
-    for first, second in (outs[:2], outs[2:4]):
-        for p in range(parts):
-            for k in range(1, groups):
-                place_slab(next(slabs), first, second, k, p)
-    for p in range(parts):
-        near, side = (
-            ref[p][:, : total_ref.shape[2]].astype(jnp.float32) for ref in (near_refs, side_refs)
-        )
-        total = part_refs[p][...] + near + side
-        total_ref[p] = total.astype(total_ref.dtype)
-        place_slab(total_ref.at[p], outs[2], outs[3], 0, p)
-    by_span = noise_ref.shape[1] == slot_refs[0].shape[0]
-    levels = lax.broadcasted_iota(jnp.int32, (gate_ref.shape[0], noise_ref.shape[1]), 0)
-    onehot = (levels == noise_ref[...]).astype(jnp.bfloat16)
-    for j, ref in enumerate(slot_refs):
-        if by_span:
-            sums = jnp.dot(onehot, ref[...], preferred_element_type=jnp.float32)
-        else:
-            sums = ref[...].astype(jnp.float32)
-        start = lax.bitwise_xor(lax.rem(place_ref[0], groups), j) * width
-        cols = pl.ds(pl.multiple_of(start, DH), width)
-        gate_ref[:, cols] = sums
-        send(gate_ref.at[:, cols], outs[4].at[:, cols])
+    for k in range(1, groups):
+        place_slab(slabs[k - 1], outs[0], outs[1], k)
+        place_slab(slabs[groups + k - 2], outs[2], outs[3], k)
+    near, side = (ref[:, : part_ref.shape[1]].astype(jnp.float32) for ref in (near_ref, side_ref))
+    total_ref[...] = (part_ref[...] + near + side).astype(total_ref.dtype)
+    place_slab(total_ref, outs[2], outs[3], 0)
+    if gate:
+        noise_ref, gate_ref = refs[0], gate_scratch[0]
+        by_span = noise_ref.shape[1] == slot_refs[0].shape[0]
+        levels = lax.broadcasted_iota(jnp.int32, (gate_ref.shape[0], noise_ref.shape[1]), 0)
+        onehot = (levels == noise_ref[...]).astype(jnp.bfloat16)
+        for j, ref in enumerate(slot_refs):
+            if by_span:
+                sums = jnp.dot(onehot, ref[...], preferred_element_type=jnp.float32)
+            else:
+                sums = ref[...].astype(jnp.float32)
+            start = lax.bitwise_xor(lax.rem(place_ref[0], groups), j) * width
+            cols = pl.ds(pl.multiple_of(start, DH), width)
+            gate_ref[:, cols] = sums
+            send(gate_ref.at[:, cols], outs[4].at[:, cols])
     for one in copies:
         one.wait()
 
@@ -354,7 +349,10 @@
     kv_far = [to_peers(slab) for slab in kv_sent]
     side_far = [lax.ppermute(slab, "ctx", side_pairs) for slab in kv_far]
     near_far = [lax.ppermute(slab, "ctx", near_pairs) for slab in kv_far]
-    qo_far = [to_peers(tie((slab, far))[0]) for slab, far in zip(qo_sent, kv_far)]
+    qo_far = [
+        to_peers(tie((slab, *done))[0])
+        for slab, done in zip(qo_sent, (kv_far[:1], (*kv_far[1:], side_own, near_own)))
+    ]
 
     sizes = (ctx_count, groups, rows, span_total, level_count, by_span)
     whole = lambda shape: pl.BlockSpec(shape, lambda i, place: (0,) * len(shape))
@@ -469,11 +467,10 @@
         if p + 1 < parts:
             side_grads, *_ = tie((side_grads, side_far[p + 1], near_far[p + 1], qo_far[p + 1]))
         if p > 0:
-            side_grads, side_back_far, back_far = tie(
-                (side_grads, side_back_far, back_far)
+            back, side_back_far, back_far = tie(
+                (back, side_back_far, back_far)
             )
             summed(p - 1)
-            *side_grads, _ = tie((*side_grads, far_sent[-1]))
         own.append(own_part)
         far.append(far_part)
         side_back_far.append(lax.ppermute(side_grads[-1], "ctx", side_pairs))
@@ -511,37 +508,34 @@
         return [rounds(after, slab) for slab in slabs]
 
     sums, _ = tie((sums, far_sent[-1]))
-    slabs = lax.cond(
-        noise_level[0] >= 0,
-        functools.partial(to_all, bits[1:2], []),
-        functools.partial(to_all, [], bits[1:2]),
-        sums,
-    )
-    slabs, grad_far, side_back_own[-1] = tie((slabs, grad_far, side_back_own[-1]))
-    arrived = [slab for part in back_far + grad_far for slab in part]
-    noise_row = noise_level.reshape(1, span_total)
-    operands = (noise_row, *own, *near_back, *side_back_own, *slabs, *arrived)
-    return tuple(
-        pl.pallas_call(
-            functools.partial(finish_kernel, groups=groups, parts=parts),
+    slabs = to_all(bits[1:2], [], sums)
+    results = [mixed, query_grad]
+    struct = jax.ShapeDtypeStruct
+    for p in range(parts):
+        gate = p + 1 == parts
+        operands = [own[p], near_back[p], side_back_own[p], *back_far[p], *grad_far[p]]
+        if gate:
+            operands += [noise_level.reshape(1, span_total), *slabs]
+        scratch = [pltpu.VMEM((2, rows, part_width), bf16)]
+        if gate:
+            scratch.append(pltpu.VMEM((level_count, full_width), f32))
+        scratch.append(pltpu.SemaphoreType.DMA((4 * groups - 2 + groups,)))
+        results = pl.pallas_call(
+            functools.partial(finish_kernel, groups=groups, parts=parts, p=p, gate=gate),
             grid_spec=pltpu.PrefetchScalarGridSpec(
                 num_scalar_prefetch=1,
-                in_specs=[in_vmem] * len(operands) + [anywhere] * 2,
-                out_specs=[anywhere] * 5,
-                scratch_shapes=[
-                    pltpu.VMEM((parts, 2, rows, part_width), bf16),
-                    pltpu.VMEM((level_count, full_width), f32),
-                    pltpu.SemaphoreType.DMA((2 * len(arrived) + 2 * parts + groups,)),
-                ],
+                in_specs=[in_vmem] * len(operands) + [anywhere] * len(results),
+                out_specs=[anywhere] * (4 + gate),
+                scratch_shapes=scratch,
             ),
-            out_shape=[jax.ShapeDtypeStruct((rows, full_width), bf16)] * 4
-            + [jax.ShapeDtypeStruct((level_count, full_width), f32)],
-            input_output_aliases={1 + len(operands): 0, 2 + len(operands): 1},
+            out_shape=[struct((rows, full_width), bf16)] * 4
+            + [struct((level_count, full_width), f32)] * gate,
+            input_output_aliases={1 + len(operands) + i: i for i in range(len(results))},
             compiler_params=small,
             cost_estimate=cheap,
             name="finish",
-        )(place, *operands, mixed, query_grad)
-    )
+        )(place, *operands, *results)
+    return tuple(results)
 
 
 def solution(mesh):

time: 108 us -> 104 us (0.963)
  starting transfers between devices: 42.2 us -> 49.2 us
  waiting for transfers between devices: 35.3 us -> 28.8 us
  local copies, waits for them, and re-layouts: 3.16 us -> 0.03 us
  Pallas kernels: 24.8 us -> 23.5 us
    ppermute x5, starting transfers between devices: 16.9 us -> 22.7 us  [shifted(): return lax.ppermute(array, 'ctx', [(i, i ^ step) for i in range(ctx_count)])]
    ppermute x2, starting transfers between devices: 0.01 us -> 5.48 us  [per_device(): near_far = [lax.ppermute(slab, 'ctx', near_pairs) for slab in kv_far]]
    ppermute x4, waiting for transfers between devices: 21.3 us -> 16.4 us  [to_peers(): arrived.append(lax.ppermute(part, 'head', pairs))]
    ppermute x1, starting transfers between devices: 4.48 us -> 0.69 us  [per_device(): side_back_own.append(lax.ppermute(side_grad_own, 'ctx', side_pairs))]
    unnamed x26 -> x14, local copies, waits for them, and re-layouts: 3.16 us -> 0.03 us
    ppermute x5, waiting for transfers between devices: 8.63 us -> 6.32 us  [shifted(): return lax.ppermute(array, 'ctx', [(i, i ^ step) for i in range(ctx_count)])]
    ppermute x4, waiting for transfers between devices: 1.23 us -> 3.28 us  [from_peers(): arrived.append(lax.ppermute(part, 'head', pairs))]
    ppermute x2, starting transfers between devices: 5.76 us -> 4.22 us  [per_device(): near_back.append(lax.ppermute(near_grad, 'ctx', near_pairs))]
  transfers between devices with their start and end apart: 25 -> 25, of which waited for: 8 -> 10; matrix products, arithmetic and copies ran while one was open for 1% -> 0% of each run, Pallas kernels for 17% -> 19%
where the time goes in v8:
time: 104 us; the launch traced here: 103 us
  starting transfers between devices  49.2 us (47%)
  waiting for transfers between devices  28.8 us (28%)
  Pallas kernels  23.5 us (23%)
    ppermute x5, starting transfers between devices, shifted(): return lax.ppermute(array, 'ctx', [(i, i ^ step) for i in range(ctx_count)])  22.7 us
    ppermute x4, waiting for transfers between devices, to_peers(): arrived.append(lax.ppermute(part, 'head', pairs))  16.4 us
    pallas_call x2, Pallas kernels, attention(): pl.pallas_call(functools.partial(attention_kernel, rows=rows, tokens=toke...  15.5 us
    ppermute x4, starting transfers between devices, to_peers(): arrived.append(lax.ppermute(part, 'head', pairs))  7.43 us
    ppermute x5, waiting for transfers between devices, shifted(): return lax.ppermute(array, 'ctx', [(i, i ^ step) for i in range(ctx_count)])  6.32 us
    ppermute x2, starting transfers between devices, per_device(): near_far = [lax.ppermute(slab, 'ctx', near_pairs) for slab in kv_far]  5.48 us
    ppermute x2, starting transfers between devices, per_device(): near_back.append(lax.ppermute(near_grad, 'ctx', near_pairs))  4.22 us
    ppermute x4, waiting for transfers between devices, from_peers(): arrived.append(lax.ppermute(part, 'head', pairs))  3.28 us
  transfers between devices with their start and end apart: 25, of which 10 were waited for; matrix products, arithmetic and copies ran while one was open for 0% of the time, Pallas kernels for 19%

profile of v8, /device:TPU:0, one launch (start us, length us, event | category | flops | bytes accessed | tf_op | source)
XLA Modules:
  0.0 102.5 jit_solution(9862995238611433588)
XLA Ops:
  0.6 0.0 copy-start.3
  0.6 0.0 copy-start.2
  0.7 0.0 copy-start.1
  0.7 0.0 copy-start.4
  0.7 2.8 %pack.3 = (bf16[2,128,1536]{2,1,0:T(8,128)(2,1)}, bf16[2,128,768]{2,1,0:T(8,128)(2,1)}, bf16[2,128,768]{2,1,0:T(8,128)(2,1)}) custom-call(s32[1]{0:T(128)} %bitcast.place_ref, bf16[128,3072]{1,0:T(8,128)(2,1)} %first_ref.3, bf16[128,3072]{1,0:T(8,128)(2,1)} %second_ref.3), custom_call_target="tpu_custom_call" | custom-call | flops 1 | bytes 1 | tf_op jit(solution)/shard_map/pack/pallas_call | solution.py:314
  3.5 0.5 collective-permute-start.2
  4.0 1.8 %collective-permute-start.1 = (bf16[2,128,1536]{2,1,0:T(8,128)(2,1)}, bf16[2,128,1536]{2,1,0:T(8,128)(2,1)S(1)}, u32[]{:S(2)}, u32[]{:S(2)}) collective-permute-start(bf16[2,128,1536]{2,1,0:T(8,128)(2,1)} %get-tuple-element.49.kv_own_ref), channel_id=1, source_target_pairs={{0,0},{2,4},{4,2},{6,8},{8,6},{10,12},{12,10},{14,16},{16,14},{18,... | collective-permute-start | bytes 2359304 | tf_op jit(solution)/shard_map/ppermute | solution.py:347
  5.8 2.5 %collective-permute-start.6 = (bf16[2,128,768]{2,1,0:T(8,128)(2,1)}, bf16[2,128,768]{2,1,0:T(8,128)(2,1)S(1)}, u32[]{:S(2)}, u32[]{:S(2)}) collective-permute-start(bf16[2,128,768]{2,1,0:T(8,128)(2,1)} %get-tuple-element.57), channel_id=1, source_target_pairs={{0,1},{1,0},{2,3},{3,2},{4,5},{5,4},{6,7},{7,6},{8,9},{9,8},{10,11... | collective-permute-start | bytes 1179656 | tf_op jit(solution)/shard_map/ppermute | solution.py:334
  8.4 0.0 collective-permute-start
  8.4 0.3 pack.2
  8.7 8.7 %collective-permute-done.6.kv_ref = bf16[2,128,768]{2,1,0:T(8,128)(2,1)S(1)} collective-permute-done((bf16[2,128,768]{2,1,0:T(8,128)(2,1)}, bf16[2,128,768]{2,1,0:T(8,128)(2,1)S(1)}, u32[]{:S(2)}, u32[]{:S(2)}) %collective-permute-start.6) | collective-permute-done | bytes 393248 | tf_op jit(solution)/shard_map/ppermute | solution.py:334
  17.4 2.4 %collective-permute-start.7 = (bf16[2,128,768]{2,1,0:T(8,128)(2,1)S(1)}, bf16[2,128,768]{2,1,0:T(8,128)(2,1)S(1)}, u32[]{:S(2)}, u32[]{:S(2)}) collective-permute-start(bf16[2,128,768]{2,1,0:T(8,128)(2,1)S(1)} %get-tuple-element.58), channel_id=1, source_target_pairs={{0,1},{1,0},{2,3},{3,2},{4,5},{5,4},{6,7},{7,6},{8,9},{9,8},{10,11... | collective-permute-start | bytes 1179656 | tf_op jit(solution)/shard_map/ppermute | solution.py:334
  19.7 0.7 collective-permute-start.9
  20.4 5.4 %collective-permute-done.kv_ref = bf16[2,128,768]{2,1,0:T(8,128)(2,1)S(1)} collective-permute-done((bf16[2,128,768]{2,1,0:T(8,128)(2,1)}, bf16[2,128,768]{2,1,0:T(8,128)(2,1)S(1)}, u32[]{:S(2)}, u32[]{:S(2)}) %collective-permute-start) | collective-permute-done | bytes 393248 | tf_op jit(solution)/shard_map/ppermute | solution.py:334
  25.8 2.6 %collective-permute-start.8 = (bf16[2,128,768]{2,1,0:T(8,128)(2,1)S(1)}, bf16[2,128,768]{2,1,0:T(8,128)(2,1)S(1)}, u32[]{:S(2)}, u32[]{:S(2)}) collective-permute-start(bf16[2,128,768]{2,1,0:T(8,128)(2,1)S(1)} %collective-permute-done.6.kv_ref), channel_id=1, source_target_pairs={{0,2},{2,0},{4,6},{6,4},{8,10},{10,8},{12,14},{14,12},{16,18},{18,... | collective-permute-start | bytes 1179656 | tf_op jit(solution)/shard_map/ppermute | solution.py:351
  28.4 0.0 collective-permute-done.2.near_own_ref
  28.4 0.7 collective-permute-start.5
  29.1 0.0 collective-permute-done.1.side_own_ref
  29.1 2.8 %collective-permute-start.4 = (bf16[2,128,768]{2,1,0:T(8,128)(2,1)S(1)}, bf16[2,128,768]{2,1,0:T(8,128)(2,1)S(1)}, u32[]{:S(2)}, u32[]{:S(2)}) collective-permute-start(bf16[2,128,768]{2,1,0:T(8,128)(2,1)S(1)} %collective-permute-done.kv_ref), channel_id=1, source_target_pairs={{0,2},{2,0},{4,6},{6,4},{8,10},{10,8},{12,14},{14,12},{16,18},{18,... | collective-permute-start | bytes 1179656 | tf_op jit(solution)/shard_map/ppermute | solution.py:351
  32.0 2.1 %collective-permute-done.7.qo_ref = bf16[2,128,768]{2,1,0:T(8,128)(2,1)S(1)} collective-permute-done((bf16[2,128,768]{2,1,0:T(8,128)(2,1)S(1)}, bf16[2,128,768]{2,1,0:T(8,128)(2,1)S(1)}, u32[]{:S(2)}, u32[]{:S(2)}) %collective-permute-start.7) | collective-permute-done | bytes 393248 | tf_op jit(solution)/shard_map/ppermute | solution.py:334
  34.1 2.5 %collective-permute-start.3 = (bf16[2,128,768]{2,1,0:T(8,128)(2,1)S(1)}, bf16[2,128,768]{2,1,0:T(8,128)(2,1)S(1)}, u32[]{:S(2)}, u32[]{:S(2)}) collective-permute-start(bf16[2,128,768]{2,1,0:T(8,128)(2,1)S(1)} %get-tuple-element.52), channel_id=1, source_target_pairs={{0,1},{1,0},{2,3},{3,2},{4,5},{5,4},{6,7},{7,6},{8,9},{9,8},{10,11... | collective-permute-start | bytes 1179656 | tf_op jit(solution)/shard_map/ppermute | solution.py:334
  36.6 0.0 copy-done.4
  36.6 1.9 %prep.1 = (f32[768,256]{1,0:T(8,128)S(1)}, f32[256,1536]{1,0:T(8,128)S(1)}, bf16[24,256]{1,0:T(8,128)(2,1)S(1)}) custom-call(s32[1]{0:T(128)} %bitcast.place_ref, s32[32,128]{1,0:T(8,128)S(1)} %bitcast.3, s32[1,24]{1,0:T(1,128)S(1)} %bitcast.4, s32[24,24]{1,0:T(8,128)S(1)} %copy-done.5, f32[128,3072]{1,0:T(8,128)S(1)} %copy-done.1), custom_call_target="tpu_custom_call" | custom-call | flops 1 | bytes 1 | tf_op jit(solution)/shard_map/prep/pallas_call | solution.py:359
  38.5 0.0 collective-permute-done.9.side_far_ref
  38.5 0.0 collective-permute-done.8.near_far_ref
  38.5 7.8 %attention.2 = (bf16[2,128,768]{2,1,0:T(8,128)(2,1)S(1)}, f32[2,128,768]{2,1,0:T(8,128)S(1)}, f32[2,128,768]{2,1,0:T(8,128)S(1)}, bf16[2,256,768]{2,1,0:T(8,128)...) custom-call(s32[1]{0:T(128)} %bitcast.place_ref, ...), custom_call_target="tpu_custom_call" | custom-call | flops 1 | bytes 1 | tf_op jit(solution)/shard_map/attention/pallas_call | solution.py:413
  46.3 0.0 collective-permute-done.5.side_far_ref
  46.3 0.0 collective-permute-done.4.near_far_ref
  46.3 0.2 collective-permute-done.3.qo_ref
  46.5 0.7 collective-permute-start.13
  47.2 4.2 %collective-permute-start.20 = (bf16[2,256,768]{2,1,0:T(8,128)(2,1)S(1)}, bf16[2,256,768]{2,1,0:T(8,128)(2,1)S(1)}, u32[]{:S(2)}, u32[]{:S(2)}) collective-permute-start(bf16[2,256,768]{2,1,0:T(8,128)(2,1)S(1)} %get-tuple-element.76), channel_id=1, source_target_pairs={{0,2},{2,0},{4,6},{6,4},{8,10},{10,8},{12,14},{14,12},{16,18},{18,... | collective-permute-start | bytes 2359304 | tf_op jit(solution)/shard_map/ppermute | solution.py:477
  51.4 1.5 %collective-permute-start.14 = (bf16[2,128,768]{2,1,0:T(8,128)(2,1)S(1)}, bf16[2,128,768]{2,1,0:T(8,128)(2,1)S(1)}, u32[]{:S(2)}, u32[]{:S(2)}) collective-permute-start(bf16[2,128,768]{2,1,0:T(8,128)(2,1)S(1)} %get-tuple-element.70), channel_id=1, source_target_pairs={{0,1},{1,0},{2,3},{3,2},{4,5},{5,4},{6,7},{7,6},{8,9},{9,8},{10,11... | collective-permute-start | bytes 1179656 | tf_op jit(solution)/shard_map/ppermute | solution.py:342
  52.9 7.7 %attention.3 = (bf16[2,128,768]{2,1,0:T(8,128)(2,1)S(1)}, f32[2,128,768]{2,1,0:T(8,128)S(1)}, f32[2,128,768]{2,1,0:T(8,128)S(1)}, bf16[2,256,768]{2,1,0:T(8,128)...) custom-call(s32[1]{0:T(128)} %bitcast.place_ref, ...), custom_call_target="tpu_custom_call", output_to_operand_aliasing={{6}: (12, {}), {7}: (13, {}), {8}: (14, {})} | custom-call | flops 1 | bytes 1 | tf_op jit(solution)/shard_map/attention/pallas_call | solution.py:413
  60.7 0.0 collective-permute-start.10
  60.7 2.6 %collective-permute-start.17 = (bf16[24,1536]{1,0:T(8,128)(2,1)S(1)}, bf16[24,1536]{1,0:T(8,128)(2,1)S(1)}, u32[]{:S(2)}, u32[]{:S(2)}) collective-permute-start(bf16[24,1536]{1,0:T(8,128)(2,1)S(1)} %get-tuple-element.72), channel_id=1, source_target_pairs={{0,24},{2,26},{4,28},{6,30},{8,16},{10,18},{12,20},{14,22},{16,8},... | collective-permute-start | bytes 221192 | tf_op jit(solution)/shard_map/ppermute | solution.py:487
  63.3 0.0 collective-permute-done.14.refs_0_
  63.3 1.8 %collective-permute-start.16 = (bf16[24,1536]{1,0:T(8,128)(2,1)S(1)}, bf16[24,1536]{1,0:T(8,128)(2,1)S(1)}, u32[]{:S(2)}, u32[]{:S(2)}) collective-permute-start(bf16[24,1536]{1,0:T(8,128)(2,1)S(1)} %get-tuple-element.72), channel_id=1, source_target_pairs={{0,16},{2,18},{4,20},{6,22},{8,24},{10,26},{12,28},{14,30},{16,0},... | collective-permute-start | bytes 221192 | tf_op jit(solution)/shard_map/ppermute | solution.py:487
  65.1 0.0 collective-permute-done.13.side_ref
  65.1 1.3 %collective-permute-start.15 = (bf16[24,1536]{1,0:T(8,128)(2,1)S(1)}, bf16[24,1536]{1,0:T(8,128)(2,1)S(1)}, u32[]{:S(2)}, u32[]{:S(2)}) collective-permute-start(bf16[24,1536]{1,0:T(8,128)(2,1)S(1)} %get-tuple-element.72), channel_id=1, source_target_pairs={{0,8},{2,10},{4,12},{6,14},{8,0},{10,2},{12,4},{14,6},{16,24},{18,... | collective-permute-start | bytes 221192 | tf_op jit(solution)/shard_map/ppermute | solution.py:487
  66.4 0.0 collective-permute-done.20.near_ref
  66.4 0.7 collective-permute-start.11
  67.1 0.1 far_sum.2
  67.2 0.2 collective-permute-done.17
  67.5 0.8 collective-permute-start.19
  68.3 2.9 %collective-permute-done.16 = bf16[24,1536]{1,0:T(8,128)(2,1)S(1)} collective-permute-done((bf16[24,1536]{1,0:T(8,128)(2,1)S(1)}, bf16[24,1536]{1,0:T(8,128)(2,1)S(1)}, u32[]{:S(2)}, u32[]{:S(2)}) %collective-permute-start.16) | collective-permute-done | bytes 73760 | tf_op jit(solution)/shard_map/ppermute | solution.py:487
  71.1 0.6 collective-permute-start.21
  71.7 0.0 collective-permute-done.15
  71.8 4.7 %collective-permute-start.18 = (bf16[24,1536]{1,0:T(8,128)(2,1)S(1)}, bf16[24,1536]{1,0:T(8,128)(2,1)S(1)}, u32[]{:S(2)}, u32[]{:S(2)}) collective-permute-start(bf16[24,1536]{1,0:T(8,128)(2,1)S(1)} %add_add_fusion), channel_id=1, source_target_pairs={{0,2},{2,0},{4,6},{6,4},{8,10},{10,8},{12,14},{14,12},{16,18},{18,... | collective-permute-start | bytes 221192 | tf_op jit(solution)/shard_map/ppermute | solution.py:487
  76.4 0.9 collective-permute-done.18
  77.4 0.0 collective-permute-done.11.side_ref
  77.4 0.7 collective-permute-start.12
  78.1 0.0 collective-permute-done.19.refs_0_
  78.1 3.3 %collective-permute-done.21.refs_1_ = bf16[2,128,768]{2,1,0:T(8,128)(2,1)S(1)} collective-permute-done((bf16[2,128,768]{2,1,0:T(8,128)(2,1)S(1)}, bf16[2,128,768]{2,1,0:T(8,128)(2,1)S(1)}, u32[]{:S(2)}, u32[]{:S(2)}) %collective-permute-start.21) | collective-permute-done | bytes 393248 | tf_op jit(solution)/shard_map/ppermute | solution.py:342
  81.4 0.0 collective-permute-done.10.near_ref
  81.4 0.1 far_sum.3
  81.5 0.2 collective-permute-start.22
  81.7 12.3 %collective-permute-start.23 = (bf16[24,1536]{1,0:T(8,128)(2,1)S(1)}, bf16[24,1536]{1,0:T(8,128)(2,1)S(1)}, u32[]{:S(2)}, u32[]{:S(2)}) collective-permute-start(bf16[24,1536]{1,0:T(8,128)(2,1)S(1)} %add.22), channel_id=1, source_target_pairs={{0,4},{2,6},{4,0},{6,2},{8,12},{10,14},{12,8},{14,10},{16,20},{18,... | collective-permute-start | bytes 221192 | tf_op jit(solution)/shard_map/ppermute | solution.py:487
  94.0 2.3 %collective-permute-done.23 = bf16[24,1536]{1,0:T(8,128)(2,1)S(1)} collective-permute-done((bf16[24,1536]{1,0:T(8,128)(2,1)S(1)}, bf16[24,1536]{1,0:T(8,128)(2,1)S(1)}, u32[]{:S(2)}, u32[]{:S(2)}) %collective-permute-start.23) | collective-permute-done | bytes 73760 | tf_op jit(solution)/shard_map/ppermute | solution.py:487
  96.4 0.6 collective-permute-start.24
  96.9 1.1 %finish.2 = (bf16[128,3072]{1,0:T(8,128)(2,1)}, bf16[128,3072]{1,0:T(8,128)(2,1)}, bf16[128,3072]{1,0:T(8,128)(2,1)}, bf16[128,3072]{1,0:T(8,128)(2,1)}) custom-call(s32[1]{0:T(128)} %bitcast.place_ref, f32[2,128,768]{2,1,0:T(8,128)S(1)} %get-tuple-element.82.part_ref, ...), custom_call_target="tpu_custom_call", output_to_operand_aliasing={{0}: (6, {}), {1}: (7, {})} | custom-call | flops 1 | bytes 1 | tf_op jit(solution)/shard_map/finish/pallas_call | solution.py:523
  98.0 0.0 collective-permute-done.12.side_ref
  98.0 2.7 %collective-permute-done.24.refs_4_ = bf16[24,1536]{1,0:T(8,128)(2,1)S(1)} collective-permute-done((bf16[24,1536]{1,0:T(8,128)(2,1)S(1)}, bf16[24,1536]{1,0:T(8,128)(2,1)S(1)}, u32[]{:S(2)}, u32[]{:S(2)}) %collective-permute-start.24) | collective-permute-done | bytes 73760 | tf_op jit(solution)/shard_map/ppermute | solution.py:507
  100.8 0.0 collective-permute-done.22.refs_1_
  100.8 1.8 %finish.3 = (bf16[128,3072]{1,0:T(8,128)(2,1)}, bf16[128,3072]{1,0:T(8,128)(2,1)}, bf16[128,3072]{1,0:T(8,128)(2,1)}, bf16[128,3072]{1,0:T(8,128)(2,1)}, f32[128,3072]{1,0:T(8,128)}) custom-call(s32[1]{0:T(128)} %bitcast.place_ref, ...), custom_call_target="tpu_custom_call", output_to_operand_aliasing={{0}: (9, {}), {1}: (10, {}), {2}: (11, {}), {3}: (12, {})} | custom-call | flops 1 | bytes 1 | tf_op jit(solution)/shard_map/finish/pallas_call | solution.py:523
  (12 shorter events, 0.1 us)
Async XLA Ops:
  0.6 7.8 %copy-start.3 = (bf16[128,3072]{1,0:T(8,128)(2,1)S(1)}, bf16[128,3072]{1,0:T(8,128)(2,1)}, u32[]{:S(2)}) copy-start(bf16[128,3072]{1,0:T(8,128)(2,1)} %second_ref.2) | copy-start | bytes 2359300
  0.6 7.7 %copy-start.2 = (bf16[128,3072]{1,0:T(8,128)(2,1)S(1)}, bf16[128,3072]{1,0:T(8,128)(2,1)}, u32[]{:S(2)}) copy-start(bf16[128,3072]{1,0:T(8,128)(2,1)} %first_ref.2) | copy-start | bytes 2359300
  0.7 35.9 %copy-start.1 = (f32[128,3072]{1,0:T(8,128)S(1)}, f32[128,3072]{1,0:T(8,128)}, u32[]{:S(2)}) copy-start(f32[128,3072]{1,0:T(8,128)} %table_ref.1) | copy-start | bytes 4718596
  0.7 35.9 %copy-start.4 = (s32[4096]{0:T(1024)S(1)}, s32[4096]{0:T(1024)}, u32[]{:S(2)}) copy-start(s32[4096]{0:T(1024)} %param.13) | copy-start | bytes 49156
  0.7 35.9 %copy-start.5 = (s32[24,24]{1,0:T(8,128)S(1)}, s32[24,24]{1,0:T(8,128)}, u32[]{:S(2)}) copy-start(s32[24,24]{1,0:T(8,128)} %mask_ref.1) | copy-start | bytes 6916
  0.7 35.9 %copy-start.6 = (s32[24]{0:T(128)S(1)}, s32[24]{0:T(128)}, u32[]{:S(2)}) copy-start(s32[24]{0:T(128)} %param.14) | copy-start | bytes 292
  3.5 24.9 %collective-permute-start.2 = (bf16[2,128,1536]{2,1,0:T(8,128)(2,1)}, bf16[2,128,1536]{2,1,0:T(8,128)(2,1)S(1)}, u32[]{:S(2)}, u32[]{:S(2)}) collective-permute-start(bf16[2,128,1536]{2,1,0:T(8,128)(2,1)} %get-tuple-element.49.kv_own_ref), channel_id=1, source_target_pairs={{0,2},{2,0},{4,6},{6,4},{8,10},{10,8},{12,14},{14,12},{16,18},{18,... | collective-permute-start | bytes 2359304 | tf_op jit(solution)/shard_map/ppermute | solution.py:348
  4.0 25.1 %collective-permute-start.1 = (bf16[2,128,1536]{2,1,0:T(8,128)(2,1)}, bf16[2,128,1536]{2,1,0:T(8,128)(2,1)S(1)}, u32[]{:S(2)}, u32[]{:S(2)}) collective-permute-start(bf16[2,128,1536]{2,1,0:T(8,128)(2,1)} %get-tuple-element.49.kv_own_ref), channel_id=1, source_target_pairs={{0,0},{2,4},{4,2},{6,8},{8,6},{10,12},{12,10},{14,16},{16,14},{18,... | collective-permute-start | bytes 2359304 | tf_op jit(solution)/shard_map/ppermute | solution.py:347
  5.8 11.6 %collective-permute-start.6 = (bf16[2,128,768]{2,1,0:T(8,128)(2,1)}, bf16[2,128,768]{2,1,0:T(8,128)(2,1)S(1)}, u32[]{:S(2)}, u32[]{:S(2)}) collective-permute-start(bf16[2,128,768]{2,1,0:T(8,128)(2,1)} %get-tuple-element.57), channel_id=1, source_target_pairs={{0,1},{1,0},{2,3},{3,2},{4,5},{5,4},{6,7},{7,6},{8,9},{9,8},{10,11... | collective-permute-start | bytes 1179656 | tf_op jit(solution)/shard_map/ppermute | solution.py:334
  8.3 30.2 %copy-start = (bf16[2,128,1536]{2,1,0:T(8,128)(2,1)S(1)}, bf16[2,128,1536]{2,1,0:T(8,128)(2,1)}, u32[]{:S(2)}) copy-start(bf16[2,128,1536]{2,1,0:T(8,128)(2,1)} %get-tuple-element.49.kv_own_ref) | copy-start | bytes 2359300
  8.4 17.4 %collective-permute-start = (bf16[2,128,768]{2,1,0:T(8,128)(2,1)}, bf16[2,128,768]{2,1,0:T(8,128)(2,1)S(1)}, u32[]{:S(2)}, u32[]{:S(2)}) collective-permute-start(bf16[2,128,768]{2,1,0:T(8,128)(2,1)} %get-tuple-element.51), channel_id=1, source_target_pairs={{0,1},{1,0},{2,3},{3,2},{4,5},{5,4},{6,7},{7,6},{8,9},{9,8},{10,11... | collective-permute-start | bytes 1179656 | tf_op jit(solution)/shard_map/ppermute | solution.py:334
  17.4 16.7 %collective-permute-start.7 = (bf16[2,128,768]{2,1,0:T(8,128)(2,1)S(1)}, bf16[2,128,768]{2,1,0:T(8,128)(2,1)S(1)}, u32[]{:S(2)}, u32[]{:S(2)}) collective-permute-start(bf16[2,128,768]{2,1,0:T(8,128)(2,1)S(1)} %get-tuple-element.58), channel_id=1, source_target_pairs={{0,1},{1,0},{2,3},{3,2},{4,5},{5,4},{6,7},{7,6},{8,9},{9,8},{10,11... | collective-permute-start | bytes 1179656 | tf_op jit(solution)/shard_map/ppermute | solution.py:334
  19.7 18.7 %collective-permute-start.9 = (bf16[2,128,768]{2,1,0:T(8,128)(2,1)S(1)}, bf16[2,128,768]{2,1,0:T(8,128)(2,1)S(1)}, u32[]{:S(2)}, u32[]{:S(2)}) collective-permute-start(bf16[2,128,768]{2,1,0:T(8,128)(2,1)S(1)} %collective-permute-done.6.kv_ref), channel_id=1, source_target_pairs={{0,0},{2,4},{4,2},{6,8},{8,6},{10,12},{12,10},{14,16},{16,14},{18,... | collective-permute-start | bytes 1179656 | tf_op jit(solution)/shard_map/ppermute | solution.py:350
  25.8 12.7 %collective-permute-start.8 = (bf16[2,128,768]{2,1,0:T(8,128)(2,1)S(1)}, bf16[2,128,768]{2,1,0:T(8,128)(2,1)S(1)}, u32[]{:S(2)}, u32[]{:S(2)}) collective-permute-start(bf16[2,128,768]{2,1,0:T(8,128)(2,1)S(1)} %collective-permute-done.6.kv_ref), channel_id=1, source_target_pairs={{0,2},{2,0},{4,6},{6,4},{8,10},{10,8},{12,14},{14,12},{16,18},{18,... | collective-permute-start | bytes 1179656 | tf_op jit(solution)/shard_map/ppermute | solution.py:351
  28.4 17.8 %collective-permute-start.5 = (bf16[2,128,768]{2,1,0:T(8,128)(2,1)S(1)}, bf16[2,128,768]{2,1,0:T(8,128)(2,1)S(1)}, u32[]{:S(2)}, u32[]{:S(2)}) collective-permute-start(bf16[2,128,768]{2,1,0:T(8,128)(2,1)S(1)} %collective-permute-done.kv_ref), channel_id=1, source_target_pairs={{0,0},{2,4},{4,2},{6,8},{8,6},{10,12},{12,10},{14,16},{16,14},{18,... | collective-permute-start | bytes 1179656 | tf_op jit(solution)/shard_map/ppermute | solution.py:350
  29.1 17.2 %collective-permute-start.4 = (bf16[2,128,768]{2,1,0:T(8,128)(2,1)S(1)}, bf16[2,128,768]{2,1,0:T(8,128)(2,1)S(1)}, u32[]{:S(2)}, u32[]{:S(2)}) collective-permute-start(bf16[2,128,768]{2,1,0:T(8,128)(2,1)S(1)} %collective-permute-done.kv_ref), channel_id=1, source_target_pairs={{0,2},{2,0},{4,6},{6,4},{8,10},{10,8},{12,14},{14,12},{16,18},{18,... | collective-permute-start | bytes 1179656 | tf_op jit(solution)/shard_map/ppermute | solution.py:351
  34.1 12.4 %collective-permute-start.3 = (bf16[2,128,768]{2,1,0:T(8,128)(2,1)S(1)}, bf16[2,128,768]{2,1,0:T(8,128)(2,1)S(1)}, u32[]{:S(2)}, u32[]{:S(2)}) collective-permute-start(bf16[2,128,768]{2,1,0:T(8,128)(2,1)S(1)} %get-tuple-element.52), channel_id=1, source_target_pairs={{0,1},{1,0},{2,3},{3,2},{4,5},{5,4},{6,7},{7,6},{8,9},{9,8},{10,11... | collective-permute-start | bytes 1179656 | tf_op jit(solution)/shard_map/ppermute | solution.py:334
  46.5 18.6 %collective-permute-start.13 = (bf16[2,256,768]{2,1,0:T(8,128)(2,1)S(1)}, bf16[2,256,768]{2,1,0:T(8,128)(2,1)S(1)}, u32[]{:S(2)}, u32[]{:S(2)}) collective-permute-start(bf16[2,256,768]{2,1,0:T(8,128)(2,1)S(1)} %get-tuple-element.69), channel_id=1, source_target_pairs={{0,0},{2,4},{4,2},{6,8},{8,6},{10,12},{12,10},{14,16},{16,14},{18,... | collective-permute-start | bytes 2359304 | tf_op jit(solution)/shard_map/ppermute | solution.py:476
  47.2 19.2 %collective-permute-start.20 = (bf16[2,256,768]{2,1,0:T(8,128)(2,1)S(1)}, bf16[2,256,768]{2,1,0:T(8,128)(2,1)S(1)}, u32[]{:S(2)}, u32[]{:S(2)}) collective-permute-start(bf16[2,256,768]{2,1,0:T(8,128)(2,1)S(1)} %get-tuple-element.76), channel_id=1, source_target_pairs={{0,2},{2,0},{4,6},{6,4},{8,10},{10,8},{12,14},{14,12},{16,18},{18,... | collective-permute-start | bytes 2359304 | tf_op jit(solution)/shard_map/ppermute | solution.py:477
  51.4 11.8 %collective-permute-start.14 = (bf16[2,128,768]{2,1,0:T(8,128)(2,1)S(1)}, bf16[2,128,768]{2,1,0:T(8,128)(2,1)S(1)}, u32[]{:S(2)}, u32[]{:S(2)}) collective-permute-start(bf16[2,128,768]{2,1,0:T(8,128)(2,1)S(1)} %get-tuple-element.70), channel_id=1, source_target_pairs={{0,1},{1,0},{2,3},{3,2},{4,5},{5,4},{6,7},{7,6},{8,9},{9,8},{10,11... | collective-permute-start | bytes 1179656 | tf_op jit(solution)/shard_map/ppermute | solution.py:342
  60.7 20.7 %collective-permute-start.10 = (bf16[2,256,768]{2,1,0:T(8,128)(2,1)S(1)}, bf16[2,256,768]{2,1,0:T(8,128)(2,1)S(1)}, u32[]{:S(2)}, u32[]{:S(2)}) collective-permute-start(bf16[2,256,768]{2,1,0:T(8,128)(2,1)S(1)} %get-tuple-element.63), channel_id=1, source_target_pairs={{0,2},{2,0},{4,6},{6,4},{8,10},{10,8},{12,14},{14,12},{16,18},{18,... | collective-permute-start | bytes 2359304 | tf_op jit(solution)/shard_map/ppermute | solution.py:477
  60.7 6.8 %collective-permute-start.17 = (bf16[24,1536]{1,0:T(8,128)(2,1)S(1)}, bf16[24,1536]{1,0:T(8,128)(2,1)S(1)}, u32[]{:S(2)}, u32[]{:S(2)}) collective-permute-start(bf16[24,1536]{1,0:T(8,128)(2,1)S(1)} %get-tuple-element.72), channel_id=1, source_target_pairs={{0,24},{2,26},{4,28},{6,30},{8,16},{10,18},{12,20},{14,22},{16,8},... | collective-permute-start | bytes 221192 | tf_op jit(solution)/shard_map/ppermute | solution.py:487
  63.3 7.9 %collective-permute-start.16 = (bf16[24,1536]{1,0:T(8,128)(2,1)S(1)}, bf16[24,1536]{1,0:T(8,128)(2,1)S(1)}, u32[]{:S(2)}, u32[]{:S(2)}) collective-permute-start(bf16[24,1536]{1,0:T(8,128)(2,1)S(1)} %get-tuple-element.72), channel_id=1, source_target_pairs={{0,16},{2,18},{4,20},{6,22},{8,24},{10,26},{12,28},{14,30},{16,0},... | collective-permute-start | bytes 221192 | tf_op jit(solution)/shard_map/ppermute | solution.py:487
  65.1 6.6 %collective-permute-start.15 = (bf16[24,1536]{1,0:T(8,128)(2,1)S(1)}, bf16[24,1536]{1,0:T(8,128)(2,1)S(1)}, u32[]{:S(2)}, u32[]{:S(2)}) collective-permute-start(bf16[24,1536]{1,0:T(8,128)(2,1)S(1)} %get-tuple-element.72), channel_id=1, source_target_pairs={{0,8},{2,10},{4,12},{6,14},{8,0},{10,2},{12,4},{14,6},{16,24},{18,... | collective-permute-start | bytes 221192 | tf_op jit(solution)/shard_map/ppermute | solution.py:487
  66.4 11.0 %collective-permute-start.11 = (bf16[2,128,768]{2,1,0:T(8,128)(2,1)S(1)}, bf16[2,128,768]{2,1,0:T(8,128)(2,1)S(1)}, u32[]{:S(2)}, u32[]{:S(2)}) collective-permute-start(bf16[2,128,768]{2,1,0:T(8,128)(2,1)S(1)} %get-tuple-element.65), channel_id=1, source_target_pairs={{0,0},{2,4},{4,2},{6,8},{8,6},{10,12},{12,10},{14,16},{16,14},{18,... | collective-permute-start | bytes 1179656 | tf_op jit(solution)/shard_map/ppermute | solution.py:476
  67.5 10.6 %collective-permute-start.19 = (bf16[2,128,768]{2,1,0:T(8,128)(2,1)S(1)}, bf16[2,128,768]{2,1,0:T(8,128)(2,1)S(1)}, u32[]{:S(2)}, u32[]{:S(2)}) collective-permute-start(bf16[2,128,768]{2,1,0:T(8,128)(2,1)S(1)} %get-tuple-element.74), channel_id=1, source_target_pairs={{0,1},{1,0},{2,3},{3,2},{4,5},{5,4},{6,7},{7,6},{8,9},{9,8},{10,11... | collective-permute-start | bytes 1179656 | tf_op jit(solution)/shard_map/ppermute | solution.py:342
  71.1 10.2 %collective-permute-start.21 = (bf16[2,128,768]{2,1,0:T(8,128)(2,1)S(1)}, bf16[2,128,768]{2,1,0:T(8,128)(2,1)S(1)}, u32[]{:S(2)}, u32[]{:S(2)}) collective-permute-start(bf16[2,128,768]{2,1,0:T(8,128)(2,1)S(1)} %far_sum.2), channel_id=1, source_target_pairs={{0,1},{1,0},{2,3},{3,2},{4,5},{5,4},{6,7},{7,6},{8,9},{9,8},{10,11... | collective-permute-start | bytes 1179656 | tf_op jit(solution)/shard_map/ppermute | solution.py:342
  71.8 5.6 %collective-permute-start.18 = (bf16[24,1536]{1,0:T(8,128)(2,1)S(1)}, bf16[24,1536]{1,0:T(8,128)(2,1)S(1)}, u32[]{:S(2)}, u32[]{:S(2)}) collective-permute-start(bf16[24,1536]{1,0:T(8,128)(2,1)S(1)} %add_add_fusion), channel_id=1, source_target_pairs={{0,2},{2,0},{4,6},{6,4},{8,10},{10,8},{12,14},{14,12},{16,18},{18,... | collective-permute-start | bytes 221192 | tf_op jit(solution)/shard_map/ppermute | solution.py:487
  77.4 20.6 %collective-permute-start.12 = (bf16[2,128,768]{2,1,0:T(8,128)(2,1)S(1)}, bf16[2,128,768]{2,1,0:T(8,128)(2,1)S(1)}, u32[]{:S(2)}, u32[]{:S(2)}) collective-permute-start(bf16[2,128,768]{2,1,0:T(8,128)(2,1)S(1)} %get-tuple-element.66), channel_id=1, source_target_pairs={{0,0},{2,4},{4,2},{6,8},{8,6},{10,12},{12,10},{14,16},{16,14},{18,... | collective-permute-start | bytes 1179656 | tf_op jit(solution)/shard_map/ppermute | solution.py:483
  81.5 19.3 %collective-permute-start.22 = (bf16[2,128,768]{2,1,0:T(8,128)(2,1)S(1)}, bf16[2,128,768]{2,1,0:T(8,128)(2,1)S(1)}, u32[]{:S(2)}, u32[]{:S(2)}) collective-permute-start(bf16[2,128,768]{2,1,0:T(8,128)(2,1)S(1)} %far_sum.3), channel_id=1, source_target_pairs={{0,1},{1,0},{2,3},{3,2},{4,5},{5,4},{6,7},{7,6},{8,9},{9,8},{10,11... | collective-permute-start | bytes 1179656 | tf_op jit(solution)/shard_map/ppermute | solution.py:342
  81.7 14.6 %collective-permute-start.23 = (bf16[24,1536]{1,0:T(8,128)(2,1)S(1)}, bf16[24,1536]{1,0:T(8,128)(2,1)S(1)}, u32[]{:S(2)}, u32[]{:S(2)}) collective-permute-start(bf16[24,1536]{1,0:T(8,128)(2,1)S(1)} %add.22), channel_id=1, source_target_pairs={{0,4},{2,6},{4,0},{6,2},{8,12},{10,14},{12,8},{14,10},{16,20},{18,... | collective-permute-start | bytes 221192 | tf_op jit(solution)/shard_map/ppermute | solution.py:487
  96.4 4.4 %collective-permute-start.24 = (bf16[24,1536]{1,0:T(8,128)(2,1)S(1)}, bf16[24,1536]{1,0:T(8,128)(2,1)S(1)}, u32[]{:S(2)}, u32[]{:S(2)}) collective-permute-start(bf16[24,1536]{1,0:T(8,128)(2,1)S(1)} %add.23.refs_3_), channel_id=1, source_target_pairs={{0,1},{1,0},{2,3},{3,2},{4,5},{5,4},{6,7},{7,6},{8,9},{9,8},{10,11... | collective-permute-start | bytes 221192 | tf_op jit(solution)/shard_map/ppermute | solution.py:507

commit v9 on v8

--- a/solution.py
+++ b/solution.py
@@ -129,7 +129,11 @@
 
     def work(j, keys, values, blocks):
         at = slice(j * DH, (j + 1) * DH)
-        keys_t, values_t = keys.T, values.T
+        unit = lax.broadcasted_iota(jnp.int32, (DH, DH), 0) == lax.broadcasted_iota(
+            jnp.int32, (DH, DH), 1
+        )
+        unit = unit.astype(bf16)
+        keys_t, values_t = dot(unit, keys, 1, 1).astype(bf16), dot(unit, values, 1, 1).astype(bf16)
         key_grad = value_grad = sums = None
         for number, (q, o, gate, g, scores, prob_grad) in enumerate(blocks):
             start = number * q_size
@@ -467,15 +471,17 @@
         if p + 1 < parts:
             side_grads, *_ = tie((side_grads, side_far[p + 1], near_far[p + 1], qo_far[p + 1]))
         if p > 0:
-            back, side_back_far, back_far = tie(
-                (back, side_back_far, back_far)
+            side_grads, side_back_far, back_far = tie(
+                (side_grads, side_back_far, back_far)
             )
-            summed(p - 1)
         own.append(own_part)
         far.append(far_part)
         side_back_far.append(lax.ppermute(side_grads[-1], "ctx", side_pairs))
         near_back.append(lax.ppermute(near_grad, "ctx", near_pairs))
         back_far.append(from_peers(back))
+        if p > 0:
+            side_back_far[p - 1], _ = tie((side_back_far[p - 1], back_far[p]))
+            summed(p - 1)
         if p + 1 < parts:
             side_back_own.append(side_back_far[p])
             continue

time: 104 us -> 107 us (1.029)
  waiting for transfers between devices: 28.8 us -> 38.8 us
  starting transfers between devices: 49.2 us -> 41.5 us
  Pallas kernels: 23.5 us -> 25.1 us
    ppermute x5, starting transfers between devices: 22.7 us -> 11.6 us  [shifted(): return lax.ppermute(array, 'ctx', [(i, i ^ step) for i in range(ctx_count)])]
    ppermute x4, waiting for transfers between devices: 3.28 us -> 11.3 us  [from_peers(): arrived.append(lax.ppermute(part, 'head', pairs))]
    ppermute x4, starting transfers between devices: 3.11 us -> 6.18 us  [from_peers(): arrived.append(lax.ppermute(part, 'head', pairs))]
    ppermute x5, waiting for transfers between devices: 6.32 us -> 8.57 us  [shifted(): return lax.ppermute(array, 'ctx', [(i, i ^ step) for i in range(ctx_count)])]
    pallas_call x2, Pallas kernels: 15.5 us -> 17 us  [attention(): pl.pallas_call(functools.partial(attention_kernel, rows=rows, tokens=toke...]
where the time goes in v9:
time: 107 us; the launch traced here: 106 us
  starting transfers between devices  41.5 us (39%)
  waiting for transfers between devices  38.8 us (36%)
  Pallas kernels  25.1 us (23%)
    pallas_call x2, Pallas kernels, attention(): pl.pallas_call(functools.partial(attention_kernel, rows=rows, tokens=toke...  17 us
    ppermute x4, waiting for transfers between devices, to_peers(): arrived.append(lax.ppermute(part, 'head', pairs))  16.2 us
    ppermute x5, starting transfers between devices, shifted(): return lax.ppermute(array, 'ctx', [(i, i ^ step) for i in range(ctx_count)])  11.6 us
    ppermute x4, waiting for transfers between devices, from_peers(): arrived.append(lax.ppermute(part, 'head', pairs))  11.3 us
    ppermute x5, waiting for transfers between devices, shifted(): return lax.ppermute(array, 'ctx', [(i, i ^ step) for i in range(ctx_count)])  8.57 us
    ppermute x4, starting transfers between devices, to_peers(): arrived.append(lax.ppermute(part, 'head', pairs))  7.43 us
    ppermute x4, starting transfers between devices, from_peers(): arrived.append(lax.ppermute(part, 'head', pairs))  6.18 us
    ppermute x2, starting transfers between devices, per_device(): near_far = [lax.ppermute(slab, 'ctx', near_pairs) for slab in kv_far]  5.48 us
  transfers between devices with their start and end apart: 25, of which 10 were waited for; matrix products, arithmetic and copies ran while one was open for 0% of the time, Pallas kernels for 19%

profile of v9, /device:TPU:0, one launch (start us, length us, event | category | flops | bytes accessed | tf_op | source)
XLA Modules:
  0.0 106.3 jit_solution(13019596501749436847)
XLA Ops:
  0.6 0.0 copy-start.3
  0.6 0.0 copy-start.2
  0.7 2.8 %pack.3 = (bf16[2,128,1536]{2,1,0:T(8,128)(2,1)}, bf16[2,128,768]{2,1,0:T(8,128)(2,1)}, bf16[2,128,768]{2,1,0:T(8,128)(2,1)}) custom-call(s32[1]{0:T(128)} %bitcast.place_ref, bf16[128,3072]{1,0:T(8,128)(2,1)} %first_ref.3, bf16[128,3072]{1,0:T(8,128)(2,1)} %second_ref.3), custom_call_target="tpu_custom_call" | custom-call | flops 1 | bytes 1 | tf_op jit(solution)/shard_map/pack/pallas_call | solution.py:318
  3.5 0.5 collective-permute-start.2
  4.0 1.8 %collective-permute-start.1 = (bf16[2,128,1536]{2,1,0:T(8,128)(2,1)}, bf16[2,128,1536]{2,1,0:T(8,128)(2,1)S(1)}, u32[]{:S(2)}, u32[]{:S(2)}) collective-permute-start(bf16[2,128,1536]{2,1,0:T(8,128)(2,1)} %get-tuple-element.51.kv_own_ref), channel_id=1, source_target_pairs={{0,0},{2,4},{4,2},{6,8},{8,6},{10,12},{12,10},{14,16},{16,14},{18,... | collective-permute-start | bytes 2359304 | tf_op jit(solution)/shard_map/ppermute | solution.py:351
  5.8 2.5 %collective-permute-start.6 = (bf16[2,128,768]{2,1,0:T(8,128)(2,1)}, bf16[2,128,768]{2,1,0:T(8,128)(2,1)S(1)}, u32[]{:S(2)}, u32[]{:S(2)}) collective-permute-start(bf16[2,128,768]{2,1,0:T(8,128)(2,1)} %get-tuple-element.59), channel_id=1, source_target_pairs={{0,1},{1,0},{2,3},{3,2},{4,5},{5,4},{6,7},{7,6},{8,9},{9,8},{10,11... | collective-permute-start | bytes 1179656 | tf_op jit(solution)/shard_map/ppermute | solution.py:338
  8.4 0.0 collective-permute-start
  8.4 0.0 copy-done.3
  8.4 0.3 pack.2
  8.7 8.7 %collective-permute-done.6.kv_ref = bf16[2,128,768]{2,1,0:T(8,128)(2,1)S(1)} collective-permute-done((bf16[2,128,768]{2,1,0:T(8,128)(2,1)}, bf16[2,128,768]{2,1,0:T(8,128)(2,1)S(1)}, u32[]{:S(2)}, u32[]{:S(2)}) %collective-permute-start.6) | collective-permute-done | bytes 393248 | tf_op jit(solution)/shard_map/ppermute | solution.py:338
  17.4 2.4 %collective-permute-start.7 = (bf16[2,128,768]{2,1,0:T(8,128)(2,1)S(1)}, bf16[2,128,768]{2,1,0:T(8,128)(2,1)S(1)}, u32[]{:S(2)}, u32[]{:S(2)}) collective-permute-start(bf16[2,128,768]{2,1,0:T(8,128)(2,1)S(1)} %get-tuple-element.60), channel_id=1, source_target_pairs={{0,1},{1,0},{2,3},{3,2},{4,5},{5,4},{6,7},{7,6},{8,9},{9,8},{10,11... | collective-permute-start | bytes 1179656 | tf_op jit(solution)/shard_map/ppermute | solution.py:338
  19.7 0.7 collective-permute-start.9
  20.4 5.4 %collective-permute-done.kv_ref = bf16[2,128,768]{2,1,0:T(8,128)(2,1)S(1)} collective-permute-done((bf16[2,128,768]{2,1,0:T(8,128)(2,1)}, bf16[2,128,768]{2,1,0:T(8,128)(2,1)S(1)}, u32[]{:S(2)}, u32[]{:S(2)}) %collective-permute-start) | collective-permute-done | bytes 393248 | tf_op jit(solution)/shard_map/ppermute | solution.py:338
  25.8 2.6 %collective-permute-start.8 = (bf16[2,128,768]{2,1,0:T(8,128)(2,1)S(1)}, bf16[2,128,768]{2,1,0:T(8,128)(2,1)S(1)}, u32[]{:S(2)}, u32[]{:S(2)}) collective-permute-start(bf16[2,128,768]{2,1,0:T(8,128)(2,1)S(1)} %collective-permute-done.6.kv_ref), channel_id=1, source_target_pairs={{0,2},{2,0},{4,6},{6,4},{8,10},{10,8},{12,14},{14,12},{16,18},{18,... | collective-permute-start | bytes 1179656 | tf_op jit(solution)/shard_map/ppermute | solution.py:355
  28.4 0.0 collective-permute-done.2.near_own_ref
  28.4 0.7 collective-permute-start.5
  29.1 0.0 collective-permute-done.1.side_own_ref
  29.1 2.8 %collective-permute-start.4 = (bf16[2,128,768]{2,1,0:T(8,128)(2,1)S(1)}, bf16[2,128,768]{2,1,0:T(8,128)(2,1)S(1)}, u32[]{:S(2)}, u32[]{:S(2)}) collective-permute-start(bf16[2,128,768]{2,1,0:T(8,128)(2,1)S(1)} %collective-permute-done.kv_ref), channel_id=1, source_target_pairs={{0,2},{2,0},{4,6},{6,4},{8,10},{10,8},{12,14},{14,12},{16,18},{18,... | collective-permute-start | bytes 1179656 | tf_op jit(solution)/shard_map/ppermute | solution.py:355
  32.0 2.1 %collective-permute-done.7.qo_ref = bf16[2,128,768]{2,1,0:T(8,128)(2,1)S(1)} collective-permute-done((bf16[2,128,768]{2,1,0:T(8,128)(2,1)S(1)}, bf16[2,128,768]{2,1,0:T(8,128)(2,1)S(1)}, u32[]{:S(2)}, u32[]{:S(2)}) %collective-permute-start.7) | collective-permute-done | bytes 393248 | tf_op jit(solution)/shard_map/ppermute | solution.py:338
  34.1 2.5 %collective-permute-start.3 = (bf16[2,128,768]{2,1,0:T(8,128)(2,1)S(1)}, bf16[2,128,768]{2,1,0:T(8,128)(2,1)S(1)}, u32[]{:S(2)}, u32[]{:S(2)}) collective-permute-start(bf16[2,128,768]{2,1,0:T(8,128)(2,1)S(1)} %get-tuple-element.54), channel_id=1, source_target_pairs={{0,1},{1,0},{2,3},{3,2},{4,5},{5,4},{6,7},{7,6},{8,9},{9,8},{10,11... | collective-permute-start | bytes 1179656 | tf_op jit(solution)/shard_map/ppermute | solution.py:338
  36.6 0.0 copy-done.5
  36.6 1.9 %prep.1 = (f32[768,256]{1,0:T(8,128)S(1)}, f32[256,1536]{1,0:T(8,128)S(1)}, bf16[24,256]{1,0:T(8,128)(2,1)S(1)}) custom-call(s32[1]{0:T(128)} %bitcast.place_ref, s32[32,128]{1,0:T(8,128)S(1)} %bitcast.3, s32[1,24]{1,0:T(1,128)S(1)} %bitcast.4, s32[24,24]{1,0:T(8,128)S(1)} %copy-done.5, f32[128,3072]{1,0:T(8,128)S(1)} %copy-done.1), custom_call_target="tpu_custom_call" | custom-call | flops 1 | bytes 1 | tf_op jit(solution)/shard_map/prep/pallas_call | solution.py:363
  38.5 0.0 collective-permute-done.9.side_far_ref
  38.5 0.0 collective-permute-done.8.near_far_ref
  38.5 0.0 copy-done
  38.5 8.5 %attention.2 = (bf16[2,128,768]{2,1,0:T(8,128)(2,1)S(1)}, f32[2,128,768]{2,1,0:T(8,128)S(1)}, f32[2,128,768]{2,1,0:T(8,128)S(1)}, bf16[2,256,768]{2,1,0:T(8,128)...) custom-call(s32[1]{0:T(128)} %bitcast.place_ref, ...), custom_call_target="tpu_custom_call" | custom-call | flops 1 | bytes 1 | tf_op jit(solution)/shard_map/attention/pallas_call | solution.py:417
  47.1 0.0 collective-permute-done.5.side_far_ref
  47.1 0.0 collective-permute-done.4.near_far_ref
  47.1 0.0 collective-permute-done.3.qo_ref
  47.1 0.7 collective-permute-start.11
  47.8 4.4 %collective-permute-start.20 = (bf16[2,256,768]{2,1,0:T(8,128)(2,1)S(1)}, bf16[2,256,768]{2,1,0:T(8,128)(2,1)S(1)}, u32[]{:S(2)}, u32[]{:S(2)}) collective-permute-start(bf16[2,256,768]{2,1,0:T(8,128)(2,1)S(1)} %get-tuple-element.80), channel_id=1, source_target_pairs={{0,2},{2,0},{4,6},{6,4},{8,10},{10,8},{12,14},{14,12},{16,18},{18,... | collective-permute-start | bytes 2359304 | tf_op jit(solution)/shard_map/ppermute | solution.py:480
  52.2 1.1 %collective-permute-start.12 = (bf16[2,128,768]{2,1,0:T(8,128)(2,1)S(1)}, bf16[2,128,768]{2,1,0:T(8,128)(2,1)S(1)}, u32[]{:S(2)}, u32[]{:S(2)}) collective-permute-start(bf16[2,128,768]{2,1,0:T(8,128)(2,1)S(1)} %get-tuple-element.70), channel_id=1, source_target_pairs={{0,1},{1,0},{2,3},{3,2},{4,5},{5,4},{6,7},{7,6},{8,9},{9,8},{10,11... | collective-permute-start | bytes 1179656 | tf_op jit(solution)/shard_map/ppermute | solution.py:346
  53.3 8.5 %attention.3 = (bf16[2,128,768]{2,1,0:T(8,128)(2,1)S(1)}, f32[2,128,768]{2,1,0:T(8,128)S(1)}, f32[2,128,768]{2,1,0:T(8,128)S(1)}, bf16[2,256,768]{2,1,0:T(8,128)...) custom-call(s32[1]{0:T(128)} %bitcast.place_ref, ...), custom_call_target="tpu_custom_call", output_to_operand_aliasing={{6}: (12, {}), {7}: (13, {}), {8}: (14, {})} | custom-call | flops 1 | bytes 1 | tf_op jit(solution)/shard_map/attention/pallas_call | solution.py:417
  61.8 1.0 collective-permute-start.15
  62.7 0.0 collective-permute-start.10
  62.7 0.6 collective-permute-done.12.refs_0_
  63.3 3.3 %collective-permute-start.18 = (bf16[24,1536]{1,0:T(8,128)(2,1)S(1)}, bf16[24,1536]{1,0:T(8,128)(2,1)S(1)}, u32[]{:S(2)}, u32[]{:S(2)}) collective-permute-start(bf16[24,1536]{1,0:T(8,128)(2,1)S(1)} %get-tuple-element.77), channel_id=1, source_target_pairs={{0,24},{2,26},{4,28},{6,30},{8,16},{10,18},{12,20},{14,22},{16,8},... | collective-permute-start | bytes 221192 | tf_op jit(solution)/shard_map/ppermute | solution.py:493
  66.6 5.9 %collective-permute-done.15.refs_0_ = bf16[2,128,768]{2,1,0:T(8,128)(2,1)S(1)} collective-permute-done((bf16[2,128,768]{2,1,0:T(8,128)(2,1)S(1)}, bf16[2,128,768]{2,1,0:T(8,128)(2,1)S(1)}, u32[]{:S(2)}, u32[]{:S(2)}) %collective-permute-start.15) | collective-permute-done | bytes 393248 | tf_op jit(solution)/shard_map/ppermute | solution.py:346
  72.6 2.6 %collective-permute-start.17 = (bf16[24,1536]{1,0:T(8,128)(2,1)S(1)}, bf16[24,1536]{1,0:T(8,128)(2,1)S(1)}, u32[]{:S(2)}, u32[]{:S(2)}) collective-permute-start(bf16[24,1536]{1,0:T(8,128)(2,1)S(1)} %get-tuple-element.77), channel_id=1, source_target_pairs={{0,16},{2,18},{4,20},{6,22},{8,24},{10,26},{12,28},{14,30},{16,0},... | collective-permute-start | bytes 221192 | tf_op jit(solution)/shard_map/ppermute | solution.py:493
  75.2 0.0 collective-permute-done.11.side_ref
  75.2 0.7 collective-permute-start.16
  75.9 0.0 collective-permute-done.20.near_ref
  75.9 0.7 collective-permute-start.13
  76.6 0.1 far_sum.2
  76.7 0.0 collective-permute-done.18
  76.7 1.6 %collective-permute-start.21 = (bf16[2,128,768]{2,1,0:T(8,128)(2,1)S(1)}, bf16[2,128,768]{2,1,0:T(8,128)(2,1)S(1)}, u32[]{:S(2)}, u32[]{:S(2)}) collective-permute-start(bf16[2,128,768]{2,1,0:T(8,128)(2,1)S(1)} %far_sum.2), channel_id=1, source_target_pairs={{0,1},{1,0},{2,3},{3,2},{4,5},{5,4},{6,7},{7,6},{8,9},{9,8},{10,11... | collective-permute-start | bytes 1179656 | tf_op jit(solution)/shard_map/ppermute | solution.py:346
  78.3 0.0 collective-permute-done.17
  78.3 1.2 %collective-permute-done.16 = bf16[24,1536]{1,0:T(8,128)(2,1)S(1)} collective-permute-done((bf16[24,1536]{1,0:T(8,128)(2,1)S(1)}, bf16[24,1536]{1,0:T(8,128)(2,1)S(1)}, u32[]{:S(2)}, u32[]{:S(2)}) %collective-permute-start.16) | collective-permute-done | bytes 73760 | tf_op jit(solution)/shard_map/ppermute | solution.py:493
  79.5 0.7 collective-permute-start.19
  80.3 0.9 collective-permute-done.19
  81.2 0.0 collective-permute-done.13.side_ref
  81.2 0.7 collective-permute-start.14
  81.9 4.8 %collective-permute-done.21.refs_1_ = bf16[2,128,768]{2,1,0:T(8,128)(2,1)S(1)} collective-permute-done((bf16[2,128,768]{2,1,0:T(8,128)(2,1)S(1)}, bf16[2,128,768]{2,1,0:T(8,128)(2,1)S(1)}, u32[]{:S(2)}, u32[]{:S(2)}) %collective-permute-start.21) | collective-permute-done | bytes 393248 | tf_op jit(solution)/shard_map/ppermute | solution.py:346
  86.7 0.0 collective-permute-done.10.near_ref
  86.7 0.1 far_sum.3
  86.8 2.5 %collective-permute-start.22 = (bf16[2,128,768]{2,1,0:T(8,128)(2,1)S(1)}, bf16[2,128,768]{2,1,0:T(8,128)(2,1)S(1)}, u32[]{:S(2)}, u32[]{:S(2)}) collective-permute-start(bf16[2,128,768]{2,1,0:T(8,128)(2,1)S(1)} %far_sum.3), channel_id=1, source_target_pairs={{0,1},{1,0},{2,3},{3,2},{4,5},{5,4},{6,7},{7,6},{8,9},{9,8},{10,11... | collective-permute-start | bytes 1179656 | tf_op jit(solution)/shard_map/ppermute | solution.py:346
  89.4 4.3 %collective-permute-start.23 = (bf16[24,1536]{1,0:T(8,128)(2,1)S(1)}, bf16[24,1536]{1,0:T(8,128)(2,1)S(1)}, u32[]{:S(2)}, u32[]{:S(2)}) collective-permute-start(bf16[24,1536]{1,0:T(8,128)(2,1)S(1)} %add.22), channel_id=1, source_target_pairs={{0,4},{2,6},{4,0},{6,2},{8,12},{10,14},{12,8},{14,10},{16,20},{18,... | collective-permute-start | bytes 221192 | tf_op jit(solution)/shard_map/ppermute | solution.py:493
  93.6 6.5 %collective-permute-done.23 = bf16[24,1536]{1,0:T(8,128)(2,1)S(1)} collective-permute-done((bf16[24,1536]{1,0:T(8,128)(2,1)S(1)}, bf16[24,1536]{1,0:T(8,128)(2,1)S(1)}, u32[]{:S(2)}, u32[]{:S(2)}) %collective-permute-start.23) | collective-permute-done | bytes 73760 | tf_op jit(solution)/shard_map/ppermute | solution.py:493
  100.1 0.7 collective-permute-start.24
  100.8 1.1 %finish.2 = (bf16[128,3072]{1,0:T(8,128)(2,1)}, bf16[128,3072]{1,0:T(8,128)(2,1)}, bf16[128,3072]{1,0:T(8,128)(2,1)}, bf16[128,3072]{1,0:T(8,128)(2,1)}) custom-call(s32[1]{0:T(128)} %bitcast.place_ref, f32[2,128,768]{2,1,0:T(8,128)S(1)} %get-tuple-element.86.part_ref, ...), custom_call_target="tpu_custom_call", output_to_operand_aliasing={{0}: (6, {}), {1}: (7, {})} | custom-call | flops 1 | bytes 1 | tf_op jit(solution)/shard_map/finish/pallas_call | solution.py:529
  101.9 2.7 %collective-permute-done.24.refs_4_ = bf16[24,1536]{1,0:T(8,128)(2,1)S(1)} collective-permute-done((bf16[24,1536]{1,0:T(8,128)(2,1)S(1)}, bf16[24,1536]{1,0:T(8,128)(2,1)S(1)}, u32[]{:S(2)}, u32[]{:S(2)}) %collective-permute-start.24) | collective-permute-done | bytes 73760 | tf_op jit(solution)/shard_map/ppermute | solution.py:513
  104.5 0.0 collective-permute-done.14.side_ref
  104.5 0.0 collective-permute-done.22.refs_1_
  104.5 1.8 %finish.3 = (bf16[128,3072]{1,0:T(8,128)(2,1)}, bf16[128,3072]{1,0:T(8,128)(2,1)}, bf16[128,3072]{1,0:T(8,128)(2,1)}, bf16[128,3072]{1,0:T(8,128)(2,1)}, f32[128,3072]{1,0:T(8,128)}) custom-call(s32[1]{0:T(128)} %bitcast.place_ref, ...), custom_call_target="tpu_custom_call", output_to_operand_aliasing={{0}: (9, {}), {1}: (10, {}), {2}: (11, {}), {3}: (12, {})} | custom-call | flops 1 | bytes 1 | tf_op jit(solution)/shard_map/finish/pallas_call | solution.py:529
  (12 shorter events, 0.1 us)
Async XLA Ops:
  0.6 7.8 %copy-start.3 = (bf16[128,3072]{1,0:T(8,128)(2,1)S(1)}, bf16[128,3072]{1,0:T(8,128)(2,1)}, u32[]{:S(2)}) copy-start(bf16[128,3072]{1,0:T(8,128)(2,1)} %second_ref.2) | copy-start | bytes 2359300
  0.6 7.7 %copy-start.2 = (bf16[128,3072]{1,0:T(8,128)(2,1)S(1)}, bf16[128,3072]{1,0:T(8,128)(2,1)}, u32[]{:S(2)}) copy-start(bf16[128,3072]{1,0:T(8,128)(2,1)} %first_ref.2) | copy-start | bytes 2359300
  0.7 35.9 %copy-start.1 = (f32[128,3072]{1,0:T(8,128)S(1)}, f32[128,3072]{1,0:T(8,128)}, u32[]{:S(2)}) copy-start(f32[128,3072]{1,0:T(8,128)} %table_ref.1) | copy-start | bytes 4718596
  0.7 35.9 %copy-start.4 = (s32[4096]{0:T(1024)S(1)}, s32[4096]{0:T(1024)}, u32[]{:S(2)}) copy-start(s32[4096]{0:T(1024)} %param.13) | copy-start | bytes 49156
  0.7 35.9 %copy-start.5 = (s32[24,24]{1,0:T(8,128)S(1)}, s32[24,24]{1,0:T(8,128)}, u32[]{:S(2)}) copy-start(s32[24,24]{1,0:T(8,128)} %mask_ref.1) | copy-start | bytes 6916
  0.7 35.9 %copy-start.6 = (s32[24]{0:T(128)S(1)}, s32[24]{0:T(128)}, u32[]{:S(2)}) copy-start(s32[24]{0:T(128)} %param.14) | copy-start | bytes 292
  3.5 24.9 %collective-permute-start.2 = (bf16[2,128,1536]{2,1,0:T(8,128)(2,1)}, bf16[2,128,1536]{2,1,0:T(8,128)(2,1)S(1)}, u32[]{:S(2)}, u32[]{:S(2)}) collective-permute-start(bf16[2,128,1536]{2,1,0:T(8,128)(2,1)} %get-tuple-element.51.kv_own_ref), channel_id=1, source_target_pairs={{0,2},{2,0},{4,6},{6,4},{8,10},{10,8},{12,14},{14,12},{16,18},{18,... | collective-permute-start | bytes 2359304 | tf_op jit(solution)/shard_map/ppermute | solution.py:352
  4.0 25.1 %collective-permute-start.1 = (bf16[2,128,1536]{2,1,0:T(8,128)(2,1)}, bf16[2,128,1536]{2,1,0:T(8,128)(2,1)S(1)}, u32[]{:S(2)}, u32[]{:S(2)}) collective-permute-start(bf16[2,128,1536]{2,1,0:T(8,128)(2,1)} %get-tuple-element.51.kv_own_ref), channel_id=1, source_target_pairs={{0,0},{2,4},{4,2},{6,8},{8,6},{10,12},{12,10},{14,16},{16,14},{18,... | collective-permute-start | bytes 2359304 | tf_op jit(solution)/shard_map/ppermute | solution.py:351
  5.8 11.6 %collective-permute-start.6 = (bf16[2,128,768]{2,1,0:T(8,128)(2,1)}, bf16[2,128,768]{2,1,0:T(8,128)(2,1)S(1)}, u32[]{:S(2)}, u32[]{:S(2)}) collective-permute-start(bf16[2,128,768]{2,1,0:T(8,128)(2,1)} %get-tuple-element.59), channel_id=1, source_target_pairs={{0,1},{1,0},{2,3},{3,2},{4,5},{5,4},{6,7},{7,6},{8,9},{9,8},{10,11... | collective-permute-start | bytes 1179656 | tf_op jit(solution)/shard_map/ppermute | solution.py:338
  8.3 30.2 %copy-start = (bf16[2,128,1536]{2,1,0:T(8,128)(2,1)S(1)}, bf16[2,128,1536]{2,1,0:T(8,128)(2,1)}, u32[]{:S(2)}) copy-start(bf16[2,128,1536]{2,1,0:T(8,128)(2,1)} %get-tuple-element.51.kv_own_ref) | copy-start | bytes 2359300
  8.4 17.4 %collective-permute-start = (bf16[2,128,768]{2,1,0:T(8,128)(2,1)}, bf16[2,128,768]{2,1,0:T(8,128)(2,1)S(1)}, u32[]{:S(2)}, u32[]{:S(2)}) collective-permute-start(bf16[2,128,768]{2,1,0:T(8,128)(2,1)} %get-tuple-element.53), channel_id=1, source_target_pairs={{0,1},{1,0},{2,3},{3,2},{4,5},{5,4},{6,7},{7,6},{8,9},{9,8},{10,11... | collective-permute-start | bytes 1179656 | tf_op jit(solution)/shard_map/ppermute | solution.py:338
  17.4 16.7 %collective-permute-start.7 = (bf16[2,128,768]{2,1,0:T(8,128)(2,1)S(1)}, bf16[2,128,768]{2,1,0:T(8,128)(2,1)S(1)}, u32[]{:S(2)}, u32[]{:S(2)}) collective-permute-start(bf16[2,128,768]{2,1,0:T(8,128)(2,1)S(1)} %get-tuple-element.60), channel_id=1, source_target_pairs={{0,1},{1,0},{2,3},{3,2},{4,5},{5,4},{6,7},{7,6},{8,9},{9,8},{10,11... | collective-permute-start | bytes 1179656 | tf_op jit(solution)/shard_map/ppermute | solution.py:338
  19.7 18.7 %collective-permute-start.9 = (bf16[2,128,768]{2,1,0:T(8,128)(2,1)S(1)}, bf16[2,128,768]{2,1,0:T(8,128)(2,1)S(1)}, u32[]{:S(2)}, u32[]{:S(2)}) collective-permute-start(bf16[2,128,768]{2,1,0:T(8,128)(2,1)S(1)} %collective-permute-done.6.kv_ref), channel_id=1, source_target_pairs={{0,0},{2,4},{4,2},{6,8},{8,6},{10,12},{12,10},{14,16},{16,14},{18,... | collective-permute-start | bytes 1179656 | tf_op jit(solution)/shard_map/ppermute | solution.py:354
  25.8 12.7 %collective-permute-start.8 = (bf16[2,128,768]{2,1,0:T(8,128)(2,1)S(1)}, bf16[2,128,768]{2,1,0:T(8,128)(2,1)S(1)}, u32[]{:S(2)}, u32[]{:S(2)}) collective-permute-start(bf16[2,128,768]{2,1,0:T(8,128)(2,1)S(1)} %collective-permute-done.6.kv_ref), channel_id=1, source_target_pairs={{0,2},{2,0},{4,6},{6,4},{8,10},{10,8},{12,14},{14,12},{16,18},{18,... | collective-permute-start | bytes 1179656 | tf_op jit(solution)/shard_map/ppermute | solution.py:355
  28.4 18.6 %collective-permute-start.5 = (bf16[2,128,768]{2,1,0:T(8,128)(2,1)S(1)}, bf16[2,128,768]{2,1,0:T(8,128)(2,1)S(1)}, u32[]{:S(2)}, u32[]{:S(2)}) collective-permute-start(bf16[2,128,768]{2,1,0:T(8,128)(2,1)S(1)} %collective-permute-done.kv_ref), channel_id=1, source_target_pairs={{0,0},{2,4},{4,2},{6,8},{8,6},{10,12},{12,10},{14,16},{16,14},{18,... | collective-permute-start | bytes 1179656 | tf_op jit(solution)/shard_map/ppermute | solution.py:354
  29.1 17.9 %collective-permute-start.4 = (bf16[2,128,768]{2,1,0:T(8,128)(2,1)S(1)}, bf16[2,128,768]{2,1,0:T(8,128)(2,1)S(1)}, u32[]{:S(2)}, u32[]{:S(2)}) collective-permute-start(bf16[2,128,768]{2,1,0:T(8,128)(2,1)S(1)} %collective-permute-done.kv_ref), channel_id=1, source_target_pairs={{0,2},{2,0},{4,6},{6,4},{8,10},{10,8},{12,14},{14,12},{16,18},{18,... | collective-permute-start | bytes 1179656 | tf_op jit(solution)/shard_map/ppermute | solution.py:355
  34.1 12.9 %collective-permute-start.3 = (bf16[2,128,768]{2,1,0:T(8,128)(2,1)S(1)}, bf16[2,128,768]{2,1,0:T(8,128)(2,1)S(1)}, u32[]{:S(2)}, u32[]{:S(2)}) collective-permute-start(bf16[2,128,768]{2,1,0:T(8,128)(2,1)S(1)} %get-tuple-element.54), channel_id=1, source_target_pairs={{0,1},{1,0},{2,3},{3,2},{4,5},{5,4},{6,7},{7,6},{8,9},{9,8},{10,11... | collective-permute-start | bytes 1179656 | tf_op jit(solution)/shard_map/ppermute | solution.py:338
  47.1 28.1 %collective-permute-start.11 = (bf16[2,256,768]{2,1,0:T(8,128)(2,1)S(1)}, bf16[2,256,768]{2,1,0:T(8,128)(2,1)S(1)}, u32[]{:S(2)}, u32[]{:S(2)}) collective-permute-start(bf16[2,256,768]{2,1,0:T(8,128)(2,1)S(1)} %get-tuple-element.69), channel_id=1, source_target_pairs={{0,0},{2,4},{4,2},{6,8},{8,6},{10,12},{12,10},{14,16},{16,14},{18,... | collective-permute-start | bytes 2359304 | tf_op jit(solution)/shard_map/ppermute | solution.py:479
  47.8 28.1 %collective-permute-start.20 = (bf16[2,256,768]{2,1,0:T(8,128)(2,1)S(1)}, bf16[2,256,768]{2,1,0:T(8,128)(2,1)S(1)}, u32[]{:S(2)}, u32[]{:S(2)}) collective-permute-start(bf16[2,256,768]{2,1,0:T(8,128)(2,1)S(1)} %get-tuple-element.80), channel_id=1, source_target_pairs={{0,2},{2,0},{4,6},{6,4},{8,10},{10,8},{12,14},{14,12},{16,18},{18,... | collective-permute-start | bytes 2359304 | tf_op jit(solution)/shard_map/ppermute | solution.py:480
  52.2 11.1 %collective-permute-start.12 = (bf16[2,128,768]{2,1,0:T(8,128)(2,1)S(1)}, bf16[2,128,768]{2,1,0:T(8,128)(2,1)S(1)}, u32[]{:S(2)}, u32[]{:S(2)}) collective-permute-start(bf16[2,128,768]{2,1,0:T(8,128)(2,1)S(1)} %get-tuple-element.70), channel_id=1, source_target_pairs={{0,1},{1,0},{2,3},{3,2},{4,5},{5,4},{6,7},{7,6},{8,9},{9,8},{10,11... | collective-permute-start | bytes 1179656 | tf_op jit(solution)/shard_map/ppermute | solution.py:346
  61.8 10.8 %collective-permute-start.15 = (bf16[2,128,768]{2,1,0:T(8,128)(2,1)S(1)}, bf16[2,128,768]{2,1,0:T(8,128)(2,1)S(1)}, u32[]{:S(2)}, u32[]{:S(2)}) collective-permute-start(bf16[2,128,768]{2,1,0:T(8,128)(2,1)S(1)} %get-tuple-element.75), channel_id=1, source_target_pairs={{0,1},{1,0},{2,3},{3,2},{4,5},{5,4},{6,7},{7,6},{8,9},{9,8},{10,11... | collective-permute-start | bytes 1179656 | tf_op jit(solution)/shard_map/ppermute | solution.py:346
  62.7 24.0 %collective-permute-start.10 = (bf16[2,256,768]{2,1,0:T(8,128)(2,1)S(1)}, bf16[2,256,768]{2,1,0:T(8,128)(2,1)S(1)}, u32[]{:S(2)}, u32[]{:S(2)}) collective-permute-start(bf16[2,256,768]{2,1,0:T(8,128)(2,1)S(1)} %get-tuple-element.65), channel_id=1, source_target_pairs={{0,2},{2,0},{4,6},{6,4},{8,10},{10,8},{12,14},{14,12},{16,18},{18,... | collective-permute-start | bytes 2359304 | tf_op jit(solution)/shard_map/ppermute | solution.py:480
  63.3 13.4 %collective-permute-start.18 = (bf16[24,1536]{1,0:T(8,128)(2,1)S(1)}, bf16[24,1536]{1,0:T(8,128)(2,1)S(1)}, u32[]{:S(2)}, u32[]{:S(2)}) collective-permute-start(bf16[24,1536]{1,0:T(8,128)(2,1)S(1)} %get-tuple-element.77), channel_id=1, source_target_pairs={{0,24},{2,26},{4,28},{6,30},{8,16},{10,18},{12,20},{14,22},{16,8},... | collective-permute-start | bytes 221192 | tf_op jit(solution)/shard_map/ppermute | solution.py:493
  72.6 5.8 %collective-permute-start.17 = (bf16[24,1536]{1,0:T(8,128)(2,1)S(1)}, bf16[24,1536]{1,0:T(8,128)(2,1)S(1)}, u32[]{:S(2)}, u32[]{:S(2)}) collective-permute-start(bf16[24,1536]{1,0:T(8,128)(2,1)S(1)} %get-tuple-element.77), channel_id=1, source_target_pairs={{0,16},{2,18},{4,20},{6,22},{8,24},{10,26},{12,28},{14,30},{16,0},... | collective-permute-start | bytes 221192 | tf_op jit(solution)/shard_map/ppermute | solution.py:493
  75.2 4.4 %collective-permute-start.16 = (bf16[24,1536]{1,0:T(8,128)(2,1)S(1)}, bf16[24,1536]{1,0:T(8,128)(2,1)S(1)}, u32[]{:S(2)}, u32[]{:S(2)}) collective-permute-start(bf16[24,1536]{1,0:T(8,128)(2,1)S(1)} %get-tuple-element.77), channel_id=1, source_target_pairs={{0,8},{2,10},{4,12},{6,14},{8,0},{10,2},{12,4},{14,6},{16,24},{18,... | collective-permute-start | bytes 221192 | tf_op jit(solution)/shard_map/ppermute | solution.py:493
  75.9 5.3 %collective-permute-start.13 = (bf16[2,128,768]{2,1,0:T(8,128)(2,1)S(1)}, bf16[2,128,768]{2,1,0:T(8,128)(2,1)S(1)}, u32[]{:S(2)}, u32[]{:S(2)}) collective-permute-start(bf16[2,128,768]{2,1,0:T(8,128)(2,1)S(1)} %get-tuple-element.72), channel_id=1, source_target_pairs={{0,0},{2,4},{4,2},{6,8},{8,6},{10,12},{12,10},{14,16},{16,14},{18,... | collective-permute-start | bytes 1179656 | tf_op jit(solution)/shard_map/ppermute | solution.py:479
  76.7 9.9 %collective-permute-start.21 = (bf16[2,128,768]{2,1,0:T(8,128)(2,1)S(1)}, bf16[2,128,768]{2,1,0:T(8,128)(2,1)S(1)}, u32[]{:S(2)}, u32[]{:S(2)}) collective-permute-start(bf16[2,128,768]{2,1,0:T(8,128)(2,1)S(1)} %far_sum.2), channel_id=1, source_target_pairs={{0,1},{1,0},{2,3},{3,2},{4,5},{5,4},{6,7},{7,6},{8,9},{9,8},{10,11... | collective-permute-start | bytes 1179656 | tf_op jit(solution)/shard_map/ppermute | solution.py:346
  79.5 1.6 %collective-permute-start.19 = (bf16[24,1536]{1,0:T(8,128)(2,1)S(1)}, bf16[24,1536]{1,0:T(8,128)(2,1)S(1)}, u32[]{:S(2)}, u32[]{:S(2)}) collective-permute-start(bf16[24,1536]{1,0:T(8,128)(2,1)S(1)} %add_add_fusion), channel_id=1, source_target_pairs={{0,2},{2,0},{4,6},{6,4},{8,10},{10,8},{12,14},{14,12},{16,18},{18,... | collective-permute-start | bytes 221192 | tf_op jit(solution)/shard_map/ppermute | solution.py:493
  81.2 23.3 %collective-permute-start.14 = (bf16[2,128,768]{2,1,0:T(8,128)(2,1)S(1)}, bf16[2,128,768]{2,1,0:T(8,128)(2,1)S(1)}, u32[]{:S(2)}, u32[]{:S(2)}) collective-permute-start(bf16[2,128,768]{2,1,0:T(8,128)(2,1)S(1)} %get-tuple-element.73), channel_id=1, source_target_pairs={{0,0},{2,4},{4,2},{6,8},{8,6},{10,12},{12,10},{14,16},{16,14},{18,... | collective-permute-start | bytes 1179656 | tf_op jit(solution)/shard_map/ppermute | solution.py:489
  86.8 17.7 %collective-permute-start.22 = (bf16[2,128,768]{2,1,0:T(8,128)(2,1)S(1)}, bf16[2,128,768]{2,1,0:T(8,128)(2,1)S(1)}, u32[]{:S(2)}, u32[]{:S(2)}) collective-permute-start(bf16[2,128,768]{2,1,0:T(8,128)(2,1)S(1)} %far_sum.3), channel_id=1, source_target_pairs={{0,1},{1,0},{2,3},{3,2},{4,5},{5,4},{6,7},{7,6},{8,9},{9,8},{10,11... | collective-permute-start | bytes 1179656 | tf_op jit(solution)/shard_map/ppermute | solution.py:346
  89.4 10.7 %collective-permute-start.23 = (bf16[24,1536]{1,0:T(8,128)(2,1)S(1)}, bf16[24,1536]{1,0:T(8,128)(2,1)S(1)}, u32[]{:S(2)}, u32[]{:S(2)}) collective-permute-start(bf16[24,1536]{1,0:T(8,128)(2,1)S(1)} %add.22), channel_id=1, source_target_pairs={{0,4},{2,6},{4,0},{6,2},{8,12},{10,14},{12,8},{14,10},{16,20},{18,... | collective-permute-start | bytes 221192 | tf_op jit(solution)/shard_map/ppermute | solution.py:493
  100.1 4.4 %collective-permute-start.24 = (bf16[24,1536]{1,0:T(8,128)(2,1)S(1)}, bf16[24,1536]{1,0:T(8,128)(2,1)S(1)}, u32[]{:S(2)}, u32[]{:S(2)}) collective-permute-start(bf16[24,1536]{1,0:T(8,128)(2,1)S(1)} %add.23.refs_3_), channel_id=1, source_target_pairs={{0,1},{1,0},{2,3},{3,2},{4,5},{5,4},{6,7},{7,6},{8,9},{9,8},{10,11... | collective-permute-start | bytes 221192 | tf_op jit(solution)/shard_map/ppermute | solution.py:513

commit v10 on v8

--- a/solution.py
+++ b/solution.py
@@ -171,11 +171,7 @@
                 back_ref[0, start - rows : start - rows + q_size, at] = mixed
                 back_ref[1, start - rows : start - rows + q_size, at] = query_grad
             dk, dv = dot(score_grad, q, 1, 0), dot(low, g, 1, 0)
-            product = o * attended
-            high = product.astype(bf16)
-            rest = (product - high.astype(f32)).astype(bf16)
-            both = dot(slot_ref[:, span], jnp.concatenate([high, rest], axis=1), 1, 0)
-            part = both[:, :DH] + both[:, DH:]
+            part = dot(slot_ref[:, span], (o * attended).astype(bf16), 1, 0)
             key_grad = dk if key_grad is None else key_grad + dk
             value_grad = dv if value_grad is None else value_grad + dv
             sums = part if sums is None else sums + part
@@ -446,6 +442,19 @@
             name="attention",
         )(place, *inputs, *joint)
 
+    def shifted(array, step):
+        return lax.ppermute(array, "ctx", [(i, i ^ step) for i in range(ctx_count)])
+
+    def rounds(steps, sums):
+        for one, two in zip(steps[::2], [*steps[1::2], None]):
+            if two is None:
+                sums = sums + shifted(sums, one)
+                continue
+            across = [shifted(sums, step) for step in (one, two, one ^ two)]
+            sums = (sums + across[0]) + (across[1] + across[2])
+        return sums
+
+    bits = [1 << n for n in range(ctx_count.bit_length() - 1)]
     def summed(p):
         far_grad = pl.pallas_call(
             far_sum_kernel,
@@ -467,36 +476,29 @@
         if p + 1 < parts:
             side_grads, *_ = tie((side_grads, side_far[p + 1], near_far[p + 1], qo_far[p + 1]))
         if p > 0:
-            back, side_back_far, back_far = tie(
-                (back, side_back_far, back_far)
+            side_grads, side_back_far = tie(
+                (side_grads, side_back_far)
             )
-            summed(p - 1)
+            joint, back_far = tie((joint, back_far))
         own.append(own_part)
         far.append(far_part)
         side_back_far.append(lax.ppermute(side_grads[-1], "ctx", side_pairs))
         near_back.append(lax.ppermute(near_grad, "ctx", near_pairs))
         back_far.append(from_peers(back))
+        if p > 0:
+            sums = rounds(bits[2:], joint[2])
+            side_back_far[p - 1], sums, _ = tie((side_back_far[p - 1], sums, back_far[p]))
+            summed(p - 1)
         if p + 1 < parts:
             side_back_own.append(side_back_far[p])
             continue
         side_grad_own, _ = tie((side_grads[0], side_back_far[p]))
         side_back_own.append(lax.ppermute(side_grad_own, "ctx", side_pairs))
-    mixed, query_grad, sums = joint
-
-    def shifted(array, step):
-        return lax.ppermute(array, "ctx", [(i, i ^ step) for i in range(ctx_count)])
-
-    def rounds(steps, sums):
-        for one, two in zip(steps[::2], [*steps[1::2], None]):
-            if two is None:
-                sums = sums + shifted(sums, one)
-                continue
-            across = [shifted(sums, step) for step in (one, two, one ^ two)]
-            sums = (sums + across[0]) + (across[1] + across[2])
-        return sums
-
-    bits = [1 << n for n in range(ctx_count.bit_length() - 1)]
-    sums = rounds(bits[:1], rounds(bits[2:], sums))
+    mixed, query_grad = joint[:2]
+    if parts == 1:
+        sums = rounds(bits[2:], joint[2])
+
+    sums = rounds(bits[:1], sums)
     side_back_far, sums, back_far, grad_far = tie((side_back_far, sums, back_far, grad_far))
     summed(parts - 1)
 

time: 104 us -> 102 us (0.981); the launches traced: 103 us -> 102 us
  starting transfers between devices: 49.2 us -> 35.3 us
  waiting for transfers between devices: 28.8 us -> 41.7 us
    ppermute x5, starting transfers between devices: 22.7 us -> 5.44 us  [shifted(): return lax.ppermute(array, 'ctx', [(i, i ^ step) for i in range(ctx_count)])]
    ppermute x4, waiting for transfers between devices: 3.28 us -> 10.7 us  [from_peers(): arrived.append(lax.ppermute(part, 'head', pairs))]
    ppermute x5, waiting for transfers between devices: 6.32 us -> 11.6 us  [shifted(): return lax.ppermute(array, 'ctx', [(i, i ^ step) for i in range(ctx_count)])]
    ppermute x4, starting transfers between devices: 3.11 us -> 4.85 us  [from_peers(): arrived.append(lax.ppermute(part, 'head', pairs))]
    ppermute x2, starting transfers between devices: 4.22 us -> 5.35 us  [per_device(): near_back.append(lax.ppermute(near_grad, 'ctx', near_pairs))]
  transfers between devices with their start and end apart: 25 -> 25, of which waited for: 10 -> 11; matrix products, arithmetic and copies ran while one was open for 0% -> 0% of each run, Pallas kernels for 19% -> 19%
where the time goes in v10:
time: 102 us
  waiting for transfers between devices  41.7 us (41%)
  starting transfers between devices  35.3 us (35%)
  Pallas kernels  23.6 us (23%)
    ppermute x4, waiting for transfers between devices, to_peers(): arrived.append(lax.ppermute(part, 'head', pairs))  16.4 us
    pallas_call x2, Pallas kernels, attention(): pl.pallas_call(functools.partial(attention_kernel, rows=rows, tokens=toke...  15.6 us
    ppermute x5, waiting for transfers between devices, shifted(): return lax.ppermute(array, 'ctx', [(i, i ^ step) for i in range(ctx_count)])  11.6 us
    ppermute x4, waiting for transfers between devices, from_peers(): arrived.append(lax.ppermute(part, 'head', pairs))  10.7 us
    ppermute x4, starting transfers between devices, to_peers(): arrived.append(lax.ppermute(part, 'head', pairs))  7.43 us
    ppermute x2, starting transfers between devices, per_device(): near_far = [lax.ppermute(slab, 'ctx', near_pairs) for slab in kv_far]  5.48 us
    ppermute x5, starting transfers between devices, shifted(): return lax.ppermute(array, 'ctx', [(i, i ^ step) for i in range(ctx_count)])  5.44 us
    ppermute x2, starting transfers between devices, per_device(): near_back.append(lax.ppermute(near_grad, 'ctx', near_pairs))  5.35 us
  transfers between devices with their start and end apart: 25, of which 11 were waited for; matrix products, arithmetic and copies ran while one was open for 0% of the time, Pallas kernels for 19%

profile of v10, /device:TPU:0, one launch (start us, length us, event | category | flops | bytes accessed | tf_op | source)
XLA Modules:
  0.0 101.6 jit_solution(4909908946048731518)
XLA Ops:
  0.6 0.0 copy-start.3
  0.6 0.0 copy-start.2
  0.7 0.0 copy-start.1
  0.7 2.8 %pack.3 = (bf16[2,128,1536]{2,1,0:T(8,128)(2,1)}, bf16[2,128,768]{2,1,0:T(8,128)(2,1)}, bf16[2,128,768]{2,1,0:T(8,128)(2,1)}) custom-call(s32[1]{0:T(128)} %bitcast.place_ref, bf16[128,3072]{1,0:T(8,128)(2,1)} %first_ref.3, bf16[128,3072]{1,0:T(8,128)(2,1)} %second_ref.3), custom_call_target="tpu_custom_call" | custom-call | flops 1 | bytes 1 | tf_op jit(solution)/shard_map/pack/pallas_call | solution.py:310
  3.5 0.5 collective-permute-start.2
  4.0 1.8 %collective-permute-start.1 = (bf16[2,128,1536]{2,1,0:T(8,128)(2,1)}, bf16[2,128,1536]{2,1,0:T(8,128)(2,1)S(1)}, u32[]{:S(2)}, u32[]{:S(2)}) collective-permute-start(bf16[2,128,1536]{2,1,0:T(8,128)(2,1)} %get-tuple-element.55.kv_own_ref), channel_id=1, source_target_pairs={{0,0},{2,4},{4,2},{6,8},{8,6},{10,12},{12,10},{14,16},{16,14},{18,... | collective-permute-start | bytes 2359304 | tf_op jit(solution)/shard_map/ppermute | solution.py:343
  5.8 2.5 %collective-permute-start.6 = (bf16[2,128,768]{2,1,0:T(8,128)(2,1)}, bf16[2,128,768]{2,1,0:T(8,128)(2,1)S(1)}, u32[]{:S(2)}, u32[]{:S(2)}) collective-permute-start(bf16[2,128,768]{2,1,0:T(8,128)(2,1)} %get-tuple-element.63), channel_id=1, source_target_pairs={{0,1},{1,0},{2,3},{3,2},{4,5},{5,4},{6,7},{7,6},{8,9},{9,8},{10,11... | collective-permute-start | bytes 1179656 | tf_op jit(solution)/shard_map/ppermute | solution.py:330
  8.4 0.0 collective-permute-start
  8.4 0.3 pack.2
  8.7 8.7 %collective-permute-done.6.kv_ref = bf16[2,128,768]{2,1,0:T(8,128)(2,1)S(1)} collective-permute-done((bf16[2,128,768]{2,1,0:T(8,128)(2,1)}, bf16[2,128,768]{2,1,0:T(8,128)(2,1)S(1)}, u32[]{:S(2)}, u32[]{:S(2)}) %collective-permute-start.6) | collective-permute-done | bytes 393248 | tf_op jit(solution)/shard_map/ppermute | solution.py:330
  17.4 2.4 %collective-permute-start.7 = (bf16[2,128,768]{2,1,0:T(8,128)(2,1)S(1)}, bf16[2,128,768]{2,1,0:T(8,128)(2,1)S(1)}, u32[]{:S(2)}, u32[]{:S(2)}) collective-permute-start(bf16[2,128,768]{2,1,0:T(8,128)(2,1)S(1)} %get-tuple-element.64), channel_id=1, source_target_pairs={{0,1},{1,0},{2,3},{3,2},{4,5},{5,4},{6,7},{7,6},{8,9},{9,8},{10,11... | collective-permute-start | bytes 1179656 | tf_op jit(solution)/shard_map/ppermute | solution.py:330
  19.7 0.7 collective-permute-start.9
  20.4 5.4 %collective-permute-done.kv_ref = bf16[2,128,768]{2,1,0:T(8,128)(2,1)S(1)} collective-permute-done((bf16[2,128,768]{2,1,0:T(8,128)(2,1)}, bf16[2,128,768]{2,1,0:T(8,128)(2,1)S(1)}, u32[]{:S(2)}, u32[]{:S(2)}) %collective-permute-start) | collective-permute-done | bytes 393248 | tf_op jit(solution)/shard_map/ppermute | solution.py:330
  25.8 2.6 %collective-permute-start.8 = (bf16[2,128,768]{2,1,0:T(8,128)(2,1)S(1)}, bf16[2,128,768]{2,1,0:T(8,128)(2,1)S(1)}, u32[]{:S(2)}, u32[]{:S(2)}) collective-permute-start(bf16[2,128,768]{2,1,0:T(8,128)(2,1)S(1)} %collective-permute-done.6.kv_ref), channel_id=1, source_target_pairs={{0,2},{2,0},{4,6},{6,4},{8,10},{10,8},{12,14},{14,12},{16,18},{18,... | collective-permute-start | bytes 1179656 | tf_op jit(solution)/shard_map/ppermute | solution.py:347
  28.4 0.0 collective-permute-done.2.near_own_ref
  28.4 0.7 collective-permute-start.5
  29.1 0.0 collective-permute-done.1.side_own_ref
  29.1 2.8 %collective-permute-start.4 = (bf16[2,128,768]{2,1,0:T(8,128)(2,1)S(1)}, bf16[2,128,768]{2,1,0:T(8,128)(2,1)S(1)}, u32[]{:S(2)}, u32[]{:S(2)}) collective-permute-start(bf16[2,128,768]{2,1,0:T(8,128)(2,1)S(1)} %collective-permute-done.kv_ref), channel_id=1, source_target_pairs={{0,2},{2,0},{4,6},{6,4},{8,10},{10,8},{12,14},{14,12},{16,18},{18,... | collective-permute-start | bytes 1179656 | tf_op jit(solution)/shard_map/ppermute | solution.py:347
  32.0 2.1 %collective-permute-done.7.qo_ref = bf16[2,128,768]{2,1,0:T(8,128)(2,1)S(1)} collective-permute-done((bf16[2,128,768]{2,1,0:T(8,128)(2,1)S(1)}, bf16[2,128,768]{2,1,0:T(8,128)(2,1)S(1)}, u32[]{:S(2)}, u32[]{:S(2)}) %collective-permute-start.7) | collective-permute-done | bytes 393248 | tf_op jit(solution)/shard_map/ppermute | solution.py:330
  34.1 2.5 %collective-permute-start.3 = (bf16[2,128,768]{2,1,0:T(8,128)(2,1)S(1)}, bf16[2,128,768]{2,1,0:T(8,128)(2,1)S(1)}, u32[]{:S(2)}, u32[]{:S(2)}) collective-permute-start(bf16[2,128,768]{2,1,0:T(8,128)(2,1)S(1)} %get-tuple-element.58), channel_id=1, source_target_pairs={{0,1},{1,0},{2,3},{3,2},{4,5},{5,4},{6,7},{7,6},{8,9},{9,8},{10,11... | collective-permute-start | bytes 1179656 | tf_op jit(solution)/shard_map/ppermute | solution.py:330
  36.6 0.0 copy-done.1
  36.6 0.0 copy-done.5
  36.6 1.9 %prep.1 = (f32[768,256]{1,0:T(8,128)S(1)}, f32[256,1536]{1,0:T(8,128)S(1)}, bf16[24,256]{1,0:T(8,128)(2,1)S(1)}) custom-call(s32[1]{0:T(128)} %bitcast.place_ref, s32[32,128]{1,0:T(8,128)S(1)} %bitcast.3, s32[1,24]{1,0:T(1,128)S(1)} %bitcast.4, s32[24,24]{1,0:T(8,128)S(1)} %copy-done.5, f32[128,3072]{1,0:T(8,128)S(1)} %copy-done.1), custom_call_target="tpu_custom_call" | custom-call | flops 1 | bytes 1 | tf_op jit(solution)/shard_map/prep/pallas_call | solution.py:355
  38.5 0.0 collective-permute-done.9.side_far_ref
  38.5 0.0 collective-permute-done.8.near_far_ref
  38.5 7.8 %attention.2 = (bf16[2,128,768]{2,1,0:T(8,128)(2,1)S(1)}, f32[2,128,768]{2,1,0:T(8,128)S(1)}, f32[2,128,768]{2,1,0:T(8,128)S(1)}, bf16[2,256,768]{2,1,0:T(8,128)...) custom-call(s32[1]{0:T(128)} %bitcast.place_ref, ...), custom_call_target="tpu_custom_call" | custom-call | flops 1 | bytes 1 | tf_op jit(solution)/shard_map/attention/pallas_call | solution.py:409
  46.3 0.0 collective-permute-start.14
  46.4 0.0 collective-permute-done.5.side_far_ref
  46.4 0.0 collective-permute-done.4.near_far_ref
  46.4 0.1 collective-permute-done.3.qo_ref
  46.5 0.7 collective-permute-start.11
  47.2 5.3 %collective-permute-start.20 = (bf16[2,256,768]{2,1,0:T(8,128)(2,1)S(1)}, bf16[2,256,768]{2,1,0:T(8,128)(2,1)S(1)}, u32[]{:S(2)}, u32[]{:S(2)}) collective-permute-start(bf16[2,256,768]{2,1,0:T(8,128)(2,1)S(1)} %get-tuple-element.88), channel_id=1, source_target_pairs={{0,2},{2,0},{4,6},{6,4},{8,10},{10,8},{12,14},{14,12},{16,18},{18,... | collective-permute-start | bytes 2359304 | tf_op jit(solution)/shard_map/ppermute | solution.py:486
  52.6 7.8 %attention.3 = (bf16[2,128,768]{2,1,0:T(8,128)(2,1)S(1)}, f32[2,128,768]{2,1,0:T(8,128)S(1)}, f32[2,128,768]{2,1,0:T(8,128)S(1)}, bf16[2,256,768]{2,1,0:T(8,128)...) custom-call(s32[1]{0:T(128)} %bitcast.place_ref, ...), custom_call_target="tpu_custom_call", output_to_operand_aliasing={{6}: (12, {}), {7}: (13, {}), {8}: (14, {})} | custom-call | flops 1 | bytes 1 | tf_op jit(solution)/shard_map/attention/pallas_call | solution.py:409
  60.3 0.0 collective-permute-done.14.refs_0_
  60.4 2.3 %collective-permute-start.17 = (bf16[24,1536]{1,0:T(8,128)(2,1)S(1)}, bf16[24,1536]{1,0:T(8,128)(2,1)S(1)}, u32[]{:S(2)}, u32[]{:S(2)}) collective-permute-start(bf16[24,1536]{1,0:T(8,128)(2,1)S(1)} %get-tuple-element.82), channel_id=1, source_target_pairs={{0,24},{2,26},{4,28},{6,30},{8,16},{10,18},{12,20},{14,22},{16,8},... | collective-permute-start | bytes 221192 | tf_op jit(solution)/shard_map/ppermute | solution.py:446
  62.7 0.7 collective-permute-start.16
  63.4 1.3 %collective-permute-start.15 = (bf16[24,1536]{1,0:T(8,128)(2,1)S(1)}, bf16[24,1536]{1,0:T(8,128)(2,1)S(1)}, u32[]{:S(2)}, u32[]{:S(2)}) collective-permute-start(bf16[24,1536]{1,0:T(8,128)(2,1)S(1)} %get-tuple-element.82), channel_id=1, source_target_pairs={{0,8},{2,10},{4,12},{6,14},{8,0},{10,2},{12,4},{14,6},{16,24},{18,... | collective-permute-start | bytes 221192 | tf_op jit(solution)/shard_map/ppermute | solution.py:446
  64.7 2.2 %collective-permute-done.17 = bf16[24,1536]{1,0:T(8,128)(2,1)S(1)} collective-permute-done((bf16[24,1536]{1,0:T(8,128)(2,1)S(1)}, bf16[24,1536]{1,0:T(8,128)(2,1)S(1)}, u32[]{:S(2)}, u32[]{:S(2)}) %collective-permute-start.17) | collective-permute-done | bytes 73760 | tf_op jit(solution)/shard_map/ppermute | solution.py:446
  66.9 1.3 %collective-permute-start.18 = (bf16[2,128,768]{2,1,0:T(8,128)(2,1)S(1)}, bf16[2,128,768]{2,1,0:T(8,128)(2,1)S(1)}, u32[]{:S(2)}, u32[]{:S(2)}) collective-permute-start(bf16[2,128,768]{2,1,0:T(8,128)(2,1)S(1)} %get-tuple-element.83), channel_id=1, source_target_pairs={{0,1},{1,0},{2,3},{3,2},{4,5},{5,4},{6,7},{7,6},{8,9},{9,8},{10,11... | collective-permute-start | bytes 1179656 | tf_op jit(solution)/shard_map/ppermute | solution.py:338
  68.2 2.1 %collective-permute-done.16 = bf16[24,1536]{1,0:T(8,128)(2,1)S(1)} collective-permute-done((bf16[24,1536]{1,0:T(8,128)(2,1)S(1)}, bf16[24,1536]{1,0:T(8,128)(2,1)S(1)}, u32[]{:S(2)}, u32[]{:S(2)}) %collective-permute-start.16) | collective-permute-done | bytes 73760 | tf_op jit(solution)/shard_map/ppermute | solution.py:446
  70.3 0.0 collective-permute-start.10
  70.3 0.0 collective-permute-done.15
  70.4 0.0 collective-permute-done.11.side_ref
  70.4 0.7 collective-permute-start.12
  71.1 5.4 %collective-permute-done.18.refs_0_ = bf16[2,128,768]{2,1,0:T(8,128)(2,1)S(1)} collective-permute-done((bf16[2,128,768]{2,1,0:T(8,128)(2,1)S(1)}, bf16[2,128,768]{2,1,0:T(8,128)(2,1)S(1)}, u32[]{:S(2)}, u32[]{:S(2)}) %collective-permute-start.18) | collective-permute-done | bytes 393248 | tf_op jit(solution)/shard_map/ppermute | solution.py:338
  76.5 0.0 collective-permute-done.20.near_ref
  76.5 0.1 far_sum.2
  76.7 1.7 %collective-permute-start.21 = (bf16[2,128,768]{2,1,0:T(8,128)(2,1)S(1)}, bf16[2,128,768]{2,1,0:T(8,128)(2,1)S(1)}, u32[]{:S(2)}, u32[]{:S(2)}) collective-permute-start(bf16[2,128,768]{2,1,0:T(8,128)(2,1)S(1)} %far_sum.2), channel_id=1, source_target_pairs={{0,1},{1,0},{2,3},{3,2},{4,5},{5,4},{6,7},{7,6},{8,9},{9,8},{10,11... | collective-permute-start | bytes 1179656 | tf_op jit(solution)/shard_map/ppermute | solution.py:338
  78.3 0.0 collective-permute-start.19
  78.3 1.3 %collective-permute-done.19 = bf16[24,1536]{1,0:T(8,128)(2,1)S(1)} collective-permute-done((bf16[24,1536]{1,0:T(8,128)(2,1)S(1)}, bf16[24,1536]{1,0:T(8,128)(2,1)S(1)}, u32[]{:S(2)}, u32[]{:S(2)}) %collective-permute-start.19) | collective-permute-done | bytes 73760 | tf_op jit(solution)/shard_map/ppermute | solution.py:446
  79.6 0.0 collective-permute-done.12.side_ref
  79.6 0.7 collective-permute-start.13
  80.3 5.2 %collective-permute-done.21.refs_1_ = bf16[2,128,768]{2,1,0:T(8,128)(2,1)S(1)} collective-permute-done((bf16[2,128,768]{2,1,0:T(8,128)(2,1)S(1)}, bf16[2,128,768]{2,1,0:T(8,128)(2,1)S(1)}, u32[]{:S(2)}, u32[]{:S(2)}) %collective-permute-start.21) | collective-permute-done | bytes 393248 | tf_op jit(solution)/shard_map/ppermute | solution.py:338
  85.6 0.0 collective-permute-done.10.near_ref
  85.6 0.1 far_sum.3
  85.7 1.8 %collective-permute-start.22 = (bf16[2,128,768]{2,1,0:T(8,128)(2,1)S(1)}, bf16[2,128,768]{2,1,0:T(8,128)(2,1)S(1)}, u32[]{:S(2)}, u32[]{:S(2)}) collective-permute-start(bf16[2,128,768]{2,1,0:T(8,128)(2,1)S(1)} %far_sum.3), channel_id=1, source_target_pairs={{0,1},{1,0},{2,3},{3,2},{4,5},{5,4},{6,7},{7,6},{8,9},{9,8},{10,11... | collective-permute-start | bytes 1179656 | tf_op jit(solution)/shard_map/ppermute | solution.py:338
  87.5 1.0 %collective-permute-start.23 = (bf16[24,1536]{1,0:T(8,128)(2,1)S(1)}, bf16[24,1536]{1,0:T(8,128)(2,1)S(1)}, u32[]{:S(2)}, u32[]{:S(2)}) collective-permute-start(bf16[24,1536]{1,0:T(8,128)(2,1)S(1)} %add.22), channel_id=1, source_target_pairs={{0,4},{2,6},{4,0},{6,2},{8,12},{10,14},{12,8},{14,10},{16,20},{18,... | collective-permute-start | bytes 221192 | tf_op jit(solution)/shard_map/ppermute | solution.py:446
  88.6 6.1 %collective-permute-done.23 = bf16[24,1536]{1,0:T(8,128)(2,1)S(1)} collective-permute-done((bf16[24,1536]{1,0:T(8,128)(2,1)S(1)}, bf16[24,1536]{1,0:T(8,128)(2,1)S(1)}, u32[]{:S(2)}, u32[]{:S(2)}) %collective-permute-start.23) | collective-permute-done | bytes 73760 | tf_op jit(solution)/shard_map/ppermute | solution.py:446
  94.7 1.1 %collective-permute-start.24 = (bf16[24,1536]{1,0:T(8,128)(2,1)S(1)}, bf16[24,1536]{1,0:T(8,128)(2,1)S(1)}, u32[]{:S(2)}, u32[]{:S(2)}) collective-permute-start(bf16[24,1536]{1,0:T(8,128)(2,1)S(1)} %add.23.refs_3_), channel_id=1, source_target_pairs={{0,1},{1,0},{2,3},{3,2},{4,5},{5,4},{6,7},{7,6},{8,9},{9,8},{10,11... | collective-permute-start | bytes 221192 | tf_op jit(solution)/shard_map/ppermute | solution.py:509
  95.8 1.1 %finish.2 = (bf16[128,3072]{1,0:T(8,128)(2,1)}, bf16[128,3072]{1,0:T(8,128)(2,1)}, bf16[128,3072]{1,0:T(8,128)(2,1)}, bf16[128,3072]{1,0:T(8,128)(2,1)}) custom-call(s32[1]{0:T(128)} %bitcast.place_ref, f32[2,128,768]{2,1,0:T(8,128)S(1)} %get-tuple-element.94.part_ref, ...), custom_call_target="tpu_custom_call", output_to_operand_aliasing={{0}: (6, {}), {1}: (7, {})} | custom-call | flops 1 | bytes 1 | tf_op jit(solution)/shard_map/finish/pallas_call | solution.py:525
  96.8 3.0 %collective-permute-done.24.refs_4_ = bf16[24,1536]{1,0:T(8,128)(2,1)S(1)} collective-permute-done((bf16[24,1536]{1,0:T(8,128)(2,1)S(1)}, bf16[24,1536]{1,0:T(8,128)(2,1)S(1)}, u32[]{:S(2)}, u32[]{:S(2)}) %collective-permute-start.24) | collective-permute-done | bytes 73760 | tf_op jit(solution)/shard_map/ppermute | solution.py:509
  99.8 0.0 collective-permute-done.13.side_ref
  99.8 0.0 collective-permute-done.22.refs_1_
  99.8 1.8 %finish.3 = (bf16[128,3072]{1,0:T(8,128)(2,1)}, bf16[128,3072]{1,0:T(8,128)(2,1)}, bf16[128,3072]{1,0:T(8,128)(2,1)}, bf16[128,3072]{1,0:T(8,128)(2,1)}, f32[128,3072]{1,0:T(8,128)}) custom-call(s32[1]{0:T(128)} %bitcast.place_ref, ...), custom_call_target="tpu_custom_call", output_to_operand_aliasing={{0}: (9, {}), {1}: (10, {}), {2}: (11, {}), {3}: (12, {})} | custom-call | flops 1 | bytes 1 | tf_op jit(solution)/shard_map/finish/pallas_call | solution.py:525
  (12 shorter events, 0.1 us)
Async XLA Ops:
  0.6 7.8 %copy-start.3 = (bf16[128,3072]{1,0:T(8,128)(2,1)S(1)}, bf16[128,3072]{1,0:T(8,128)(2,1)}, u32[]{:S(2)}) copy-start(bf16[128,3072]{1,0:T(8,128)(2,1)} %second_ref.2) | copy-start | bytes 2359300
  0.6 7.7 %copy-start.2 = (bf16[128,3072]{1,0:T(8,128)(2,1)S(1)}, bf16[128,3072]{1,0:T(8,128)(2,1)}, u32[]{:S(2)}) copy-start(bf16[128,3072]{1,0:T(8,128)(2,1)} %first_ref.2) | copy-start | bytes 2359300
  0.7 35.9 %copy-start.1 = (f32[128,3072]{1,0:T(8,128)S(1)}, f32[128,3072]{1,0:T(8,128)}, u32[]{:S(2)}) copy-start(f32[128,3072]{1,0:T(8,128)} %table_ref.1) | copy-start | bytes 4718596
  0.7 35.9 %copy-start.4 = (s32[4096]{0:T(1024)S(1)}, s32[4096]{0:T(1024)}, u32[]{:S(2)}) copy-start(s32[4096]{0:T(1024)} %param.13) | copy-start | bytes 49156
  0.7 35.9 %copy-start.5 = (s32[24,24]{1,0:T(8,128)S(1)}, s32[24,24]{1,0:T(8,128)}, u32[]{:S(2)}) copy-start(s32[24,24]{1,0:T(8,128)} %mask_ref.1) | copy-start | bytes 6916
  0.7 35.9 %copy-start.6 = (s32[24]{0:T(128)S(1)}, s32[24]{0:T(128)}, u32[]{:S(2)}) copy-start(s32[24]{0:T(128)} %param.14) | copy-start | bytes 292
  3.5 24.9 %collective-permute-start.2 = (bf16[2,128,1536]{2,1,0:T(8,128)(2,1)}, bf16[2,128,1536]{2,1,0:T(8,128)(2,1)S(1)}, u32[]{:S(2)}, u32[]{:S(2)}) collective-permute-start(bf16[2,128,1536]{2,1,0:T(8,128)(2,1)} %get-tuple-element.55.kv_own_ref), channel_id=1, source_target_pairs={{0,2},{2,0},{4,6},{6,4},{8,10},{10,8},{12,14},{14,12},{16,18},{18,... | collective-permute-start | bytes 2359304 | tf_op jit(solution)/shard_map/ppermute | solution.py:344
  4.0 25.1 %collective-permute-start.1 = (bf16[2,128,1536]{2,1,0:T(8,128)(2,1)}, bf16[2,128,1536]{2,1,0:T(8,128)(2,1)S(1)}, u32[]{:S(2)}, u32[]{:S(2)}) collective-permute-start(bf16[2,128,1536]{2,1,0:T(8,128)(2,1)} %get-tuple-element.55.kv_own_ref), channel_id=1, source_target_pairs={{0,0},{2,4},{4,2},{6,8},{8,6},{10,12},{12,10},{14,16},{16,14},{18,... | collective-permute-start | bytes 2359304 | tf_op jit(solution)/shard_map/ppermute | solution.py:343
  5.8 11.6 %collective-permute-start.6 = (bf16[2,128,768]{2,1,0:T(8,128)(2,1)}, bf16[2,128,768]{2,1,0:T(8,128)(2,1)S(1)}, u32[]{:S(2)}, u32[]{:S(2)}) collective-permute-start(bf16[2,128,768]{2,1,0:T(8,128)(2,1)} %get-tuple-element.63), channel_id=1, source_target_pairs={{0,1},{1,0},{2,3},{3,2},{4,5},{5,4},{6,7},{7,6},{8,9},{9,8},{10,11... | collective-permute-start | bytes 1179656 | tf_op jit(solution)/shard_map/ppermute | solution.py:330
  8.3 30.2 %copy-start = (bf16[2,128,1536]{2,1,0:T(8,128)(2,1)S(1)}, bf16[2,128,1536]{2,1,0:T(8,128)(2,1)}, u32[]{:S(2)}) copy-start(bf16[2,128,1536]{2,1,0:T(8,128)(2,1)} %get-tuple-element.55.kv_own_ref) | copy-start | bytes 2359300
  8.4 17.4 %collective-permute-start = (bf16[2,128,768]{2,1,0:T(8,128)(2,1)}, bf16[2,128,768]{2,1,0:T(8,128)(2,1)S(1)}, u32[]{:S(2)}, u32[]{:S(2)}) collective-permute-start(bf16[2,128,768]{2,1,0:T(8,128)(2,1)} %get-tuple-element.57), channel_id=1, source_target_pairs={{0,1},{1,0},{2,3},{3,2},{4,5},{5,4},{6,7},{7,6},{8,9},{9,8},{10,11... | collective-permute-start | bytes 1179656 | tf_op jit(solution)/shard_map/ppermute | solution.py:330
  17.4 16.7 %collective-permute-start.7 = (bf16[2,128,768]{2,1,0:T(8,128)(2,1)S(1)}, bf16[2,128,768]{2,1,0:T(8,128)(2,1)S(1)}, u32[]{:S(2)}, u32[]{:S(2)}) collective-permute-start(bf16[2,128,768]{2,1,0:T(8,128)(2,1)S(1)} %get-tuple-element.64), channel_id=1, source_target_pairs={{0,1},{1,0},{2,3},{3,2},{4,5},{5,4},{6,7},{7,6},{8,9},{9,8},{10,11... | collective-permute-start | bytes 1179656 | tf_op jit(solution)/shard_map/ppermute | solution.py:330
  19.7 18.7 %collective-permute-start.9 = (bf16[2,128,768]{2,1,0:T(8,128)(2,1)S(1)}, bf16[2,128,768]{2,1,0:T(8,128)(2,1)S(1)}, u32[]{:S(2)}, u32[]{:S(2)}) collective-permute-start(bf16[2,128,768]{2,1,0:T(8,128)(2,1)S(1)} %collective-permute-done.6.kv_ref), channel_id=1, source_target_pairs={{0,0},{2,4},{4,2},{6,8},{8,6},{10,12},{12,10},{14,16},{16,14},{18,... | collective-permute-start | bytes 1179656 | tf_op jit(solution)/shard_map/ppermute | solution.py:346
  25.8 12.7 %collective-permute-start.8 = (bf16[2,128,768]{2,1,0:T(8,128)(2,1)S(1)}, bf16[2,128,768]{2,1,0:T(8,128)(2,1)S(1)}, u32[]{:S(2)}, u32[]{:S(2)}) collective-permute-start(bf16[2,128,768]{2,1,0:T(8,128)(2,1)S(1)} %collective-permute-done.6.kv_ref), channel_id=1, source_target_pairs={{0,2},{2,0},{4,6},{6,4},{8,10},{10,8},{12,14},{14,12},{16,18},{18,... | collective-permute-start | bytes 1179656 | tf_op jit(solution)/shard_map/ppermute | solution.py:347
  28.4 17.9 %collective-permute-start.5 = (bf16[2,128,768]{2,1,0:T(8,128)(2,1)S(1)}, bf16[2,128,768]{2,1,0:T(8,128)(2,1)S(1)}, u32[]{:S(2)}, u32[]{:S(2)}) collective-permute-start(bf16[2,128,768]{2,1,0:T(8,128)(2,1)S(1)} %collective-permute-done.kv_ref), channel_id=1, source_target_pairs={{0,0},{2,4},{4,2},{6,8},{8,6},{10,12},{12,10},{14,16},{16,14},{18,... | collective-permute-start | bytes 1179656 | tf_op jit(solution)/shard_map/ppermute | solution.py:346
  29.1 17.2 %collective-permute-start.4 = (bf16[2,128,768]{2,1,0:T(8,128)(2,1)S(1)}, bf16[2,128,768]{2,1,0:T(8,128)(2,1)S(1)}, u32[]{:S(2)}, u32[]{:S(2)}) collective-permute-start(bf16[2,128,768]{2,1,0:T(8,128)(2,1)S(1)} %collective-permute-done.kv_ref), channel_id=1, source_target_pairs={{0,2},{2,0},{4,6},{6,4},{8,10},{10,8},{12,14},{14,12},{16,18},{18,... | collective-permute-start | bytes 1179656 | tf_op jit(solution)/shard_map/ppermute | solution.py:347
  34.1 12.4 %collective-permute-start.3 = (bf16[2,128,768]{2,1,0:T(8,128)(2,1)S(1)}, bf16[2,128,768]{2,1,0:T(8,128)(2,1)S(1)}, u32[]{:S(2)}, u32[]{:S(2)}) collective-permute-start(bf16[2,128,768]{2,1,0:T(8,128)(2,1)S(1)} %get-tuple-element.58), channel_id=1, source_target_pairs={{0,1},{1,0},{2,3},{3,2},{4,5},{5,4},{6,7},{7,6},{8,9},{9,8},{10,11... | collective-permute-start | bytes 1179656 | tf_op jit(solution)/shard_map/ppermute | solution.py:330
  46.3 14.0 %collective-permute-start.14 = (bf16[2,128,768]{2,1,0:T(8,128)(2,1)S(1)}, bf16[2,128,768]{2,1,0:T(8,128)(2,1)S(1)}, u32[]{:S(2)}, u32[]{:S(2)}) collective-permute-start(bf16[2,128,768]{2,1,0:T(8,128)(2,1)S(1)} %get-tuple-element.81), channel_id=1, source_target_pairs={{0,1},{1,0},{2,3},{3,2},{4,5},{5,4},{6,7},{7,6},{8,9},{9,8},{10,11... | collective-permute-start | bytes 1179656 | tf_op jit(solution)/shard_map/ppermute | solution.py:338
  46.5 23.9 %collective-permute-start.11 = (bf16[2,256,768]{2,1,0:T(8,128)(2,1)S(1)}, bf16[2,256,768]{2,1,0:T(8,128)(2,1)S(1)}, u32[]{:S(2)}, u32[]{:S(2)}) collective-permute-start(bf16[2,256,768]{2,1,0:T(8,128)(2,1)S(1)} %get-tuple-element.73), channel_id=1, source_target_pairs={{0,0},{2,4},{4,2},{6,8},{8,6},{10,12},{12,10},{14,16},{16,14},{18,... | collective-permute-start | bytes 2359304 | tf_op jit(solution)/shard_map/ppermute | solution.py:485
  47.2 29.3 %collective-permute-start.20 = (bf16[2,256,768]{2,1,0:T(8,128)(2,1)S(1)}, bf16[2,256,768]{2,1,0:T(8,128)(2,1)S(1)}, u32[]{:S(2)}, u32[]{:S(2)}) collective-permute-start(bf16[2,256,768]{2,1,0:T(8,128)(2,1)S(1)} %get-tuple-element.88), channel_id=1, source_target_pairs={{0,2},{2,0},{4,6},{6,4},{8,10},{10,8},{12,14},{14,12},{16,18},{18,... | collective-permute-start | bytes 2359304 | tf_op jit(solution)/shard_map/ppermute | solution.py:486
  60.4 6.5 %collective-permute-start.17 = (bf16[24,1536]{1,0:T(8,128)(2,1)S(1)}, bf16[24,1536]{1,0:T(8,128)(2,1)S(1)}, u32[]{:S(2)}, u32[]{:S(2)}) collective-permute-start(bf16[24,1536]{1,0:T(8,128)(2,1)S(1)} %get-tuple-element.82), channel_id=1, source_target_pairs={{0,24},{2,26},{4,28},{6,30},{8,16},{10,18},{12,20},{14,22},{16,8},... | collective-permute-start | bytes 221192 | tf_op jit(solution)/shard_map/ppermute | solution.py:446
  62.7 7.7 %collective-permute-start.16 = (bf16[24,1536]{1,0:T(8,128)(2,1)S(1)}, bf16[24,1536]{1,0:T(8,128)(2,1)S(1)}, u32[]{:S(2)}, u32[]{:S(2)}) collective-permute-start(bf16[24,1536]{1,0:T(8,128)(2,1)S(1)} %get-tuple-element.82), channel_id=1, source_target_pairs={{0,16},{2,18},{4,20},{6,22},{8,24},{10,26},{12,28},{14,30},{16,0},... | collective-permute-start | bytes 221192 | tf_op jit(solution)/shard_map/ppermute | solution.py:446
  63.4 7.0 %collective-permute-start.15 = (bf16[24,1536]{1,0:T(8,128)(2,1)S(1)}, bf16[24,1536]{1,0:T(8,128)(2,1)S(1)}, u32[]{:S(2)}, u32[]{:S(2)}) collective-permute-start(bf16[24,1536]{1,0:T(8,128)(2,1)S(1)} %get-tuple-element.82), channel_id=1, source_target_pairs={{0,8},{2,10},{4,12},{6,14},{8,0},{10,2},{12,4},{14,6},{16,24},{18,... | collective-permute-start | bytes 221192 | tf_op jit(solution)/shard_map/ppermute | solution.py:446
  66.9 9.6 %collective-permute-start.18 = (bf16[2,128,768]{2,1,0:T(8,128)(2,1)S(1)}, bf16[2,128,768]{2,1,0:T(8,128)(2,1)S(1)}, u32[]{:S(2)}, u32[]{:S(2)}) collective-permute-start(bf16[2,128,768]{2,1,0:T(8,128)(2,1)S(1)} %get-tuple-element.83), channel_id=1, source_target_pairs={{0,1},{1,0},{2,3},{3,2},{4,5},{5,4},{6,7},{7,6},{8,9},{9,8},{10,11... | collective-permute-start | bytes 1179656 | tf_op jit(solution)/shard_map/ppermute | solution.py:338
  70.3 15.2 %collective-permute-start.10 = (bf16[2,256,768]{2,1,0:T(8,128)(2,1)S(1)}, bf16[2,256,768]{2,1,0:T(8,128)(2,1)S(1)}, u32[]{:S(2)}, u32[]{:S(2)}) collective-permute-start(bf16[2,256,768]{2,1,0:T(8,128)(2,1)S(1)} %get-tuple-element.69), channel_id=1, source_target_pairs={{0,2},{2,0},{4,6},{6,4},{8,10},{10,8},{12,14},{14,12},{16,18},{18,... | collective-permute-start | bytes 2359304 | tf_op jit(solution)/shard_map/ppermute | solution.py:486
  70.4 9.3 %collective-permute-start.12 = (bf16[2,128,768]{2,1,0:T(8,128)(2,1)S(1)}, bf16[2,128,768]{2,1,0:T(8,128)(2,1)S(1)}, u32[]{:S(2)}, u32[]{:S(2)}) collective-permute-start(bf16[2,128,768]{2,1,0:T(8,128)(2,1)S(1)} %get-tuple-element.75), channel_id=1, source_target_pairs={{0,0},{2,4},{4,2},{6,8},{8,6},{10,12},{12,10},{14,16},{16,14},{18,... | collective-permute-start | bytes 1179656 | tf_op jit(solution)/shard_map/ppermute | solution.py:485
  76.7 8.9 %collective-permute-start.21 = (bf16[2,128,768]{2,1,0:T(8,128)(2,1)S(1)}, bf16[2,128,768]{2,1,0:T(8,128)(2,1)S(1)}, u32[]{:S(2)}, u32[]{:S(2)}) collective-permute-start(bf16[2,128,768]{2,1,0:T(8,128)(2,1)S(1)} %far_sum.2), channel_id=1, source_target_pairs={{0,1},{1,0},{2,3},{3,2},{4,5},{5,4},{6,7},{7,6},{8,9},{9,8},{10,11... | collective-permute-start | bytes 1179656 | tf_op jit(solution)/shard_map/ppermute | solution.py:338
  78.3 1.3 %collective-permute-start.19 = (bf16[24,1536]{1,0:T(8,128)(2,1)S(1)}, bf16[24,1536]{1,0:T(8,128)(2,1)S(1)}, u32[]{:S(2)}, u32[]{:S(2)}) collective-permute-start(bf16[24,1536]{1,0:T(8,128)(2,1)S(1)} %add_add_fusion), channel_id=1, source_target_pairs={{0,2},{2,0},{4,6},{6,4},{8,10},{10,8},{12,14},{14,12},{16,18},{18,... | collective-permute-start | bytes 221192 | tf_op jit(solution)/shard_map/ppermute | solution.py:446
  79.6 20.2 %collective-permute-start.13 = (bf16[2,128,768]{2,1,0:T(8,128)(2,1)S(1)}, bf16[2,128,768]{2,1,0:T(8,128)(2,1)S(1)}, u32[]{:S(2)}, u32[]{:S(2)}) collective-permute-start(bf16[2,128,768]{2,1,0:T(8,128)(2,1)S(1)} %get-tuple-element.76), channel_id=1, source_target_pairs={{0,0},{2,4},{4,2},{6,8},{8,6},{10,12},{12,10},{14,16},{16,14},{18,... | collective-permute-start | bytes 1179656 | tf_op jit(solution)/shard_map/ppermute | solution.py:496
  85.7 14.1 %collective-permute-start.22 = (bf16[2,128,768]{2,1,0:T(8,128)(2,1)S(1)}, bf16[2,128,768]{2,1,0:T(8,128)(2,1)S(1)}, u32[]{:S(2)}, u32[]{:S(2)}) collective-permute-start(bf16[2,128,768]{2,1,0:T(8,128)(2,1)S(1)} %far_sum.3), channel_id=1, source_target_pairs={{0,1},{1,0},{2,3},{3,2},{4,5},{5,4},{6,7},{7,6},{8,9},{9,8},{10,11... | collective-permute-start | bytes 1179656 | tf_op jit(solution)/shard_map/ppermute | solution.py:338
  87.5 7.1 %collective-permute-start.23 = (bf16[24,1536]{1,0:T(8,128)(2,1)S(1)}, bf16[24,1536]{1,0:T(8,128)(2,1)S(1)}, u32[]{:S(2)}, u32[]{:S(2)}) collective-permute-start(bf16[24,1536]{1,0:T(8,128)(2,1)S(1)} %add.22), channel_id=1, source_target_pairs={{0,4},{2,6},{4,0},{6,2},{8,12},{10,14},{12,8},{14,10},{16,20},{18,... | collective-permute-start | bytes 221192 | tf_op jit(solution)/shard_map/ppermute | solution.py:446
  94.7 5.2 %collective-permute-start.24 = (bf16[24,1536]{1,0:T(8,128)(2,1)S(1)}, bf16[24,1536]{1,0:T(8,128)(2,1)S(1)}, u32[]{:S(2)}, u32[]{:S(2)}) collective-permute-start(bf16[24,1536]{1,0:T(8,128)(2,1)S(1)} %add.23.refs_3_), channel_id=1, source_target_pairs={{0,1},{1,0},{2,3},{3,2},{4,5},{5,4},{6,7},{7,6},{8,9},{9,8},{10,11... | collective-permute-start | bytes 221192 | tf_op jit(solution)/shard_map/ppermute | solution.py:509

commit v11 on v10

--- a/solution.py
+++ b/solution.py
@@ -293,8 +293,7 @@
     tie = lax.optimization_barrier
 
     near_pairs = [(i, i ^ 1) for i in range(ctx_count)]
-    side_of = [i - 1 + 2 * (i % 2) for i in range(ctx_count)]
-    side_pairs = [(i, j if 0 <= j < ctx_count else i) for i, j in enumerate(side_of)]
+    side_pairs = [(i, (i - 1 + 2 * (i % 2)) % ctx_count) for i in range(ctx_count)]
 
     whole = lambda shape: pl.BlockSpec(shape, lambda i, place: (0,) * len(shape))
     limit = (26 if tokens <= 256 else 56) * 1024 * 1024

time: 102 us -> 98.5 us (0.966)
  starting transfers between devices: 35.3 us -> 31.8 us
    ppermute x2, starting transfers between devices: 5.48 us -> 0.01 us  [per_device(): near_far = [lax.ppermute(slab, 'ctx', near_pairs) for slab in kv_far]]
    ppermute x4, waiting for transfers between devices: 16.4 us -> 21.4 us  [to_peers(): arrived.append(lax.ppermute(part, 'head', pairs))]
    ppermute x2, starting transfers between devices: 5.35 us -> 0.78 us  [per_device(): near_back.append(lax.ppermute(near_grad, 'ctx', near_pairs))]
    ppermute x1, starting transfers between devices: 1.78 us -> 5.64 us  [per_device(): side_own = lax.ppermute(kv_own, 'ctx', side_pairs)]
    ppermute x4, waiting for transfers between devices: 10.7 us -> 7.26 us  [from_peers(): arrived.append(lax.ppermute(part, 'head', pairs))]
    ppermute x2, starting transfers between devices: 1.39 us -> 3.99 us  [per_device(): side_back_far.append(lax.ppermute(side_grads[-1], 'ctx', side_pairs))]
    ppermute x4, starting transfers between devices: 7.43 us -> 5.06 us  [to_peers(): arrived.append(lax.ppermute(part, 'head', pairs))]
    ppermute x1, starting transfers between devices: 0.69 us -> 2.91 us  [per_device(): side_back_own.append(lax.ppermute(side_grad_own, 'ctx', side_pairs))]
  transfers between devices with their start and end apart: 25 -> 25, of which waited for: 11 -> 10; matrix products, arithmetic and copies ran while one was open for 0% -> 0% of each run, Pallas kernels for 19% -> 19%
where the time goes in v11:
time: 98.5 us; the launch traced here: 98.3 us
  waiting for transfers between devices  42 us (43%)
  starting transfers between devices  31.8 us (32%)
  Pallas kernels  23.6 us (24%)
    ppermute x4, waiting for transfers between devices, to_peers(): arrived.append(lax.ppermute(part, 'head', pairs))  21.4 us
    pallas_call x2, Pallas kernels, attention(): pl.pallas_call(functools.partial(attention_kernel, rows=rows, tokens=toke...  15.6 us
    ppermute x5, waiting for transfers between devices, shifted(): return lax.ppermute(array, 'ctx', [(i, i ^ step) for i in range(ctx_count)])  12 us
    ppermute x4, waiting for transfers between devices, from_peers(): arrived.append(lax.ppermute(part, 'head', pairs))  7.26 us
    ppermute x1, starting transfers between devices, per_device(): side_own = lax.ppermute(kv_own, 'ctx', side_pairs)  5.64 us
    ppermute x4, starting transfers between devices, from_peers(): arrived.append(lax.ppermute(part, 'head', pairs))  5.6 us
    ppermute x4, starting transfers between devices, to_peers(): arrived.append(lax.ppermute(part, 'head', pairs))  5.06 us
    ppermute x5, starting transfers between devices, shifted(): return lax.ppermute(array, 'ctx', [(i, i ^ step) for i in range(ctx_count)])  4.62 us
  transfers between devices with their start and end apart: 25, of which 10 were waited for; matrix products, arithmetic and copies ran while one was open for 0% of the time, Pallas kernels for 19%

profile of v11, /device:TPU:0, one launch (start us, length us, event | category | flops | bytes accessed | tf_op | source)
XLA Modules:
  0.0 98.3 jit_solution(15672167475804204042)
XLA Ops:
  0.6 0.0 copy-start.3
  0.6 0.0 copy-start.2
  0.7 0.0 copy-start.1
  0.7 2.8 %pack.3 = (bf16[2,128,1536]{2,1,0:T(8,128)(2,1)}, bf16[2,128,768]{2,1,0:T(8,128)(2,1)}, bf16[2,128,768]{2,1,0:T(8,128)(2,1)}) custom-call(s32[1]{0:T(128)} %bitcast.place_ref, bf16[128,3072]{1,0:T(8,128)(2,1)} %first_ref.3, bf16[128,3072]{1,0:T(8,128)(2,1)} %second_ref.3), custom_call_target="tpu_custom_call" | custom-call | flops 1 | bytes 1 | tf_op jit(solution)/shard_map/pack/pallas_call | solution.py:309
  3.5 0.5 collective-permute-start.2
  4.0 5.6 %collective-permute-start.1 = (bf16[2,128,1536]{2,1,0:T(8,128)(2,1)}, bf16[2,128,1536]{2,1,0:T(8,128)(2,1)S(1)}, u32[]{:S(2)}, u32[]{:S(2)}) collective-permute-start(bf16[2,128,1536]{2,1,0:T(8,128)(2,1)} %get-tuple-element.55.kv_own_ref), channel_id=1, source_target_pairs={{0,30},{2,4},{4,2},{6,8},{8,6},{10,12},{12,10},{14,16},{16,14},{18... | collective-permute-start | bytes 2359304 | tf_op jit(solution)/shard_map/ppermute | solution.py:342
  9.7 1.5 %collective-permute-start.6 = (bf16[2,128,768]{2,1,0:T(8,128)(2,1)}, bf16[2,128,768]{2,1,0:T(8,128)(2,1)S(1)}, u32[]{:S(2)}, u32[]{:S(2)}) collective-permute-start(bf16[2,128,768]{2,1,0:T(8,128)(2,1)} %get-tuple-element.63), channel_id=1, source_target_pairs={{0,1},{1,0},{2,3},{3,2},{4,5},{5,4},{6,7},{7,6},{8,9},{9,8},{10,11... | collective-permute-start | bytes 1179656 | tf_op jit(solution)/shard_map/ppermute | solution.py:329
  11.2 0.5 collective-permute-start
  11.7 0.0 copy-done.3
  11.7 0.3 pack.2
  12.0 10.0 %collective-permute-done.6.kv_ref = bf16[2,128,768]{2,1,0:T(8,128)(2,1)S(1)} collective-permute-done((bf16[2,128,768]{2,1,0:T(8,128)(2,1)}, bf16[2,128,768]{2,1,0:T(8,128)(2,1)S(1)}, u32[]{:S(2)}, u32[]{:S(2)}) %collective-permute-start.6) | collective-permute-done | bytes 393248 | tf_op jit(solution)/shard_map/ppermute | solution.py:329
  21.9 1.5 %collective-permute-start.7 = (bf16[2,128,768]{2,1,0:T(8,128)(2,1)S(1)}, bf16[2,128,768]{2,1,0:T(8,128)(2,1)S(1)}, u32[]{:S(2)}, u32[]{:S(2)}) collective-permute-start(bf16[2,128,768]{2,1,0:T(8,128)(2,1)S(1)} %get-tuple-element.64), channel_id=1, source_target_pairs={{0,1},{1,0},{2,3},{3,2},{4,5},{5,4},{6,7},{7,6},{8,9},{9,8},{10,11... | collective-permute-start | bytes 1179656 | tf_op jit(solution)/shard_map/ppermute | solution.py:329
  23.5 0.0 collective-permute-start.9
  23.5 6.9 %collective-permute-done.kv_ref = bf16[2,128,768]{2,1,0:T(8,128)(2,1)S(1)} collective-permute-done((bf16[2,128,768]{2,1,0:T(8,128)(2,1)}, bf16[2,128,768]{2,1,0:T(8,128)(2,1)S(1)}, u32[]{:S(2)}, u32[]{:S(2)}) %collective-permute-start) | collective-permute-done | bytes 393248 | tf_op jit(solution)/shard_map/ppermute | solution.py:329
  30.4 0.0 collective-permute-start.8
  30.4 0.0 collective-permute-done.2.near_own_ref
  30.4 0.6 collective-permute-start.5
  31.0 0.0 collective-permute-done.1.side_own_ref
  31.0 0.0 collective-permute-start.4
  31.0 4.5 %collective-permute-done.7.qo_ref = bf16[2,128,768]{2,1,0:T(8,128)(2,1)S(1)} collective-permute-done((bf16[2,128,768]{2,1,0:T(8,128)(2,1)S(1)}, bf16[2,128,768]{2,1,0:T(8,128)(2,1)S(1)}, u32[]{:S(2)}, u32[]{:S(2)}) %collective-permute-start.7) | collective-permute-done | bytes 393248 | tf_op jit(solution)/shard_map/ppermute | solution.py:329
  35.5 1.5 %collective-permute-start.3 = (bf16[2,128,768]{2,1,0:T(8,128)(2,1)S(1)}, bf16[2,128,768]{2,1,0:T(8,128)(2,1)S(1)}, u32[]{:S(2)}, u32[]{:S(2)}) collective-permute-start(bf16[2,128,768]{2,1,0:T(8,128)(2,1)S(1)} %get-tuple-element.58), channel_id=1, source_target_pairs={{0,1},{1,0},{2,3},{3,2},{4,5},{5,4},{6,7},{7,6},{8,9},{9,8},{10,11... | collective-permute-start | bytes 1179656 | tf_op jit(solution)/shard_map/ppermute | solution.py:329
  37.0 0.0 copy-done.4
  37.0 1.9 %prep.1 = (f32[768,256]{1,0:T(8,128)S(1)}, f32[256,1536]{1,0:T(8,128)S(1)}, bf16[24,256]{1,0:T(8,128)(2,1)S(1)}) custom-call(s32[1]{0:T(128)} %bitcast.place_ref, s32[32,128]{1,0:T(8,128)S(1)} %bitcast.3, s32[1,24]{1,0:T(1,128)S(1)} %bitcast.4, s32[24,24]{1,0:T(8,128)S(1)} %copy-done.5, f32[128,3072]{1,0:T(8,128)S(1)} %copy-done.1), custom_call_target="tpu_custom_call" | custom-call | flops 1 | bytes 1 | tf_op jit(solution)/shard_map/prep/pallas_call | solution.py:354
  38.9 0.0 collective-permute-done.9.side_far_ref
  38.9 0.0 collective-permute-done.8.near_far_ref
  38.9 7.8 %attention.2 = (bf16[2,128,768]{2,1,0:T(8,128)(2,1)S(1)}, f32[2,128,768]{2,1,0:T(8,128)S(1)}, f32[2,128,768]{2,1,0:T(8,128)S(1)}, bf16[2,256,768]{2,1,0:T(8,128)...) custom-call(s32[1]{0:T(128)} %bitcast.place_ref, ...), custom_call_target="tpu_custom_call" | custom-call | flops 1 | bytes 1 | tf_op jit(solution)/shard_map/attention/pallas_call | solution.py:408
  46.7 0.5 collective-permute-start.14
  47.2 0.0 collective-permute-done.5.side_far_ref
  47.2 0.0 collective-permute-done.4.near_far_ref
  47.2 0.0 collective-permute-done.3.qo_ref
  47.2 0.8 collective-permute-start.11
  48.0 0.8 collective-permute-start.20
  48.8 7.8 %attention.3 = (bf16[2,128,768]{2,1,0:T(8,128)(2,1)S(1)}, f32[2,128,768]{2,1,0:T(8,128)S(1)}, f32[2,128,768]{2,1,0:T(8,128)S(1)}, bf16[2,256,768]{2,1,0:T(8,128)...) custom-call(s32[1]{0:T(128)} %bitcast.place_ref, ...), custom_call_target="tpu_custom_call", output_to_operand_aliasing={{6}: (12, {}), {7}: (13, {}), {8}: (14, {})} | custom-call | flops 1 | bytes 1 | tf_op jit(solution)/shard_map/attention/pallas_call | solution.py:408
  56.6 0.0 collective-permute-done.14.refs_0_
  56.6 4.0 %collective-permute-start.17 = (bf16[24,1536]{1,0:T(8,128)(2,1)S(1)}, bf16[24,1536]{1,0:T(8,128)(2,1)S(1)}, u32[]{:S(2)}, u32[]{:S(2)}) collective-permute-start(bf16[24,1536]{1,0:T(8,128)(2,1)S(1)} %get-tuple-element.82), channel_id=1, source_target_pairs={{0,24},{2,26},{4,28},{6,30},{8,16},{10,18},{12,20},{14,22},{16,8},... | collective-permute-start | bytes 221192 | tf_op jit(solution)/shard_map/ppermute | solution.py:445
  60.7 0.0 collective-permute-start.16
  60.7 0.6 collective-permute-start.15
  61.2 2.4 %collective-permute-done.17 = bf16[24,1536]{1,0:T(8,128)(2,1)S(1)} collective-permute-done((bf16[24,1536]{1,0:T(8,128)(2,1)S(1)}, bf16[24,1536]{1,0:T(8,128)(2,1)S(1)}, u32[]{:S(2)}, u32[]{:S(2)}) %collective-permute-start.17) | collective-permute-done | bytes 73760 | tf_op jit(solution)/shard_map/ppermute | solution.py:445
  63.6 1.5 %collective-permute-start.18 = (bf16[2,128,768]{2,1,0:T(8,128)(2,1)S(1)}, bf16[2,128,768]{2,1,0:T(8,128)(2,1)S(1)}, u32[]{:S(2)}, u32[]{:S(2)}) collective-permute-start(bf16[2,128,768]{2,1,0:T(8,128)(2,1)S(1)} %get-tuple-element.83), channel_id=1, source_target_pairs={{0,1},{1,0},{2,3},{3,2},{4,5},{5,4},{6,7},{7,6},{8,9},{9,8},{10,11... | collective-permute-start | bytes 1179656 | tf_op jit(solution)/shard_map/ppermute | solution.py:337
  65.1 1.5 %collective-permute-done.16 = bf16[24,1536]{1,0:T(8,128)(2,1)S(1)} collective-permute-done((bf16[24,1536]{1,0:T(8,128)(2,1)S(1)}, bf16[24,1536]{1,0:T(8,128)(2,1)S(1)}, u32[]{:S(2)}, u32[]{:S(2)}) %collective-permute-start.16) | collective-permute-done | bytes 73760 | tf_op jit(solution)/shard_map/ppermute | solution.py:445
  66.6 0.0 collective-permute-start.10
  66.6 0.0 collective-permute-done.15
  66.6 0.0 collective-permute-done.11.side_ref
  66.6 3.2 %collective-permute-start.12 = (bf16[2,128,768]{2,1,0:T(8,128)(2,1)S(1)}, bf16[2,128,768]{2,1,0:T(8,128)(2,1)S(1)}, u32[]{:S(2)}, u32[]{:S(2)}) collective-permute-start(bf16[2,128,768]{2,1,0:T(8,128)(2,1)S(1)} %get-tuple-element.75), channel_id=1, source_target_pairs={{0,30},{2,4},{4,2},{6,8},{8,6},{10,12},{12,10},{14,16},{16,14},{18... | collective-permute-start | bytes 1179656 | tf_op jit(solution)/shard_map/ppermute | solution.py:484
  69.8 3.8 %collective-permute-done.18.refs_0_ = bf16[2,128,768]{2,1,0:T(8,128)(2,1)S(1)} collective-permute-done((bf16[2,128,768]{2,1,0:T(8,128)(2,1)S(1)}, bf16[2,128,768]{2,1,0:T(8,128)(2,1)S(1)}, u32[]{:S(2)}, u32[]{:S(2)}) %collective-permute-start.18) | collective-permute-done | bytes 393248 | tf_op jit(solution)/shard_map/ppermute | solution.py:337
  73.7 0.0 collective-permute-done.20.near_ref
  73.7 0.1 far_sum.2
  73.8 1.8 %collective-permute-start.21 = (bf16[2,128,768]{2,1,0:T(8,128)(2,1)S(1)}, bf16[2,128,768]{2,1,0:T(8,128)(2,1)S(1)}, u32[]{:S(2)}, u32[]{:S(2)}) collective-permute-start(bf16[2,128,768]{2,1,0:T(8,128)(2,1)S(1)} %far_sum.2), channel_id=1, source_target_pairs={{0,1},{1,0},{2,3},{3,2},{4,5},{5,4},{6,7},{7,6},{8,9},{9,8},{10,11... | collective-permute-start | bytes 1179656 | tf_op jit(solution)/shard_map/ppermute | solution.py:337
  75.6 0.0 collective-permute-start.19
  75.6 1.3 %collective-permute-done.19 = bf16[24,1536]{1,0:T(8,128)(2,1)S(1)} collective-permute-done((bf16[24,1536]{1,0:T(8,128)(2,1)S(1)}, bf16[24,1536]{1,0:T(8,128)(2,1)S(1)}, u32[]{:S(2)}, u32[]{:S(2)}) %collective-permute-start.19) | collective-permute-done | bytes 73760 | tf_op jit(solution)/shard_map/ppermute | solution.py:445
  76.9 0.0 collective-permute-done.12.side_ref
  76.9 2.9 %collective-permute-start.13 = (bf16[2,128,768]{2,1,0:T(8,128)(2,1)S(1)}, bf16[2,128,768]{2,1,0:T(8,128)(2,1)S(1)}, u32[]{:S(2)}, u32[]{:S(2)}) collective-permute-start(bf16[2,128,768]{2,1,0:T(8,128)(2,1)S(1)} %get-tuple-element.76), channel_id=1, source_target_pairs={{0,30},{2,4},{4,2},{6,8},{8,6},{10,12},{12,10},{14,16},{16,14},{18... | collective-permute-start | bytes 1179656 | tf_op jit(solution)/shard_map/ppermute | solution.py:495
  79.8 3.4 %collective-permute-done.21.refs_1_ = bf16[2,128,768]{2,1,0:T(8,128)(2,1)S(1)} collective-permute-done((bf16[2,128,768]{2,1,0:T(8,128)(2,1)S(1)}, bf16[2,128,768]{2,1,0:T(8,128)(2,1)S(1)}, u32[]{:S(2)}, u32[]{:S(2)}) %collective-permute-start.21) | collective-permute-done | bytes 393248 | tf_op jit(solution)/shard_map/ppermute | solution.py:337
  83.2 0.0 collective-permute-done.10.near_ref
  83.2 0.1 far_sum.3
  83.4 1.8 %collective-permute-start.22 = (bf16[2,128,768]{2,1,0:T(8,128)(2,1)S(1)}, bf16[2,128,768]{2,1,0:T(8,128)(2,1)S(1)}, u32[]{:S(2)}, u32[]{:S(2)}) collective-permute-start(bf16[2,128,768]{2,1,0:T(8,128)(2,1)S(1)} %far_sum.3), channel_id=1, source_target_pairs={{0,1},{1,0},{2,3},{3,2},{4,5},{5,4},{6,7},{7,6},{8,9},{9,8},{10,11... | collective-permute-start | bytes 1179656 | tf_op jit(solution)/shard_map/ppermute | solution.py:337
  85.2 0.0 collective-permute-start.23
  85.2 6.9 %collective-permute-done.23 = bf16[24,1536]{1,0:T(8,128)(2,1)S(1)} collective-permute-done((bf16[24,1536]{1,0:T(8,128)(2,1)S(1)}, bf16[24,1536]{1,0:T(8,128)(2,1)S(1)}, u32[]{:S(2)}, u32[]{:S(2)}) %collective-permute-start.23) | collective-permute-done | bytes 73760 | tf_op jit(solution)/shard_map/ppermute | solution.py:445
  92.1 2.1 %collective-permute-start.24 = (bf16[24,1536]{1,0:T(8,128)(2,1)S(1)}, bf16[24,1536]{1,0:T(8,128)(2,1)S(1)}, u32[]{:S(2)}, u32[]{:S(2)}) collective-permute-start(bf16[24,1536]{1,0:T(8,128)(2,1)S(1)} %add.23.refs_3_), channel_id=1, source_target_pairs={{0,1},{1,0},{2,3},{3,2},{4,5},{5,4},{6,7},{7,6},{8,9},{9,8},{10,11... | collective-permute-start | bytes 221192 | tf_op jit(solution)/shard_map/ppermute | solution.py:508
  94.2 1.1 %finish.2 = (bf16[128,3072]{1,0:T(8,128)(2,1)}, bf16[128,3072]{1,0:T(8,128)(2,1)}, bf16[128,3072]{1,0:T(8,128)(2,1)}, bf16[128,3072]{1,0:T(8,128)(2,1)}) custom-call(s32[1]{0:T(128)} %bitcast.place_ref, f32[2,128,768]{2,1,0:T(8,128)S(1)} %get-tuple-element.94.part_ref, ...), custom_call_target="tpu_custom_call", output_to_operand_aliasing={{0}: (6, {}), {1}: (7, {})} | custom-call | flops 1 | bytes 1 | tf_op jit(solution)/shard_map/finish/pallas_call | solution.py:524
  95.3 1.3 %collective-permute-done.24.refs_4_ = bf16[24,1536]{1,0:T(8,128)(2,1)S(1)} collective-permute-done((bf16[24,1536]{1,0:T(8,128)(2,1)S(1)}, bf16[24,1536]{1,0:T(8,128)(2,1)S(1)}, u32[]{:S(2)}, u32[]{:S(2)}) %collective-permute-start.24) | collective-permute-done | bytes 73760 | tf_op jit(solution)/shard_map/ppermute | solution.py:508
  96.5 0.0 collective-permute-done.13.side_ref
  96.5 0.0 collective-permute-done.22.refs_1_
  96.5 1.8 %finish.3 = (bf16[128,3072]{1,0:T(8,128)(2,1)}, bf16[128,3072]{1,0:T(8,128)(2,1)}, bf16[128,3072]{1,0:T(8,128)(2,1)}, bf16[128,3072]{1,0:T(8,128)(2,1)}, f32[128,3072]{1,0:T(8,128)}) custom-call(s32[1]{0:T(128)} %bitcast.place_ref, ...), custom_call_target="tpu_custom_call", output_to_operand_aliasing={{0}: (9, {}), {1}: (10, {}), {2}: (11, {}), {3}: (12, {})} | custom-call | flops 1 | bytes 1 | tf_op jit(solution)/shard_map/finish/pallas_call | solution.py:524
  (12 shorter events, 0.1 us)
Async XLA Ops:
  0.6 11.1 %copy-start.3 = (bf16[128,3072]{1,0:T(8,128)(2,1)S(1)}, bf16[128,3072]{1,0:T(8,128)(2,1)}, u32[]{:S(2)}) copy-start(bf16[128,3072]{1,0:T(8,128)(2,1)} %second_ref.2) | copy-start | bytes 2359300
  0.6 11.1 %copy-start.2 = (bf16[128,3072]{1,0:T(8,128)(2,1)S(1)}, bf16[128,3072]{1,0:T(8,128)(2,1)}, u32[]{:S(2)}) copy-start(bf16[128,3072]{1,0:T(8,128)(2,1)} %first_ref.2) | copy-start | bytes 2359300
  0.7 36.3 %copy-start.1 = (f32[128,3072]{1,0:T(8,128)S(1)}, f32[128,3072]{1,0:T(8,128)}, u32[]{:S(2)}) copy-start(f32[128,3072]{1,0:T(8,128)} %table_ref.1) | copy-start | bytes 4718596
  0.7 36.3 %copy-start.4 = (s32[4096]{0:T(1024)S(1)}, s32[4096]{0:T(1024)}, u32[]{:S(2)}) copy-start(s32[4096]{0:T(1024)} %param.13) | copy-start | bytes 49156
  0.7 36.3 %copy-start.5 = (s32[24,24]{1,0:T(8,128)S(1)}, s32[24,24]{1,0:T(8,128)}, u32[]{:S(2)}) copy-start(s32[24,24]{1,0:T(8,128)} %mask_ref.1) | copy-start | bytes 6916
  0.7 36.3 %copy-start.6 = (s32[24]{0:T(128)S(1)}, s32[24]{0:T(128)}, u32[]{:S(2)}) copy-start(s32[24]{0:T(128)} %param.14) | copy-start | bytes 292
  3.5 26.9 %collective-permute-start.2 = (bf16[2,128,1536]{2,1,0:T(8,128)(2,1)}, bf16[2,128,1536]{2,1,0:T(8,128)(2,1)S(1)}, u32[]{:S(2)}, u32[]{:S(2)}) collective-permute-start(bf16[2,128,1536]{2,1,0:T(8,128)(2,1)} %get-tuple-element.55.kv_own_ref), channel_id=1, source_target_pairs={{0,2},{2,0},{4,6},{6,4},{8,10},{10,8},{12,14},{14,12},{16,18},{18,... | collective-permute-start | bytes 2359304 | tf_op jit(solution)/shard_map/ppermute | solution.py:343
  4.0 26.9 %collective-permute-start.1 = (bf16[2,128,1536]{2,1,0:T(8,128)(2,1)}, bf16[2,128,1536]{2,1,0:T(8,128)(2,1)S(1)}, u32[]{:S(2)}, u32[]{:S(2)}) collective-permute-start(bf16[2,128,1536]{2,1,0:T(8,128)(2,1)} %get-tuple-element.55.kv_own_ref), channel_id=1, source_target_pairs={{0,30},{2,4},{4,2},{6,8},{8,6},{10,12},{12,10},{14,16},{16,14},{18... | collective-permute-start | bytes 2359304 | tf_op jit(solution)/shard_map/ppermute | solution.py:342
  9.7 12.3 %collective-permute-start.6 = (bf16[2,128,768]{2,1,0:T(8,128)(2,1)}, bf16[2,128,768]{2,1,0:T(8,128)(2,1)S(1)}, u32[]{:S(2)}, u32[]{:S(2)}) collective-permute-start(bf16[2,128,768]{2,1,0:T(8,128)(2,1)} %get-tuple-element.63), channel_id=1, source_target_pairs={{0,1},{1,0},{2,3},{3,2},{4,5},{5,4},{6,7},{7,6},{8,9},{9,8},{10,11... | collective-permute-start | bytes 1179656 | tf_op jit(solution)/shard_map/ppermute | solution.py:329
  11.2 27.7 %copy-start = (bf16[2,128,1536]{2,1,0:T(8,128)(2,1)S(1)}, bf16[2,128,1536]{2,1,0:T(8,128)(2,1)}, u32[]{:S(2)}) copy-start(bf16[2,128,1536]{2,1,0:T(8,128)(2,1)} %get-tuple-element.55.kv_own_ref) | copy-start | bytes 2359300
  11.2 19.2 %collective-permute-start = (bf16[2,128,768]{2,1,0:T(8,128)(2,1)}, bf16[2,128,768]{2,1,0:T(8,128)(2,1)S(1)}, u32[]{:S(2)}, u32[]{:S(2)}) collective-permute-start(bf16[2,128,768]{2,1,0:T(8,128)(2,1)} %get-tuple-element.57), channel_id=1, source_target_pairs={{0,1},{1,0},{2,3},{3,2},{4,5},{5,4},{6,7},{7,6},{8,9},{9,8},{10,11... | collective-permute-start | bytes 1179656 | tf_op jit(solution)/shard_map/ppermute | solution.py:329
  21.9 13.5 %collective-permute-start.7 = (bf16[2,128,768]{2,1,0:T(8,128)(2,1)S(1)}, bf16[2,128,768]{2,1,0:T(8,128)(2,1)S(1)}, u32[]{:S(2)}, u32[]{:S(2)}) collective-permute-start(bf16[2,128,768]{2,1,0:T(8,128)(2,1)S(1)} %get-tuple-element.64), channel_id=1, source_target_pairs={{0,1},{1,0},{2,3},{3,2},{4,5},{5,4},{6,7},{7,6},{8,9},{9,8},{10,11... | collective-permute-start | bytes 1179656 | tf_op jit(solution)/shard_map/ppermute | solution.py:329
  23.5 15.4 %collective-permute-start.9 = (bf16[2,128,768]{2,1,0:T(8,128)(2,1)S(1)}, bf16[2,128,768]{2,1,0:T(8,128)(2,1)S(1)}, u32[]{:S(2)}, u32[]{:S(2)}) collective-permute-start(bf16[2,128,768]{2,1,0:T(8,128)(2,1)S(1)} %collective-permute-done.6.kv_ref), channel_id=1, source_target_pairs={{0,30},{2,4},{4,2},{6,8},{8,6},{10,12},{12,10},{14,16},{16,14},{18... | collective-permute-start | bytes 1179656 | tf_op jit(solution)/shard_map/ppermute | solution.py:345
  30.4 8.5 %collective-permute-start.8 = (bf16[2,128,768]{2,1,0:T(8,128)(2,1)S(1)}, bf16[2,128,768]{2,1,0:T(8,128)(2,1)S(1)}, u32[]{:S(2)}, u32[]{:S(2)}) collective-permute-start(bf16[2,128,768]{2,1,0:T(8,128)(2,1)S(1)} %collective-permute-done.6.kv_ref), channel_id=1, source_target_pairs={{0,2},{2,0},{4,6},{6,4},{8,10},{10,8},{12,14},{14,12},{16,18},{18,... | collective-permute-start | bytes 1179656 | tf_op jit(solution)/shard_map/ppermute | solution.py:346
  30.4 16.9 %collective-permute-start.5 = (bf16[2,128,768]{2,1,0:T(8,128)(2,1)S(1)}, bf16[2,128,768]{2,1,0:T(8,128)(2,1)S(1)}, u32[]{:S(2)}, u32[]{:S(2)}) collective-permute-start(bf16[2,128,768]{2,1,0:T(8,128)(2,1)S(1)} %collective-permute-done.kv_ref), channel_id=1, source_target_pairs={{0,30},{2,4},{4,2},{6,8},{8,6},{10,12},{12,10},{14,16},{16,14},{18... | collective-permute-start | bytes 1179656 | tf_op jit(solution)/shard_map/ppermute | solution.py:345
  31.0 16.3 %collective-permute-start.4 = (bf16[2,128,768]{2,1,0:T(8,128)(2,1)S(1)}, bf16[2,128,768]{2,1,0:T(8,128)(2,1)S(1)}, u32[]{:S(2)}, u32[]{:S(2)}) collective-permute-start(bf16[2,128,768]{2,1,0:T(8,128)(2,1)S(1)} %collective-permute-done.kv_ref), channel_id=1, source_target_pairs={{0,2},{2,0},{4,6},{6,4},{8,10},{10,8},{12,14},{14,12},{16,18},{18,... | collective-permute-start | bytes 1179656 | tf_op jit(solution)/shard_map/ppermute | solution.py:346
  35.5 11.8 %collective-permute-start.3 = (bf16[2,128,768]{2,1,0:T(8,128)(2,1)S(1)}, bf16[2,128,768]{2,1,0:T(8,128)(2,1)S(1)}, u32[]{:S(2)}, u32[]{:S(2)}) collective-permute-start(bf16[2,128,768]{2,1,0:T(8,128)(2,1)S(1)} %get-tuple-element.58), channel_id=1, source_target_pairs={{0,1},{1,0},{2,3},{3,2},{4,5},{5,4},{6,7},{7,6},{8,9},{9,8},{10,11... | collective-permute-start | bytes 1179656 | tf_op jit(solution)/shard_map/ppermute | solution.py:329
  46.7 9.9 %collective-permute-start.14 = (bf16[2,128,768]{2,1,0:T(8,128)(2,1)S(1)}, bf16[2,128,768]{2,1,0:T(8,128)(2,1)S(1)}, u32[]{:S(2)}, u32[]{:S(2)}) collective-permute-start(bf16[2,128,768]{2,1,0:T(8,128)(2,1)S(1)} %get-tuple-element.81), channel_id=1, source_target_pairs={{0,1},{1,0},{2,3},{3,2},{4,5},{5,4},{6,7},{7,6},{8,9},{9,8},{10,11... | collective-permute-start | bytes 1179656 | tf_op jit(solution)/shard_map/ppermute | solution.py:337
  47.2 19.4 %collective-permute-start.11 = (bf16[2,256,768]{2,1,0:T(8,128)(2,1)S(1)}, bf16[2,256,768]{2,1,0:T(8,128)(2,1)S(1)}, u32[]{:S(2)}, u32[]{:S(2)}) collective-permute-start(bf16[2,256,768]{2,1,0:T(8,128)(2,1)S(1)} %get-tuple-element.73), channel_id=1, source_target_pairs={{0,30},{2,4},{4,2},{6,8},{8,6},{10,12},{12,10},{14,16},{16,14},{18... | collective-permute-start | bytes 2359304 | tf_op jit(solution)/shard_map/ppermute | solution.py:484
  48.0 25.6 %collective-permute-start.20 = (bf16[2,256,768]{2,1,0:T(8,128)(2,1)S(1)}, bf16[2,256,768]{2,1,0:T(8,128)(2,1)S(1)}, u32[]{:S(2)}, u32[]{:S(2)}) collective-permute-start(bf16[2,256,768]{2,1,0:T(8,128)(2,1)S(1)} %get-tuple-element.88), channel_id=1, source_target_pairs={{0,2},{2,0},{4,6},{6,4},{8,10},{10,8},{12,14},{14,12},{16,18},{18,... | collective-permute-start | bytes 2359304 | tf_op jit(solution)/shard_map/ppermute | solution.py:485
  56.6 7.0 %collective-permute-start.17 = (bf16[24,1536]{1,0:T(8,128)(2,1)S(1)}, bf16[24,1536]{1,0:T(8,128)(2,1)S(1)}, u32[]{:S(2)}, u32[]{:S(2)}) collective-permute-start(bf16[24,1536]{1,0:T(8,128)(2,1)S(1)} %get-tuple-element.82), channel_id=1, source_target_pairs={{0,24},{2,26},{4,28},{6,30},{8,16},{10,18},{12,20},{14,22},{16,8},... | collective-permute-start | bytes 221192 | tf_op jit(solution)/shard_map/ppermute | solution.py:445
  60.7 5.9 %collective-permute-start.16 = (bf16[24,1536]{1,0:T(8,128)(2,1)S(1)}, bf16[24,1536]{1,0:T(8,128)(2,1)S(1)}, u32[]{:S(2)}, u32[]{:S(2)}) collective-permute-start(bf16[24,1536]{1,0:T(8,128)(2,1)S(1)} %get-tuple-element.82), channel_id=1, source_target_pairs={{0,16},{2,18},{4,20},{6,22},{8,24},{10,26},{12,28},{14,30},{16,0},... | collective-permute-start | bytes 221192 | tf_op jit(solution)/shard_map/ppermute | solution.py:445
  60.7 5.9 %collective-permute-start.15 = (bf16[24,1536]{1,0:T(8,128)(2,1)S(1)}, bf16[24,1536]{1,0:T(8,128)(2,1)S(1)}, u32[]{:S(2)}, u32[]{:S(2)}) collective-permute-start(bf16[24,1536]{1,0:T(8,128)(2,1)S(1)} %get-tuple-element.82), channel_id=1, source_target_pairs={{0,8},{2,10},{4,12},{6,14},{8,0},{10,2},{12,4},{14,6},{16,24},{18,... | collective-permute-start | bytes 221192 | tf_op jit(solution)/shard_map/ppermute | solution.py:445
  63.6 10.0 %collective-permute-start.18 = (bf16[2,128,768]{2,1,0:T(8,128)(2,1)S(1)}, bf16[2,128,768]{2,1,0:T(8,128)(2,1)S(1)}, u32[]{:S(2)}, u32[]{:S(2)}) collective-permute-start(bf16[2,128,768]{2,1,0:T(8,128)(2,1)S(1)} %get-tuple-element.83), channel_id=1, source_target_pairs={{0,1},{1,0},{2,3},{3,2},{4,5},{5,4},{6,7},{7,6},{8,9},{9,8},{10,11... | collective-permute-start | bytes 1179656 | tf_op jit(solution)/shard_map/ppermute | solution.py:337
  66.6 16.7 %collective-permute-start.10 = (bf16[2,256,768]{2,1,0:T(8,128)(2,1)S(1)}, bf16[2,256,768]{2,1,0:T(8,128)(2,1)S(1)}, u32[]{:S(2)}, u32[]{:S(2)}) collective-permute-start(bf16[2,256,768]{2,1,0:T(8,128)(2,1)S(1)} %get-tuple-element.69), channel_id=1, source_target_pairs={{0,2},{2,0},{4,6},{6,4},{8,10},{10,8},{12,14},{14,12},{16,18},{18,... | collective-permute-start | bytes 2359304 | tf_op jit(solution)/shard_map/ppermute | solution.py:485
  66.6 10.3 %collective-permute-start.12 = (bf16[2,128,768]{2,1,0:T(8,128)(2,1)S(1)}, bf16[2,128,768]{2,1,0:T(8,128)(2,1)S(1)}, u32[]{:S(2)}, u32[]{:S(2)}) collective-permute-start(bf16[2,128,768]{2,1,0:T(8,128)(2,1)S(1)} %get-tuple-element.75), channel_id=1, source_target_pairs={{0,30},{2,4},{4,2},{6,8},{8,6},{10,12},{12,10},{14,16},{16,14},{18... | collective-permute-start | bytes 1179656 | tf_op jit(solution)/shard_map/ppermute | solution.py:484
  73.8 9.4 %collective-permute-start.21 = (bf16[2,128,768]{2,1,0:T(8,128)(2,1)S(1)}, bf16[2,128,768]{2,1,0:T(8,128)(2,1)S(1)}, u32[]{:S(2)}, u32[]{:S(2)}) collective-permute-start(bf16[2,128,768]{2,1,0:T(8,128)(2,1)S(1)} %far_sum.2), channel_id=1, source_target_pairs={{0,1},{1,0},{2,3},{3,2},{4,5},{5,4},{6,7},{7,6},{8,9},{9,8},{10,11... | collective-permute-start | bytes 1179656 | tf_op jit(solution)/shard_map/ppermute | solution.py:337
  75.6 1.3 %collective-permute-start.19 = (bf16[24,1536]{1,0:T(8,128)(2,1)S(1)}, bf16[24,1536]{1,0:T(8,128)(2,1)S(1)}, u32[]{:S(2)}, u32[]{:S(2)}) collective-permute-start(bf16[24,1536]{1,0:T(8,128)(2,1)S(1)} %add_add_fusion), channel_id=1, source_target_pairs={{0,2},{2,0},{4,6},{6,4},{8,10},{10,8},{12,14},{14,12},{16,18},{18,... | collective-permute-start | bytes 221192 | tf_op jit(solution)/shard_map/ppermute | solution.py:445
  76.9 19.6 %collective-permute-start.13 = (bf16[2,128,768]{2,1,0:T(8,128)(2,1)S(1)}, bf16[2,128,768]{2,1,0:T(8,128)(2,1)S(1)}, u32[]{:S(2)}, u32[]{:S(2)}) collective-permute-start(bf16[2,128,768]{2,1,0:T(8,128)(2,1)S(1)} %get-tuple-element.76), channel_id=1, source_target_pairs={{0,30},{2,4},{4,2},{6,8},{8,6},{10,12},{12,10},{14,16},{16,14},{18... | collective-permute-start | bytes 1179656 | tf_op jit(solution)/shard_map/ppermute | solution.py:495
  83.4 13.2 %collective-permute-start.22 = (bf16[2,128,768]{2,1,0:T(8,128)(2,1)S(1)}, bf16[2,128,768]{2,1,0:T(8,128)(2,1)S(1)}, u32[]{:S(2)}, u32[]{:S(2)}) collective-permute-start(bf16[2,128,768]{2,1,0:T(8,128)(2,1)S(1)} %far_sum.3), channel_id=1, source_target_pairs={{0,1},{1,0},{2,3},{3,2},{4,5},{5,4},{6,7},{7,6},{8,9},{9,8},{10,11... | collective-permute-start | bytes 1179656 | tf_op jit(solution)/shard_map/ppermute | solution.py:337
  85.2 6.9 %collective-permute-start.23 = (bf16[24,1536]{1,0:T(8,128)(2,1)S(1)}, bf16[24,1536]{1,0:T(8,128)(2,1)S(1)}, u32[]{:S(2)}, u32[]{:S(2)}) collective-permute-start(bf16[24,1536]{1,0:T(8,128)(2,1)S(1)} %add.22), channel_id=1, source_target_pairs={{0,4},{2,6},{4,0},{6,2},{8,12},{10,14},{12,8},{14,10},{16,20},{18,... | collective-permute-start | bytes 221192 | tf_op jit(solution)/shard_map/ppermute | solution.py:445
  92.1 4.4 %collective-permute-start.24 = (bf16[24,1536]{1,0:T(8,128)(2,1)S(1)}, bf16[24,1536]{1,0:T(8,128)(2,1)S(1)}, u32[]{:S(2)}, u32[]{:S(2)}) collective-permute-start(bf16[24,1536]{1,0:T(8,128)(2,1)S(1)} %add.23.refs_3_), channel_id=1, source_target_pairs={{0,1},{1,0},{2,3},{3,2},{4,5},{5,4},{6,7},{7,6},{8,9},{9,8},{10,11... | collective-permute-start | bytes 221192 | tf_op jit(solution)/shard_map/ppermute | solution.py:508

commit v12 on v11

--- a/solution.py
+++ b/solution.py
@@ -94,10 +94,11 @@
     qo_own_ref, kv_own_ref, qo_ref, kv_ref,
     near_own_ref, near_far_ref, side_own_ref, side_far_ref,
     gate_ref, bias_ref, slot_ref,
-    *rest, rows, tokens, q_size, heads, apart,
+    *rest, rows, tokens, q_size, heads, steps, offset, apart,
 ):
-    back_ref, own_ref, far_ref, near_grad_ref, *side_grad_refs = rest[-8 - apart : -3]
-    mixed_ref, dq_ref, sums_ref = rest[-3:]
+    back_ref, own_ref, far_ref, near_grad_ref, result_ref, *side_grad_refs, sums_ref = rest[
+        -7 - apart :
+    ]
     scale = 1.0 / math.sqrt(DH)
     bf16, f32 = jnp.bfloat16, jnp.float32
     tile = 32
@@ -107,28 +108,33 @@
             left, right, (((left_dim,), (right_dim,)), ((), ())), preferred_element_type=f32
         )
 
+    def columns(j):
+        start = pl.multiple_of(j * DH, DH)
+        return pl.ds(start, DH), pl.ds(pl.multiple_of(start + offset, DH), DH)
+
     def load(j):
-        at = slice(j * DH, (j + 1) * DH)
+        at, at_all = columns(j)
         keys, values = [], []
-        for ref in (
-            kv_own_ref, kv_ref, near_own_ref, near_far_ref, side_own_ref, side_far_ref
+        for ref, cols in (
+            (kv_own_ref, at_all), (kv_ref, at), (near_own_ref, at_all), (near_far_ref, at),
+            (side_own_ref, at_all), (side_far_ref, at),
         ):
-            keys.append(ref[0, :, at])
-            values.append(ref[1, :, at])
+            keys.append(ref[0, :, cols])
+            values.append(ref[1, :, cols])
         keys, values = jnp.concatenate(keys, axis=0), jnp.concatenate(values, axis=0)
-        queries = jnp.concatenate([qo_own_ref[0, :, at], qo_ref[0, :, at]], axis=0)
-        cotangent = jnp.concatenate([qo_own_ref[1, :, at], qo_ref[1, :, at]], axis=0)
+        queries = jnp.concatenate([qo_own_ref[0, :, at_all], qo_ref[0, :, at]], axis=0)
+        cotangent = jnp.concatenate([qo_own_ref[1, :, at_all], qo_ref[1, :, at]], axis=0)
         blocks = []
         for start in range(0, tokens, q_size):
             span = slice(start, start + q_size)
             q, o = queries[span], cotangent[span].astype(f32)
-            gate = gate_ref[span, at]
+            gate = gate_ref[span, at_all]
             g = (gate * o).astype(bf16)
             blocks.append((q, o, gate, g, dot(keys, q, 1, 1), dot(values, g, 1, 1)))
         return keys, values, blocks
 
     def work(j, keys, values, blocks):
-        at = slice(j * DH, (j + 1) * DH)
+        at, at_all = columns(j)
         keys_t, values_t = keys.T, values.T
         key_grad = value_grad = sums = None
         for number, (q, o, gate, g, scores, prob_grad) in enumerate(blocks):
@@ -163,8 +169,8 @@
             query_grad = (dot(keys_t, score_grad, 1, 0) * scale).astype(bf16).T
             mixed = (gate * attended).astype(bf16)
             if start == 0:
-                mixed_ref[:, at] = mixed[:rows]
-                dq_ref[:, at] = query_grad[:rows]
+                result_ref[0, :, at] = mixed[:rows]
+                result_ref[1, :, at] = query_grad[:rows]
                 back_ref[0, : q_size - rows, at] = mixed[rows:]
                 back_ref[1, : q_size - rows, at] = query_grad[rows:]
             else:
@@ -175,7 +181,7 @@
             key_grad = dk if key_grad is None else key_grad + dk
             value_grad = dv if value_grad is None else value_grad + dv
             sums = part if sums is None else sums + part
-        sums_ref[:, at] = sums.astype(bf16)
+        sums_ref[:, at_all] = sums.astype(bf16)
         for i, grad in ((0, key_grad * scale), (1, value_grad)):
             own_ref[i, :, at] = grad[:rows]
             far_ref[i, :, at] = grad[rows:tokens]
@@ -187,11 +193,19 @@
             else:
                 side_grad_refs[0][i, :, at] = low[tokens:]
 
-    ready = load(0)
-    for j in range(heads):
-        following = load(j + 1) if j + 1 < heads else None
-        work(j, *ready)
-        ready = following
+    def some(step, carry):
+        first = step * heads
+        ready = load(first)
+        for j in range(heads):
+            following = load(first + j + 1) if j + 1 < heads else None
+            work(first + j, *ready)
+            ready = following
+        return carry
+
+    if steps == 1:
+        some(0, 0)
+    else:
+        lax.fori_loop(0, steps, some, 0)
 
 
 def pack_kernel(place_ref, first_ref, second_ref, own_ref, *rest, groups):
@@ -224,7 +238,9 @@
     out_ref[...] = (total + side).astype(out_ref.dtype)
 
 
-def finish_kernel(place_ref, part_ref, near_ref, side_ref, *refs, groups, parts, p, gate):
+def finish_kernel(
+    place_ref, part_ref, near_ref, side_ref, result_ref, *refs, groups, parts, p, gate
+):
     slabs, refs = refs[: 2 * (groups - 1)], refs[2 * (groups - 1) :]
     slot_refs = refs[1 : 1 + groups] if gate else ()
     scratch = 3 if gate else 2
@@ -244,6 +260,7 @@
         for i, ref in enumerate((first, second)):
             send(slab.at[i], ref.at[:, cols])
 
+    place_slab(result_ref, outs[0], outs[1], 0)
     for k in range(1, groups):
         place_slab(slabs[k - 1], outs[0], outs[1], k)
         place_slab(slabs[groups + k - 2], outs[2], outs[3], k)
@@ -384,20 +401,18 @@
         gate_table,
     )
 
-    batch = next(n for n in (3, 2, 1) if part_heads % n == 0) if tokens <= 256 else 1
-    steps = part_heads // batch
-    block = batch * DH
+    direct = tokens <= 256
+    batch = next(n for n in (3, 2, 1) if part_heads % n == 0) if direct else 1
     q_size = min(256, tokens)
 
     def attention(p, joint):
-        pair = lambda count: pl.BlockSpec((2, count, block), lambda i, place: (0, 0, i))
+        pair = lambda count: pl.BlockSpec((2, count, DH), lambda i, place: (0, 0, i))
         at_part = lambda count: pl.BlockSpec(
-            (2, count, block), lambda i, place: (0, 0, p * steps + i)
+            (2, count, DH), lambda i, place: (0, 0, p * part_heads + i)
         )
-        at_head = pl.BlockSpec(
-            (rows, block), lambda i, place: (0, (head_at(place) * parts + p) * steps + i)
+        column = lambda count: pl.BlockSpec(
+            (count, DH), lambda i, place: (0, p * part_heads + i)
         )
-        column = lambda count: pl.BlockSpec((count, block), lambda i, place: (0, p * steps + i))
         struct = jax.ShapeDtypeStruct
         side_counts = (rows, far_rows) if p + 1 == parts else (tokens,)
         inputs = [
@@ -405,37 +420,36 @@
             near_own, near_far[p], side_own, side_far[p],
             gate, bias, slot,
         ]
+        in_specs = [
+            at_part(rows), at_part(rows), pair(far_rows), pair(far_rows),
+            at_part(rows), pair(far_rows), at_part(rows), pair(far_rows),
+            column(tokens), whole((3 * tokens, tokens)), whole((slots, tokens)),
+        ]
+        counts = (far_rows, rows, far_rows, tokens, rows, *side_counts)
+        out_specs = [*[pair(count) for count in counts], column(slots)]
+        if direct:
+            in_specs, out_specs = [in_vmem] * len(in_specs), [in_vmem] * len(out_specs)
+        types = [f32 if i in (1, 2) else bf16 for i in range(len(counts))]
         return pl.pallas_call(
             functools.partial(
                 attention_kernel,
-                rows=rows, tokens=tokens, q_size=q_size, heads=batch, apart=p + 1 == parts,
+                rows=rows, tokens=tokens, q_size=q_size, apart=p + 1 == parts, heads=batch,
+                steps=part_heads // batch if direct else 1,
+                offset=p * part_width if direct else 0,
             ),
             grid_spec=pltpu.PrefetchScalarGridSpec(
                 num_scalar_prefetch=1,
-                grid=(steps,),
-                in_specs=[
-                    at_part(rows), at_part(rows), pair(far_rows), pair(far_rows),
-                    at_part(rows), pair(far_rows), at_part(rows), pair(far_rows),
-                    column(tokens), whole((3 * tokens, tokens)), whole((slots, tokens)),
-                ]
-                + [pl.BlockSpec(memory_space=pl.ANY)] * len(joint),
-                out_specs=[
-                    pair(far_rows), pair(rows), pair(far_rows), pair(tokens),
-                    *[pair(count) for count in side_counts],
-                    at_head, at_head, column(slots),
-                ],
+                grid=(1,) if direct else (part_heads,),
+                in_specs=in_specs + [anywhere] * len(joint),
+                out_specs=out_specs,
             ),
             out_shape=[
-                struct((2, far_rows, part_width), bf16),
-                struct((2, rows, part_width), f32),
-                struct((2, far_rows, part_width), f32),
-                struct((2, tokens, part_width), bf16),
-                *[struct((2, count, part_width), bf16) for count in side_counts],
-                struct((rows, full_width), bf16),
-                struct((rows, full_width), bf16),
+                *[
+                    struct((2, count, part_width), kind) for count, kind in zip(counts, types)
+                ],
                 struct((slots, width), bf16),
             ],
-            input_output_aliases={1 + len(inputs) + i: 4 + len(side_counts) + i for i in range(len(joint))},
+            input_output_aliases={1 + len(inputs) + i: len(counts) + i for i in range(len(joint))},
             compiler_params=params,
             cost_estimate=cheap,
             name="attention",
@@ -467,11 +481,12 @@
         far_sent.append(far_grad)
         grad_far.append(from_peers(far_grad))
 
-    joint, own, far = (), [], []
+    joint, own, far, own_results = (), [], [], []
     back_far, side_back_far, near_back, side_back_own, far_sent, grad_far = [], [], [], [], [], []
     for p in range(parts):
-        back, own_part, far_part, near_grad, *rest = attention(p, joint)
-        side_grads, joint = rest[:-3], rest[-3:]
+        back, own_part, far_part, near_grad, result, *rest = attention(p, joint)
+        side_grads, joint = rest[:-1], rest[-1:]
+        own_results.append(result)
         if p + 1 < parts:
             side_grads, *_ = tie((side_grads, side_far[p + 1], near_far[p + 1], qo_far[p + 1]))
         if p > 0:
@@ -485,7 +500,7 @@
         near_back.append(lax.ppermute(near_grad, "ctx", near_pairs))
         back_far.append(from_peers(back))
         if p > 0:
-            sums = rounds(bits[2:], joint[2])
+            sums = rounds(bits[2:], joint[0])
             side_back_far[p - 1], sums, _ = tie((side_back_far[p - 1], sums, back_far[p]))
             summed(p - 1)
         if p + 1 < parts:
@@ -493,9 +508,8 @@
             continue
         side_grad_own, _ = tie((side_grads[0], side_back_far[p]))
         side_back_own.append(lax.ppermute(side_grad_own, "ctx", side_pairs))
-    mixed, query_grad = joint[:2]
     if parts == 1:
-        sums = rounds(bits[2:], joint[2])
+        sums = rounds(bits[2:], joint[0])
 
     sums = rounds(bits[:1], sums)
     side_back_far, sums, back_far, grad_far = tie((side_back_far, sums, back_far, grad_far))
@@ -510,17 +524,17 @@
 
     sums, _ = tie((sums, far_sent[-1]))
     slabs = to_all(bits[1:2], [], sums)
-    results = [mixed, query_grad]
+    results = []
     struct = jax.ShapeDtypeStruct
     for p in range(parts):
         gate = p + 1 == parts
-        operands = [own[p], near_back[p], side_back_own[p], *back_far[p], *grad_far[p]]
+        operands = [own[p], near_back[p], side_back_own[p], own_results[p], *back_far[p], *grad_far[p]]
         if gate:
             operands += [noise_level.reshape(1, span_total), *slabs]
         scratch = [pltpu.VMEM((2, rows, part_width), bf16)]
         if gate:
             scratch.append(pltpu.VMEM((level_count, full_width), f32))
-        scratch.append(pltpu.SemaphoreType.DMA((4 * groups - 2 + groups,)))
+        scratch.append(pltpu.SemaphoreType.DMA((4 * groups + groups,)))
         results = pl.pallas_call(
             functools.partial(finish_kernel, groups=groups, parts=parts, p=p, gate=gate),
             grid_spec=pltpu.PrefetchScalarGridSpec(

time: 98.5 us -> 97.3 us (0.988)
  Pallas kernels: 23.6 us -> 21.1 us
  waiting for transfers between devices: 42 us -> 43.5 us
    pallas_call x2, Pallas kernels: 15.6 us -> 12.8 us  [attention(): pl.pallas_call(functools.partial(attention_kernel, rows=rows, tokens=toke...]
    ppermute x4, waiting for transfers between devices: 7.26 us -> 8.53 us  [from_peers(): arrived.append(lax.ppermute(part, 'head', pairs))]
  transfers between devices with their start and end apart: 25 -> 25, of which waited for: 10 -> 11; matrix products, arithmetic and copies ran while one was open for 0% -> 0% of each run, Pallas kernels for 19% -> 17%
where the time goes in v12:
time: 97.3 us; the launch traced here: 97.2 us
  waiting for transfers between devices  43.5 us (45%)
  starting transfers between devices  31.7 us (33%)
  Pallas kernels  21.1 us (22%)
    ppermute x4, waiting for transfers between devices, to_peers(): arrived.append(lax.ppermute(part, 'head', pairs))  21.4 us
    pallas_call x2, Pallas kernels, attention(): pl.pallas_call(functools.partial(attention_kernel, rows=rows, tokens=toke...  12.8 us
    ppermute x5, waiting for transfers between devices, shifted(): return lax.ppermute(array, 'ctx', [(i, i ^ step) for i in range(ctx_count)])  12.3 us
    ppermute x4, waiting for transfers between devices, from_peers(): arrived.append(lax.ppermute(part, 'head', pairs))  8.53 us
    ppermute x1, starting transfers between devices, per_device(): side_own = lax.ppermute(kv_own, 'ctx', side_pairs)  5.64 us
    ppermute x4, starting transfers between devices, from_peers(): arrived.append(lax.ppermute(part, 'head', pairs))  5.57 us
    ppermute x5, starting transfers between devices, shifted(): return lax.ppermute(array, 'ctx', [(i, i ^ step) for i in range(ctx_count)])  5.48 us
    ppermute x4, starting transfers between devices, to_peers(): arrived.append(lax.ppermute(part, 'head', pairs))  5.06 us
  transfers between devices with their start and end apart: 25, of which 11 were waited for; matrix products, arithmetic and copies ran while one was open for 0% of the time, Pallas kernels for 17%

profile of v12, /device:TPU:0, one launch (start us, length us, event | category | flops | bytes accessed | tf_op | source)
XLA Modules:
  0.0 97.2 jit_solution(8157323783361429922)
XLA Ops:
  0.6 0.0 copy-start.3
  0.6 0.0 copy-start.2
  0.7 0.0 copy-start.1
  0.7 0.0 copy-start.4
  0.7 2.8 %pack.3 = (bf16[2,128,1536]{2,1,0:T(8,128)(2,1)}, bf16[2,128,768]{2,1,0:T(8,128)(2,1)}, bf16[2,128,768]{2,1,0:T(8,128)(2,1)}) custom-call(s32[1]{0:T(128)} %bitcast.place_ref, bf16[128,3072]{1,0:T(8,128)(2,1)} %first_ref.3, bf16[128,3072]{1,0:T(8,128)(2,1)} %second_ref.3), custom_call_target="tpu_custom_call" | custom-call | flops 1 | bytes 1 | tf_op jit(solution)/shard_map/pack/pallas_call | solution.py:326
  3.5 0.5 collective-permute-start.2
  4.0 5.6 %collective-permute-start.1 = (bf16[2,128,1536]{2,1,0:T(8,128)(2,1)}, bf16[2,128,1536]{2,1,0:T(8,128)(2,1)S(1)}, u32[]{:S(2)}, u32[]{:S(2)}) collective-permute-start(bf16[2,128,1536]{2,1,0:T(8,128)(2,1)} %get-tuple-element.51.kv_own_ref), channel_id=1, source_target_pairs={{0,30},{2,4},{4,2},{6,8},{8,6},{10,12},{12,10},{14,16},{16,14},{18... | collective-permute-start | bytes 2359304 | tf_op jit(solution)/shard_map/ppermute | solution.py:359
  9.7 1.5 %collective-permute-start.6 = (bf16[2,128,768]{2,1,0:T(8,128)(2,1)}, bf16[2,128,768]{2,1,0:T(8,128)(2,1)S(1)}, u32[]{:S(2)}, u32[]{:S(2)}) collective-permute-start(bf16[2,128,768]{2,1,0:T(8,128)(2,1)} %get-tuple-element.59), channel_id=1, source_target_pairs={{0,1},{1,0},{2,3},{3,2},{4,5},{5,4},{6,7},{7,6},{8,9},{9,8},{10,11... | collective-permute-start | bytes 1179656 | tf_op jit(solution)/shard_map/ppermute | solution.py:346
  11.2 0.5 collective-permute-start
  11.7 0.3 pack.2
  12.0 10.0 %collective-permute-done.6.kv_ref = bf16[2,128,768]{2,1,0:T(8,128)(2,1)S(1)} collective-permute-done((bf16[2,128,768]{2,1,0:T(8,128)(2,1)}, bf16[2,128,768]{2,1,0:T(8,128)(2,1)S(1)}, u32[]{:S(2)}, u32[]{:S(2)}) %collective-permute-start.6) | collective-permute-done | bytes 393248 | tf_op jit(solution)/shard_map/ppermute | solution.py:346
  21.9 1.5 %collective-permute-start.7 = (bf16[2,128,768]{2,1,0:T(8,128)(2,1)S(1)}, bf16[2,128,768]{2,1,0:T(8,128)(2,1)S(1)}, u32[]{:S(2)}, u32[]{:S(2)}) collective-permute-start(bf16[2,128,768]{2,1,0:T(8,128)(2,1)S(1)} %get-tuple-element.60), channel_id=1, source_target_pairs={{0,1},{1,0},{2,3},{3,2},{4,5},{5,4},{6,7},{7,6},{8,9},{9,8},{10,11... | collective-permute-start | bytes 1179656 | tf_op jit(solution)/shard_map/ppermute | solution.py:346
  23.5 0.0 collective-permute-start.9
  23.5 6.9 %collective-permute-done.kv_ref = bf16[2,128,768]{2,1,0:T(8,128)(2,1)S(1)} collective-permute-done((bf16[2,128,768]{2,1,0:T(8,128)(2,1)}, bf16[2,128,768]{2,1,0:T(8,128)(2,1)S(1)}, u32[]{:S(2)}, u32[]{:S(2)}) %collective-permute-start) | collective-permute-done | bytes 393248 | tf_op jit(solution)/shard_map/ppermute | solution.py:346
  30.4 0.0 collective-permute-start.8
  30.4 0.0 collective-permute-done.2.near_own_ref
  30.4 0.6 collective-permute-start.5
  31.0 0.0 collective-permute-done.1.side_own_ref
  31.0 0.0 collective-permute-start.4
  31.0 4.5 %collective-permute-done.7.qo_ref = bf16[2,128,768]{2,1,0:T(8,128)(2,1)S(1)} collective-permute-done((bf16[2,128,768]{2,1,0:T(8,128)(2,1)S(1)}, bf16[2,128,768]{2,1,0:T(8,128)(2,1)S(1)}, u32[]{:S(2)}, u32[]{:S(2)}) %collective-permute-start.7) | collective-permute-done | bytes 393248 | tf_op jit(solution)/shard_map/ppermute | solution.py:346
  35.5 1.5 %collective-permute-start.3 = (bf16[2,128,768]{2,1,0:T(8,128)(2,1)S(1)}, bf16[2,128,768]{2,1,0:T(8,128)(2,1)S(1)}, u32[]{:S(2)}, u32[]{:S(2)}) collective-permute-start(bf16[2,128,768]{2,1,0:T(8,128)(2,1)S(1)} %get-tuple-element.54), channel_id=1, source_target_pairs={{0,1},{1,0},{2,3},{3,2},{4,5},{5,4},{6,7},{7,6},{8,9},{9,8},{10,11... | collective-permute-start | bytes 1179656 | tf_op jit(solution)/shard_map/ppermute | solution.py:346
  37.0 0.0 copy-done.6
  37.0 1.9 %prep.1 = (f32[768,256]{1,0:T(8,128)S(1)}, f32[256,1536]{1,0:T(8,128)S(1)}, bf16[24,256]{1,0:T(8,128)(2,1)S(1)}) custom-call(s32[1]{0:T(128)} %bitcast.place_ref, s32[32,128]{1,0:T(8,128)S(1)} %bitcast.3, s32[1,24]{1,0:T(1,128)S(1)} %bitcast.4, s32[24,24]{1,0:T(8,128)S(1)} %copy-done.5, f32[128,3072]{1,0:T(8,128)S(1)} %copy-done.1), custom_call_target="tpu_custom_call" | custom-call | flops 1 | bytes 1 | tf_op jit(solution)/shard_map/prep/pallas_call | solution.py:371
  38.9 0.0 collective-permute-done.9.side_far_ref
  38.9 0.0 collective-permute-done.8.near_far_ref
  38.9 6.4 %attention.2 = (bf16[2,128,768]{2,1,0:T(8,128)(2,1)S(1)}, f32[2,128,768]{2,1,0:T(8,128)S(1)}, f32[2,128,768]{2,1,0:T(8,128)S(1)}, bf16[2,256,768]{2,1,0:T(8,128)...) custom-call(s32[1]{0:T(128)} %bitcast.place_ref, ...), custom_call_target="tpu_custom_call" | custom-call | flops 1 | bytes 1 | tf_op jit(solution)/shard_map/attention/pallas_call | solution.py:433
  45.3 0.6 collective-permute-start.14
  45.9 0.0 collective-permute-done.5.side_far_ref
  45.9 0.0 collective-permute-done.4.near_far_ref
  45.9 0.0 collective-permute-done.3.qo_ref
  45.9 0.8 collective-permute-start.11
  46.7 0.8 collective-permute-start.20
  47.5 6.4 %attention.3 = (bf16[2,128,768]{2,1,0:T(8,128)(2,1)S(1)}, f32[2,128,768]{2,1,0:T(8,128)S(1)}, f32[2,128,768]{2,1,0:T(8,128)S(1)}, bf16[2,256,768]{2,1,0:T(8,128)...) custom-call(s32[1]{0:T(128)} %bitcast.place_ref, ...), custom_call_target="tpu_custom_call", output_to_operand_aliasing={{7}: (12, {})} | custom-call | flops 1 | bytes 1 | tf_op jit(solution)/shard_map/attention/pallas_call | solution.py:433
  53.8 0.6 collective-permute-done.14.refs_0_
  54.4 4.9 %collective-permute-start.17 = (bf16[24,1536]{1,0:T(8,128)(2,1)S(1)}, bf16[24,1536]{1,0:T(8,128)(2,1)S(1)}, u32[]{:S(2)}, u32[]{:S(2)}) collective-permute-start(bf16[24,1536]{1,0:T(8,128)(2,1)S(1)} %get-tuple-element.75), channel_id=1, source_target_pairs={{0,24},{2,26},{4,28},{6,30},{8,16},{10,18},{12,20},{14,22},{16,8},... | collective-permute-start | bytes 221192 | tf_op jit(solution)/shard_map/ppermute | solution.py:459
  59.3 0.0 collective-permute-start.16
  59.3 0.6 collective-permute-start.15
  59.9 2.5 %collective-permute-done.17 = bf16[24,1536]{1,0:T(8,128)(2,1)S(1)} collective-permute-done((bf16[24,1536]{1,0:T(8,128)(2,1)S(1)}, bf16[24,1536]{1,0:T(8,128)(2,1)S(1)}, u32[]{:S(2)}, u32[]{:S(2)}) %collective-permute-start.17) | collective-permute-done | bytes 73760 | tf_op jit(solution)/shard_map/ppermute | solution.py:459
  62.4 1.4 %collective-permute-start.18 = (bf16[2,128,768]{2,1,0:T(8,128)(2,1)S(1)}, bf16[2,128,768]{2,1,0:T(8,128)(2,1)S(1)}, u32[]{:S(2)}, u32[]{:S(2)}) collective-permute-start(bf16[2,128,768]{2,1,0:T(8,128)(2,1)S(1)} %get-tuple-element.76), channel_id=1, source_target_pairs={{0,1},{1,0},{2,3},{3,2},{4,5},{5,4},{6,7},{7,6},{8,9},{9,8},{10,11... | collective-permute-start | bytes 1179656 | tf_op jit(solution)/shard_map/ppermute | solution.py:354
  63.8 1.6 %collective-permute-done.16 = bf16[24,1536]{1,0:T(8,128)(2,1)S(1)} collective-permute-done((bf16[24,1536]{1,0:T(8,128)(2,1)S(1)}, bf16[24,1536]{1,0:T(8,128)(2,1)S(1)}, u32[]{:S(2)}, u32[]{:S(2)}) %collective-permute-start.16) | collective-permute-done | bytes 73760 | tf_op jit(solution)/shard_map/ppermute | solution.py:459
  65.4 0.0 collective-permute-start.10
  65.4 0.0 collective-permute-done.15
  65.4 0.0 collective-permute-done.11.side_ref
  65.4 2.7 %collective-permute-start.12 = (bf16[2,128,768]{2,1,0:T(8,128)(2,1)S(1)}, bf16[2,128,768]{2,1,0:T(8,128)(2,1)S(1)}, u32[]{:S(2)}, u32[]{:S(2)}) collective-permute-start(bf16[2,128,768]{2,1,0:T(8,128)(2,1)S(1)} %get-tuple-element.69), channel_id=1, source_target_pairs={{0,30},{2,4},{4,2},{6,8},{8,6},{10,12},{12,10},{14,16},{16,14},{18... | collective-permute-start | bytes 1179656 | tf_op jit(solution)/shard_map/ppermute | solution.py:499
  68.1 4.2 %collective-permute-done.18.refs_0_ = bf16[2,128,768]{2,1,0:T(8,128)(2,1)S(1)} collective-permute-done((bf16[2,128,768]{2,1,0:T(8,128)(2,1)S(1)}, bf16[2,128,768]{2,1,0:T(8,128)(2,1)S(1)}, u32[]{:S(2)}, u32[]{:S(2)}) %collective-permute-start.18) | collective-permute-done | bytes 393248 | tf_op jit(solution)/shard_map/ppermute | solution.py:354
  72.3 0.0 collective-permute-done.20.near_ref
  72.3 0.2 far_sum.2
  72.5 1.8 %collective-permute-start.21 = (bf16[2,128,768]{2,1,0:T(8,128)(2,1)S(1)}, bf16[2,128,768]{2,1,0:T(8,128)(2,1)S(1)}, u32[]{:S(2)}, u32[]{:S(2)}) collective-permute-start(bf16[2,128,768]{2,1,0:T(8,128)(2,1)S(1)} %far_sum.2), channel_id=1, source_target_pairs={{0,1},{1,0},{2,3},{3,2},{4,5},{5,4},{6,7},{7,6},{8,9},{9,8},{10,11... | collective-permute-start | bytes 1179656 | tf_op jit(solution)/shard_map/ppermute | solution.py:354
  74.3 0.0 collective-permute-start.19
  74.3 1.3 %collective-permute-done.19 = bf16[24,1536]{1,0:T(8,128)(2,1)S(1)} collective-permute-done((bf16[24,1536]{1,0:T(8,128)(2,1)S(1)}, bf16[24,1536]{1,0:T(8,128)(2,1)S(1)}, u32[]{:S(2)}, u32[]{:S(2)}) %collective-permute-start.19) | collective-permute-done | bytes 73760 | tf_op jit(solution)/shard_map/ppermute | solution.py:459
  75.6 0.0 collective-permute-done.12.side_ref
  75.6 2.6 %collective-permute-start.13 = (bf16[2,128,768]{2,1,0:T(8,128)(2,1)S(1)}, bf16[2,128,768]{2,1,0:T(8,128)(2,1)S(1)}, u32[]{:S(2)}, u32[]{:S(2)}) collective-permute-start(bf16[2,128,768]{2,1,0:T(8,128)(2,1)S(1)} %get-tuple-element.70), channel_id=1, source_target_pairs={{0,30},{2,4},{4,2},{6,8},{8,6},{10,12},{12,10},{14,16},{16,14},{18... | collective-permute-start | bytes 1179656 | tf_op jit(solution)/shard_map/ppermute | solution.py:510
  78.2 3.8 %collective-permute-done.21.refs_1_ = bf16[2,128,768]{2,1,0:T(8,128)(2,1)S(1)} collective-permute-done((bf16[2,128,768]{2,1,0:T(8,128)(2,1)S(1)}, bf16[2,128,768]{2,1,0:T(8,128)(2,1)S(1)}, u32[]{:S(2)}, u32[]{:S(2)}) %collective-permute-start.21) | collective-permute-done | bytes 393248 | tf_op jit(solution)/shard_map/ppermute | solution.py:354
  81.9 0.0 collective-permute-done.10.near_ref
  81.9 0.1 far_sum.3
  82.1 1.8 %collective-permute-start.22 = (bf16[2,128,768]{2,1,0:T(8,128)(2,1)S(1)}, bf16[2,128,768]{2,1,0:T(8,128)(2,1)S(1)}, u32[]{:S(2)}, u32[]{:S(2)}) collective-permute-start(bf16[2,128,768]{2,1,0:T(8,128)(2,1)S(1)} %far_sum.3), channel_id=1, source_target_pairs={{0,1},{1,0},{2,3},{3,2},{4,5},{5,4},{6,7},{7,6},{8,9},{9,8},{10,11... | collective-permute-start | bytes 1179656 | tf_op jit(solution)/shard_map/ppermute | solution.py:354
  83.9 0.0 collective-permute-start.23
  83.9 7.0 %collective-permute-done.23 = bf16[24,1536]{1,0:T(8,128)(2,1)S(1)} collective-permute-done((bf16[24,1536]{1,0:T(8,128)(2,1)S(1)}, bf16[24,1536]{1,0:T(8,128)(2,1)S(1)}, u32[]{:S(2)}, u32[]{:S(2)}) %collective-permute-start.23) | collective-permute-done | bytes 73760 | tf_op jit(solution)/shard_map/ppermute | solution.py:459
  90.9 2.0 %collective-permute-start.24 = (bf16[24,1536]{1,0:T(8,128)(2,1)S(1)}, bf16[24,1536]{1,0:T(8,128)(2,1)S(1)}, u32[]{:S(2)}, u32[]{:S(2)}) collective-permute-start(bf16[24,1536]{1,0:T(8,128)(2,1)S(1)} %add.23.refs_3_), channel_id=1, source_target_pairs={{0,1},{1,0},{2,3},{3,2},{4,5},{5,4},{6,7},{7,6},{8,9},{9,8},{10,11... | collective-permute-start | bytes 221192 | tf_op jit(solution)/shard_map/ppermute | solution.py:522
  92.9 1.2 %finish.2 = (bf16[128,3072]{1,0:T(8,128)(2,1)}, bf16[128,3072]{1,0:T(8,128)(2,1)}, bf16[128,3072]{1,0:T(8,128)(2,1)}, bf16[128,3072]{1,0:T(8,128)(2,1)}) custom-call(s32[1]{0:T(128)} %bitcast.place_ref, f32[2,128,768]{2,1,0:T(8,128)S(1)} %get-tuple-element.87.part_ref, bf16[2,256,768]{2,1,0:T(8,128)(2,1)S(1)} %collective-permute-done.20.near_ref, ...), custom_call_target="tpu_custom_call" | custom-call | flops 1 | bytes 1 | tf_op jit(solution)/shard_map/finish/pallas_call | solution.py:538
  94.1 1.2 %collective-permute-done.24.refs_4_ = bf16[24,1536]{1,0:T(8,128)(2,1)S(1)} collective-permute-done((bf16[24,1536]{1,0:T(8,128)(2,1)S(1)}, bf16[24,1536]{1,0:T(8,128)(2,1)S(1)}, u32[]{:S(2)}, u32[]{:S(2)}) %collective-permute-start.24) | collective-permute-done | bytes 73760 | tf_op jit(solution)/shard_map/ppermute | solution.py:522
  95.3 0.0 collective-permute-done.13.side_ref
  95.3 0.0 collective-permute-done.22.refs_1_
  95.3 1.9 %finish.3 = (bf16[128,3072]{1,0:T(8,128)(2,1)}, bf16[128,3072]{1,0:T(8,128)(2,1)}, bf16[128,3072]{1,0:T(8,128)(2,1)}, bf16[128,3072]{1,0:T(8,128)(2,1)}, f32[128,3072]{1,0:T(8,128)}) custom-call(s32[1]{0:T(128)} %bitcast.place_ref, ...), custom_call_target="tpu_custom_call", output_to_operand_aliasing={{0}: (10, {}), {1}: (11, {}), {2}: (12, {}), {3}: (13, {})} | custom-call | flops 1 | bytes 1 | tf_op jit(solution)/shard_map/finish/pallas_call | solution.py:538
  (12 shorter events, 0.1 us)
Async XLA Ops:
  0.6 11.1 %copy-start.3 = (bf16[128,3072]{1,0:T(8,128)(2,1)S(1)}, bf16[128,3072]{1,0:T(8,128)(2,1)}, u32[]{:S(2)}) copy-start(bf16[128,3072]{1,0:T(8,128)(2,1)} %second_ref.2) | copy-start | bytes 2359300
  0.6 11.1 %copy-start.2 = (bf16[128,3072]{1,0:T(8,128)(2,1)S(1)}, bf16[128,3072]{1,0:T(8,128)(2,1)}, u32[]{:S(2)}) copy-start(bf16[128,3072]{1,0:T(8,128)(2,1)} %first_ref.2) | copy-start | bytes 2359300
  0.7 36.3 %copy-start.1 = (f32[128,3072]{1,0:T(8,128)S(1)}, f32[128,3072]{1,0:T(8,128)}, u32[]{:S(2)}) copy-start(f32[128,3072]{1,0:T(8,128)} %table_ref.1) | copy-start | bytes 4718596
  0.7 36.3 %copy-start.4 = (s32[4096]{0:T(1024)S(1)}, s32[4096]{0:T(1024)}, u32[]{:S(2)}) copy-start(s32[4096]{0:T(1024)} %param.13) | copy-start | bytes 49156
  0.7 36.3 %copy-start.5 = (s32[24,24]{1,0:T(8,128)S(1)}, s32[24,24]{1,0:T(8,128)}, u32[]{:S(2)}) copy-start(s32[24,24]{1,0:T(8,128)} %mask_ref.1) | copy-start | bytes 6916
  0.7 36.3 %copy-start.6 = (s32[24]{0:T(128)S(1)}, s32[24]{0:T(128)}, u32[]{:S(2)}) copy-start(s32[24]{0:T(128)} %param.14) | copy-start | bytes 292
  3.5 26.9 %collective-permute-start.2 = (bf16[2,128,1536]{2,1,0:T(8,128)(2,1)}, bf16[2,128,1536]{2,1,0:T(8,128)(2,1)S(1)}, u32[]{:S(2)}, u32[]{:S(2)}) collective-permute-start(bf16[2,128,1536]{2,1,0:T(8,128)(2,1)} %get-tuple-element.51.kv_own_ref), channel_id=1, source_target_pairs={{0,2},{2,0},{4,6},{6,4},{8,10},{10,8},{12,14},{14,12},{16,18},{18,... | collective-permute-start | bytes 2359304 | tf_op jit(solution)/shard_map/ppermute | solution.py:360
  4.0 26.9 %collective-permute-start.1 = (bf16[2,128,1536]{2,1,0:T(8,128)(2,1)}, bf16[2,128,1536]{2,1,0:T(8,128)(2,1)S(1)}, u32[]{:S(2)}, u32[]{:S(2)}) collective-permute-start(bf16[2,128,1536]{2,1,0:T(8,128)(2,1)} %get-tuple-element.51.kv_own_ref), channel_id=1, source_target_pairs={{0,30},{2,4},{4,2},{6,8},{8,6},{10,12},{12,10},{14,16},{16,14},{18... | collective-permute-start | bytes 2359304 | tf_op jit(solution)/shard_map/ppermute | solution.py:359
  9.7 12.3 %collective-permute-start.6 = (bf16[2,128,768]{2,1,0:T(8,128)(2,1)}, bf16[2,128,768]{2,1,0:T(8,128)(2,1)S(1)}, u32[]{:S(2)}, u32[]{:S(2)}) collective-permute-start(bf16[2,128,768]{2,1,0:T(8,128)(2,1)} %get-tuple-element.59), channel_id=1, source_target_pairs={{0,1},{1,0},{2,3},{3,2},{4,5},{5,4},{6,7},{7,6},{8,9},{9,8},{10,11... | collective-permute-start | bytes 1179656 | tf_op jit(solution)/shard_map/ppermute | solution.py:346
  11.2 27.7 %copy-start = (bf16[2,128,1536]{2,1,0:T(8,128)(2,1)S(1)}, bf16[2,128,1536]{2,1,0:T(8,128)(2,1)}, u32[]{:S(2)}) copy-start(bf16[2,128,1536]{2,1,0:T(8,128)(2,1)} %get-tuple-element.51.kv_own_ref) | copy-start | bytes 2359300
  11.2 19.2 %collective-permute-start = (bf16[2,128,768]{2,1,0:T(8,128)(2,1)}, bf16[2,128,768]{2,1,0:T(8,128)(2,1)S(1)}, u32[]{:S(2)}, u32[]{:S(2)}) collective-permute-start(bf16[2,128,768]{2,1,0:T(8,128)(2,1)} %get-tuple-element.53), channel_id=1, source_target_pairs={{0,1},{1,0},{2,3},{3,2},{4,5},{5,4},{6,7},{7,6},{8,9},{9,8},{10,11... | collective-permute-start | bytes 1179656 | tf_op jit(solution)/shard_map/ppermute | solution.py:346
  21.9 13.5 %collective-permute-start.7 = (bf16[2,128,768]{2,1,0:T(8,128)(2,1)S(1)}, bf16[2,128,768]{2,1,0:T(8,128)(2,1)S(1)}, u32[]{:S(2)}, u32[]{:S(2)}) collective-permute-start(bf16[2,128,768]{2,1,0:T(8,128)(2,1)S(1)} %get-tuple-element.60), channel_id=1, source_target_pairs={{0,1},{1,0},{2,3},{3,2},{4,5},{5,4},{6,7},{7,6},{8,9},{9,8},{10,11... | collective-permute-start | bytes 1179656 | tf_op jit(solution)/shard_map/ppermute | solution.py:346
  23.5 15.4 %collective-permute-start.9 = (bf16[2,128,768]{2,1,0:T(8,128)(2,1)S(1)}, bf16[2,128,768]{2,1,0:T(8,128)(2,1)S(1)}, u32[]{:S(2)}, u32[]{:S(2)}) collective-permute-start(bf16[2,128,768]{2,1,0:T(8,128)(2,1)S(1)} %collective-permute-done.6.kv_ref), channel_id=1, source_target_pairs={{0,30},{2,4},{4,2},{6,8},{8,6},{10,12},{12,10},{14,16},{16,14},{18... | collective-permute-start | bytes 1179656 | tf_op jit(solution)/shard_map/ppermute | solution.py:362
  30.4 8.5 %collective-permute-start.8 = (bf16[2,128,768]{2,1,0:T(8,128)(2,1)S(1)}, bf16[2,128,768]{2,1,0:T(8,128)(2,1)S(1)}, u32[]{:S(2)}, u32[]{:S(2)}) collective-permute-start(bf16[2,128,768]{2,1,0:T(8,128)(2,1)S(1)} %collective-permute-done.6.kv_ref), channel_id=1, source_target_pairs={{0,2},{2,0},{4,6},{6,4},{8,10},{10,8},{12,14},{14,12},{16,18},{18,... | collective-permute-start | bytes 1179656 | tf_op jit(solution)/shard_map/ppermute | solution.py:363
  30.4 15.5 %collective-permute-start.5 = (bf16[2,128,768]{2,1,0:T(8,128)(2,1)S(1)}, bf16[2,128,768]{2,1,0:T(8,128)(2,1)S(1)}, u32[]{:S(2)}, u32[]{:S(2)}) collective-permute-start(bf16[2,128,768]{2,1,0:T(8,128)(2,1)S(1)} %collective-permute-done.kv_ref), channel_id=1, source_target_pairs={{0,30},{2,4},{4,2},{6,8},{8,6},{10,12},{12,10},{14,16},{16,14},{18... | collective-permute-start | bytes 1179656 | tf_op jit(solution)/shard_map/ppermute | solution.py:362
  31.0 14.9 %collective-permute-start.4 = (bf16[2,128,768]{2,1,0:T(8,128)(2,1)S(1)}, bf16[2,128,768]{2,1,0:T(8,128)(2,1)S(1)}, u32[]{:S(2)}, u32[]{:S(2)}) collective-permute-start(bf16[2,128,768]{2,1,0:T(8,128)(2,1)S(1)} %collective-permute-done.kv_ref), channel_id=1, source_target_pairs={{0,2},{2,0},{4,6},{6,4},{8,10},{10,8},{12,14},{14,12},{16,18},{18,... | collective-permute-start | bytes 1179656 | tf_op jit(solution)/shard_map/ppermute | solution.py:363
  35.5 10.4 %collective-permute-start.3 = (bf16[2,128,768]{2,1,0:T(8,128)(2,1)S(1)}, bf16[2,128,768]{2,1,0:T(8,128)(2,1)S(1)}, u32[]{:S(2)}, u32[]{:S(2)}) collective-permute-start(bf16[2,128,768]{2,1,0:T(8,128)(2,1)S(1)} %get-tuple-element.54), channel_id=1, source_target_pairs={{0,1},{1,0},{2,3},{3,2},{4,5},{5,4},{6,7},{7,6},{8,9},{9,8},{10,11... | collective-permute-start | bytes 1179656 | tf_op jit(solution)/shard_map/ppermute | solution.py:346
  45.3 9.1 %collective-permute-start.14 = (bf16[2,128,768]{2,1,0:T(8,128)(2,1)S(1)}, bf16[2,128,768]{2,1,0:T(8,128)(2,1)S(1)}, u32[]{:S(2)}, u32[]{:S(2)}) collective-permute-start(bf16[2,128,768]{2,1,0:T(8,128)(2,1)S(1)} %get-tuple-element.74), channel_id=1, source_target_pairs={{0,1},{1,0},{2,3},{3,2},{4,5},{5,4},{6,7},{7,6},{8,9},{9,8},{10,11... | collective-permute-start | bytes 1179656 | tf_op jit(solution)/shard_map/ppermute | solution.py:354
  45.9 19.5 %collective-permute-start.11 = (bf16[2,256,768]{2,1,0:T(8,128)(2,1)S(1)}, bf16[2,256,768]{2,1,0:T(8,128)(2,1)S(1)}, u32[]{:S(2)}, u32[]{:S(2)}) collective-permute-start(bf16[2,256,768]{2,1,0:T(8,128)(2,1)S(1)} %get-tuple-element.67), channel_id=1, source_target_pairs={{0,30},{2,4},{4,2},{6,8},{8,6},{10,12},{12,10},{14,16},{16,14},{18... | collective-permute-start | bytes 2359304 | tf_op jit(solution)/shard_map/ppermute | solution.py:499
  46.7 25.6 %collective-permute-start.20 = (bf16[2,256,768]{2,1,0:T(8,128)(2,1)S(1)}, bf16[2,256,768]{2,1,0:T(8,128)(2,1)S(1)}, u32[]{:S(2)}, u32[]{:S(2)}) collective-permute-start(bf16[2,256,768]{2,1,0:T(8,128)(2,1)S(1)} %get-tuple-element.81), channel_id=1, source_target_pairs={{0,2},{2,0},{4,6},{6,4},{8,10},{10,8},{12,14},{14,12},{16,18},{18,... | collective-permute-start | bytes 2359304 | tf_op jit(solution)/shard_map/ppermute | solution.py:500
  54.4 8.0 %collective-permute-start.17 = (bf16[24,1536]{1,0:T(8,128)(2,1)S(1)}, bf16[24,1536]{1,0:T(8,128)(2,1)S(1)}, u32[]{:S(2)}, u32[]{:S(2)}) collective-permute-start(bf16[24,1536]{1,0:T(8,128)(2,1)S(1)} %get-tuple-element.75), channel_id=1, source_target_pairs={{0,24},{2,26},{4,28},{6,30},{8,16},{10,18},{12,20},{14,22},{16,8},... | collective-permute-start | bytes 221192 | tf_op jit(solution)/shard_map/ppermute | solution.py:459
  59.3 6.0 %collective-permute-start.16 = (bf16[24,1536]{1,0:T(8,128)(2,1)S(1)}, bf16[24,1536]{1,0:T(8,128)(2,1)S(1)}, u32[]{:S(2)}, u32[]{:S(2)}) collective-permute-start(bf16[24,1536]{1,0:T(8,128)(2,1)S(1)} %get-tuple-element.75), channel_id=1, source_target_pairs={{0,16},{2,18},{4,20},{6,22},{8,24},{10,26},{12,28},{14,30},{16,0},... | collective-permute-start | bytes 221192 | tf_op jit(solution)/shard_map/ppermute | solution.py:459
  59.3 6.0 %collective-permute-start.15 = (bf16[24,1536]{1,0:T(8,128)(2,1)S(1)}, bf16[24,1536]{1,0:T(8,128)(2,1)S(1)}, u32[]{:S(2)}, u32[]{:S(2)}) collective-permute-start(bf16[24,1536]{1,0:T(8,128)(2,1)S(1)} %get-tuple-element.75), channel_id=1, source_target_pairs={{0,8},{2,10},{4,12},{6,14},{8,0},{10,2},{12,4},{14,6},{16,24},{18,... | collective-permute-start | bytes 221192 | tf_op jit(solution)/shard_map/ppermute | solution.py:459
  62.4 9.9 %collective-permute-start.18 = (bf16[2,128,768]{2,1,0:T(8,128)(2,1)S(1)}, bf16[2,128,768]{2,1,0:T(8,128)(2,1)S(1)}, u32[]{:S(2)}, u32[]{:S(2)}) collective-permute-start(bf16[2,128,768]{2,1,0:T(8,128)(2,1)S(1)} %get-tuple-element.76), channel_id=1, source_target_pairs={{0,1},{1,0},{2,3},{3,2},{4,5},{5,4},{6,7},{7,6},{8,9},{9,8},{10,11... | collective-permute-start | bytes 1179656 | tf_op jit(solution)/shard_map/ppermute | solution.py:354
  65.4 16.6 %collective-permute-start.10 = (bf16[2,256,768]{2,1,0:T(8,128)(2,1)S(1)}, bf16[2,256,768]{2,1,0:T(8,128)(2,1)S(1)}, u32[]{:S(2)}, u32[]{:S(2)}) collective-permute-start(bf16[2,256,768]{2,1,0:T(8,128)(2,1)S(1)} %get-tuple-element.63), channel_id=1, source_target_pairs={{0,2},{2,0},{4,6},{6,4},{8,10},{10,8},{12,14},{14,12},{16,18},{18,... | collective-permute-start | bytes 2359304 | tf_op jit(solution)/shard_map/ppermute | solution.py:500
  65.4 10.2 %collective-permute-start.12 = (bf16[2,128,768]{2,1,0:T(8,128)(2,1)S(1)}, bf16[2,128,768]{2,1,0:T(8,128)(2,1)S(1)}, u32[]{:S(2)}, u32[]{:S(2)}) collective-permute-start(bf16[2,128,768]{2,1,0:T(8,128)(2,1)S(1)} %get-tuple-element.69), channel_id=1, source_target_pairs={{0,30},{2,4},{4,2},{6,8},{8,6},{10,12},{12,10},{14,16},{16,14},{18... | collective-permute-start | bytes 1179656 | tf_op jit(solution)/shard_map/ppermute | solution.py:499
  72.5 9.5 %collective-permute-start.21 = (bf16[2,128,768]{2,1,0:T(8,128)(2,1)S(1)}, bf16[2,128,768]{2,1,0:T(8,128)(2,1)S(1)}, u32[]{:S(2)}, u32[]{:S(2)}) collective-permute-start(bf16[2,128,768]{2,1,0:T(8,128)(2,1)S(1)} %far_sum.2), channel_id=1, source_target_pairs={{0,1},{1,0},{2,3},{3,2},{4,5},{5,4},{6,7},{7,6},{8,9},{9,8},{10,11... | collective-permute-start | bytes 1179656 | tf_op jit(solution)/shard_map/ppermute | solution.py:354
  74.3 1.3 %collective-permute-start.19 = (bf16[24,1536]{1,0:T(8,128)(2,1)S(1)}, bf16[24,1536]{1,0:T(8,128)(2,1)S(1)}, u32[]{:S(2)}, u32[]{:S(2)}) collective-permute-start(bf16[24,1536]{1,0:T(8,128)(2,1)S(1)} %add_add_fusion), channel_id=1, source_target_pairs={{0,2},{2,0},{4,6},{6,4},{8,10},{10,8},{12,14},{14,12},{16,18},{18,... | collective-permute-start | bytes 221192 | tf_op jit(solution)/shard_map/ppermute | solution.py:459
  75.6 19.7 %collective-permute-start.13 = (bf16[2,128,768]{2,1,0:T(8,128)(2,1)S(1)}, bf16[2,128,768]{2,1,0:T(8,128)(2,1)S(1)}, u32[]{:S(2)}, u32[]{:S(2)}) collective-permute-start(bf16[2,128,768]{2,1,0:T(8,128)(2,1)S(1)} %get-tuple-element.70), channel_id=1, source_target_pairs={{0,30},{2,4},{4,2},{6,8},{8,6},{10,12},{12,10},{14,16},{16,14},{18... | collective-permute-start | bytes 1179656 | tf_op jit(solution)/shard_map/ppermute | solution.py:510
  82.1 13.2 %collective-permute-start.22 = (bf16[2,128,768]{2,1,0:T(8,128)(2,1)S(1)}, bf16[2,128,768]{2,1,0:T(8,128)(2,1)S(1)}, u32[]{:S(2)}, u32[]{:S(2)}) collective-permute-start(bf16[2,128,768]{2,1,0:T(8,128)(2,1)S(1)} %far_sum.3), channel_id=1, source_target_pairs={{0,1},{1,0},{2,3},{3,2},{4,5},{5,4},{6,7},{7,6},{8,9},{9,8},{10,11... | collective-permute-start | bytes 1179656 | tf_op jit(solution)/shard_map/ppermute | solution.py:354
  83.9 7.0 %collective-permute-start.23 = (bf16[24,1536]{1,0:T(8,128)(2,1)S(1)}, bf16[24,1536]{1,0:T(8,128)(2,1)S(1)}, u32[]{:S(2)}, u32[]{:S(2)}) collective-permute-start(bf16[24,1536]{1,0:T(8,128)(2,1)S(1)} %add.22), channel_id=1, source_target_pairs={{0,4},{2,6},{4,0},{6,2},{8,12},{10,14},{12,8},{14,10},{16,20},{18,... | collective-permute-start | bytes 221192 | tf_op jit(solution)/shard_map/ppermute | solution.py:459
  90.9 4.4 %collective-permute-start.24 = (bf16[24,1536]{1,0:T(8,128)(2,1)S(1)}, bf16[24,1536]{1,0:T(8,128)(2,1)S(1)}, u32[]{:S(2)}, u32[]{:S(2)}) collective-permute-start(bf16[24,1536]{1,0:T(8,128)(2,1)S(1)} %add.23.refs_3_), channel_id=1, source_target_pairs={{0,1},{1,0},{2,3},{3,2},{4,5},{5,4},{6,7},{7,6},{8,9},{9,8},{10,11... | collective-permute-start | bytes 221192 | tf_op jit(solution)/shard_map/ppermute | solution.py:522

commit v13 on v12

--- a/solution.py
+++ b/solution.py
@@ -208,25 +208,22 @@
         lax.fori_loop(0, steps, some, 0)
 
 
-def pack_kernel(place_ref, first_ref, second_ref, own_ref, *rest, groups):
-    *far_refs, sems = rest
-    rows, width = own_ref.shape[1:]
+def pack_kernel(place_ref, first_ref, second_ref, *rest, peers, groups):
+    *slab_refs, sems = rest
+    rows = first_ref.shape[0]
+    width = first_ref.shape[1] // groups
     copies = []
-
-    def copy(ref, start, to):
-        cols = pl.ds(pl.multiple_of(start, DH), to.shape[1])
-        copies.append(pltpu.make_async_copy(ref.at[:, cols], to, sems.at[len(copies)]))
-        copies[-1].start()
-
-    for k in (*range(1, groups), 0):
+    for number, k in enumerate(peers):
         start = lax.rem(place_ref[0] + k, groups) * width
         for i, ref in enumerate((first_ref, second_ref)):
-            if k == 0:
-                copy(ref, start, own_ref.at[i])
-                continue
-            for p, far_ref in enumerate(far_refs):
-                at = pl.ds((k - 1) * rows, rows)
-                copy(ref, start + p * far_ref.shape[2], far_ref.at[i, at])
+            for p, slab_ref in enumerate(slab_refs):
+                part = slab_ref.shape[2]
+                cols = pl.ds(pl.multiple_of(start + p * part, DH), part)
+                to = slab_ref.at[i, pl.ds(number * rows, rows)]
+                copies.append(
+                    pltpu.make_async_copy(ref.at[:, cols], to, sems.at[len(copies)])
+                )
+                copies[-1].start()
     for one in copies:
         one.wait()
 
@@ -321,18 +318,17 @@
     anywhere = pl.BlockSpec(memory_space=pl.ANY)
     small = pltpu.CompilerParams(vmem_limit_bytes=(12 if tokens <= 256 else 36) * 1024 * 1024)
 
-    def pack(first, second, params):
-        far_shape = (2, far_rows, part_width)
+    def pack(first, second, peers, count, params):
+        shape = (2, len(peers) * rows, width // count)
         return pl.pallas_call(
-            functools.partial(pack_kernel, groups=groups),
+            functools.partial(pack_kernel, peers=peers, groups=groups),
             grid_spec=pltpu.PrefetchScalarGridSpec(
                 num_scalar_prefetch=1,
                 in_specs=[anywhere] * 2,
-                out_specs=[in_vmem] * (1 + parts),
-                scratch_shapes=[pltpu.SemaphoreType.DMA((2 + 2 * (groups - 1) * parts,))],
+                out_specs=[in_vmem] * count,
+                scratch_shapes=[pltpu.SemaphoreType.DMA((2 * len(peers) * count,))],
             ),
-            out_shape=[jax.ShapeDtypeStruct((2, rows, width), bf16)]
-            + [jax.ShapeDtypeStruct(far_shape, bf16)] * parts,
+            out_shape=[jax.ShapeDtypeStruct(shape, bf16)] * count,
             compiler_params=params,
             cost_estimate=cheap,
             name="pack",
@@ -354,8 +350,11 @@
             arrived.append(lax.ppermute(part, "head", pairs))
         return arrived
 
-    kv_own, *kv_sent = pack(key_rows, value_rows, alone)
-    qo_own, *qo_sent = pack(queries, out_cotangent, small)
+    others = tuple(range(1, groups))
+    (kv_own,) = pack(key_rows, value_rows, (0,), 1, alone)
+    kv_sent = pack(key_rows, value_rows, others, parts, alone)
+    (qo_own,) = pack(queries, out_cotangent, (0,), 1, small)
+    qo_sent = pack(queries, out_cotangent, others, parts, small)
     side_own = lax.ppermute(kv_own, "ctx", side_pairs)
     near_own = lax.ppermute(kv_own, "ctx", near_pairs)
     kv_far = [to_peers(slab) for slab in kv_sent]
@@ -511,7 +510,7 @@
     if parts == 1:
         sums = rounds(bits[2:], joint[0])
 
-    sums = rounds(bits[:1], sums)
+    sums = rounds(bits[1:2], rounds(bits[:1], sums))
     side_back_far, sums, back_far, grad_far = tie((side_back_far, sums, back_far, grad_far))
     summed(parts - 1)
 
@@ -523,7 +522,7 @@
         return [rounds(after, slab) for slab in slabs]
 
     sums, _ = tie((sums, far_sent[-1]))
-    slabs = to_all(bits[1:2], [], sums)
+    slabs = to_all([], [], sums)
     results = []
     struct = jax.ShapeDtypeStruct
     for p in range(parts):

time: 97.3 us -> 97.2 us (level)
  starting transfers between devices: 31.7 us -> 30.2 us
  Pallas kernels: 21.1 us -> 22.3 us
    ppermute x1, waiting for transfers between devices: 1.21 us -> 8.67 us  [to_all(): slabs = slabs + [lax.ppermute(slab, 'head', pairs) for slab in slabs]]
    ppermute x4, waiting for transfers between devices: 8.53 us -> 3.69 us  [from_peers(): arrived.append(lax.ppermute(part, 'head', pairs))]
    ppermute x5, waiting for transfers between devices: 12.3 us -> 9.42 us  [shifted(): return lax.ppermute(array, 'ctx', [(i, i ^ step) for i in range(ctx_count)])]
    ppermute x1, starting transfers between devices: 1.98 us -> 0.37 us  [to_all(): slabs = slabs + [lax.ppermute(slab, 'head', pairs) for slab in slabs]]
    pallas_call x2 -> x4, Pallas kernels: 3.06 us -> 4.5 us  [pack(): pl.pallas_call(functools.partial(pack_kernel, peers=peers, groups=groups)...]
    ppermute x5, starting transfers between devices: 5.48 us -> 6.49 us  [shifted(): return lax.ppermute(array, 'ctx', [(i, i ^ step) for i in range(ctx_count)])]
  transfers between devices with their start and end apart: 25 -> 25, of which waited for: 11 -> 9; matrix products, arithmetic and copies ran while one was open for 0% -> 0% of each run, Pallas kernels for 17% -> 19%
where the time goes in v13:
time: 97.2 us; the launch traced here: 96.7 us
  waiting for transfers between devices  43.2 us (44%)
  starting transfers between devices  30.2 us (31%)
  Pallas kernels  22.3 us (23%)
    ppermute x4, waiting for transfers between devices, to_peers(): arrived.append(lax.ppermute(part, 'head', pairs))  21.4 us
    pallas_call x2, Pallas kernels, attention(): pl.pallas_call(functools.partial(attention_kernel, rows=rows, tokens=toke...  12.6 us
    ppermute x5, waiting for transfers between devices, shifted(): return lax.ppermute(array, 'ctx', [(i, i ^ step) for i in range(ctx_count)])  9.42 us
    ppermute x1, waiting for transfers between devices, to_all(): slabs = slabs + [lax.ppermute(slab, 'head', pairs) for slab in slabs]  8.67 us
    ppermute x5, starting transfers between devices, shifted(): return lax.ppermute(array, 'ctx', [(i, i ^ step) for i in range(ctx_count)])  6.49 us
    ppermute x1, starting transfers between devices, per_device(): side_own = lax.ppermute(kv_own, 'ctx', side_pairs)  5.64 us
    ppermute x4, starting transfers between devices, from_peers(): arrived.append(lax.ppermute(part, 'head', pairs))  5.33 us
    ppermute x4, starting transfers between devices, to_peers(): arrived.append(lax.ppermute(part, 'head', pairs))  5.13 us
  transfers between devices with their start and end apart: 25, of which 9 were waited for; matrix products, arithmetic and copies ran while one was open for 0% of the time, Pallas kernels for 19%

profile of v13, /device:TPU:0, one launch (start us, length us, event | category | flops | bytes accessed | tf_op | source)
XLA Modules:
  0.0 96.7 jit_solution(3687384982243120488)
XLA Ops:
  0.7 2.1 %pack.5.kv_own_ref = bf16[2,128,1536]{2,1,0:T(8,128)(2,1)} custom-call(s32[1]{0:T(128)} %bitcast.place_ref, bf16[128,3072]{1,0:T(8,128)(2,1)} %first_ref.7, bf16[128,3072]{1,0:T(8,128)(2,1)} %second_ref.7), custom_call_target="tpu_custom_call" | custom-call | flops 1 | bytes 1 | tf_op jit(solution)/shard_map/pack/pallas_call | solution.py:323
  2.8 0.5 collective-permute-start.2
  3.3 5.6 %collective-permute-start.1 = (bf16[2,128,1536]{2,1,0:T(8,128)(2,1)}, bf16[2,128,1536]{2,1,0:T(8,128)(2,1)S(1)}, u32[]{:S(2)}, u32[]{:S(2)}) collective-permute-start(bf16[2,128,1536]{2,1,0:T(8,128)(2,1)} %pack.5.kv_own_ref), channel_id=1, source_target_pairs={{0,30},{2,4},{4,2},{6,8},{8,6},{10,12},{12,10},{14,16},{16,14},{18... | collective-permute-start | bytes 2359304 | tf_op jit(solution)/shard_map/ppermute | solution.py:358
  9.0 2.1 %pack.7 = (bf16[2,128,768]{2,1,0:T(8,128)(2,1)}, bf16[2,128,768]{2,1,0:T(8,128)(2,1)}) custom-call(s32[1]{0:T(128)} %bitcast.place_ref, bf16[128,3072]{1,0:T(8,128)(2,1)} %first_ref.7, bf16[128,3072]{1,0:T(8,128)(2,1)} %second_ref.7), custom_call_target="tpu_custom_call" | custom-call | flops 1 | bytes 1 | tf_op jit(solution)/shard_map/pack/pallas_call | solution.py:323
  11.1 1.6 %collective-permute-start.6 = (bf16[2,128,768]{2,1,0:T(8,128)(2,1)}, bf16[2,128,768]{2,1,0:T(8,128)(2,1)S(1)}, u32[]{:S(2)}, u32[]{:S(2)}) collective-permute-start(bf16[2,128,768]{2,1,0:T(8,128)(2,1)} %get-tuple-element.55), channel_id=1, source_target_pairs={{0,1},{1,0},{2,3},{3,2},{4,5},{5,4},{6,7},{7,6},{8,9},{9,8},{10,11... | collective-permute-start | bytes 1179656 | tf_op jit(solution)/shard_map/ppermute | solution.py:342
  12.7 0.5 collective-permute-start
  13.2 0.2 pack.6
  13.3 0.0 copy-start.3
  13.4 0.0 copy-start.4
  13.4 0.0 copy-start.5
  13.4 0.0 copy-start.6
  13.4 10.0 %collective-permute-done.6.kv_ref = bf16[2,128,768]{2,1,0:T(8,128)(2,1)S(1)} collective-permute-done((bf16[2,128,768]{2,1,0:T(8,128)(2,1)}, bf16[2,128,768]{2,1,0:T(8,128)(2,1)S(1)}, u32[]{:S(2)}, u32[]{:S(2)}) %collective-permute-start.6) | collective-permute-done | bytes 393248 | tf_op jit(solution)/shard_map/ppermute | solution.py:342
  23.4 1.5 %collective-permute-start.7 = (bf16[2,128,768]{2,1,0:T(8,128)(2,1)S(1)}, bf16[2,128,768]{2,1,0:T(8,128)(2,1)S(1)}, u32[]{:S(2)}, u32[]{:S(2)}) collective-permute-start(bf16[2,128,768]{2,1,0:T(8,128)(2,1)S(1)} %get-tuple-element.56), channel_id=1, source_target_pairs={{0,1},{1,0},{2,3},{3,2},{4,5},{5,4},{6,7},{7,6},{8,9},{9,8},{10,11... | collective-permute-start | bytes 1179656 | tf_op jit(solution)/shard_map/ppermute | solution.py:342
  24.9 0.0 collective-permute-start.9
  24.9 6.9 %collective-permute-done.kv_ref = bf16[2,128,768]{2,1,0:T(8,128)(2,1)S(1)} collective-permute-done((bf16[2,128,768]{2,1,0:T(8,128)(2,1)}, bf16[2,128,768]{2,1,0:T(8,128)(2,1)S(1)}, u32[]{:S(2)}, u32[]{:S(2)}) %collective-permute-start) | collective-permute-done | bytes 393248 | tf_op jit(solution)/shard_map/ppermute | solution.py:342
  31.8 0.0 collective-permute-start.8
  31.8 0.0 collective-permute-done.2.near_own_ref
  31.9 0.6 collective-permute-start.5
  32.4 0.0 collective-permute-done.1.side_own_ref
  32.4 0.0 collective-permute-start.4
  32.5 4.5 %collective-permute-done.7.qo_ref = bf16[2,128,768]{2,1,0:T(8,128)(2,1)S(1)} collective-permute-done((bf16[2,128,768]{2,1,0:T(8,128)(2,1)S(1)}, bf16[2,128,768]{2,1,0:T(8,128)(2,1)S(1)}, u32[]{:S(2)}, u32[]{:S(2)}) %collective-permute-start.7) | collective-permute-done | bytes 393248 | tf_op jit(solution)/shard_map/ppermute | solution.py:342
  36.9 1.5 %collective-permute-start.3 = (bf16[2,128,768]{2,1,0:T(8,128)(2,1)S(1)}, bf16[2,128,768]{2,1,0:T(8,128)(2,1)S(1)}, u32[]{:S(2)}, u32[]{:S(2)}) collective-permute-start(bf16[2,128,768]{2,1,0:T(8,128)(2,1)S(1)} %get-tuple-element.50), channel_id=1, source_target_pairs={{0,1},{1,0},{2,3},{3,2},{4,5},{5,4},{6,7},{7,6},{8,9},{9,8},{10,11... | collective-permute-start | bytes 1179656 | tf_op jit(solution)/shard_map/ppermute | solution.py:342
  38.5 0.1 pack.4.qo_own_ref
  38.6 1.9 %prep.1 = (f32[768,256]{1,0:T(8,128)S(1)}, f32[256,1536]{1,0:T(8,128)S(1)}, bf16[24,256]{1,0:T(8,128)(2,1)S(1)}) custom-call(s32[1]{0:T(128)} %bitcast.place_ref, s32[32,128]{1,0:T(8,128)S(1)} %bitcast.3, s32[1,24]{1,0:T(1,128)S(1)} %bitcast.4, s32[24,24]{1,0:T(8,128)S(1)} %copy-done.5, f32[128,3072]{1,0:T(8,128)S(1)} %copy-done.3), custom_call_target="tpu_custom_call" | custom-call | flops 1 | bytes 1 | tf_op jit(solution)/shard_map/prep/pallas_call | solution.py:370
  40.5 0.0 collective-permute-done.9.side_far_ref
  40.5 0.0 collective-permute-done.8.near_far_ref
  40.5 6.3 %attention.2 = (bf16[2,128,768]{2,1,0:T(8,128)(2,1)S(1)}, f32[2,128,768]{2,1,0:T(8,128)S(1)}, f32[2,128,768]{2,1,0:T(8,128)S(1)}, bf16[2,256,768]{2,1,0:T(8,128)...) custom-call(s32[1]{0:T(128)} %bitcast.place_ref, ...), custom_call_target="tpu_custom_call" | custom-call | flops 1 | bytes 1 | tf_op jit(solution)/shard_map/attention/pallas_call | solution.py:432
  46.8 0.6 collective-permute-start.14
  47.4 0.0 collective-permute-done.5.side_far_ref
  47.4 0.0 collective-permute-done.4.near_far_ref
  47.4 0.0 collective-permute-done.3.qo_ref
  47.4 0.8 collective-permute-start.11
  48.2 0.5 collective-permute-start.21
  48.7 6.3 %attention.3 = (bf16[2,128,768]{2,1,0:T(8,128)(2,1)S(1)}, f32[2,128,768]{2,1,0:T(8,128)S(1)}, f32[2,128,768]{2,1,0:T(8,128)S(1)}, bf16[2,256,768]{2,1,0:T(8,128)...) custom-call(s32[1]{0:T(128)} %bitcast.place_ref, ...), custom_call_target="tpu_custom_call", output_to_operand_aliasing={{7}: (12, {})} | custom-call | flops 1 | bytes 1 | tf_op jit(solution)/shard_map/attention/pallas_call | solution.py:432
  55.0 0.0 collective-permute-done.14.refs_0_
  55.1 4.9 %collective-permute-start.17 = (bf16[24,1536]{1,0:T(8,128)(2,1)S(1)}, bf16[24,1536]{1,0:T(8,128)(2,1)S(1)}, u32[]{:S(2)}, u32[]{:S(2)}) collective-permute-start(bf16[24,1536]{1,0:T(8,128)(2,1)S(1)} %get-tuple-element.71), channel_id=1, source_target_pairs={{0,24},{2,26},{4,28},{6,30},{8,16},{10,18},{12,20},{14,22},{16,8},... | collective-permute-start | bytes 221192 | tf_op jit(solution)/shard_map/ppermute | solution.py:458
  59.9 0.0 collective-permute-start.16
  59.9 0.6 collective-permute-start.15
  60.5 4.2 %collective-permute-done.17 = bf16[24,1536]{1,0:T(8,128)(2,1)S(1)} collective-permute-done((bf16[24,1536]{1,0:T(8,128)(2,1)S(1)}, bf16[24,1536]{1,0:T(8,128)(2,1)S(1)}, u32[]{:S(2)}, u32[]{:S(2)}) %collective-permute-start.17) | collective-permute-done | bytes 73760 | tf_op jit(solution)/shard_map/ppermute | solution.py:458
  64.6 1.4 %collective-permute-start.18 = (bf16[2,128,768]{2,1,0:T(8,128)(2,1)S(1)}, bf16[2,128,768]{2,1,0:T(8,128)(2,1)S(1)}, u32[]{:S(2)}, u32[]{:S(2)}) collective-permute-start(bf16[2,128,768]{2,1,0:T(8,128)(2,1)S(1)} %get-tuple-element.72), channel_id=1, source_target_pairs={{0,1},{1,0},{2,3},{3,2},{4,5},{5,4},{6,7},{7,6},{8,9},{9,8},{10,11... | collective-permute-start | bytes 1179656 | tf_op jit(solution)/shard_map/ppermute | solution.py:350
  66.0 0.6 collective-permute-done.16
  66.7 0.0 collective-permute-start.10
  66.7 0.0 collective-permute-done.15
  66.7 0.0 collective-permute-done.11.side_ref
  66.7 2.9 %collective-permute-start.12 = (bf16[2,128,768]{2,1,0:T(8,128)(2,1)S(1)}, bf16[2,128,768]{2,1,0:T(8,128)(2,1)S(1)}, u32[]{:S(2)}, u32[]{:S(2)}) collective-permute-start(bf16[2,128,768]{2,1,0:T(8,128)(2,1)S(1)} %get-tuple-element.65), channel_id=1, source_target_pairs={{0,30},{2,4},{4,2},{6,8},{8,6},{10,12},{12,10},{14,16},{16,14},{18... | collective-permute-start | bytes 1179656 | tf_op jit(solution)/shard_map/ppermute | solution.py:498
  69.6 3.7 %collective-permute-done.18.refs_0_ = bf16[2,128,768]{2,1,0:T(8,128)(2,1)S(1)} collective-permute-done((bf16[2,128,768]{2,1,0:T(8,128)(2,1)S(1)}, bf16[2,128,768]{2,1,0:T(8,128)(2,1)S(1)}, u32[]{:S(2)}, u32[]{:S(2)}) %collective-permute-start.18) | collective-permute-done | bytes 393248 | tf_op jit(solution)/shard_map/ppermute | solution.py:350
  73.3 0.0 collective-permute-done.21.near_ref
  73.3 0.1 far_sum.2
  73.4 1.7 %collective-permute-start.22 = (bf16[2,128,768]{2,1,0:T(8,128)(2,1)S(1)}, bf16[2,128,768]{2,1,0:T(8,128)(2,1)S(1)}, u32[]{:S(2)}, u32[]{:S(2)}) collective-permute-start(bf16[2,128,768]{2,1,0:T(8,128)(2,1)S(1)} %far_sum.2), channel_id=1, source_target_pairs={{0,1},{1,0},{2,3},{3,2},{4,5},{5,4},{6,7},{7,6},{8,9},{9,8},{10,11... | collective-permute-start | bytes 1179656 | tf_op jit(solution)/shard_map/ppermute | solution.py:350
  75.1 0.0 collective-permute-start.19
  75.1 1.3 %collective-permute-done.19 = bf16[24,1536]{1,0:T(8,128)(2,1)S(1)} collective-permute-done((bf16[24,1536]{1,0:T(8,128)(2,1)S(1)}, bf16[24,1536]{1,0:T(8,128)(2,1)S(1)}, u32[]{:S(2)}, u32[]{:S(2)}) %collective-permute-start.19) | collective-permute-done | bytes 73760 | tf_op jit(solution)/shard_map/ppermute | solution.py:458
  76.4 1.1 %collective-permute-start.20 = (bf16[24,1536]{1,0:T(8,128)(2,1)S(1)}, bf16[24,1536]{1,0:T(8,128)(2,1)S(1)}, u32[]{:S(2)}, u32[]{:S(2)}) collective-permute-start(bf16[24,1536]{1,0:T(8,128)(2,1)S(1)} %add.22), channel_id=1, source_target_pairs={{0,4},{2,6},{4,0},{6,2},{8,12},{10,14},{12,8},{14,10},{16,20},{18,... | collective-permute-start | bytes 221192 | tf_op jit(solution)/shard_map/ppermute | solution.py:458
  77.4 3.4 %collective-permute-done.20 = bf16[24,1536]{1,0:T(8,128)(2,1)S(1)} collective-permute-done((bf16[24,1536]{1,0:T(8,128)(2,1)S(1)}, bf16[24,1536]{1,0:T(8,128)(2,1)S(1)}, u32[]{:S(2)}, u32[]{:S(2)}) %collective-permute-start.20) | collective-permute-done | bytes 73760 | tf_op jit(solution)/shard_map/ppermute | solution.py:458
  80.8 0.0 collective-permute-done.12.side_ref
  80.8 1.8 %collective-permute-start.13 = (bf16[2,128,768]{2,1,0:T(8,128)(2,1)S(1)}, bf16[2,128,768]{2,1,0:T(8,128)(2,1)S(1)}, u32[]{:S(2)}, u32[]{:S(2)}) collective-permute-start(bf16[2,128,768]{2,1,0:T(8,128)(2,1)S(1)} %get-tuple-element.66), channel_id=1, source_target_pairs={{0,30},{2,4},{4,2},{6,8},{8,6},{10,12},{12,10},{14,16},{16,14},{18... | collective-permute-start | bytes 1179656 | tf_op jit(solution)/shard_map/ppermute | solution.py:509
  82.7 0.0 collective-permute-done.22.refs_1_
  82.7 0.0 collective-permute-done.10.near_ref
  82.7 0.1 far_sum.3
  82.8 1.7 %collective-permute-start.23 = (bf16[2,128,768]{2,1,0:T(8,128)(2,1)S(1)}, bf16[2,128,768]{2,1,0:T(8,128)(2,1)S(1)}, u32[]{:S(2)}, u32[]{:S(2)}) collective-permute-start(bf16[2,128,768]{2,1,0:T(8,128)(2,1)S(1)} %far_sum.3), channel_id=1, source_target_pairs={{0,1},{1,0},{2,3},{3,2},{4,5},{5,4},{6,7},{7,6},{8,9},{9,8},{10,11... | collective-permute-start | bytes 1179656 | tf_op jit(solution)/shard_map/ppermute | solution.py:350
  84.5 0.4 collective-permute-start.24
  84.9 1.2 %finish.2 = (bf16[128,3072]{1,0:T(8,128)(2,1)}, bf16[128,3072]{1,0:T(8,128)(2,1)}, bf16[128,3072]{1,0:T(8,128)(2,1)}, bf16[128,3072]{1,0:T(8,128)(2,1)}) custom-call(s32[1]{0:T(128)} %bitcast.place_ref, f32[2,128,768]{2,1,0:T(8,128)S(1)} %get-tuple-element.83.part_ref, bf16[2,256,768]{2,1,0:T(8,128)(2,1)S(1)} %collective-permute-done.21.near_ref, ...), custom_call_target="tpu_custom_call" | custom-call | flops 1 | bytes 1 | tf_op jit(solution)/shard_map/finish/pallas_call | solution.py:537
  86.1 8.7 %collective-permute-done.24.refs_4_ = bf16[24,1536]{1,0:T(8,128)(2,1)S(1)} collective-permute-done((bf16[24,1536]{1,0:T(8,128)(2,1)S(1)}, bf16[24,1536]{1,0:T(8,128)(2,1)S(1)}, u32[]{:S(2)}, u32[]{:S(2)}) %collective-permute-start.24) | collective-permute-done | bytes 73760 | tf_op jit(solution)/shard_map/ppermute | solution.py:521
  94.8 0.0 collective-permute-done.13.side_ref
  94.8 1.9 %finish.3 = (bf16[128,3072]{1,0:T(8,128)(2,1)}, bf16[128,3072]{1,0:T(8,128)(2,1)}, bf16[128,3072]{1,0:T(8,128)(2,1)}, bf16[128,3072]{1,0:T(8,128)(2,1)}, f32[128,3072]{1,0:T(8,128)}) custom-call(s32[1]{0:T(128)} %bitcast.place_ref, ...), custom_call_target="tpu_custom_call", output_to_operand_aliasing={{0}: (10, {}), {1}: (11, {}), {2}: (12, {}), {3}: (13, {})} | custom-call | flops 1 | bytes 1 | tf_op jit(solution)/shard_map/finish/pallas_call | solution.py:537
  (14 shorter events, 0.1 us)
Async XLA Ops:
  0.6 12.5 %copy-start.1 = (bf16[128,3072]{1,0:T(8,128)(2,1)S(1)}, bf16[128,3072]{1,0:T(8,128)(2,1)}, u32[]{:S(2)}) copy-start(bf16[128,3072]{1,0:T(8,128)(2,1)} %first_ref.6) | copy-start | bytes 2359300
  0.6 12.5 %copy-start.2 = (bf16[128,3072]{1,0:T(8,128)(2,1)S(1)}, bf16[128,3072]{1,0:T(8,128)(2,1)}, u32[]{:S(2)}) copy-start(bf16[128,3072]{1,0:T(8,128)(2,1)} %second_ref.6) | copy-start | bytes 2359300
  2.8 29.1 %collective-permute-start.2 = (bf16[2,128,1536]{2,1,0:T(8,128)(2,1)}, bf16[2,128,1536]{2,1,0:T(8,128)(2,1)S(1)}, u32[]{:S(2)}, u32[]{:S(2)}) collective-permute-start(bf16[2,128,1536]{2,1,0:T(8,128)(2,1)} %pack.5.kv_own_ref), channel_id=1, source_target_pairs={{0,2},{2,0},{4,6},{6,4},{8,10},{10,8},{12,14},{14,12},{16,18},{18,... | collective-permute-start | bytes 2359304 | tf_op jit(solution)/shard_map/ppermute | solution.py:359
  3.3 29.1 %collective-permute-start.1 = (bf16[2,128,1536]{2,1,0:T(8,128)(2,1)}, bf16[2,128,1536]{2,1,0:T(8,128)(2,1)S(1)}, u32[]{:S(2)}, u32[]{:S(2)}) collective-permute-start(bf16[2,128,1536]{2,1,0:T(8,128)(2,1)} %pack.5.kv_own_ref), channel_id=1, source_target_pairs={{0,30},{2,4},{4,2},{6,8},{8,6},{10,12},{12,10},{14,16},{16,14},{18... | collective-permute-start | bytes 2359304 | tf_op jit(solution)/shard_map/ppermute | solution.py:358
  11.1 12.3 %collective-permute-start.6 = (bf16[2,128,768]{2,1,0:T(8,128)(2,1)}, bf16[2,128,768]{2,1,0:T(8,128)(2,1)S(1)}, u32[]{:S(2)}, u32[]{:S(2)}) collective-permute-start(bf16[2,128,768]{2,1,0:T(8,128)(2,1)} %get-tuple-element.55), channel_id=1, source_target_pairs={{0,1},{1,0},{2,3},{3,2},{4,5},{5,4},{6,7},{7,6},{8,9},{9,8},{10,11... | collective-permute-start | bytes 1179656 | tf_op jit(solution)/shard_map/ppermute | solution.py:342
  12.7 19.2 %collective-permute-start = (bf16[2,128,768]{2,1,0:T(8,128)(2,1)}, bf16[2,128,768]{2,1,0:T(8,128)(2,1)S(1)}, u32[]{:S(2)}, u32[]{:S(2)}) collective-permute-start(bf16[2,128,768]{2,1,0:T(8,128)(2,1)} %get-tuple-element.49), channel_id=1, source_target_pairs={{0,1},{1,0},{2,3},{3,2},{4,5},{5,4},{6,7},{7,6},{8,9},{9,8},{10,11... | collective-permute-start | bytes 1179656 | tf_op jit(solution)/shard_map/ppermute | solution.py:342
  13.3 25.2 %copy-start.3 = (f32[128,3072]{1,0:T(8,128)S(1)}, f32[128,3072]{1,0:T(8,128)}, u32[]{:S(2)}) copy-start(f32[128,3072]{1,0:T(8,128)} %table_ref.1) | copy-start | bytes 4718596
  13.4 25.2 %copy-start.4 = (s32[4096]{0:T(1024)S(1)}, s32[4096]{0:T(1024)}, u32[]{:S(2)}) copy-start(s32[4096]{0:T(1024)} %param.13) | copy-start | bytes 49156
  13.4 25.2 %copy-start.5 = (s32[24,24]{1,0:T(8,128)S(1)}, s32[24,24]{1,0:T(8,128)}, u32[]{:S(2)}) copy-start(s32[24,24]{1,0:T(8,128)} %mask_ref.1) | copy-start | bytes 6916
  13.4 25.2 %copy-start.6 = (s32[24]{0:T(128)S(1)}, s32[24]{0:T(128)}, u32[]{:S(2)}) copy-start(s32[24]{0:T(128)} %param.14) | copy-start | bytes 292
  23.4 13.5 %collective-permute-start.7 = (bf16[2,128,768]{2,1,0:T(8,128)(2,1)S(1)}, bf16[2,128,768]{2,1,0:T(8,128)(2,1)S(1)}, u32[]{:S(2)}, u32[]{:S(2)}) collective-permute-start(bf16[2,128,768]{2,1,0:T(8,128)(2,1)S(1)} %get-tuple-element.56), channel_id=1, source_target_pairs={{0,1},{1,0},{2,3},{3,2},{4,5},{5,4},{6,7},{7,6},{8,9},{9,8},{10,11... | collective-permute-start | bytes 1179656 | tf_op jit(solution)/shard_map/ppermute | solution.py:342
  24.9 15.5 %collective-permute-start.9 = (bf16[2,128,768]{2,1,0:T(8,128)(2,1)S(1)}, bf16[2,128,768]{2,1,0:T(8,128)(2,1)S(1)}, u32[]{:S(2)}, u32[]{:S(2)}) collective-permute-start(bf16[2,128,768]{2,1,0:T(8,128)(2,1)S(1)} %collective-permute-done.6.kv_ref), channel_id=1, source_target_pairs={{0,30},{2,4},{4,2},{6,8},{8,6},{10,12},{12,10},{14,16},{16,14},{18... | collective-permute-start | bytes 1179656 | tf_op jit(solution)/shard_map/ppermute | solution.py:361
  31.8 8.6 %collective-permute-start.8 = (bf16[2,128,768]{2,1,0:T(8,128)(2,1)S(1)}, bf16[2,128,768]{2,1,0:T(8,128)(2,1)S(1)}, u32[]{:S(2)}, u32[]{:S(2)}) collective-permute-start(bf16[2,128,768]{2,1,0:T(8,128)(2,1)S(1)} %collective-permute-done.6.kv_ref), channel_id=1, source_target_pairs={{0,2},{2,0},{4,6},{6,4},{8,10},{10,8},{12,14},{14,12},{16,18},{18,... | collective-permute-start | bytes 1179656 | tf_op jit(solution)/shard_map/ppermute | solution.py:362
  31.9 15.5 %collective-permute-start.5 = (bf16[2,128,768]{2,1,0:T(8,128)(2,1)S(1)}, bf16[2,128,768]{2,1,0:T(8,128)(2,1)S(1)}, u32[]{:S(2)}, u32[]{:S(2)}) collective-permute-start(bf16[2,128,768]{2,1,0:T(8,128)(2,1)S(1)} %collective-permute-done.kv_ref), channel_id=1, source_target_pairs={{0,30},{2,4},{4,2},{6,8},{8,6},{10,12},{12,10},{14,16},{16,14},{18... | collective-permute-start | bytes 1179656 | tf_op jit(solution)/shard_map/ppermute | solution.py:361
  32.4 14.9 %collective-permute-start.4 = (bf16[2,128,768]{2,1,0:T(8,128)(2,1)S(1)}, bf16[2,128,768]{2,1,0:T(8,128)(2,1)S(1)}, u32[]{:S(2)}, u32[]{:S(2)}) collective-permute-start(bf16[2,128,768]{2,1,0:T(8,128)(2,1)S(1)} %collective-permute-done.kv_ref), channel_id=1, source_target_pairs={{0,2},{2,0},{4,6},{6,4},{8,10},{10,8},{12,14},{14,12},{16,18},{18,... | collective-permute-start | bytes 1179656 | tf_op jit(solution)/shard_map/ppermute | solution.py:362
  32.4 8.0 %copy-start = (bf16[2,128,1536]{2,1,0:T(8,128)(2,1)S(1)}, bf16[2,128,1536]{2,1,0:T(8,128)(2,1)}, u32[]{:S(2)}) copy-start(bf16[2,128,1536]{2,1,0:T(8,128)(2,1)} %pack.5.kv_own_ref) | copy-start | bytes 2359300
  36.9 10.5 %collective-permute-start.3 = (bf16[2,128,768]{2,1,0:T(8,128)(2,1)S(1)}, bf16[2,128,768]{2,1,0:T(8,128)(2,1)S(1)}, u32[]{:S(2)}, u32[]{:S(2)}) collective-permute-start(bf16[2,128,768]{2,1,0:T(8,128)(2,1)S(1)} %get-tuple-element.50), channel_id=1, source_target_pairs={{0,1},{1,0},{2,3},{3,2},{4,5},{5,4},{6,7},{7,6},{8,9},{9,8},{10,11... | collective-permute-start | bytes 1179656 | tf_op jit(solution)/shard_map/ppermute | solution.py:342
  46.8 8.2 %collective-permute-start.14 = (bf16[2,128,768]{2,1,0:T(8,128)(2,1)S(1)}, bf16[2,128,768]{2,1,0:T(8,128)(2,1)S(1)}, u32[]{:S(2)}, u32[]{:S(2)}) collective-permute-start(bf16[2,128,768]{2,1,0:T(8,128)(2,1)S(1)} %get-tuple-element.70), channel_id=1, source_target_pairs={{0,1},{1,0},{2,3},{3,2},{4,5},{5,4},{6,7},{7,6},{8,9},{9,8},{10,11... | collective-permute-start | bytes 1179656 | tf_op jit(solution)/shard_map/ppermute | solution.py:350
  47.4 19.3 %collective-permute-start.11 = (bf16[2,256,768]{2,1,0:T(8,128)(2,1)S(1)}, bf16[2,256,768]{2,1,0:T(8,128)(2,1)S(1)}, u32[]{:S(2)}, u32[]{:S(2)}) collective-permute-start(bf16[2,256,768]{2,1,0:T(8,128)(2,1)S(1)} %get-tuple-element.63), channel_id=1, source_target_pairs={{0,30},{2,4},{4,2},{6,8},{8,6},{10,12},{12,10},{14,16},{16,14},{18... | collective-permute-start | bytes 2359304 | tf_op jit(solution)/shard_map/ppermute | solution.py:498
  48.2 25.1 %collective-permute-start.21 = (bf16[2,256,768]{2,1,0:T(8,128)(2,1)S(1)}, bf16[2,256,768]{2,1,0:T(8,128)(2,1)S(1)}, u32[]{:S(2)}, u32[]{:S(2)}) collective-permute-start(bf16[2,256,768]{2,1,0:T(8,128)(2,1)S(1)} %get-tuple-element.77), channel_id=1, source_target_pairs={{0,2},{2,0},{4,6},{6,4},{8,10},{10,8},{12,14},{14,12},{16,18},{18,... | collective-permute-start | bytes 2359304 | tf_op jit(solution)/shard_map/ppermute | solution.py:499
  55.1 9.6 %collective-permute-start.17 = (bf16[24,1536]{1,0:T(8,128)(2,1)S(1)}, bf16[24,1536]{1,0:T(8,128)(2,1)S(1)}, u32[]{:S(2)}, u32[]{:S(2)}) collective-permute-start(bf16[24,1536]{1,0:T(8,128)(2,1)S(1)} %get-tuple-element.71), channel_id=1, source_target_pairs={{0,24},{2,26},{4,28},{6,30},{8,16},{10,18},{12,20},{14,22},{16,8},... | collective-permute-start | bytes 221192 | tf_op jit(solution)/shard_map/ppermute | solution.py:458
  59.9 6.7 %collective-permute-start.16 = (bf16[24,1536]{1,0:T(8,128)(2,1)S(1)}, bf16[24,1536]{1,0:T(8,128)(2,1)S(1)}, u32[]{:S(2)}, u32[]{:S(2)}) collective-permute-start(bf16[24,1536]{1,0:T(8,128)(2,1)S(1)} %get-tuple-element.71), channel_id=1, source_target_pairs={{0,16},{2,18},{4,20},{6,22},{8,24},{10,26},{12,28},{14,30},{16,0},... | collective-permute-start | bytes 221192 | tf_op jit(solution)/shard_map/ppermute | solution.py:458
  59.9 6.7 %collective-permute-start.15 = (bf16[24,1536]{1,0:T(8,128)(2,1)S(1)}, bf16[24,1536]{1,0:T(8,128)(2,1)S(1)}, u32[]{:S(2)}, u32[]{:S(2)}) collective-permute-start(bf16[24,1536]{1,0:T(8,128)(2,1)S(1)} %get-tuple-element.71), channel_id=1, source_target_pairs={{0,8},{2,10},{4,12},{6,14},{8,0},{10,2},{12,4},{14,6},{16,24},{18,... | collective-permute-start | bytes 221192 | tf_op jit(solution)/shard_map/ppermute | solution.py:458
  64.6 8.7 %collective-permute-start.18 = (bf16[2,128,768]{2,1,0:T(8,128)(2,1)S(1)}, bf16[2,128,768]{2,1,0:T(8,128)(2,1)S(1)}, u32[]{:S(2)}, u32[]{:S(2)}) collective-permute-start(bf16[2,128,768]{2,1,0:T(8,128)(2,1)S(1)} %get-tuple-element.72), channel_id=1, source_target_pairs={{0,1},{1,0},{2,3},{3,2},{4,5},{5,4},{6,7},{7,6},{8,9},{9,8},{10,11... | collective-permute-start | bytes 1179656 | tf_op jit(solution)/shard_map/ppermute | solution.py:350
  66.7 16.0 %collective-permute-start.10 = (bf16[2,256,768]{2,1,0:T(8,128)(2,1)S(1)}, bf16[2,256,768]{2,1,0:T(8,128)(2,1)S(1)}, u32[]{:S(2)}, u32[]{:S(2)}) collective-permute-start(bf16[2,256,768]{2,1,0:T(8,128)(2,1)S(1)} %get-tuple-element.59), channel_id=1, source_target_pairs={{0,2},{2,0},{4,6},{6,4},{8,10},{10,8},{12,14},{14,12},{16,18},{18,... | collective-permute-start | bytes 2359304 | tf_op jit(solution)/shard_map/ppermute | solution.py:499
  66.7 14.1 %collective-permute-start.12 = (bf16[2,128,768]{2,1,0:T(8,128)(2,1)S(1)}, bf16[2,128,768]{2,1,0:T(8,128)(2,1)S(1)}, u32[]{:S(2)}, u32[]{:S(2)}) collective-permute-start(bf16[2,128,768]{2,1,0:T(8,128)(2,1)S(1)} %get-tuple-element.65), channel_id=1, source_target_pairs={{0,30},{2,4},{4,2},{6,8},{8,6},{10,12},{12,10},{14,16},{16,14},{18... | collective-permute-start | bytes 1179656 | tf_op jit(solution)/shard_map/ppermute | solution.py:498
  73.4 9.2 %collective-permute-start.22 = (bf16[2,128,768]{2,1,0:T(8,128)(2,1)S(1)}, bf16[2,128,768]{2,1,0:T(8,128)(2,1)S(1)}, u32[]{:S(2)}, u32[]{:S(2)}) collective-permute-start(bf16[2,128,768]{2,1,0:T(8,128)(2,1)S(1)} %far_sum.2), channel_id=1, source_target_pairs={{0,1},{1,0},{2,3},{3,2},{4,5},{5,4},{6,7},{7,6},{8,9},{9,8},{10,11... | collective-permute-start | bytes 1179656 | tf_op jit(solution)/shard_map/ppermute | solution.py:350
  75.1 1.3 %collective-permute-start.19 = (bf16[24,1536]{1,0:T(8,128)(2,1)S(1)}, bf16[24,1536]{1,0:T(8,128)(2,1)S(1)}, u32[]{:S(2)}, u32[]{:S(2)}) collective-permute-start(bf16[24,1536]{1,0:T(8,128)(2,1)S(1)} %add_add_fusion), channel_id=1, source_target_pairs={{0,2},{2,0},{4,6},{6,4},{8,10},{10,8},{12,14},{14,12},{16,18},{18,... | collective-permute-start | bytes 221192 | tf_op jit(solution)/shard_map/ppermute | solution.py:458
  76.4 4.4 %collective-permute-start.20 = (bf16[24,1536]{1,0:T(8,128)(2,1)S(1)}, bf16[24,1536]{1,0:T(8,128)(2,1)S(1)}, u32[]{:S(2)}, u32[]{:S(2)}) collective-permute-start(bf16[24,1536]{1,0:T(8,128)(2,1)S(1)} %add.22), channel_id=1, source_target_pairs={{0,4},{2,6},{4,0},{6,2},{8,12},{10,14},{12,8},{14,10},{16,20},{18,... | collective-permute-start | bytes 221192 | tf_op jit(solution)/shard_map/ppermute | solution.py:458
  80.8 14.0 %collective-permute-start.13 = (bf16[2,128,768]{2,1,0:T(8,128)(2,1)S(1)}, bf16[2,128,768]{2,1,0:T(8,128)(2,1)S(1)}, u32[]{:S(2)}, u32[]{:S(2)}) collective-permute-start(bf16[2,128,768]{2,1,0:T(8,128)(2,1)S(1)} %get-tuple-element.66), channel_id=1, source_target_pairs={{0,30},{2,4},{4,2},{6,8},{8,6},{10,12},{12,10},{14,16},{16,14},{18... | collective-permute-start | bytes 1179656 | tf_op jit(solution)/shard_map/ppermute | solution.py:509
  82.8 12.0 %collective-permute-start.23 = (bf16[2,128,768]{2,1,0:T(8,128)(2,1)S(1)}, bf16[2,128,768]{2,1,0:T(8,128)(2,1)S(1)}, u32[]{:S(2)}, u32[]{:S(2)}) collective-permute-start(bf16[2,128,768]{2,1,0:T(8,128)(2,1)S(1)} %far_sum.3), channel_id=1, source_target_pairs={{0,1},{1,0},{2,3},{3,2},{4,5},{5,4},{6,7},{7,6},{8,9},{9,8},{10,11... | collective-permute-start | bytes 1179656 | tf_op jit(solution)/shard_map/ppermute | solution.py:350
  84.5 10.3 %collective-permute-start.24 = (bf16[24,1536]{1,0:T(8,128)(2,1)S(1)}, bf16[24,1536]{1,0:T(8,128)(2,1)S(1)}, u32[]{:S(2)}, u32[]{:S(2)}) collective-permute-start(bf16[24,1536]{1,0:T(8,128)(2,1)S(1)} %add.23.refs_3_), channel_id=1, source_target_pairs={{0,1},{1,0},{2,3},{3,2},{4,5},{5,4},{6,7},{7,6},{8,9},{9,8},{10,11... | collective-permute-start | bytes 221192 | tf_op jit(solution)/shard_map/ppermute | solution.py:521

commit v14 on v12

--- a/solution.py
+++ b/solution.py
@@ -500,7 +500,7 @@
         near_back.append(lax.ppermute(near_grad, "ctx", near_pairs))
         back_far.append(from_peers(back))
         if p > 0:
-            sums = rounds(bits[2:], joint[0])
+            sums = rounds(bits[2:], rounds(bits[:1], joint[0]))
             side_back_far[p - 1], sums, _ = tie((side_back_far[p - 1], sums, back_far[p]))
             summed(p - 1)
         if p + 1 < parts:
@@ -509,9 +509,9 @@
         side_grad_own, _ = tie((side_grads[0], side_back_far[p]))
         side_back_own.append(lax.ppermute(side_grad_own, "ctx", side_pairs))
     if parts == 1:
-        sums = rounds(bits[2:], joint[0])
-
-    sums = rounds(bits[:1], sums)
+        sums = rounds(bits[2:], rounds(bits[:1], joint[0]))
+
+    sums = rounds(bits[1:2], sums)
     side_back_far, sums, back_far, grad_far = tie((side_back_far, sums, back_far, grad_far))
     summed(parts - 1)
 
@@ -523,7 +523,7 @@
         return [rounds(after, slab) for slab in slabs]
 
     sums, _ = tie((sums, far_sent[-1]))
-    slabs = to_all(bits[1:2], [], sums)
+    slabs = to_all([], [], sums)
     results = []
     struct = jax.ShapeDtypeStruct
     for p in range(parts):

time: 97.3 us -> 97 us (level); the launches traced: 97.2 us -> 95.8 us
  starting transfers between devices: 31.7 us -> 29.4 us
    ppermute x1, waiting for transfers between devices: 1.21 us -> 6.83 us  [to_all(): slabs = slabs + [lax.ppermute(slab, 'head', pairs) for slab in slabs]]
    ppermute x4, waiting for transfers between devices: 8.53 us -> 5.14 us  [from_peers(): arrived.append(lax.ppermute(part, 'head', pairs))]
    ppermute x1, starting transfers between devices: 1.98 us -> 0.59 us  [to_all(): slabs = slabs + [lax.ppermute(slab, 'head', pairs) for slab in slabs]]
    ppermute x5, waiting for transfers between devices: 12.3 us -> 11 us  [shifted(): return lax.ppermute(array, 'ctx', [(i, i ^ step) for i in range(ctx_count)])]
where the time goes in v14:
time: 97 us; the launch traced here: 95.8 us
  waiting for transfers between devices  44.3 us (46%)
  starting transfers between devices  29.4 us (30%)
  Pallas kernels  21.1 us (22%)
    ppermute x4, waiting for transfers between devices, to_peers(): arrived.append(lax.ppermute(part, 'head', pairs))  21.4 us
    pallas_call x2, Pallas kernels, attention(): pl.pallas_call(functools.partial(attention_kernel, rows=rows, tokens=toke...  12.8 us
    ppermute x5, waiting for transfers between devices, shifted(): return lax.ppermute(array, 'ctx', [(i, i ^ step) for i in range(ctx_count)])  11 us
    ppermute x1, waiting for transfers between devices, to_all(): slabs = slabs + [lax.ppermute(slab, 'head', pairs) for slab in slabs]  6.83 us
    ppermute x1, starting transfers between devices, per_device(): side_own = lax.ppermute(kv_own, 'ctx', side_pairs)  5.64 us
    ppermute x5, starting transfers between devices, shifted(): return lax.ppermute(array, 'ctx', [(i, i ^ step) for i in range(ctx_count)])  5.62 us
    ppermute x4, waiting for transfers between devices, from_peers(): arrived.append(lax.ppermute(part, 'head', pairs))  5.14 us
    ppermute x4, starting transfers between devices, to_peers(): arrived.append(lax.ppermute(part, 'head', pairs))  5.06 us
  transfers between devices with their start and end apart: 25, of which 11 were waited for; matrix products, arithmetic and copies ran while one was open for 0% of the time, Pallas kernels for 17%

profile of v14, /device:TPU:0, one launch (start us, length us, event | category | flops | bytes accessed | tf_op | source)
XLA Modules:
  0.0 95.8 jit_solution(10449473008633777470)
XLA Ops:
  0.6 0.0 copy-start.3
  0.6 0.0 copy-start.2
  0.7 0.0 copy-start.1
  0.7 0.0 copy-start.4
  0.7 2.8 %pack.3 = (bf16[2,128,1536]{2,1,0:T(8,128)(2,1)}, bf16[2,128,768]{2,1,0:T(8,128)(2,1)}, bf16[2,128,768]{2,1,0:T(8,128)(2,1)}) custom-call(s32[1]{0:T(128)} %bitcast.place_ref, bf16[128,3072]{1,0:T(8,128)(2,1)} %first_ref.3, bf16[128,3072]{1,0:T(8,128)(2,1)} %second_ref.3), custom_call_target="tpu_custom_call" | custom-call | flops 1 | bytes 1 | tf_op jit(solution)/shard_map/pack/pallas_call | solution.py:326
  3.5 0.5 collective-permute-start.2
  4.0 5.6 %collective-permute-start.1 = (bf16[2,128,1536]{2,1,0:T(8,128)(2,1)}, bf16[2,128,1536]{2,1,0:T(8,128)(2,1)S(1)}, u32[]{:S(2)}, u32[]{:S(2)}) collective-permute-start(bf16[2,128,1536]{2,1,0:T(8,128)(2,1)} %get-tuple-element.51.kv_own_ref), channel_id=1, source_target_pairs={{0,30},{2,4},{4,2},{6,8},{8,6},{10,12},{12,10},{14,16},{16,14},{18... | collective-permute-start | bytes 2359304 | tf_op jit(solution)/shard_map/ppermute | solution.py:359
  9.7 1.5 %collective-permute-start.6 = (bf16[2,128,768]{2,1,0:T(8,128)(2,1)}, bf16[2,128,768]{2,1,0:T(8,128)(2,1)S(1)}, u32[]{:S(2)}, u32[]{:S(2)}) collective-permute-start(bf16[2,128,768]{2,1,0:T(8,128)(2,1)} %get-tuple-element.59), channel_id=1, source_target_pairs={{0,1},{1,0},{2,3},{3,2},{4,5},{5,4},{6,7},{7,6},{8,9},{9,8},{10,11... | collective-permute-start | bytes 1179656 | tf_op jit(solution)/shard_map/ppermute | solution.py:346
  11.2 0.5 collective-permute-start
  11.7 0.3 pack.2
  12.0 10.0 %collective-permute-done.6.kv_ref = bf16[2,128,768]{2,1,0:T(8,128)(2,1)S(1)} collective-permute-done((bf16[2,128,768]{2,1,0:T(8,128)(2,1)}, bf16[2,128,768]{2,1,0:T(8,128)(2,1)S(1)}, u32[]{:S(2)}, u32[]{:S(2)}) %collective-permute-start.6) | collective-permute-done | bytes 393248 | tf_op jit(solution)/shard_map/ppermute | solution.py:346
  21.9 1.5 %collective-permute-start.7 = (bf16[2,128,768]{2,1,0:T(8,128)(2,1)S(1)}, bf16[2,128,768]{2,1,0:T(8,128)(2,1)S(1)}, u32[]{:S(2)}, u32[]{:S(2)}) collective-permute-start(bf16[2,128,768]{2,1,0:T(8,128)(2,1)S(1)} %get-tuple-element.60), channel_id=1, source_target_pairs={{0,1},{1,0},{2,3},{3,2},{4,5},{5,4},{6,7},{7,6},{8,9},{9,8},{10,11... | collective-permute-start | bytes 1179656 | tf_op jit(solution)/shard_map/ppermute | solution.py:346
  23.5 0.0 collective-permute-start.9
  23.5 6.9 %collective-permute-done.kv_ref = bf16[2,128,768]{2,1,0:T(8,128)(2,1)S(1)} collective-permute-done((bf16[2,128,768]{2,1,0:T(8,128)(2,1)}, bf16[2,128,768]{2,1,0:T(8,128)(2,1)S(1)}, u32[]{:S(2)}, u32[]{:S(2)}) %collective-permute-start) | collective-permute-done | bytes 393248 | tf_op jit(solution)/shard_map/ppermute | solution.py:346
  30.4 0.0 collective-permute-start.8
  30.4 0.0 collective-permute-done.2.near_own_ref
  30.4 0.6 collective-permute-start.5
  31.0 0.0 collective-permute-done.1.side_own_ref
  31.0 0.0 collective-permute-start.4
  31.0 4.5 %collective-permute-done.7.qo_ref = bf16[2,128,768]{2,1,0:T(8,128)(2,1)S(1)} collective-permute-done((bf16[2,128,768]{2,1,0:T(8,128)(2,1)S(1)}, bf16[2,128,768]{2,1,0:T(8,128)(2,1)S(1)}, u32[]{:S(2)}, u32[]{:S(2)}) %collective-permute-start.7) | collective-permute-done | bytes 393248 | tf_op jit(solution)/shard_map/ppermute | solution.py:346
  35.5 1.5 %collective-permute-start.3 = (bf16[2,128,768]{2,1,0:T(8,128)(2,1)S(1)}, bf16[2,128,768]{2,1,0:T(8,128)(2,1)S(1)}, u32[]{:S(2)}, u32[]{:S(2)}) collective-permute-start(bf16[2,128,768]{2,1,0:T(8,128)(2,1)S(1)} %get-tuple-element.54), channel_id=1, source_target_pairs={{0,1},{1,0},{2,3},{3,2},{4,5},{5,4},{6,7},{7,6},{8,9},{9,8},{10,11... | collective-permute-start | bytes 1179656 | tf_op jit(solution)/shard_map/ppermute | solution.py:346
  37.0 0.0 copy-done.6
  37.0 1.9 %prep.1 = (f32[768,256]{1,0:T(8,128)S(1)}, f32[256,1536]{1,0:T(8,128)S(1)}, bf16[24,256]{1,0:T(8,128)(2,1)S(1)}) custom-call(s32[1]{0:T(128)} %bitcast.place_ref, s32[32,128]{1,0:T(8,128)S(1)} %bitcast.3, s32[1,24]{1,0:T(1,128)S(1)} %bitcast.4, s32[24,24]{1,0:T(8,128)S(1)} %copy-done.5, f32[128,3072]{1,0:T(8,128)S(1)} %copy-done.1), custom_call_target="tpu_custom_call" | custom-call | flops 1 | bytes 1 | tf_op jit(solution)/shard_map/prep/pallas_call | solution.py:371
  38.9 0.0 collective-permute-done.9.side_far_ref
  38.9 0.0 collective-permute-done.8.near_far_ref
  38.9 6.4 %attention.2 = (bf16[2,128,768]{2,1,0:T(8,128)(2,1)S(1)}, f32[2,128,768]{2,1,0:T(8,128)S(1)}, f32[2,128,768]{2,1,0:T(8,128)S(1)}, bf16[2,256,768]{2,1,0:T(8,128)...) custom-call(s32[1]{0:T(128)} %bitcast.place_ref, ...), custom_call_target="tpu_custom_call" | custom-call | flops 1 | bytes 1 | tf_op jit(solution)/shard_map/attention/pallas_call | solution.py:433
  45.3 0.6 collective-permute-start.14
  45.9 0.0 collective-permute-done.5.side_far_ref
  45.9 0.0 collective-permute-done.4.near_far_ref
  45.9 0.0 collective-permute-done.3.qo_ref
  45.9 0.8 collective-permute-start.11
  46.7 0.8 collective-permute-start.21
  47.5 6.4 %attention.3 = (bf16[2,128,768]{2,1,0:T(8,128)(2,1)S(1)}, f32[2,128,768]{2,1,0:T(8,128)S(1)}, f32[2,128,768]{2,1,0:T(8,128)S(1)}, bf16[2,256,768]{2,1,0:T(8,128)...) custom-call(s32[1]{0:T(128)} %bitcast.place_ref, ...), custom_call_target="tpu_custom_call", output_to_operand_aliasing={{7}: (12, {})} | custom-call | flops 1 | bytes 1 | tf_op jit(solution)/shard_map/attention/pallas_call | solution.py:433
  53.8 0.6 collective-permute-done.14.refs_0_
  54.4 0.0 collective-permute-start.15
  54.4 1.3 %collective-permute-done.15 = bf16[24,1536]{1,0:T(8,128)(2,1)S(1)} collective-permute-done((bf16[24,1536]{1,0:T(8,128)(2,1)S(1)}, bf16[24,1536]{1,0:T(8,128)(2,1)S(1)}, u32[]{:S(2)}, u32[]{:S(2)}) %collective-permute-start.15) | collective-permute-done | bytes 73760 | tf_op jit(solution)/shard_map/ppermute | solution.py:459
  55.7 5.0 %collective-permute-start.18 = (bf16[24,1536]{1,0:T(8,128)(2,1)S(1)}, bf16[24,1536]{1,0:T(8,128)(2,1)S(1)}, u32[]{:S(2)}, u32[]{:S(2)}) collective-permute-start(bf16[24,1536]{1,0:T(8,128)(2,1)S(1)} %add.19), channel_id=1, source_target_pairs={{0,24},{2,26},{4,28},{6,30},{8,16},{10,18},{12,20},{14,22},{16,8},... | collective-permute-start | bytes 221192 | tf_op jit(solution)/shard_map/ppermute | solution.py:459
  60.7 0.0 collective-permute-start.17
  60.7 0.6 collective-permute-start.16
  61.3 2.3 %collective-permute-done.18 = bf16[24,1536]{1,0:T(8,128)(2,1)S(1)} collective-permute-done((bf16[24,1536]{1,0:T(8,128)(2,1)S(1)}, bf16[24,1536]{1,0:T(8,128)(2,1)S(1)}, u32[]{:S(2)}, u32[]{:S(2)}) %collective-permute-start.18) | collective-permute-done | bytes 73760 | tf_op jit(solution)/shard_map/ppermute | solution.py:459
  63.7 1.5 %collective-permute-start.19 = (bf16[2,128,768]{2,1,0:T(8,128)(2,1)S(1)}, bf16[2,128,768]{2,1,0:T(8,128)(2,1)S(1)}, u32[]{:S(2)}, u32[]{:S(2)}) collective-permute-start(bf16[2,128,768]{2,1,0:T(8,128)(2,1)S(1)} %get-tuple-element.76), channel_id=1, source_target_pairs={{0,1},{1,0},{2,3},{3,2},{4,5},{5,4},{6,7},{7,6},{8,9},{9,8},{10,11... | collective-permute-start | bytes 1179656 | tf_op jit(solution)/shard_map/ppermute | solution.py:354
  65.1 2.1 %collective-permute-done.17 = bf16[24,1536]{1,0:T(8,128)(2,1)S(1)} collective-permute-done((bf16[24,1536]{1,0:T(8,128)(2,1)S(1)}, bf16[24,1536]{1,0:T(8,128)(2,1)S(1)}, u32[]{:S(2)}, u32[]{:S(2)}) %collective-permute-start.17) | collective-permute-done | bytes 73760 | tf_op jit(solution)/shard_map/ppermute | solution.py:459
  67.2 0.0 collective-permute-start.10
  67.2 0.0 collective-permute-done.16
  67.2 0.0 collective-permute-done.11.side_ref
  67.2 3.0 %collective-permute-start.12 = (bf16[2,128,768]{2,1,0:T(8,128)(2,1)S(1)}, bf16[2,128,768]{2,1,0:T(8,128)(2,1)S(1)}, u32[]{:S(2)}, u32[]{:S(2)}) collective-permute-start(bf16[2,128,768]{2,1,0:T(8,128)(2,1)S(1)} %get-tuple-element.69), channel_id=1, source_target_pairs={{0,30},{2,4},{4,2},{6,8},{8,6},{10,12},{12,10},{14,16},{16,14},{18... | collective-permute-start | bytes 1179656 | tf_op jit(solution)/shard_map/ppermute | solution.py:499
  70.2 3.7 %collective-permute-done.19.refs_0_ = bf16[2,128,768]{2,1,0:T(8,128)(2,1)S(1)} collective-permute-done((bf16[2,128,768]{2,1,0:T(8,128)(2,1)S(1)}, bf16[2,128,768]{2,1,0:T(8,128)(2,1)S(1)}, u32[]{:S(2)}, u32[]{:S(2)}) %collective-permute-start.19) | collective-permute-done | bytes 393248 | tf_op jit(solution)/shard_map/ppermute | solution.py:354
  74.0 0.0 collective-permute-done.21.near_ref
  74.0 0.2 far_sum.2
  74.2 1.5 %collective-permute-start.22 = (bf16[2,128,768]{2,1,0:T(8,128)(2,1)S(1)}, bf16[2,128,768]{2,1,0:T(8,128)(2,1)S(1)}, u32[]{:S(2)}, u32[]{:S(2)}) collective-permute-start(bf16[2,128,768]{2,1,0:T(8,128)(2,1)S(1)} %far_sum.2), channel_id=1, source_target_pairs={{0,1},{1,0},{2,3},{3,2},{4,5},{5,4},{6,7},{7,6},{8,9},{9,8},{10,11... | collective-permute-start | bytes 1179656 | tf_op jit(solution)/shard_map/ppermute | solution.py:354
  75.7 0.0 collective-permute-start.20
  75.7 5.3 %collective-permute-done.20 = bf16[24,1536]{1,0:T(8,128)(2,1)S(1)} collective-permute-done((bf16[24,1536]{1,0:T(8,128)(2,1)S(1)}, bf16[24,1536]{1,0:T(8,128)(2,1)S(1)}, u32[]{:S(2)}, u32[]{:S(2)}) %collective-permute-start.20) | collective-permute-done | bytes 73760 | tf_op jit(solution)/shard_map/ppermute | solution.py:459
  81.0 0.0 collective-permute-done.12.side_ref
  81.0 1.8 %collective-permute-start.13 = (bf16[2,128,768]{2,1,0:T(8,128)(2,1)S(1)}, bf16[2,128,768]{2,1,0:T(8,128)(2,1)S(1)}, u32[]{:S(2)}, u32[]{:S(2)}) collective-permute-start(bf16[2,128,768]{2,1,0:T(8,128)(2,1)S(1)} %get-tuple-element.70), channel_id=1, source_target_pairs={{0,30},{2,4},{4,2},{6,8},{8,6},{10,12},{12,10},{14,16},{16,14},{18... | collective-permute-start | bytes 1179656 | tf_op jit(solution)/shard_map/ppermute | solution.py:510
  82.8 0.8 collective-permute-done.22.refs_1_
  83.6 0.0 collective-permute-done.10.near_ref
  83.6 0.1 far_sum.3
  83.7 1.5 %collective-permute-start.23 = (bf16[2,128,768]{2,1,0:T(8,128)(2,1)S(1)}, bf16[2,128,768]{2,1,0:T(8,128)(2,1)S(1)}, u32[]{:S(2)}, u32[]{:S(2)}) collective-permute-start(bf16[2,128,768]{2,1,0:T(8,128)(2,1)S(1)} %far_sum.3), channel_id=1, source_target_pairs={{0,1},{1,0},{2,3},{3,2},{4,5},{5,4},{6,7},{7,6},{8,9},{9,8},{10,11... | collective-permute-start | bytes 1179656 | tf_op jit(solution)/shard_map/ppermute | solution.py:354
  85.2 0.6 collective-permute-start.24
  85.8 1.2 %finish.2 = (bf16[128,3072]{1,0:T(8,128)(2,1)}, bf16[128,3072]{1,0:T(8,128)(2,1)}, bf16[128,3072]{1,0:T(8,128)(2,1)}, bf16[128,3072]{1,0:T(8,128)(2,1)}) custom-call(s32[1]{0:T(128)} %bitcast.place_ref, f32[2,128,768]{2,1,0:T(8,128)S(1)} %get-tuple-element.87.part_ref, bf16[2,256,768]{2,1,0:T(8,128)(2,1)S(1)} %collective-permute-done.21.near_ref, ...), custom_call_target="tpu_custom_call" | custom-call | flops 1 | bytes 1 | tf_op jit(solution)/shard_map/finish/pallas_call | solution.py:538
  87.1 6.8 %collective-permute-done.24.refs_4_ = bf16[24,1536]{1,0:T(8,128)(2,1)S(1)} collective-permute-done((bf16[24,1536]{1,0:T(8,128)(2,1)S(1)}, bf16[24,1536]{1,0:T(8,128)(2,1)S(1)}, u32[]{:S(2)}, u32[]{:S(2)}) %collective-permute-start.24) | collective-permute-done | bytes 73760 | tf_op jit(solution)/shard_map/ppermute | solution.py:522
  93.9 0.0 collective-permute-done.13.side_ref
  93.9 0.0 collective-permute-done.23.refs_1_
  93.9 1.9 %finish.3 = (bf16[128,3072]{1,0:T(8,128)(2,1)}, bf16[128,3072]{1,0:T(8,128)(2,1)}, bf16[128,3072]{1,0:T(8,128)(2,1)}, bf16[128,3072]{1,0:T(8,128)(2,1)}, f32[128,3072]{1,0:T(8,128)}) custom-call(s32[1]{0:T(128)} %bitcast.place_ref, ...), custom_call_target="tpu_custom_call", output_to_operand_aliasing={{0}: (10, {}), {1}: (11, {}), {2}: (12, {}), {3}: (13, {})} | custom-call | flops 1 | bytes 1 | tf_op jit(solution)/shard_map/finish/pallas_call | solution.py:538
  (12 shorter events, 0.1 us)
Async XLA Ops:
  0.6 11.1 %copy-start.3 = (bf16[128,3072]{1,0:T(8,128)(2,1)S(1)}, bf16[128,3072]{1,0:T(8,128)(2,1)}, u32[]{:S(2)}) copy-start(bf16[128,3072]{1,0:T(8,128)(2,1)} %second_ref.2) | copy-start | bytes 2359300
  0.6 11.1 %copy-start.2 = (bf16[128,3072]{1,0:T(8,128)(2,1)S(1)}, bf16[128,3072]{1,0:T(8,128)(2,1)}, u32[]{:S(2)}) copy-start(bf16[128,3072]{1,0:T(8,128)(2,1)} %first_ref.2) | copy-start | bytes 2359300
  0.7 36.3 %copy-start.1 = (f32[128,3072]{1,0:T(8,128)S(1)}, f32[128,3072]{1,0:T(8,128)}, u32[]{:S(2)}) copy-start(f32[128,3072]{1,0:T(8,128)} %table_ref.1) | copy-start | bytes 4718596
  0.7 36.3 %copy-start.4 = (s32[4096]{0:T(1024)S(1)}, s32[4096]{0:T(1024)}, u32[]{:S(2)}) copy-start(s32[4096]{0:T(1024)} %param.13) | copy-start | bytes 49156
  0.7 36.3 %copy-start.5 = (s32[24,24]{1,0:T(8,128)S(1)}, s32[24,24]{1,0:T(8,128)}, u32[]{:S(2)}) copy-start(s32[24,24]{1,0:T(8,128)} %mask_ref.1) | copy-start | bytes 6916
  0.7 36.3 %copy-start.6 = (s32[24]{0:T(128)S(1)}, s32[24]{0:T(128)}, u32[]{:S(2)}) copy-start(s32[24]{0:T(128)} %param.14) | copy-start | bytes 292
  3.5 26.9 %collective-permute-start.2 = (bf16[2,128,1536]{2,1,0:T(8,128)(2,1)}, bf16[2,128,1536]{2,1,0:T(8,128)(2,1)S(1)}, u32[]{:S(2)}, u32[]{:S(2)}) collective-permute-start(bf16[2,128,1536]{2,1,0:T(8,128)(2,1)} %get-tuple-element.51.kv_own_ref), channel_id=1, source_target_pairs={{0,2},{2,0},{4,6},{6,4},{8,10},{10,8},{12,14},{14,12},{16,18},{18,... | collective-permute-start | bytes 2359304 | tf_op jit(solution)/shard_map/ppermute | solution.py:360
  4.0 26.9 %collective-permute-start.1 = (bf16[2,128,1536]{2,1,0:T(8,128)(2,1)}, bf16[2,128,1536]{2,1,0:T(8,128)(2,1)S(1)}, u32[]{:S(2)}, u32[]{:S(2)}) collective-permute-start(bf16[2,128,1536]{2,1,0:T(8,128)(2,1)} %get-tuple-element.51.kv_own_ref), channel_id=1, source_target_pairs={{0,30},{2,4},{4,2},{6,8},{8,6},{10,12},{12,10},{14,16},{16,14},{18... | collective-permute-start | bytes 2359304 | tf_op jit(solution)/shard_map/ppermute | solution.py:359
  9.7 12.3 %collective-permute-start.6 = (bf16[2,128,768]{2,1,0:T(8,128)(2,1)}, bf16[2,128,768]{2,1,0:T(8,128)(2,1)S(1)}, u32[]{:S(2)}, u32[]{:S(2)}) collective-permute-start(bf16[2,128,768]{2,1,0:T(8,128)(2,1)} %get-tuple-element.59), channel_id=1, source_target_pairs={{0,1},{1,0},{2,3},{3,2},{4,5},{5,4},{6,7},{7,6},{8,9},{9,8},{10,11... | collective-permute-start | bytes 1179656 | tf_op jit(solution)/shard_map/ppermute | solution.py:346
  11.2 27.7 %copy-start = (bf16[2,128,1536]{2,1,0:T(8,128)(2,1)S(1)}, bf16[2,128,1536]{2,1,0:T(8,128)(2,1)}, u32[]{:S(2)}) copy-start(bf16[2,128,1536]{2,1,0:T(8,128)(2,1)} %get-tuple-element.51.kv_own_ref) | copy-start | bytes 2359300
  11.2 19.2 %collective-permute-start = (bf16[2,128,768]{2,1,0:T(8,128)(2,1)}, bf16[2,128,768]{2,1,0:T(8,128)(2,1)S(1)}, u32[]{:S(2)}, u32[]{:S(2)}) collective-permute-start(bf16[2,128,768]{2,1,0:T(8,128)(2,1)} %get-tuple-element.53), channel_id=1, source_target_pairs={{0,1},{1,0},{2,3},{3,2},{4,5},{5,4},{6,7},{7,6},{8,9},{9,8},{10,11... | collective-permute-start | bytes 1179656 | tf_op jit(solution)/shard_map/ppermute | solution.py:346
  21.9 13.5 %collective-permute-start.7 = (bf16[2,128,768]{2,1,0:T(8,128)(2,1)S(1)}, bf16[2,128,768]{2,1,0:T(8,128)(2,1)S(1)}, u32[]{:S(2)}, u32[]{:S(2)}) collective-permute-start(bf16[2,128,768]{2,1,0:T(8,128)(2,1)S(1)} %get-tuple-element.60), channel_id=1, source_target_pairs={{0,1},{1,0},{2,3},{3,2},{4,5},{5,4},{6,7},{7,6},{8,9},{9,8},{10,11... | collective-permute-start | bytes 1179656 | tf_op jit(solution)/shard_map/ppermute | solution.py:346
  23.5 15.4 %collective-permute-start.9 = (bf16[2,128,768]{2,1,0:T(8,128)(2,1)S(1)}, bf16[2,128,768]{2,1,0:T(8,128)(2,1)S(1)}, u32[]{:S(2)}, u32[]{:S(2)}) collective-permute-start(bf16[2,128,768]{2,1,0:T(8,128)(2,1)S(1)} %collective-permute-done.6.kv_ref), channel_id=1, source_target_pairs={{0,30},{2,4},{4,2},{6,8},{8,6},{10,12},{12,10},{14,16},{16,14},{18... | collective-permute-start | bytes 1179656 | tf_op jit(solution)/shard_map/ppermute | solution.py:362
  30.4 8.5 %collective-permute-start.8 = (bf16[2,128,768]{2,1,0:T(8,128)(2,1)S(1)}, bf16[2,128,768]{2,1,0:T(8,128)(2,1)S(1)}, u32[]{:S(2)}, u32[]{:S(2)}) collective-permute-start(bf16[2,128,768]{2,1,0:T(8,128)(2,1)S(1)} %collective-permute-done.6.kv_ref), channel_id=1, source_target_pairs={{0,2},{2,0},{4,6},{6,4},{8,10},{10,8},{12,14},{14,12},{16,18},{18,... | collective-permute-start | bytes 1179656 | tf_op jit(solution)/shard_map/ppermute | solution.py:363
  30.4 15.5 %collective-permute-start.5 = (bf16[2,128,768]{2,1,0:T(8,128)(2,1)S(1)}, bf16[2,128,768]{2,1,0:T(8,128)(2,1)S(1)}, u32[]{:S(2)}, u32[]{:S(2)}) collective-permute-start(bf16[2,128,768]{2,1,0:T(8,128)(2,1)S(1)} %collective-permute-done.kv_ref), channel_id=1, source_target_pairs={{0,30},{2,4},{4,2},{6,8},{8,6},{10,12},{12,10},{14,16},{16,14},{18... | collective-permute-start | bytes 1179656 | tf_op jit(solution)/shard_map/ppermute | solution.py:362
  31.0 14.9 %collective-permute-start.4 = (bf16[2,128,768]{2,1,0:T(8,128)(2,1)S(1)}, bf16[2,128,768]{2,1,0:T(8,128)(2,1)S(1)}, u32[]{:S(2)}, u32[]{:S(2)}) collective-permute-start(bf16[2,128,768]{2,1,0:T(8,128)(2,1)S(1)} %collective-permute-done.kv_ref), channel_id=1, source_target_pairs={{0,2},{2,0},{4,6},{6,4},{8,10},{10,8},{12,14},{14,12},{16,18},{18,... | collective-permute-start | bytes 1179656 | tf_op jit(solution)/shard_map/ppermute | solution.py:363
  35.5 10.4 %collective-permute-start.3 = (bf16[2,128,768]{2,1,0:T(8,128)(2,1)S(1)}, bf16[2,128,768]{2,1,0:T(8,128)(2,1)S(1)}, u32[]{:S(2)}, u32[]{:S(2)}) collective-permute-start(bf16[2,128,768]{2,1,0:T(8,128)(2,1)S(1)} %get-tuple-element.54), channel_id=1, source_target_pairs={{0,1},{1,0},{2,3},{3,2},{4,5},{5,4},{6,7},{7,6},{8,9},{9,8},{10,11... | collective-permute-start | bytes 1179656 | tf_op jit(solution)/shard_map/ppermute | solution.py:346
  45.3 9.1 %collective-permute-start.14 = (bf16[2,128,768]{2,1,0:T(8,128)(2,1)S(1)}, bf16[2,128,768]{2,1,0:T(8,128)(2,1)S(1)}, u32[]{:S(2)}, u32[]{:S(2)}) collective-permute-start(bf16[2,128,768]{2,1,0:T(8,128)(2,1)S(1)} %get-tuple-element.74), channel_id=1, source_target_pairs={{0,1},{1,0},{2,3},{3,2},{4,5},{5,4},{6,7},{7,6},{8,9},{9,8},{10,11... | collective-permute-start | bytes 1179656 | tf_op jit(solution)/shard_map/ppermute | solution.py:354
  45.9 21.3 %collective-permute-start.11 = (bf16[2,256,768]{2,1,0:T(8,128)(2,1)S(1)}, bf16[2,256,768]{2,1,0:T(8,128)(2,1)S(1)}, u32[]{:S(2)}, u32[]{:S(2)}) collective-permute-start(bf16[2,256,768]{2,1,0:T(8,128)(2,1)S(1)} %get-tuple-element.67), channel_id=1, source_target_pairs={{0,30},{2,4},{4,2},{6,8},{8,6},{10,12},{12,10},{14,16},{16,14},{18... | collective-permute-start | bytes 2359304 | tf_op jit(solution)/shard_map/ppermute | solution.py:499
  46.7 27.3 %collective-permute-start.21 = (bf16[2,256,768]{2,1,0:T(8,128)(2,1)S(1)}, bf16[2,256,768]{2,1,0:T(8,128)(2,1)S(1)}, u32[]{:S(2)}, u32[]{:S(2)}) collective-permute-start(bf16[2,256,768]{2,1,0:T(8,128)(2,1)S(1)} %get-tuple-element.81), channel_id=1, source_target_pairs={{0,2},{2,0},{4,6},{6,4},{8,10},{10,8},{12,14},{14,12},{16,18},{18,... | collective-permute-start | bytes 2359304 | tf_op jit(solution)/shard_map/ppermute | solution.py:500
  54.4 1.3 %collective-permute-start.15 = (bf16[24,1536]{1,0:T(8,128)(2,1)S(1)}, bf16[24,1536]{1,0:T(8,128)(2,1)S(1)}, u32[]{:S(2)}, u32[]{:S(2)}) collective-permute-start(bf16[24,1536]{1,0:T(8,128)(2,1)S(1)} %get-tuple-element.75), channel_id=1, source_target_pairs={{0,2},{2,0},{4,6},{6,4},{8,10},{10,8},{12,14},{14,12},{16,18},{18,... | collective-permute-start | bytes 221192 | tf_op jit(solution)/shard_map/ppermute | solution.py:459
  55.7 8.0 %collective-permute-start.18 = (bf16[24,1536]{1,0:T(8,128)(2,1)S(1)}, bf16[24,1536]{1,0:T(8,128)(2,1)S(1)}, u32[]{:S(2)}, u32[]{:S(2)}) collective-permute-start(bf16[24,1536]{1,0:T(8,128)(2,1)S(1)} %add.19), channel_id=1, source_target_pairs={{0,24},{2,26},{4,28},{6,30},{8,16},{10,18},{12,20},{14,22},{16,8},... | collective-permute-start | bytes 221192 | tf_op jit(solution)/shard_map/ppermute | solution.py:459
  60.7 6.5 %collective-permute-start.17 = (bf16[24,1536]{1,0:T(8,128)(2,1)S(1)}, bf16[24,1536]{1,0:T(8,128)(2,1)S(1)}, u32[]{:S(2)}, u32[]{:S(2)}) collective-permute-start(bf16[24,1536]{1,0:T(8,128)(2,1)S(1)} %add.19), channel_id=1, source_target_pairs={{0,16},{2,18},{4,20},{6,22},{8,24},{10,26},{12,28},{14,30},{16,0},... | collective-permute-start | bytes 221192 | tf_op jit(solution)/shard_map/ppermute | solution.py:459
  60.7 6.5 %collective-permute-start.16 = (bf16[24,1536]{1,0:T(8,128)(2,1)S(1)}, bf16[24,1536]{1,0:T(8,128)(2,1)S(1)}, u32[]{:S(2)}, u32[]{:S(2)}) collective-permute-start(bf16[24,1536]{1,0:T(8,128)(2,1)S(1)} %add.19), channel_id=1, source_target_pairs={{0,8},{2,10},{4,12},{6,14},{8,0},{10,2},{12,4},{14,6},{16,24},{18,... | collective-permute-start | bytes 221192 | tf_op jit(solution)/shard_map/ppermute | solution.py:459
  63.7 10.3 %collective-permute-start.19 = (bf16[2,128,768]{2,1,0:T(8,128)(2,1)S(1)}, bf16[2,128,768]{2,1,0:T(8,128)(2,1)S(1)}, u32[]{:S(2)}, u32[]{:S(2)}) collective-permute-start(bf16[2,128,768]{2,1,0:T(8,128)(2,1)S(1)} %get-tuple-element.76), channel_id=1, source_target_pairs={{0,1},{1,0},{2,3},{3,2},{4,5},{5,4},{6,7},{7,6},{8,9},{9,8},{10,11... | collective-permute-start | bytes 1179656 | tf_op jit(solution)/shard_map/ppermute | solution.py:354
  67.2 16.4 %collective-permute-start.10 = (bf16[2,256,768]{2,1,0:T(8,128)(2,1)S(1)}, bf16[2,256,768]{2,1,0:T(8,128)(2,1)S(1)}, u32[]{:S(2)}, u32[]{:S(2)}) collective-permute-start(bf16[2,256,768]{2,1,0:T(8,128)(2,1)S(1)} %get-tuple-element.63), channel_id=1, source_target_pairs={{0,2},{2,0},{4,6},{6,4},{8,10},{10,8},{12,14},{14,12},{16,18},{18,... | collective-permute-start | bytes 2359304 | tf_op jit(solution)/shard_map/ppermute | solution.py:500
  67.2 13.8 %collective-permute-start.12 = (bf16[2,128,768]{2,1,0:T(8,128)(2,1)S(1)}, bf16[2,128,768]{2,1,0:T(8,128)(2,1)S(1)}, u32[]{:S(2)}, u32[]{:S(2)}) collective-permute-start(bf16[2,128,768]{2,1,0:T(8,128)(2,1)S(1)} %get-tuple-element.69), channel_id=1, source_target_pairs={{0,30},{2,4},{4,2},{6,8},{8,6},{10,12},{12,10},{14,16},{16,14},{18... | collective-permute-start | bytes 1179656 | tf_op jit(solution)/shard_map/ppermute | solution.py:499
  74.2 9.5 %collective-permute-start.22 = (bf16[2,128,768]{2,1,0:T(8,128)(2,1)S(1)}, bf16[2,128,768]{2,1,0:T(8,128)(2,1)S(1)}, u32[]{:S(2)}, u32[]{:S(2)}) collective-permute-start(bf16[2,128,768]{2,1,0:T(8,128)(2,1)S(1)} %far_sum.2), channel_id=1, source_target_pairs={{0,1},{1,0},{2,3},{3,2},{4,5},{5,4},{6,7},{7,6},{8,9},{9,8},{10,11... | collective-permute-start | bytes 1179656 | tf_op jit(solution)/shard_map/ppermute | solution.py:354
  75.7 5.3 %collective-permute-start.20 = (bf16[24,1536]{1,0:T(8,128)(2,1)S(1)}, bf16[24,1536]{1,0:T(8,128)(2,1)S(1)}, u32[]{:S(2)}, u32[]{:S(2)}) collective-permute-start(bf16[24,1536]{1,0:T(8,128)(2,1)S(1)} %add_add_fusion), channel_id=1, source_target_pairs={{0,4},{2,6},{4,0},{6,2},{8,12},{10,14},{12,8},{14,10},{16,20},{18,... | collective-permute-start | bytes 221192 | tf_op jit(solution)/shard_map/ppermute | solution.py:459
  81.0 12.9 %collective-permute-start.13 = (bf16[2,128,768]{2,1,0:T(8,128)(2,1)S(1)}, bf16[2,128,768]{2,1,0:T(8,128)(2,1)S(1)}, u32[]{:S(2)}, u32[]{:S(2)}) collective-permute-start(bf16[2,128,768]{2,1,0:T(8,128)(2,1)S(1)} %get-tuple-element.70), channel_id=1, source_target_pairs={{0,30},{2,4},{4,2},{6,8},{8,6},{10,12},{12,10},{14,16},{16,14},{18... | collective-permute-start | bytes 1179656 | tf_op jit(solution)/shard_map/ppermute | solution.py:510
  83.7 10.2 %collective-permute-start.23 = (bf16[2,128,768]{2,1,0:T(8,128)(2,1)S(1)}, bf16[2,128,768]{2,1,0:T(8,128)(2,1)S(1)}, u32[]{:S(2)}, u32[]{:S(2)}) collective-permute-start(bf16[2,128,768]{2,1,0:T(8,128)(2,1)S(1)} %far_sum.3), channel_id=1, source_target_pairs={{0,1},{1,0},{2,3},{3,2},{4,5},{5,4},{6,7},{7,6},{8,9},{9,8},{10,11... | collective-permute-start | bytes 1179656 | tf_op jit(solution)/shard_map/ppermute | solution.py:354
  85.2 8.7 %collective-permute-start.24 = (bf16[24,1536]{1,0:T(8,128)(2,1)S(1)}, bf16[24,1536]{1,0:T(8,128)(2,1)S(1)}, u32[]{:S(2)}, u32[]{:S(2)}) collective-permute-start(bf16[24,1536]{1,0:T(8,128)(2,1)S(1)} %add.23.refs_3_), channel_id=1, source_target_pairs={{0,1},{1,0},{2,3},{3,2},{4,5},{5,4},{6,7},{7,6},{8,9},{9,8},{10,11... | collective-permute-start | bytes 221192 | tf_op jit(solution)/shard_map/ppermute | solution.py:522

commit v15 on v14

--- a/solution.py
+++ b/solution.py
@@ -402,7 +402,7 @@
     )
 
     direct = tokens <= 256
-    batch = next(n for n in (3, 2, 1) if part_heads % n == 0) if direct else 1
+    batch = next(n for n in (6, 3, 2, 1) if part_heads % n == 0) if direct else 1
     q_size = min(256, tokens)
 
     def attention(p, joint):

time: 97 us -> 96.9 us (level)
  no operation moved by 1% of the time
where the time goes in v15:
time: 96.9 us; the launch traced here: 95.7 us
  waiting for transfers between devices  44.3 us (46%)
  starting transfers between devices  29.5 us (30%)
  Pallas kernels  20.8 us (21%)
  between operations  0.97 us (1%)
    ppermute x4, waiting for transfers between devices, to_peers(): arrived.append(lax.ppermute(part, 'head', pairs))  21.4 us
    pallas_call x2, Pallas kernels, attention(): pl.pallas_call(functools.partial(attention_kernel, rows=rows, tokens=toke...  12.5 us
    ppermute x5, waiting for transfers between devices, shifted(): return lax.ppermute(array, 'ctx', [(i, i ^ step) for i in range(ctx_count)])  11 us
    ppermute x1, waiting for transfers between devices, to_all(): slabs = slabs + [lax.ppermute(slab, 'head', pairs) for slab in slabs]  6.84 us
    ppermute x1, starting transfers between devices, per_device(): side_own = lax.ppermute(kv_own, 'ctx', side_pairs)  5.64 us
    ppermute x5, starting transfers between devices, shifted(): return lax.ppermute(array, 'ctx', [(i, i ^ step) for i in range(ctx_count)])  5.62 us
    ppermute x4, waiting for transfers between devices, from_peers(): arrived.append(lax.ppermute(part, 'head', pairs))  5.16 us
    ppermute x4, starting transfers between devices, from_peers(): arrived.append(lax.ppermute(part, 'head', pairs))  5.08 us
  transfers between devices with their start and end apart: 25, of which 11 were waited for; matrix products, arithmetic and copies ran while one was open for 0% of the time, Pallas kernels for 17%

profile of v15, /device:TPU:0, one launch (start us, length us, event | category | flops | bytes accessed | tf_op | source)
XLA Modules:
  0.0 95.7 jit_solution(7564279006374517520)
XLA Ops:
  0.7 0.0 copy-start.1
  0.7 0.0 copy-start.4
  0.7 0.0 copy-start.5
  0.7 0.0 copy-start.6
  0.7 2.8 %pack.3 = (bf16[2,128,1536]{2,1,0:T(8,128)(2,1)}, bf16[2,128,768]{2,1,0:T(8,128)(2,1)}, bf16[2,128,768]{2,1,0:T(8,128)(2,1)}) custom-call(s32[1]{0:T(128)} %bitcast.place_ref, bf16[128,3072]{1,0:T(8,128)(2,1)} %first_ref.3, bf16[128,3072]{1,0:T(8,128)(2,1)} %second_ref.3), custom_call_target="tpu_custom_call" | custom-call | flops 1 | bytes 1 | tf_op jit(solution)/shard_map/pack/pallas_call | solution.py:326
  3.5 0.5 collective-permute-start.2
  4.0 5.6 %collective-permute-start.1 = (bf16[2,128,1536]{2,1,0:T(8,128)(2,1)}, bf16[2,128,1536]{2,1,0:T(8,128)(2,1)S(1)}, u32[]{:S(2)}, u32[]{:S(2)}) collective-permute-start(bf16[2,128,1536]{2,1,0:T(8,128)(2,1)} %get-tuple-element.51.kv_own_ref), channel_id=1, source_target_pairs={{0,30},{2,4},{4,2},{6,8},{8,6},{10,12},{12,10},{14,16},{16,14},{18... | collective-permute-start | bytes 2359304 | tf_op jit(solution)/shard_map/ppermute | solution.py:359
  9.7 1.5 %collective-permute-start.6 = (bf16[2,128,768]{2,1,0:T(8,128)(2,1)}, bf16[2,128,768]{2,1,0:T(8,128)(2,1)S(1)}, u32[]{:S(2)}, u32[]{:S(2)}) collective-permute-start(bf16[2,128,768]{2,1,0:T(8,128)(2,1)} %get-tuple-element.59), channel_id=1, source_target_pairs={{0,1},{1,0},{2,3},{3,2},{4,5},{5,4},{6,7},{7,6},{8,9},{9,8},{10,11... | collective-permute-start | bytes 1179656 | tf_op jit(solution)/shard_map/ppermute | solution.py:346
  11.2 0.5 collective-permute-start
  11.7 0.0 copy-done.2
  11.7 0.3 pack.2
  12.0 10.0 %collective-permute-done.6.kv_ref = bf16[2,128,768]{2,1,0:T(8,128)(2,1)S(1)} collective-permute-done((bf16[2,128,768]{2,1,0:T(8,128)(2,1)}, bf16[2,128,768]{2,1,0:T(8,128)(2,1)S(1)}, u32[]{:S(2)}, u32[]{:S(2)}) %collective-permute-start.6) | collective-permute-done | bytes 393248 | tf_op jit(solution)/shard_map/ppermute | solution.py:346
  21.9 1.5 %collective-permute-start.7 = (bf16[2,128,768]{2,1,0:T(8,128)(2,1)S(1)}, bf16[2,128,768]{2,1,0:T(8,128)(2,1)S(1)}, u32[]{:S(2)}, u32[]{:S(2)}) collective-permute-start(bf16[2,128,768]{2,1,0:T(8,128)(2,1)S(1)} %get-tuple-element.60), channel_id=1, source_target_pairs={{0,1},{1,0},{2,3},{3,2},{4,5},{5,4},{6,7},{7,6},{8,9},{9,8},{10,11... | collective-permute-start | bytes 1179656 | tf_op jit(solution)/shard_map/ppermute | solution.py:346
  23.5 0.0 collective-permute-start.9
  23.5 6.9 %collective-permute-done.kv_ref = bf16[2,128,768]{2,1,0:T(8,128)(2,1)S(1)} collective-permute-done((bf16[2,128,768]{2,1,0:T(8,128)(2,1)}, bf16[2,128,768]{2,1,0:T(8,128)(2,1)S(1)}, u32[]{:S(2)}, u32[]{:S(2)}) %collective-permute-start) | collective-permute-done | bytes 393248 | tf_op jit(solution)/shard_map/ppermute | solution.py:346
  30.4 0.0 collective-permute-start.8
  30.4 0.0 collective-permute-done.2.near_own_ref
  30.4 0.6 collective-permute-start.5
  31.0 0.0 collective-permute-done.1.side_own_ref
  31.0 0.0 collective-permute-start.4
  31.0 4.5 %collective-permute-done.7.qo_ref = bf16[2,128,768]{2,1,0:T(8,128)(2,1)S(1)} collective-permute-done((bf16[2,128,768]{2,1,0:T(8,128)(2,1)S(1)}, bf16[2,128,768]{2,1,0:T(8,128)(2,1)S(1)}, u32[]{:S(2)}, u32[]{:S(2)}) %collective-permute-start.7) | collective-permute-done | bytes 393248 | tf_op jit(solution)/shard_map/ppermute | solution.py:346
  35.5 1.5 %collective-permute-start.3 = (bf16[2,128,768]{2,1,0:T(8,128)(2,1)S(1)}, bf16[2,128,768]{2,1,0:T(8,128)(2,1)S(1)}, u32[]{:S(2)}, u32[]{:S(2)}) collective-permute-start(bf16[2,128,768]{2,1,0:T(8,128)(2,1)S(1)} %get-tuple-element.54), channel_id=1, source_target_pairs={{0,1},{1,0},{2,3},{3,2},{4,5},{5,4},{6,7},{7,6},{8,9},{9,8},{10,11... | collective-permute-start | bytes 1179656 | tf_op jit(solution)/shard_map/ppermute | solution.py:346
  37.0 1.9 %prep.1 = (f32[768,256]{1,0:T(8,128)S(1)}, f32[256,1536]{1,0:T(8,128)S(1)}, bf16[24,256]{1,0:T(8,128)(2,1)S(1)}) custom-call(s32[1]{0:T(128)} %bitcast.place_ref, s32[32,128]{1,0:T(8,128)S(1)} %bitcast.3, s32[1,24]{1,0:T(1,128)S(1)} %bitcast.4, s32[24,24]{1,0:T(8,128)S(1)} %copy-done.5, f32[128,3072]{1,0:T(8,128)S(1)} %copy-done.1), custom_call_target="tpu_custom_call" | custom-call | flops 1 | bytes 1 | tf_op jit(solution)/shard_map/prep/pallas_call | solution.py:371
  38.9 0.0 collective-permute-done.9.side_far_ref
  38.9 0.0 collective-permute-done.8.near_far_ref
  38.9 6.1 %attention.2 = (bf16[2,128,768]{2,1,0:T(8,128)(2,1)S(1)}, f32[2,128,768]{2,1,0:T(8,128)S(1)}, f32[2,128,768]{2,1,0:T(8,128)S(1)}, bf16[2,256,768]{2,1,0:T(8,128)...) custom-call(s32[1]{0:T(128)} %bitcast.place_ref, ...), custom_call_target="tpu_custom_call" | custom-call | flops 1 | bytes 1 | tf_op jit(solution)/shard_map/attention/pallas_call | solution.py:433
  45.0 0.6 collective-permute-start.14
  45.6 0.0 collective-permute-done.5.side_far_ref
  45.6 0.0 collective-permute-done.4.near_far_ref
  45.6 0.0 collective-permute-done.3.qo_ref
  45.6 0.8 collective-permute-start.11
  46.4 0.8 collective-permute-start.21
  47.2 6.3 %attention.3 = (bf16[2,128,768]{2,1,0:T(8,128)(2,1)S(1)}, f32[2,128,768]{2,1,0:T(8,128)S(1)}, f32[2,128,768]{2,1,0:T(8,128)S(1)}, bf16[2,256,768]{2,1,0:T(8,128)...) custom-call(s32[1]{0:T(128)} %bitcast.place_ref, ...), custom_call_target="tpu_custom_call", output_to_operand_aliasing={{7}: (12, {})} | custom-call | flops 1 | bytes 1 | tf_op jit(solution)/shard_map/attention/pallas_call | solution.py:433
  53.6 0.6 collective-permute-done.14.refs_0_
  54.1 0.0 collective-permute-start.15
  54.2 1.3 %collective-permute-done.15 = bf16[24,1536]{1,0:T(8,128)(2,1)S(1)} collective-permute-done((bf16[24,1536]{1,0:T(8,128)(2,1)S(1)}, bf16[24,1536]{1,0:T(8,128)(2,1)S(1)}, u32[]{:S(2)}, u32[]{:S(2)}) %collective-permute-start.15) | collective-permute-done | bytes 73760 | tf_op jit(solution)/shard_map/ppermute | solution.py:459
  55.4 5.0 %collective-permute-start.18 = (bf16[24,1536]{1,0:T(8,128)(2,1)S(1)}, bf16[24,1536]{1,0:T(8,128)(2,1)S(1)}, u32[]{:S(2)}, u32[]{:S(2)}) collective-permute-start(bf16[24,1536]{1,0:T(8,128)(2,1)S(1)} %add.19), channel_id=1, source_target_pairs={{0,24},{2,26},{4,28},{6,30},{8,16},{10,18},{12,20},{14,22},{16,8},... | collective-permute-start | bytes 221192 | tf_op jit(solution)/shard_map/ppermute | solution.py:459
  60.4 0.0 collective-permute-start.17
  60.4 0.6 collective-permute-start.16
  61.1 2.3 %collective-permute-done.18 = bf16[24,1536]{1,0:T(8,128)(2,1)S(1)} collective-permute-done((bf16[24,1536]{1,0:T(8,128)(2,1)S(1)}, bf16[24,1536]{1,0:T(8,128)(2,1)S(1)}, u32[]{:S(2)}, u32[]{:S(2)}) %collective-permute-start.18) | collective-permute-done | bytes 73760 | tf_op jit(solution)/shard_map/ppermute | solution.py:459
  63.4 1.5 %collective-permute-start.19 = (bf16[2,128,768]{2,1,0:T(8,128)(2,1)S(1)}, bf16[2,128,768]{2,1,0:T(8,128)(2,1)S(1)}, u32[]{:S(2)}, u32[]{:S(2)}) collective-permute-start(bf16[2,128,768]{2,1,0:T(8,128)(2,1)S(1)} %get-tuple-element.76), channel_id=1, source_target_pairs={{0,1},{1,0},{2,3},{3,2},{4,5},{5,4},{6,7},{7,6},{8,9},{9,8},{10,11... | collective-permute-start | bytes 1179656 | tf_op jit(solution)/shard_map/ppermute | solution.py:354
  64.9 2.1 %collective-permute-done.17 = bf16[24,1536]{1,0:T(8,128)(2,1)S(1)} collective-permute-done((bf16[24,1536]{1,0:T(8,128)(2,1)S(1)}, bf16[24,1536]{1,0:T(8,128)(2,1)S(1)}, u32[]{:S(2)}, u32[]{:S(2)}) %collective-permute-start.17) | collective-permute-done | bytes 73760 | tf_op jit(solution)/shard_map/ppermute | solution.py:459
  66.9 0.0 collective-permute-start.10
  66.9 0.0 collective-permute-done.16
  66.9 0.0 collective-permute-done.11.side_ref
  67.0 3.0 %collective-permute-start.12 = (bf16[2,128,768]{2,1,0:T(8,128)(2,1)S(1)}, bf16[2,128,768]{2,1,0:T(8,128)(2,1)S(1)}, u32[]{:S(2)}, u32[]{:S(2)}) collective-permute-start(bf16[2,128,768]{2,1,0:T(8,128)(2,1)S(1)} %get-tuple-element.69), channel_id=1, source_target_pairs={{0,30},{2,4},{4,2},{6,8},{8,6},{10,12},{12,10},{14,16},{16,14},{18... | collective-permute-start | bytes 1179656 | tf_op jit(solution)/shard_map/ppermute | solution.py:499
  70.0 3.7 %collective-permute-done.19.refs_0_ = bf16[2,128,768]{2,1,0:T(8,128)(2,1)S(1)} collective-permute-done((bf16[2,128,768]{2,1,0:T(8,128)(2,1)S(1)}, bf16[2,128,768]{2,1,0:T(8,128)(2,1)S(1)}, u32[]{:S(2)}, u32[]{:S(2)}) %collective-permute-start.19) | collective-permute-done | bytes 393248 | tf_op jit(solution)/shard_map/ppermute | solution.py:354
  73.7 0.0 collective-permute-done.21.near_ref
  73.7 0.2 far_sum.2
  73.9 1.5 %collective-permute-start.22 = (bf16[2,128,768]{2,1,0:T(8,128)(2,1)S(1)}, bf16[2,128,768]{2,1,0:T(8,128)(2,1)S(1)}, u32[]{:S(2)}, u32[]{:S(2)}) collective-permute-start(bf16[2,128,768]{2,1,0:T(8,128)(2,1)S(1)} %far_sum.2), channel_id=1, source_target_pairs={{0,1},{1,0},{2,3},{3,2},{4,5},{5,4},{6,7},{7,6},{8,9},{9,8},{10,11... | collective-permute-start | bytes 1179656 | tf_op jit(solution)/shard_map/ppermute | solution.py:354
  75.4 0.0 collective-permute-start.20
  75.4 5.3 %collective-permute-done.20 = bf16[24,1536]{1,0:T(8,128)(2,1)S(1)} collective-permute-done((bf16[24,1536]{1,0:T(8,128)(2,1)S(1)}, bf16[24,1536]{1,0:T(8,128)(2,1)S(1)}, u32[]{:S(2)}, u32[]{:S(2)}) %collective-permute-start.20) | collective-permute-done | bytes 73760 | tf_op jit(solution)/shard_map/ppermute | solution.py:459
  80.7 0.0 collective-permute-done.12.side_ref
  80.7 1.8 %collective-permute-start.13 = (bf16[2,128,768]{2,1,0:T(8,128)(2,1)S(1)}, bf16[2,128,768]{2,1,0:T(8,128)(2,1)S(1)}, u32[]{:S(2)}, u32[]{:S(2)}) collective-permute-start(bf16[2,128,768]{2,1,0:T(8,128)(2,1)S(1)} %get-tuple-element.70), channel_id=1, source_target_pairs={{0,30},{2,4},{4,2},{6,8},{8,6},{10,12},{12,10},{14,16},{16,14},{18... | collective-permute-start | bytes 1179656 | tf_op jit(solution)/shard_map/ppermute | solution.py:510
  82.5 0.8 collective-permute-done.22.refs_1_
  83.3 0.0 collective-permute-done.10.near_ref
  83.3 0.1 far_sum.3
  83.5 1.5 %collective-permute-start.23 = (bf16[2,128,768]{2,1,0:T(8,128)(2,1)S(1)}, bf16[2,128,768]{2,1,0:T(8,128)(2,1)S(1)}, u32[]{:S(2)}, u32[]{:S(2)}) collective-permute-start(bf16[2,128,768]{2,1,0:T(8,128)(2,1)S(1)} %far_sum.3), channel_id=1, source_target_pairs={{0,1},{1,0},{2,3},{3,2},{4,5},{5,4},{6,7},{7,6},{8,9},{9,8},{10,11... | collective-permute-start | bytes 1179656 | tf_op jit(solution)/shard_map/ppermute | solution.py:354
  85.0 0.6 collective-permute-start.24
  85.6 1.2 %finish.2 = (bf16[128,3072]{1,0:T(8,128)(2,1)}, bf16[128,3072]{1,0:T(8,128)(2,1)}, bf16[128,3072]{1,0:T(8,128)(2,1)}, bf16[128,3072]{1,0:T(8,128)(2,1)}) custom-call(s32[1]{0:T(128)} %bitcast.place_ref, f32[2,128,768]{2,1,0:T(8,128)S(1)} %get-tuple-element.87.part_ref, bf16[2,256,768]{2,1,0:T(8,128)(2,1)S(1)} %collective-permute-done.21.near_ref, ...), custom_call_target="tpu_custom_call" | custom-call | flops 1 | bytes 1 | tf_op jit(solution)/shard_map/finish/pallas_call | solution.py:538
  86.8 6.8 %collective-permute-done.24.refs_4_ = bf16[24,1536]{1,0:T(8,128)(2,1)S(1)} collective-permute-done((bf16[24,1536]{1,0:T(8,128)(2,1)S(1)}, bf16[24,1536]{1,0:T(8,128)(2,1)S(1)}, u32[]{:S(2)}, u32[]{:S(2)}) %collective-permute-start.24) | collective-permute-done | bytes 73760 | tf_op jit(solution)/shard_map/ppermute | solution.py:522
  93.6 0.0 collective-permute-done.13.side_ref
  93.7 0.0 collective-permute-done.23.refs_1_
  93.7 1.9 %finish.3 = (bf16[128,3072]{1,0:T(8,128)(2,1)}, bf16[128,3072]{1,0:T(8,128)(2,1)}, bf16[128,3072]{1,0:T(8,128)(2,1)}, bf16[128,3072]{1,0:T(8,128)(2,1)}, f32[128,3072]{1,0:T(8,128)}) custom-call(s32[1]{0:T(128)} %bitcast.place_ref, ...), custom_call_target="tpu_custom_call", output_to_operand_aliasing={{0}: (10, {}), {1}: (11, {}), {2}: (12, {}), {3}: (13, {})} | custom-call | flops 1 | bytes 1 | tf_op jit(solution)/shard_map/finish/pallas_call | solution.py:538
  (12 shorter events, 0.1 us)
Async XLA Ops:
  0.6 11.1 %copy-start.3 = (bf16[128,3072]{1,0:T(8,128)(2,1)S(1)}, bf16[128,3072]{1,0:T(8,128)(2,1)}, u32[]{:S(2)}) copy-start(bf16[128,3072]{1,0:T(8,128)(2,1)} %second_ref.2) | copy-start | bytes 2359300
  0.6 11.1 %copy-start.2 = (bf16[128,3072]{1,0:T(8,128)(2,1)S(1)}, bf16[128,3072]{1,0:T(8,128)(2,1)}, u32[]{:S(2)}) copy-start(bf16[128,3072]{1,0:T(8,128)(2,1)} %first_ref.2) | copy-start | bytes 2359300
  0.7 36.3 %copy-start.1 = (f32[128,3072]{1,0:T(8,128)S(1)}, f32[128,3072]{1,0:T(8,128)}, u32[]{:S(2)}) copy-start(f32[128,3072]{1,0:T(8,128)} %table_ref.1) | copy-start | bytes 4718596
  0.7 36.3 %copy-start.4 = (s32[4096]{0:T(1024)S(1)}, s32[4096]{0:T(1024)}, u32[]{:S(2)}) copy-start(s32[4096]{0:T(1024)} %param.13) | copy-start | bytes 49156
  0.7 36.3 %copy-start.5 = (s32[24,24]{1,0:T(8,128)S(1)}, s32[24,24]{1,0:T(8,128)}, u32[]{:S(2)}) copy-start(s32[24,24]{1,0:T(8,128)} %mask_ref.1) | copy-start | bytes 6916
  0.7 36.3 %copy-start.6 = (s32[24]{0:T(128)S(1)}, s32[24]{0:T(128)}, u32[]{:S(2)}) copy-start(s32[24]{0:T(128)} %param.14) | copy-start | bytes 292
  3.5 26.9 %collective-permute-start.2 = (bf16[2,128,1536]{2,1,0:T(8,128)(2,1)}, bf16[2,128,1536]{2,1,0:T(8,128)(2,1)S(1)}, u32[]{:S(2)}, u32[]{:S(2)}) collective-permute-start(bf16[2,128,1536]{2,1,0:T(8,128)(2,1)} %get-tuple-element.51.kv_own_ref), channel_id=1, source_target_pairs={{0,2},{2,0},{4,6},{6,4},{8,10},{10,8},{12,14},{14,12},{16,18},{18,... | collective-permute-start | bytes 2359304 | tf_op jit(solution)/shard_map/ppermute | solution.py:360
  4.0 26.9 %collective-permute-start.1 = (bf16[2,128,1536]{2,1,0:T(8,128)(2,1)}, bf16[2,128,1536]{2,1,0:T(8,128)(2,1)S(1)}, u32[]{:S(2)}, u32[]{:S(2)}) collective-permute-start(bf16[2,128,1536]{2,1,0:T(8,128)(2,1)} %get-tuple-element.51.kv_own_ref), channel_id=1, source_target_pairs={{0,30},{2,4},{4,2},{6,8},{8,6},{10,12},{12,10},{14,16},{16,14},{18... | collective-permute-start | bytes 2359304 | tf_op jit(solution)/shard_map/ppermute | solution.py:359
  9.7 12.3 %collective-permute-start.6 = (bf16[2,128,768]{2,1,0:T(8,128)(2,1)}, bf16[2,128,768]{2,1,0:T(8,128)(2,1)S(1)}, u32[]{:S(2)}, u32[]{:S(2)}) collective-permute-start(bf16[2,128,768]{2,1,0:T(8,128)(2,1)} %get-tuple-element.59), channel_id=1, source_target_pairs={{0,1},{1,0},{2,3},{3,2},{4,5},{5,4},{6,7},{7,6},{8,9},{9,8},{10,11... | collective-permute-start | bytes 1179656 | tf_op jit(solution)/shard_map/ppermute | solution.py:346
  11.2 27.7 %copy-start = (bf16[2,128,1536]{2,1,0:T(8,128)(2,1)S(1)}, bf16[2,128,1536]{2,1,0:T(8,128)(2,1)}, u32[]{:S(2)}) copy-start(bf16[2,128,1536]{2,1,0:T(8,128)(2,1)} %get-tuple-element.51.kv_own_ref) | copy-start | bytes 2359300
  11.2 19.2 %collective-permute-start = (bf16[2,128,768]{2,1,0:T(8,128)(2,1)}, bf16[2,128,768]{2,1,0:T(8,128)(2,1)S(1)}, u32[]{:S(2)}, u32[]{:S(2)}) collective-permute-start(bf16[2,128,768]{2,1,0:T(8,128)(2,1)} %get-tuple-element.53), channel_id=1, source_target_pairs={{0,1},{1,0},{2,3},{3,2},{4,5},{5,4},{6,7},{7,6},{8,9},{9,8},{10,11... | collective-permute-start | bytes 1179656 | tf_op jit(solution)/shard_map/ppermute | solution.py:346
  21.9 13.5 %collective-permute-start.7 = (bf16[2,128,768]{2,1,0:T(8,128)(2,1)S(1)}, bf16[2,128,768]{2,1,0:T(8,128)(2,1)S(1)}, u32[]{:S(2)}, u32[]{:S(2)}) collective-permute-start(bf16[2,128,768]{2,1,0:T(8,128)(2,1)S(1)} %get-tuple-element.60), channel_id=1, source_target_pairs={{0,1},{1,0},{2,3},{3,2},{4,5},{5,4},{6,7},{7,6},{8,9},{9,8},{10,11... | collective-permute-start | bytes 1179656 | tf_op jit(solution)/shard_map/ppermute | solution.py:346
  23.5 15.4 %collective-permute-start.9 = (bf16[2,128,768]{2,1,0:T(8,128)(2,1)S(1)}, bf16[2,128,768]{2,1,0:T(8,128)(2,1)S(1)}, u32[]{:S(2)}, u32[]{:S(2)}) collective-permute-start(bf16[2,128,768]{2,1,0:T(8,128)(2,1)S(1)} %collective-permute-done.6.kv_ref), channel_id=1, source_target_pairs={{0,30},{2,4},{4,2},{6,8},{8,6},{10,12},{12,10},{14,16},{16,14},{18... | collective-permute-start | bytes 1179656 | tf_op jit(solution)/shard_map/ppermute | solution.py:362
  30.4 8.5 %collective-permute-start.8 = (bf16[2,128,768]{2,1,0:T(8,128)(2,1)S(1)}, bf16[2,128,768]{2,1,0:T(8,128)(2,1)S(1)}, u32[]{:S(2)}, u32[]{:S(2)}) collective-permute-start(bf16[2,128,768]{2,1,0:T(8,128)(2,1)S(1)} %collective-permute-done.6.kv_ref), channel_id=1, source_target_pairs={{0,2},{2,0},{4,6},{6,4},{8,10},{10,8},{12,14},{14,12},{16,18},{18,... | collective-permute-start | bytes 1179656 | tf_op jit(solution)/shard_map/ppermute | solution.py:363
  30.4 15.2 %collective-permute-start.5 = (bf16[2,128,768]{2,1,0:T(8,128)(2,1)S(1)}, bf16[2,128,768]{2,1,0:T(8,128)(2,1)S(1)}, u32[]{:S(2)}, u32[]{:S(2)}) collective-permute-start(bf16[2,128,768]{2,1,0:T(8,128)(2,1)S(1)} %collective-permute-done.kv_ref), channel_id=1, source_target_pairs={{0,30},{2,4},{4,2},{6,8},{8,6},{10,12},{12,10},{14,16},{16,14},{18... | collective-permute-start | bytes 1179656 | tf_op jit(solution)/shard_map/ppermute | solution.py:362
  31.0 14.6 %collective-permute-start.4 = (bf16[2,128,768]{2,1,0:T(8,128)(2,1)S(1)}, bf16[2,128,768]{2,1,0:T(8,128)(2,1)S(1)}, u32[]{:S(2)}, u32[]{:S(2)}) collective-permute-start(bf16[2,128,768]{2,1,0:T(8,128)(2,1)S(1)} %collective-permute-done.kv_ref), channel_id=1, source_target_pairs={{0,2},{2,0},{4,6},{6,4},{8,10},{10,8},{12,14},{14,12},{16,18},{18,... | collective-permute-start | bytes 1179656 | tf_op jit(solution)/shard_map/ppermute | solution.py:363
  35.5 10.2 %collective-permute-start.3 = (bf16[2,128,768]{2,1,0:T(8,128)(2,1)S(1)}, bf16[2,128,768]{2,1,0:T(8,128)(2,1)S(1)}, u32[]{:S(2)}, u32[]{:S(2)}) collective-permute-start(bf16[2,128,768]{2,1,0:T(8,128)(2,1)S(1)} %get-tuple-element.54), channel_id=1, source_target_pairs={{0,1},{1,0},{2,3},{3,2},{4,5},{5,4},{6,7},{7,6},{8,9},{9,8},{10,11... | collective-permute-start | bytes 1179656 | tf_op jit(solution)/shard_map/ppermute | solution.py:346
  45.0 9.1 %collective-permute-start.14 = (bf16[2,128,768]{2,1,0:T(8,128)(2,1)S(1)}, bf16[2,128,768]{2,1,0:T(8,128)(2,1)S(1)}, u32[]{:S(2)}, u32[]{:S(2)}) collective-permute-start(bf16[2,128,768]{2,1,0:T(8,128)(2,1)S(1)} %get-tuple-element.74), channel_id=1, source_target_pairs={{0,1},{1,0},{2,3},{3,2},{4,5},{5,4},{6,7},{7,6},{8,9},{9,8},{10,11... | collective-permute-start | bytes 1179656 | tf_op jit(solution)/shard_map/ppermute | solution.py:354
  45.6 21.3 %collective-permute-start.11 = (bf16[2,256,768]{2,1,0:T(8,128)(2,1)S(1)}, bf16[2,256,768]{2,1,0:T(8,128)(2,1)S(1)}, u32[]{:S(2)}, u32[]{:S(2)}) collective-permute-start(bf16[2,256,768]{2,1,0:T(8,128)(2,1)S(1)} %get-tuple-element.67), channel_id=1, source_target_pairs={{0,30},{2,4},{4,2},{6,8},{8,6},{10,12},{12,10},{14,16},{16,14},{18... | collective-permute-start | bytes 2359304 | tf_op jit(solution)/shard_map/ppermute | solution.py:499
  46.4 27.3 %collective-permute-start.21 = (bf16[2,256,768]{2,1,0:T(8,128)(2,1)S(1)}, bf16[2,256,768]{2,1,0:T(8,128)(2,1)S(1)}, u32[]{:S(2)}, u32[]{:S(2)}) collective-permute-start(bf16[2,256,768]{2,1,0:T(8,128)(2,1)S(1)} %get-tuple-element.81), channel_id=1, source_target_pairs={{0,2},{2,0},{4,6},{6,4},{8,10},{10,8},{12,14},{14,12},{16,18},{18,... | collective-permute-start | bytes 2359304 | tf_op jit(solution)/shard_map/ppermute | solution.py:500
  54.1 1.3 %collective-permute-start.15 = (bf16[24,1536]{1,0:T(8,128)(2,1)S(1)}, bf16[24,1536]{1,0:T(8,128)(2,1)S(1)}, u32[]{:S(2)}, u32[]{:S(2)}) collective-permute-start(bf16[24,1536]{1,0:T(8,128)(2,1)S(1)} %get-tuple-element.75), channel_id=1, source_target_pairs={{0,2},{2,0},{4,6},{6,4},{8,10},{10,8},{12,14},{14,12},{16,18},{18,... | collective-permute-start | bytes 221192 | tf_op jit(solution)/shard_map/ppermute | solution.py:459
  55.4 8.0 %collective-permute-start.18 = (bf16[24,1536]{1,0:T(8,128)(2,1)S(1)}, bf16[24,1536]{1,0:T(8,128)(2,1)S(1)}, u32[]{:S(2)}, u32[]{:S(2)}) collective-permute-start(bf16[24,1536]{1,0:T(8,128)(2,1)S(1)} %add.19), channel_id=1, source_target_pairs={{0,24},{2,26},{4,28},{6,30},{8,16},{10,18},{12,20},{14,22},{16,8},... | collective-permute-start | bytes 221192 | tf_op jit(solution)/shard_map/ppermute | solution.py:459
  60.4 6.5 %collective-permute-start.17 = (bf16[24,1536]{1,0:T(8,128)(2,1)S(1)}, bf16[24,1536]{1,0:T(8,128)(2,1)S(1)}, u32[]{:S(2)}, u32[]{:S(2)}) collective-permute-start(bf16[24,1536]{1,0:T(8,128)(2,1)S(1)} %add.19), channel_id=1, source_target_pairs={{0,16},{2,18},{4,20},{6,22},{8,24},{10,26},{12,28},{14,30},{16,0},... | collective-permute-start | bytes 221192 | tf_op jit(solution)/shard_map/ppermute | solution.py:459
  60.4 6.5 %collective-permute-start.16 = (bf16[24,1536]{1,0:T(8,128)(2,1)S(1)}, bf16[24,1536]{1,0:T(8,128)(2,1)S(1)}, u32[]{:S(2)}, u32[]{:S(2)}) collective-permute-start(bf16[24,1536]{1,0:T(8,128)(2,1)S(1)} %add.19), channel_id=1, source_target_pairs={{0,8},{2,10},{4,12},{6,14},{8,0},{10,2},{12,4},{14,6},{16,24},{18,... | collective-permute-start | bytes 221192 | tf_op jit(solution)/shard_map/ppermute | solution.py:459
  63.4 10.3 %collective-permute-start.19 = (bf16[2,128,768]{2,1,0:T(8,128)(2,1)S(1)}, bf16[2,128,768]{2,1,0:T(8,128)(2,1)S(1)}, u32[]{:S(2)}, u32[]{:S(2)}) collective-permute-start(bf16[2,128,768]{2,1,0:T(8,128)(2,1)S(1)} %get-tuple-element.76), channel_id=1, source_target_pairs={{0,1},{1,0},{2,3},{3,2},{4,5},{5,4},{6,7},{7,6},{8,9},{9,8},{10,11... | collective-permute-start | bytes 1179656 | tf_op jit(solution)/shard_map/ppermute | solution.py:354
  66.9 16.4 %collective-permute-start.10 = (bf16[2,256,768]{2,1,0:T(8,128)(2,1)S(1)}, bf16[2,256,768]{2,1,0:T(8,128)(2,1)S(1)}, u32[]{:S(2)}, u32[]{:S(2)}) collective-permute-start(bf16[2,256,768]{2,1,0:T(8,128)(2,1)S(1)} %get-tuple-element.63), channel_id=1, source_target_pairs={{0,2},{2,0},{4,6},{6,4},{8,10},{10,8},{12,14},{14,12},{16,18},{18,... | collective-permute-start | bytes 2359304 | tf_op jit(solution)/shard_map/ppermute | solution.py:500
  67.0 13.8 %collective-permute-start.12 = (bf16[2,128,768]{2,1,0:T(8,128)(2,1)S(1)}, bf16[2,128,768]{2,1,0:T(8,128)(2,1)S(1)}, u32[]{:S(2)}, u32[]{:S(2)}) collective-permute-start(bf16[2,128,768]{2,1,0:T(8,128)(2,1)S(1)} %get-tuple-element.69), channel_id=1, source_target_pairs={{0,30},{2,4},{4,2},{6,8},{8,6},{10,12},{12,10},{14,16},{16,14},{18... | collective-permute-start | bytes 1179656 | tf_op jit(solution)/shard_map/ppermute | solution.py:499
  73.9 9.5 %collective-permute-start.22 = (bf16[2,128,768]{2,1,0:T(8,128)(2,1)S(1)}, bf16[2,128,768]{2,1,0:T(8,128)(2,1)S(1)}, u32[]{:S(2)}, u32[]{:S(2)}) collective-permute-start(bf16[2,128,768]{2,1,0:T(8,128)(2,1)S(1)} %far_sum.2), channel_id=1, source_target_pairs={{0,1},{1,0},{2,3},{3,2},{4,5},{5,4},{6,7},{7,6},{8,9},{9,8},{10,11... | collective-permute-start | bytes 1179656 | tf_op jit(solution)/shard_map/ppermute | solution.py:354
  75.4 5.3 %collective-permute-start.20 = (bf16[24,1536]{1,0:T(8,128)(2,1)S(1)}, bf16[24,1536]{1,0:T(8,128)(2,1)S(1)}, u32[]{:S(2)}, u32[]{:S(2)}) collective-permute-start(bf16[24,1536]{1,0:T(8,128)(2,1)S(1)} %add_add_fusion), channel_id=1, source_target_pairs={{0,4},{2,6},{4,0},{6,2},{8,12},{10,14},{12,8},{14,10},{16,20},{18,... | collective-permute-start | bytes 221192 | tf_op jit(solution)/shard_map/ppermute | solution.py:459
  80.7 12.9 %collective-permute-start.13 = (bf16[2,128,768]{2,1,0:T(8,128)(2,1)S(1)}, bf16[2,128,768]{2,1,0:T(8,128)(2,1)S(1)}, u32[]{:S(2)}, u32[]{:S(2)}) collective-permute-start(bf16[2,128,768]{2,1,0:T(8,128)(2,1)S(1)} %get-tuple-element.70), channel_id=1, source_target_pairs={{0,30},{2,4},{4,2},{6,8},{8,6},{10,12},{12,10},{14,16},{16,14},{18... | collective-permute-start | bytes 1179656 | tf_op jit(solution)/shard_map/ppermute | solution.py:510
  83.5 10.2 %collective-permute-start.23 = (bf16[2,128,768]{2,1,0:T(8,128)(2,1)S(1)}, bf16[2,128,768]{2,1,0:T(8,128)(2,1)S(1)}, u32[]{:S(2)}, u32[]{:S(2)}) collective-permute-start(bf16[2,128,768]{2,1,0:T(8,128)(2,1)S(1)} %far_sum.3), channel_id=1, source_target_pairs={{0,1},{1,0},{2,3},{3,2},{4,5},{5,4},{6,7},{7,6},{8,9},{9,8},{10,11... | collective-permute-start | bytes 1179656 | tf_op jit(solution)/shard_map/ppermute | solution.py:354
  85.0 8.6 %collective-permute-start.24 = (bf16[24,1536]{1,0:T(8,128)(2,1)S(1)}, bf16[24,1536]{1,0:T(8,128)(2,1)S(1)}, u32[]{:S(2)}, u32[]{:S(2)}) collective-permute-start(bf16[24,1536]{1,0:T(8,128)(2,1)S(1)} %add.23.refs_3_), channel_id=1, source_target_pairs={{0,1},{1,0},{2,3},{3,2},{4,5},{5,4},{6,7},{7,6},{8,9},{9,8},{10,11... | collective-permute-start | bytes 221192 | tf_op jit(solution)/shard_map/ppermute | solution.py:522
